TPU v7x, 32 devices: a whole 2x2x4 slice. The times are simulated.
32 devices in a mesh: fsdp: 4 (over y, x), ctx: 4 (over z), tp: 2 (over core).
Axes of the slice: x: 2, y: 2, z: 4, core: 2. Of those that a mesh axis runs over, the one named last changes fastest.
Arguments:
- inputs: bfloat16 [8, 1024, 2048], P('fsdp', 'ctx'), may hold values from -6 to 6
- lengths: int32 [8], P('fsdp'), may hold values from 256 to 1024, as said below
- cotangent: bfloat16 [8, 1024, 2048], P('fsdp', 'ctx'), may hold values from -6 to 6
- norm1_gain: bfloat16 [2048], P(('fsdp', 'ctx')), may hold values from 0.5 to 1.5
- w_query: bfloat16 [2048, 2048], P(('fsdp', 'ctx'), 'tp'), may hold values from -0.5 to 0.5
- w_key: bfloat16 [2048, 512], P(('fsdp', 'ctx'), 'tp'), may hold values from -0.5 to 0.5
- w_value: bfloat16 [2048, 512], P(('fsdp', 'ctx'), 'tp'), may hold values from -0.125 to 0.125
- w_out: bfloat16 [2048, 2048], P(('fsdp', 'ctx'), 'tp'), may hold values from -1 to 1
- norm2_gain: bfloat16 [2048], P(('fsdp', 'ctx')), may hold values from 0.5 to 1.5
- w_gate: bfloat16 [2048, 8192], P(('fsdp', 'ctx'), 'tp'), may hold values from -0.125 to 0.125
- w_up: bfloat16 [2048, 8192], P(('fsdp', 'ctx'), 'tp'), may hold values from -0.125 to 0.125
- w_down: bfloat16 [2048, 8192], P(('fsdp', 'ctx'), 'tp'), may hold values from -0.25 to 0.25
Outputs:
- output: bfloat16 [8, 1024, 2048], P('fsdp', 'ctx')
- input_grad: bfloat16 [8, 1024, 2048], P('fsdp', 'ctx')
- norm1_gain_grad: float32 [2048], P(('fsdp', 'ctx'))
- w_query_grad: float32 [2048, 2048], P(('fsdp', 'ctx'), 'tp')
- w_key_grad: float32 [2048, 512], P(('fsdp', 'ctx'), 'tp')
- w_value_grad: float32 [2048, 512], P(('fsdp', 'ctx'), 'tp')
- w_out_grad: float32 [2048, 2048], P(('fsdp', 'ctx'), 'tp')
- norm2_gain_grad: float32 [2048], P(('fsdp', 'ctx'))
- w_gate_grad: float32 [2048, 8192], P(('fsdp', 'ctx'), 'tp')
- w_up_grad: float32 [2048, 8192], P(('fsdp', 'ctx'), 'tp')
- w_down_grad: float32 [2048, 8192], P(('fsdp', 'ctx'), 'tp')
Inputs may be any that keep to these rules, and one draw needn't show every extreme that they name: `lengths`: in each aligned group of 2 sequences at least one has length 1024.
All inputs are finite; a program needn't handle non-finite values.
Results may differ from a plain program's by a relative error of at most 0.015.
Values may be sent and summed in bfloat16 or wider, within the bound.
A program may use at most 256 MiB of HBM per device.

v0:
```python
from functools import partial

import jax
import jax.numpy as jnp
from jax import lax
from jax.sharding import PartitionSpec as P

HD = 64


norm_eps = 1e-05
residual_scale = 0.22
score_scale = 1.0 / 64.0
rope_base = 10000000.0
masked_score = -1e30


def rope_tables(positions, head_dim):
    half_dim = head_dim // 2
    frequency = rope_base ** (-(jnp.arange(half_dim, dtype=jnp.float32) * 2.0) / head_dim)
    angles = positions.astype(jnp.float32)[:, None] * frequency[None, :]
    return (
        jnp.concatenate([jnp.cos(angles), jnp.cos(angles)], -1),
        jnp.concatenate([jnp.sin(angles), jnp.sin(angles)], -1),
    )


def rotate(values_in, cosines, sines):
    half_dim = values_in.shape[-1] // 2
    turned = jnp.concatenate([-values_in[..., half_dim:], values_in[..., :half_dim]], -1)
    return values_in * cosines + turned * sines


def unrotate(grad_in, cosines, sines):
    half_dim = grad_in.shape[-1] // 2
    scaled = grad_in * sines
    return grad_in * cosines + jnp.concatenate(
        [scaled[..., half_dim:], -scaled[..., :half_dim]], -1
    )


def rms_scale(values_in):
    return lax.rsqrt(jnp.mean(values_in * values_in, -1, keepdims=True) + norm_eps)


def norm_back(grad_normed, values_in, scale, gain):
    scaled_grad = grad_normed * gain
    return scale * scaled_grad - values_in * scale**3 * jnp.mean(
        scaled_grad * values_in, -1, keepdims=True
    )


def masked_scores(grouped_query_rows, key_row_block, key_mask):
    scores = (
        jnp.einsum(
            "sqgd,skd->sgqk", grouped_query_rows, key_row_block, preferred_element_type=jnp.float32
        )
        * score_scale
    )
    return jnp.where(key_mask[:, None], scores, masked_score)


def attend_forward(block_item, key_mask):
    grouped_query_rows, key_row_block, value_row_block = block_item
    scores = masked_scores(grouped_query_rows, key_row_block, key_mask)
    top_score = jnp.max(scores, -1, keepdims=True)
    exp_scores = jnp.exp(scores - top_score)
    total_mass = jnp.sum(exp_scores, -1, keepdims=True)
    probs_low = (exp_scores / total_mass).astype(jnp.bfloat16)
    head_output = jnp.einsum(
        "sgqk,skd->sqgd", probs_low, value_row_block, preferred_element_type=jnp.float32
    )
    return (head_output.astype(jnp.bfloat16), top_score + jnp.log(total_mass))


def attend_backward(block_item, key_mask):
    grouped_query_rows, key_row_block, value_row_block, out_grad, log_mass = block_item
    scores = masked_scores(grouped_query_rows, key_row_block, key_mask)
    attention_probabilities = jnp.exp(scores - log_mass)
    probs_low = attention_probabilities.astype(jnp.bfloat16)
    value_grad = jnp.einsum(
        "sgqk,sqgd->skd", probs_low, out_grad, preferred_element_type=jnp.float32
    )
    probs_grad = jnp.einsum(
        "sqgd,skd->sgqk", out_grad, value_row_block, preferred_element_type=jnp.float32
    )
    score_grad = (
        attention_probabilities
        * (probs_grad - jnp.sum(attention_probabilities * probs_grad, -1, keepdims=True))
    ).astype(jnp.bfloat16)
    query_grad = (
        jnp.einsum("sgqk,skd->sqgd", score_grad, key_row_block, preferred_element_type=jnp.float32)
        * score_scale
    )
    key_grad = (
        jnp.einsum(
            "sgqk,sqgd->skd", score_grad, grouped_query_rows, preferred_element_type=jnp.float32
        )
        * score_scale
    )
    return (query_grad, key_grad, value_grad)


def local(
    inputs,
    lengths,
    cotangent,
    norm1_gain,
    w_query,
    w_key,
    w_value,
    w_out,
    norm2_gain,
    w_gate,
    w_up,
    w_down,
):
    seq_count, local_rows, model_width = inputs.shape
    full_rows = local_rows * lax.axis_size("ctx")
    positions = lax.axis_index("ctx") * local_rows + jnp.arange(local_rows, dtype=jnp.int32)
    key_places = jnp.arange(full_rows, dtype=jnp.int32)
    valid_rows = (positions[None, :] < lengths[:, None]).astype(jnp.float32)[..., None]
    key_mask = (key_places[None, None, :] <= positions[None, :, None]) & (
        key_places[None, None, :] < lengths[:, None, None]
    )
    cosines, sines = rope_tables(positions, HD)
    head_cos = cosines[None, :, None, :]
    head_sin = sines[None, :, None, :]
    attn_set = (
        lax.all_gather(norm1_gain, ("fsdp", "ctx"), axis=0, tiled=True),
        lax.all_gather(w_query, ("fsdp", "ctx"), axis=0, tiled=True),
        lax.all_gather(w_key, ("fsdp", "ctx"), axis=0, tiled=True),
        lax.all_gather(w_value, ("fsdp", "ctx"), axis=0, tiled=True),
        lax.all_gather(w_out, ("fsdp", "ctx"), axis=0, tiled=True),
    )
    gain_one, query_full, key_full, value_full, out_full = attn_set
    query_heads = query_full.shape[1] // HD
    kv_heads = key_full.shape[1] // HD
    group_size = query_heads // kv_heads
    layer_in = inputs.astype(jnp.float32)
    first_rms = rms_scale(layer_in)
    first_normed = (layer_in * first_rms * gain_one.astype(jnp.float32)).astype(jnp.bfloat16)
    query_lin = jnp.dot(first_normed, query_full, preferred_element_type=jnp.float32).reshape(
        seq_count, local_rows, query_heads, HD
    )
    query_rot = rotate(query_lin, head_cos, head_sin).astype(jnp.bfloat16)
    key_lin = jnp.dot(first_normed, key_full, preferred_element_type=jnp.float32).reshape(
        seq_count, local_rows, kv_heads, HD
    )
    key_rot = (
        rotate(key_lin, head_cos, head_sin)
        .astype(jnp.bfloat16)
        .reshape(seq_count, local_rows, kv_heads * HD)
    )
    value_low = jnp.dot(first_normed, value_full, preferred_element_type=jnp.float32).astype(
        jnp.bfloat16
    )
    key_all, value_all = (
        lax.all_gather(key_rot, "ctx", axis=1, tiled=True),
        lax.all_gather(value_low, "ctx", axis=1, tiled=True),
    )
    key_split = jnp.moveaxis(key_all.reshape(seq_count, full_rows, kv_heads, HD), 2, 0)
    value_split = jnp.moveaxis(value_all.reshape(seq_count, full_rows, kv_heads, HD), 2, 0)
    query_split = jnp.moveaxis(
        query_rot.reshape(seq_count, local_rows, kv_heads, group_size, HD), 2, 0
    )
    head_output, log_mass = lax.map(
        partial(attend_forward, key_mask=key_mask), (query_split, key_split, value_split)
    )
    attended = jnp.moveaxis(head_output, 0, 2).reshape(seq_count, local_rows, query_heads * HD)
    attn_part = jnp.einsum("sqj,dj->sqd", attended, out_full, preferred_element_type=jnp.float32)
    attn_branch = lax.psum(attn_part, "tp")
    middle = layer_in + residual_scale * attn_branch
    mlp_set = (
        lax.all_gather(norm2_gain, ("fsdp", "ctx"), axis=0, tiled=True),
        lax.all_gather(w_gate, ("fsdp", "ctx"), axis=0, tiled=True),
        lax.all_gather(w_up, ("fsdp", "ctx"), axis=0, tiled=True),
        lax.all_gather(w_down, ("fsdp", "ctx"), axis=0, tiled=True),
    )
    gain_two, gate_full, up_full, down_full = mlp_set
    second_rms = rms_scale(middle)
    second_normed = (middle * second_rms * gain_two.astype(jnp.float32)).astype(jnp.bfloat16)
    gate_lin = jnp.dot(second_normed, gate_full, preferred_element_type=jnp.float32)
    up_lin = jnp.dot(second_normed, up_full, preferred_element_type=jnp.float32)
    gate_sig = jax.nn.sigmoid(gate_lin)
    gate_act = gate_lin * gate_sig
    hidden = (gate_act * up_lin).astype(jnp.bfloat16)
    ff_part = jnp.einsum("sqf,df->sqd", hidden, down_full, preferred_element_type=jnp.float32)
    ff_branch = lax.psum(ff_part.astype(jnp.bfloat16), "tp").astype(jnp.float32)
    output = (valid_rows * (middle + residual_scale * ff_branch)).astype(jnp.bfloat16)
    back = cotangent.astype(jnp.float32) * valid_rows
    mlp_back = (
        lax.all_gather(norm2_gain, ("fsdp", "ctx"), axis=0, tiled=True),
        lax.all_gather(w_gate, ("fsdp", "ctx"), axis=0, tiled=True),
        lax.all_gather(w_up, ("fsdp", "ctx"), axis=0, tiled=True),
        lax.all_gather(w_down, ("fsdp", "ctx"), axis=0, tiled=True),
    )
    gain_two, gate_full, up_full, down_full = mlp_back
    ff_grad = (residual_scale * back).astype(jnp.bfloat16)
    down_term = jnp.einsum("sqd,sqf->df", ff_grad, hidden, preferred_element_type=jnp.float32)
    hidden_grad = jnp.einsum("sqd,df->sqf", ff_grad, down_full, preferred_element_type=jnp.float32)
    gate_grad = (hidden_grad * up_lin * gate_sig * (1.0 + gate_lin * (1.0 - gate_sig))).astype(
        jnp.bfloat16
    )
    up_grad = (hidden_grad * gate_act).astype(jnp.bfloat16)
    gate_term = jnp.einsum(
        "sqd,sqf->df", second_normed, gate_grad, preferred_element_type=jnp.float32
    )
    up_term = jnp.einsum("sqd,sqf->df", second_normed, up_grad, preferred_element_type=jnp.float32)
    second_part = jnp.einsum(
        "sqf,df->sqd", gate_grad, gate_full, preferred_element_type=jnp.float32
    ) + jnp.einsum("sqf,df->sqd", up_grad, up_full, preferred_element_type=jnp.float32)
    second_grad = lax.psum(second_part, "tp")
    gain_two_term = jnp.sum(second_grad * middle * second_rms, axis=(0, 1))
    middle_grad = back + norm_back(second_grad, middle, second_rms, gain_two.astype(jnp.float32))
    mlp_grads = (
        lax.psum_scatter(gain_two_term, ("fsdp", "ctx"), scatter_dimension=0, tiled=True),
        lax.psum_scatter(gate_term, ("fsdp", "ctx"), scatter_dimension=0, tiled=True),
        lax.psum_scatter(up_term, ("fsdp", "ctx"), scatter_dimension=0, tiled=True),
        lax.psum_scatter(down_term, ("fsdp", "ctx"), scatter_dimension=0, tiled=True),
    )
    attn_back = (
        lax.all_gather(norm1_gain, ("fsdp", "ctx"), axis=0, tiled=True),
        lax.all_gather(w_query, ("fsdp", "ctx"), axis=0, tiled=True),
        lax.all_gather(w_key, ("fsdp", "ctx"), axis=0, tiled=True),
        lax.all_gather(w_value, ("fsdp", "ctx"), axis=0, tiled=True),
        lax.all_gather(w_out, ("fsdp", "ctx"), axis=0, tiled=True),
    )
    gain_one, query_full, key_full, value_full, out_full = attn_back
    attn_grad = (residual_scale * middle_grad).astype(jnp.bfloat16)
    out_term = jnp.einsum("sqd,sqj->dj", attn_grad, attended, preferred_element_type=jnp.float32)
    attended_grad = jnp.einsum(
        "sqd,dj->sqj", attn_grad, out_full, preferred_element_type=jnp.float32
    ).astype(jnp.bfloat16)
    grad_split = jnp.moveaxis(
        attended_grad.reshape(seq_count, local_rows, kv_heads, group_size, HD), 2, 0
    )
    query_back, key_back, value_back = lax.map(
        partial(attend_backward, key_mask=key_mask),
        (query_split, key_split, value_split, grad_split, log_mass),
    )
    query_back = jnp.moveaxis(query_back, 0, 2).reshape(seq_count, local_rows, query_heads, HD)
    query_grad = (
        unrotate(query_back, head_cos, head_sin)
        .astype(jnp.bfloat16)
        .reshape(seq_count, local_rows, query_heads * HD)
    )
    key_spread = jnp.moveaxis(key_back, 0, 2).reshape(seq_count, full_rows, kv_heads * HD)
    value_spread = jnp.moveaxis(value_back, 0, 2).reshape(seq_count, full_rows, kv_heads * HD)
    key_own, value_own = (
        lax.psum_scatter(key_spread, "ctx", scatter_dimension=1, tiled=True),
        lax.psum_scatter(value_spread, "ctx", scatter_dimension=1, tiled=True),
    )
    key_grad = (
        unrotate(key_own.reshape(seq_count, local_rows, kv_heads, HD), head_cos, head_sin)
        .astype(jnp.bfloat16)
        .reshape(seq_count, local_rows, kv_heads * HD)
    )
    value_grad = value_own.astype(jnp.bfloat16)
    query_term = jnp.einsum(
        "sqd,sqj->dj", first_normed, query_grad, preferred_element_type=jnp.float32
    )
    key_term = jnp.einsum("sqd,sqj->dj", first_normed, key_grad, preferred_element_type=jnp.float32)
    value_term = jnp.einsum(
        "sqd,sqj->dj", first_normed, value_grad, preferred_element_type=jnp.float32
    )
    first_part = jnp.einsum(
        "sqj,dj->sqd", query_grad, query_full, preferred_element_type=jnp.float32
    )
    first_part = first_part + jnp.einsum(
        "sqj,dj->sqd", key_grad, key_full, preferred_element_type=jnp.float32
    )
    first_part = first_part + jnp.einsum(
        "sqj,dj->sqd", value_grad, value_full, preferred_element_type=jnp.float32
    )
    first_grad = lax.psum(first_part.astype(jnp.bfloat16), "tp").astype(jnp.float32)
    gain_one_term = jnp.sum(first_grad * layer_in * first_rms, axis=(0, 1))
    input_grad = (
        middle_grad + norm_back(first_grad, layer_in, first_rms, gain_one.astype(jnp.float32))
    ).astype(jnp.bfloat16)
    attn_grads = (
        lax.psum_scatter(gain_one_term, ("fsdp", "ctx"), scatter_dimension=0, tiled=True),
        lax.psum_scatter(query_term, ("fsdp", "ctx"), scatter_dimension=0, tiled=True),
        lax.psum_scatter(key_term, ("fsdp", "ctx"), scatter_dimension=0, tiled=True),
        lax.psum_scatter(value_term, ("fsdp", "ctx"), scatter_dimension=0, tiled=True),
        lax.psum_scatter(out_term, ("fsdp", "ctx"), scatter_dimension=0, tiled=True),
    )
    return (
        output,
        input_grad,
        attn_grads[0],
        attn_grads[1],
        attn_grads[2],
        attn_grads[3],
        attn_grads[4],
        mlp_grads[0],
        mlp_grads[1],
        mlp_grads[2],
        mlp_grads[3],
    )


def solution(mesh):
    placed = (
        P("fsdp", "ctx", None),
        P("fsdp"),
        P("fsdp", "ctx", None),
        P(("fsdp", "ctx")),
        P(("fsdp", "ctx"), "tp"),
        P(("fsdp", "ctx"), "tp"),
        P(("fsdp", "ctx"), "tp"),
        P(("fsdp", "ctx"), "tp"),
        P(("fsdp", "ctx")),
        P(("fsdp", "ctx"), "tp"),
        P(("fsdp", "ctx"), "tp"),
        P(("fsdp", "ctx"), "tp"),
    )
    return jax.shard_map(
        local,
        mesh=mesh,
        in_specs=placed,
        out_specs=(
            P("fsdp", "ctx", None),
            P("fsdp", "ctx", None),
            P(("fsdp", "ctx")),
            P(("fsdp", "ctx"), "tp"),
            P(("fsdp", "ctx"), "tp"),
            P(("fsdp", "ctx"), "tp"),
            P(("fsdp", "ctx"), "tp"),
            P(("fsdp", "ctx")),
            P(("fsdp", "ctx"), "tp"),
            P(("fsdp", "ctx"), "tp"),
            P(("fsdp", "ctx"), "tp"),
        ),
        check_vma=False,
    )
```

profile of v0, /device:TPU:16, one launch (start us, length us, event | category | flops | bytes accessed | tf_op | source)
XLA Modules:
  0.0 3847.4 jit_solution(15046611783011281480)
XLA Ops:
  9.6 36.2 all-gather
  69.2 50.6 %all-gather.16.cloned.1.call-done = bf16[2048,256]{0,1:T(8,128)(2,1)} async-done(((bf16[128,256]{0,1:T(8,128)(2,1)}), bf16[2048,256]{0,1:T(8,128)(2,1)}) %all-gather.16.cloned.1.call-update) | async-done | bytes 1048592 | tf_op jit(solution)/shard_map/all_gather | solution.py:132
  125.6 23.8 all-gather.14.cloned.1.call-done
  152.0 27.0 all-gather.18.cloned.1.call-done
  180.3 77.7 %all-gather.20.cloned.1.call-done = bf16[2048,1024]{1,0:T(8,128)(2,1)} async-done(((bf16[128,1024]{1,0:T(8,128)(2,1)}), bf16[2048,1024]{1,0:T(8,128)(2,1)}) %all-gather.20.cloned.1.call-update) | async-done | bytes 4194320 | tf_op jit(solution)/shard_map/all_gather | solution.py:131
  264.6 36.8 while.28
  301.4 33.7 all-gather.22.cloned.1.call-done
  344.2 34.0 all-gather.1
  383.7 181.1 %all-gather.26.cloned.1.call-done = bf16[2048,4096]{1,0:T(8,128)(2,1)} async-done(((bf16[128,4096]{1,0:T(8,128)(2,1)}), bf16[2048,4096]{1,0:T(8,128)(2,1)}) %all-gather.26.cloned.1.call-update) | async-done | bytes 16777232 | tf_op jit(solution)/shard_map/all_gather | solution.py:177
  579.4 178.4 %all-gather.28.cloned.1.call-done = bf16[2048,4096]{1,0:T(8,128)(2,1)} async-done(((bf16[128,4096]{1,0:T(8,128)(2,1)}), bf16[2048,4096]{1,0:T(8,128)(2,1)}) %all-gather.28.cloned.1.call-update) | async-done | bytes 16777232 | tf_op jit(solution)/shard_map/all_gather | solution.py:178
  772.8 177.7 %all-gather.24.cloned.1.call-done = bf16[2048,4096]{1,0:T(8,128)(2,1)} async-done(((bf16[128,4096]{1,0:T(8,128)(2,1)}), bf16[2048,4096]{1,0:T(8,128)(2,1)}) %all-gather.24.cloned.1.call-update) | async-done | bytes 16777232 | tf_op jit(solution)/shard_map/all_gather | solution.py:176
  950.6 23.3 multiply_convert_fusion.1
  1001.5 27.9 all-reduce.10.cloned.1.call-done
  1042.9 60.2 %while.29 = (s32[]{:T(128)}, f32[4,2,256,4,64]{2,4,3,0,1:T(8,128)}, f32[4,2,1024,64]{2,3,1,0:T(8,128)}, f32[4,2,1024,64]{2,3,0,1:T(8,128)}, bf16[4,2,1024,64]{2,...) while((s32[]{:T(128)}, f32[4,2,256,4,64]{2,4,3,0,1:T(8,128)}, ...), condition=%wide.region_12.13_spmd.clone, body=%wide.region_10.12_spmd.clone.sunk | while | flops 1374418944 | bytes 72940696 | solution.py:238
  1129.6 21.0 reduce-scatter.10.cloned.1.call-done
  1156.4 40.3 %reduce-scatter.12.cloned.1.call-done = f32[2,256,256]{1,2,0:T(8,128)} async-done(((f32[2,1024,256]{1,2,0:T(8,128)}), f32[2,256,256]{1,2,0:T(8,128)}) %reduce-scatter.12.cloned.1.call-update) | async-done | bytes 524304 | tf_op jit(solution)/shard_map/reduce_scatter | solution.py:252
  1225.8 18.4 convolution_bitcast_fusion.3
  1286.3 72.3 %all-reduce.2 = (f32[2048]{0:T(1024)S(1)}, f32[2048]{0:T(1024)S(1)}) all-reduce(f32[2048]{0:T(1024)S(1)} %get-tuple-element.194, f32[2048]{0:T(1024)S(1)} %copy-done.25), channel_id=4, replica_groups=mesh['fsdp'=4,'ctx'=4,'tp'=2] {'fsdp','ctx'}, use_global_device_ids=true, to_apply=%region_18.19.clone | all-reduce | flops 4096 | bytes 32768
  1367.4 30.7 reduce-scatter.18.cloned.1.call-done
  1398.1 184.6 %reduce-scatter.14.cloned.1.call-done = f32[128,1024]{1,0:T(8,128)} async-done(((f32[2048,1024]{1,0:T(8,128)}), f32[128,1024]{1,0:T(8,128)}) %reduce-scatter.14.cloned.1.call-update) | async-done | bytes 524304 | tf_op jit(solution)/shard_map/reduce_scatter | solution.py:283
  1582.6 182.7 %reduce-scatter.20.cloned.1.call-done = f32[128,1024]{1,0:T(8,128)} async-done(((f32[2048,1024]{1,0:T(8,128)}), f32[128,1024]{1,0:T(8,128)}) %reduce-scatter.20.cloned.1.call-update) | async-done | bytes 524304 | tf_op jit(solution)/shard_map/reduce_scatter | solution.py:286
  1765.3 691.7 %reduce-scatter.22.cloned.1.call-done = f32[128,4096]{1,0:T(8,128)} async-done(((f32[2048,4096]{1,0:T(8,128)}), f32[128,4096]{1,0:T(8,128)}) %reduce-scatter.22.cloned.1.call-update) | async-done | bytes 2097168 | tf_op jit(solution)/shard_map/reduce_scatter | solution.py:218
  2457.0 691.6 %reduce-scatter.24.cloned.1.call-done = f32[128,4096]{1,0:T(8,128)} async-done(((f32[2048,4096]{1,0:T(8,128)}), f32[128,4096]{1,0:T(8,128)}) %reduce-scatter.24.cloned.1.call-update) | async-done | bytes 2097168 | tf_op jit(solution)/shard_map/reduce_scatter | solution.py:219
  3148.6 691.7 %reduce-scatter.26.cloned.1.call-done = f32[128,4096]{1,0:T(8,128)} async-done(((f32[2048,4096]{1,0:T(8,128)}), f32[128,4096]{1,0:T(8,128)}) %reduce-scatter.26.cloned.1.call-update) | async-done | bytes 2097168 | tf_op jit(solution)/shard_map/reduce_scatter | solution.py:220
  (258 shorter events, 335.0 us)
Async XLA Ops:
  7.2 58.4 %all-gather.12.cloned.1.call-start = ((), (), s32[]{:S(2)}) async-start(), calls=%async_computation.9 | async-start | bytes 1114112 | tf_op jit(solution)/shard_map/all_gather | solution.py:133
  7.9 111.9 %all-gather.16.cloned.1.call-start = ((), (), s32[]{:S(2)}) async-start(), calls=%async_computation.11 | async-start | bytes 1114112 | tf_op jit(solution)/shard_map/all_gather | solution.py:132
  9.6 139.9 %all-gather.14.cloned.1.call-start = ((), (), s32[]{:S(2)}) async-start(), calls=%async_computation.10 | async-start | bytes 1310720 | tf_op jit(solution)/shard_map/all_gather | solution.py:160
  45.8 212.2 %copy-start.23 = (f32[16,1,128]{2,1,0:T(1,128)}, f32[16,1,128]{2,1,0:T(1,128)S(1)}, u32[]{:S(2)}) copy-start(f32[16,1,128]{2,1,0:T(1,128)S(1)} %convert_element_type.133) | copy-start | bytes 24580
  68.9 110.1 %all-gather.18.cloned.1.call-start = ((), (), s32[]{:S(2)}) async-start(), calls=%async_computation.12 | async-start | bytes 1310720 | tf_op jit(solution)/shard_map/all_gather | solution.py:159
  123.6 134.4 %all-gather.20.cloned.1.call-start = ((), (), s32[]{:S(2)}) async-start(), calls=%async_computation.13 | async-start | bytes 4456448 | tf_op jit(solution)/shard_map/all_gather | solution.py:131
  124.2 210.9 %all-gather.22.cloned.1.call-start = ((), (), s32[]{:S(2)}) async-start(), calls=%async_computation.14 | async-start | bytes 4456448 | tf_op jit(solution)/shard_map/all_gather | solution.py:134
  124.7 253.6 %all-reduce.8.cloned.1.call-start = ((), (), s32[]{:S(2)}) async-start(), calls=%async_computation.15 | async-start | bytes 8388608 | tf_op jit(solution)/shard_map/psum | solution.py:172
  342.1 222.7 %all-gather.26.cloned.1.call-start = ((), (), s32[]{:S(2)}) async-start(), calls=%async_computation.17 | async-start | bytes 17825792 | tf_op jit(solution)/shard_map/all_gather | solution.py:177
  342.8 415.0 %all-gather.28.cloned.1.call-start = ((), (), s32[]{:S(2)}) async-start(), calls=%async_computation.18 | async-start | bytes 17825792 | tf_op jit(solution)/shard_map/all_gather | solution.py:178
  343.6 607.0 %all-gather.24.cloned.1.call-start = ((), (), s32[]{:S(2)}) async-start(), calls=%async_computation.16 | async-start | bytes 17825792 | tf_op jit(solution)/shard_map/all_gather | solution.py:176
  344.1 685.2 %all-reduce.10.cloned.1.call-start = ((), (), s32[]{:S(2)}) async-start(), calls=%async_computation.19 | async-start | bytes 8388608 | tf_op jit(solution)/shard_map/psum | solution.py:213
  378.3 656.3 %copy-start.28 = (f32[2,256]{1,0:T(2,128)}, f32[2,256]{1,0:T(2,128)S(1)}, u32[]{:S(2)}) copy-start(f32[2,256]{1,0:T(2,128)S(1)} %compare_convert_fusion) | copy-start | bytes 6148
  383.7 566.9 %copy-start.13 = (bf16[2,256,2048]{2,1,0:T(8,128)(2,1)}, bf16[2,256,2048]{2,1,0:T(8,128)(2,1)S(1)}, u32[]{:S(2)}) copy-start(bf16[2,256,2048]{2,1,0:T(8,128)(2,1)S(1)} %multiply_convert_fusion.6) | copy-start | bytes 6291460
  1001.4 149.1 %reduce-scatter.10.cloned.1.call-start = ((), (), s32[]{:S(2)}) async-start(), calls=%async_computation.20 | async-start | bytes 2621440 | tf_op jit(solution)/shard_map/reduce_scatter | solution.py:251
  1106.3 90.5 %reduce-scatter.12.cloned.1.call-start = ((), (), s32[]{:S(2)}) async-start(), calls=%async_computation.21 | async-start | bytes 2621440 | tf_op jit(solution)/shard_map/reduce_scatter | solution.py:252
  1107.0 176.1 %all-reduce.12.cloned.1.call-start = ((), (), s32[]{:S(2)}) async-start(), calls=%async_computation.29 | async-start | bytes 8388608 | tf_op jit(solution)/shard_map/psum | solution.py:189
  1202.5 164.9 %reduce-scatter.16.cloned.1.call-start = ((), (), s32[]{:S(2)}) async-start(), calls=%async_computation.23 | async-start | bytes 2228224 | tf_op jit(solution)/shard_map/reduce_scatter | solution.py:284
  1206.4 191.6 %reduce-scatter.18.cloned.1.call-start = ((), (), s32[]{:S(2)}) async-start(), calls=%async_computation.24 | async-start | bytes 2228224 | tf_op jit(solution)/shard_map/reduce_scatter | solution.py:285
  1209.9 372.7 %reduce-scatter.14.cloned.1.call-start = ((), (), s32[]{:S(2)}) async-start(), calls=%async_computation.22 | async-start | bytes 8912896 | tf_op jit(solution)/shard_map/reduce_scatter | solution.py:283
  1216.3 549.0 %reduce-scatter.20.cloned.1.call-start = ((), (), s32[]{:S(2)}) async-start(), calls=%async_computation.25 | async-start | bytes 8912896 | tf_op jit(solution)/shard_map/reduce_scatter | solution.py:286
  1225.8 1231.3 %reduce-scatter.22.cloned.1.call-start = ((), (), s32[]{:S(2)}) async-start(), calls=%async_computation.26 | async-start | bytes 35651584 | tf_op jit(solution)/shard_map/reduce_scatter | solution.py:218
  1244.3 1904.3 %reduce-scatter.24.cloned.1.call-start = ((), (), s32[]{:S(2)}) async-start(), calls=%async_computation.27 | async-start | bytes 35651584 | tf_op jit(solution)/shard_map/reduce_scatter | solution.py:219
  1262.4 2577.9 %reduce-scatter.26.cloned.1.call-start = ((), (), s32[]{:S(2)}) async-start(), calls=%async_computation.28 | async-start | bytes 35651584 | tf_op jit(solution)/shard_map/reduce_scatter | solution.py:220
  (41 other events, 1040.1 us)
Sparse Core Ops, SparseCore 0:
  10.8 54.7 all-gather.11
  68.8 50.9 all-gather.15
  122.0 27.4 all-gather.13
  151.4 27.4 all-gather.17
  181.6 76.4 all-gather.19
  260.6 74.3 all-gather.21
  342.2 27.7 all-reduce.7
  373.1 191.6 all-gather.25
  567.9 189.7 all-gather.27
  760.8 189.7 all-gather.23
  1001.6 27.7 all-reduce.9
  1106.4 44.1 reduce-scatter.9
  1153.5 43.1 reduce-scatter.11
  1202.6 28.7 all-reduce.11
  1234.2 80.6 reduce-scatter.15
  1317.7 80.2 reduce-scatter.17
  1400.9 181.7 reduce-scatter.13
  1585.5 179.7 reduce-scatter.19
  1768.4 688.6 reduce-scatter.21
  2459.9 688.6 reduce-scatter.23
  3151.7 688.6 reduce-scatter.25
where the time goes:
time: 3850 us
  waiting for transfers between devices  3330 us (86%)
  matrix products  274 us (7%)
  blocking collectives  143 us (4%)
  other arithmetic  51.8 us (1%)
    reduce_scatter x1, waiting for transfers between devices, local(): lax.psum_scatter(down_term, ('fsdp', 'ctx'), scatter_dimension=0, tiled=T...  692 us
    reduce_scatter x1, waiting for transfers between devices, local(): lax.psum_scatter(gate_term, ('fsdp', 'ctx'), scatter_dimension=0, tiled=T...  692 us
    reduce_scatter x1, waiting for transfers between devices, local(): lax.psum_scatter(up_term, ('fsdp', 'ctx'), scatter_dimension=0, tiled=True)  692 us
    reduce_scatter x1, waiting for transfers between devices, local(): lax.psum_scatter(query_term, ('fsdp', 'ctx'), scatter_dimension=0, tiled=...  185 us
    reduce_scatter x1, waiting for transfers between devices, local(): lax.psum_scatter(out_term, ('fsdp', 'ctx'), scatter_dimension=0, tiled=True)  183 us
    all_gather x1, waiting for transfers between devices, local(): lax.all_gather(w_up, ('fsdp', 'ctx'), axis=0, tiled=True)  181 us
    all_gather x1, waiting for transfers between devices, local(): lax.all_gather(w_down, ('fsdp', 'ctx'), axis=0, tiled=True)  178 us
    all_gather x1, waiting for transfers between devices, local(): lax.all_gather(w_gate, ('fsdp', 'ctx'), axis=0, tiled=True)  178 us
  transfers between devices with their start and end apart: 21, of which 18 were waited for; matrix products, arithmetic and copies ran while one was open for 5% of the time, Pallas kernels for 0%

commit v1 on v0

v1 whole, which is shorter than its diff:
```python
from functools import partial

import jax
import jax.numpy as jnp
from jax import lax
from jax.sharding import PartitionSpec as P

HD = 64


norm_eps = 1e-05
residual_scale = 0.22
score_scale = 1.0 / 64.0
rope_base = 10000000.0
masked_score = -1e30


def rope_tables(positions, head_dim):
    half_dim = head_dim // 2
    frequency = rope_base ** (-(jnp.arange(half_dim, dtype=jnp.float32) * 2.0) / head_dim)
    angles = positions.astype(jnp.float32)[:, None] * frequency[None, :]
    return (
        jnp.concatenate([jnp.cos(angles), jnp.cos(angles)], -1),
        jnp.concatenate([jnp.sin(angles), jnp.sin(angles)], -1),
    )


def rotate(values_in, cosines, sines):
    half_dim = values_in.shape[-1] // 2
    turned = jnp.concatenate([-values_in[..., half_dim:], values_in[..., :half_dim]], -1)
    return values_in * cosines + turned * sines


def unrotate(grad_in, cosines, sines):
    half_dim = grad_in.shape[-1] // 2
    scaled = grad_in * sines
    return grad_in * cosines + jnp.concatenate(
        [scaled[..., half_dim:], -scaled[..., :half_dim]], -1
    )


def rms_scale(values_in):
    return lax.rsqrt(jnp.mean(values_in * values_in, -1, keepdims=True) + norm_eps)


def norm_back(grad_normed, values_in, scale, gain):
    scaled_grad = grad_normed * gain
    return scale * scaled_grad - values_in * scale**3 * jnp.mean(
        scaled_grad * values_in, -1, keepdims=True
    )


def masked_scores(grouped_query_rows, key_row_block, key_mask):
    scores = (
        jnp.einsum(
            "sqgd,skd->sgqk", grouped_query_rows, key_row_block, preferred_element_type=jnp.float32
        )
        * score_scale
    )
    return jnp.where(key_mask[:, None], scores, masked_score)


def attend_forward(block_item, key_mask):
    grouped_query_rows, key_row_block, value_row_block = block_item
    scores = masked_scores(grouped_query_rows, key_row_block, key_mask)
    top_score = jnp.max(scores, -1, keepdims=True)
    exp_scores = jnp.exp(scores - top_score)
    total_mass = jnp.sum(exp_scores, -1, keepdims=True)
    probs_low = (exp_scores / total_mass).astype(jnp.bfloat16)
    head_output = jnp.einsum(
        "sgqk,skd->sqgd", probs_low, value_row_block, preferred_element_type=jnp.float32
    )
    return (head_output.astype(jnp.bfloat16), top_score + jnp.log(total_mass))


def attend_backward(block_item, key_mask):
    grouped_query_rows, key_row_block, value_row_block, out_grad, log_mass = block_item
    scores = masked_scores(grouped_query_rows, key_row_block, key_mask)
    attention_probabilities = jnp.exp(scores - log_mass)
    probs_low = attention_probabilities.astype(jnp.bfloat16)
    value_grad = jnp.einsum(
        "sgqk,sqgd->skd", probs_low, out_grad, preferred_element_type=jnp.float32
    )
    probs_grad = jnp.einsum(
        "sqgd,skd->sgqk", out_grad, value_row_block, preferred_element_type=jnp.float32
    )
    score_grad = (
        attention_probabilities
        * (probs_grad - jnp.sum(attention_probabilities * probs_grad, -1, keepdims=True))
    ).astype(jnp.bfloat16)
    query_grad = (
        jnp.einsum("sgqk,skd->sqgd", score_grad, key_row_block, preferred_element_type=jnp.float32)
        * score_scale
    )
    key_grad = (
        jnp.einsum(
            "sgqk,sqgd->skd", score_grad, grouped_query_rows, preferred_element_type=jnp.float32
        )
        * score_scale
    )
    return (query_grad, key_grad, value_grad)


def local(
    inputs,
    lengths,
    cotangent,
    norm1_gain,
    w_query,
    w_key,
    w_value,
    w_out,
    norm2_gain,
    w_gate,
    w_up,
    w_down,
):
    seq_count, local_rows, model_width = inputs.shape
    tokens = seq_count * local_rows
    fsdp = lax.axis_size("fsdp")
    ctx = lax.axis_size("ctx")
    full_rows = local_rows * ctx
    shard = w_query.shape[0]
    positions = lax.axis_index("ctx") * local_rows + jnp.arange(local_rows, dtype=jnp.int32)
    key_places = jnp.arange(full_rows, dtype=jnp.int32)
    valid_rows = (positions[None, :] < lengths[:, None]).astype(jnp.float32)[..., None]
    key_mask = (key_places[None, None, :] <= positions[None, :, None]) & (
        key_places[None, None, :] < lengths[:, None, None]
    )
    cosines, sines = rope_tables(positions, HD)
    head_cos = cosines[None, :, None, :]
    head_sin = sines[None, :, None, :]
    query_width = w_query.shape[1]
    kv_width = w_key.shape[1]

    gains = jnp.pad(jnp.stack([norm1_gain, norm2_gain], 1), ((0, 0), (0, 126)))
    qkv_full = lax.all_gather(
        jnp.concatenate([w_query, w_key, w_value, gains], 1), ("fsdp", "ctx"), axis=0, tiled=True
    )
    out_full = lax.all_gather(w_out, ("fsdp", "ctx"), axis=0, tiled=True)
    query_full = qkv_full[:, :query_width]
    key_full = qkv_full[:, query_width : query_width + kv_width]
    value_full = qkv_full[:, query_width + kv_width : query_width + 2 * kv_width]
    gain_one = qkv_full[:, query_width + 2 * kv_width].astype(jnp.float32)
    gain_two = qkv_full[:, query_width + 2 * kv_width + 1].astype(jnp.float32)
    kv_end = query_width + 2 * kv_width

    def spread_units(weight):
        swapped = lax.all_to_all(weight, "fsdp", 1, 0, tiled=True)
        units = swapped.shape[1]
        whole = lax.all_gather(swapped.reshape(fsdp, shard, units), "ctx", axis=1, tiled=True)
        return whole.reshape(model_width, units)

    gate_full = spread_units(w_gate)
    up_full = spread_units(w_up)
    down_full = spread_units(w_down)
    units = gate_full.shape[1]

    back = cotangent.astype(jnp.float32) * valid_rows
    ff_grad = (residual_scale * back).astype(jnp.bfloat16).reshape(tokens, model_width)
    ff_grad_all = lax.all_gather(ff_grad, "fsdp", axis=0, tiled=True)

    query_heads = query_width // HD
    kv_heads = kv_width // HD
    group_size = query_heads // kv_heads
    layer_in = inputs.astype(jnp.float32)
    first_rms = rms_scale(layer_in)
    first_normed = (layer_in * first_rms * gain_one).astype(jnp.bfloat16)
    qkv_lin = jnp.dot(
        first_normed.reshape(tokens, model_width),
        qkv_full[:, :kv_end],
        preferred_element_type=jnp.float32,
    ).reshape(seq_count, local_rows, kv_end)
    query_rot = rotate(
        qkv_lin[..., :query_width].reshape(seq_count, local_rows, query_heads, HD),
        head_cos,
        head_sin,
    ).astype(jnp.bfloat16)
    key_rot = (
        rotate(
            qkv_lin[..., query_width : query_width + kv_width].reshape(
                seq_count, local_rows, kv_heads, HD
            ),
            head_cos,
            head_sin,
        )
        .astype(jnp.bfloat16)
        .reshape(seq_count, local_rows, kv_width)
    )
    value_low = qkv_lin[..., query_width + kv_width :].astype(jnp.bfloat16)
    kv_all = lax.all_gather(
        jnp.concatenate([key_rot, value_low], -1), "ctx", axis=1, tiled=True
    )
    key_split = jnp.moveaxis(
        kv_all[..., :kv_width].reshape(seq_count, full_rows, kv_heads, HD), 2, 0
    )
    value_split = jnp.moveaxis(
        kv_all[..., kv_width:].reshape(seq_count, full_rows, kv_heads, HD), 2, 0
    )
    query_split = jnp.moveaxis(
        query_rot.reshape(seq_count, local_rows, kv_heads, group_size, HD), 2, 0
    )
    head_output, log_mass = lax.map(
        partial(attend_forward, key_mask=key_mask), (query_split, key_split, value_split)
    )
    attended = jnp.moveaxis(head_output, 0, 2).reshape(tokens, query_width)
    attn_part = jnp.einsum("tj,dj->td", attended, out_full, preferred_element_type=jnp.float32)
    attn_branch = lax.psum(attn_part.astype(jnp.bfloat16), "tp").astype(jnp.float32)
    middle = layer_in + residual_scale * attn_branch.reshape(layer_in.shape)

    second_rms = rms_scale(middle)
    second_normed = (middle * second_rms * gain_two).astype(jnp.bfloat16)
    normed_all = lax.all_gather(
        second_normed.reshape(tokens, model_width), "fsdp", axis=0, tiled=True
    )
    gate_lin = jnp.dot(normed_all, gate_full, preferred_element_type=jnp.float32)
    up_lin = jnp.dot(normed_all, up_full, preferred_element_type=jnp.float32)
    gate_sig = jax.nn.sigmoid(gate_lin)
    gate_act = gate_lin * gate_sig
    hidden = (gate_act * up_lin).astype(jnp.bfloat16)

    hidden_grad = jnp.dot(ff_grad_all, down_full, preferred_element_type=jnp.float32)
    gate_grad = (hidden_grad * up_lin * gate_sig * (1.0 + gate_lin * (1.0 - gate_sig))).astype(
        jnp.bfloat16
    )
    up_grad = (hidden_grad * gate_act).astype(jnp.bfloat16)
    second_part = jnp.einsum(
        "tf,df->td", gate_grad, gate_full, preferred_element_type=jnp.float32
    ) + jnp.einsum("tf,df->td", up_grad, up_full, preferred_element_type=jnp.float32)

    def gather_sum(part):
        own = lax.psum_scatter(
            part.astype(jnp.bfloat16), "fsdp", scatter_dimension=0, tiled=True
        )
        return lax.psum(own, "tp").astype(jnp.float32).reshape(layer_in.shape)

    second_grad = gather_sum(second_part)

    def return_units(left, right):
        term = jnp.einsum("td,tf->df", left, right, preferred_element_type=jnp.float32)
        own = lax.psum_scatter(
            term.astype(jnp.bfloat16).reshape(fsdp, ctx * shard, units),
            "ctx",
            scatter_dimension=1,
            tiled=True,
        )
        return lax.all_to_all(
            own.reshape(fsdp * shard, units), "fsdp", 0, 1, tiled=True
        ).astype(jnp.float32)

    w_down_grad = return_units(ff_grad_all, hidden)
    w_gate_grad = return_units(normed_all, gate_grad)
    w_up_grad = return_units(normed_all, up_grad)

    ff_part = jnp.einsum("tf,df->td", hidden, down_full, preferred_element_type=jnp.float32)
    ff_branch = gather_sum(ff_part)
    output = (valid_rows * (middle + residual_scale * ff_branch)).astype(jnp.bfloat16)

    gain_two_term = jnp.sum(second_grad * middle * second_rms, axis=(0, 1))
    middle_grad = back + norm_back(second_grad, middle, second_rms, gain_two)

    attn_grad = (residual_scale * middle_grad).astype(jnp.bfloat16).reshape(tokens, model_width)
    out_term = jnp.einsum("td,tj->dj", attn_grad, attended, preferred_element_type=jnp.float32)
    w_out_grad = lax.psum_scatter(
        out_term.astype(jnp.bfloat16), ("fsdp", "ctx"), scatter_dimension=0, tiled=True
    ).astype(jnp.float32)
    attended_grad = jnp.dot(attn_grad, out_full, preferred_element_type=jnp.float32).astype(
        jnp.bfloat16
    )
    grad_split = jnp.moveaxis(
        attended_grad.reshape(seq_count, local_rows, kv_heads, group_size, HD), 2, 0
    )
    query_back, key_back, value_back = lax.map(
        partial(attend_backward, key_mask=key_mask),
        (query_split, key_split, value_split, grad_split, log_mass),
    )
    query_back = jnp.moveaxis(query_back, 0, 2).reshape(seq_count, local_rows, query_heads, HD)
    query_grad = (
        unrotate(query_back, head_cos, head_sin).astype(jnp.bfloat16).reshape(tokens, query_width)
    )
    key_spread = jnp.moveaxis(key_back, 0, 2).reshape(seq_count, full_rows, kv_width)
    value_spread = jnp.moveaxis(value_back, 0, 2).reshape(seq_count, full_rows, kv_width)
    kv_own = lax.psum_scatter(
        jnp.concatenate([key_spread, value_spread], -1).astype(jnp.bfloat16),
        "ctx",
        scatter_dimension=1,
        tiled=True,
    ).astype(jnp.float32)
    key_grad = (
        unrotate(
            kv_own[..., :kv_width].reshape(seq_count, local_rows, kv_heads, HD), head_cos, head_sin
        )
        .astype(jnp.bfloat16)
        .reshape(tokens, kv_width)
    )
    value_grad = kv_own[..., kv_width:].astype(jnp.bfloat16).reshape(tokens, kv_width)
    qkv_grad = jnp.concatenate([query_grad, key_grad, value_grad], -1)
    qkv_term = jnp.einsum(
        "td,tj->dj",
        first_normed.reshape(tokens, model_width),
        qkv_grad,
        preferred_element_type=jnp.float32,
    )
    first_part = jnp.einsum(
        "tj,dj->td", qkv_grad, qkv_full[:, :kv_end], preferred_element_type=jnp.float32
    )
    first_grad = (
        lax.psum(first_part.astype(jnp.bfloat16), "tp")
        .astype(jnp.float32)
        .reshape(layer_in.shape)
    )
    gain_one_term = jnp.sum(first_grad * layer_in * first_rms, axis=(0, 1))
    input_grad = (
        middle_grad + norm_back(first_grad, layer_in, first_rms, gain_one)
    ).astype(jnp.bfloat16)
    qkv_own = lax.psum_scatter(
        qkv_term.astype(jnp.bfloat16), ("fsdp", "ctx"), scatter_dimension=0, tiled=True
    ).astype(jnp.float32)
    gain_own = lax.psum_scatter(
        jnp.stack([gain_one_term, gain_two_term], 1), ("fsdp", "ctx"), scatter_dimension=0, tiled=True
    )
    return (
        output,
        input_grad,
        gain_own[:, 0],
        qkv_own[:, :query_width],
        qkv_own[:, query_width : query_width + kv_width],
        qkv_own[:, query_width + kv_width :],
        w_out_grad,
        gain_own[:, 1],
        w_gate_grad,
        w_up_grad,
        w_down_grad,
    )


def solution(mesh):
    placed = (
        P("fsdp", "ctx", None),
        P("fsdp"),
        P("fsdp", "ctx", None),
        P(("fsdp", "ctx")),
        P(("fsdp", "ctx"), "tp"),
        P(("fsdp", "ctx"), "tp"),
        P(("fsdp", "ctx"), "tp"),
        P(("fsdp", "ctx"), "tp"),
        P(("fsdp", "ctx")),
        P(("fsdp", "ctx"), "tp"),
        P(("fsdp", "ctx"), "tp"),
        P(("fsdp", "ctx"), "tp"),
    )
    return jax.shard_map(
        local,
        mesh=mesh,
        in_specs=placed,
        out_specs=(
            P("fsdp", "ctx", None),
            P("fsdp", "ctx", None),
            P(("fsdp", "ctx")),
            P(("fsdp", "ctx"), "tp"),
            P(("fsdp", "ctx"), "tp"),
            P(("fsdp", "ctx"), "tp"),
            P(("fsdp", "ctx"), "tp"),
            P(("fsdp", "ctx")),
            P(("fsdp", "ctx"), "tp"),
            P(("fsdp", "ctx"), "tp"),
            P(("fsdp", "ctx"), "tp"),
        ),
        check_vma=False,
    )
```

time: 3850 us -> 1690 us (0.44)
  waiting for transfers between devices: 3330 us -> 1200 us
  blocking collectives: 143 us -> 49.9 us
  local copies, waits for them, and re-layouts: 28.1 us -> 87.3 us
    reduce_scatter x9 -> x8, waiting for transfers between devices: 2530 us -> 611 us  [the longest x3 200 us: return_units(): lax.psum_scatter(term.astype(jnp.bfloat16).reshape(fsdp, ctx * shard, uni...]
    all_gather x9 -> x8, waiting for transfers between devices: 767 us -> 489 us  [the longest x3 184 us: spread_units(): lax.all_gather(swapped.reshape(fsdp, shard, units), 'ctx', axis=1, tiled=...]
    unnamed x1 -> x0, blocking collectives: 72.3 us -> none
    all_gather x2 -> x0, blocking collectives: 70.2 us -> none  [the longest x1 36.2 us: local(): lax.all_gather(norm1_gain, ('fsdp', 'ctx'), axis=0, tiled=True)]
    unnamed x21, waiting for transfers between devices: 4.57 us -> 68.6 us
    all_to_all x0 -> x3, blocking collectives: none -> 49.9 us  [spread_units(): swapped = lax.all_to_all(weight, 'fsdp', 1, 0, tiled=True)]
    dot_general x21 -> x15, matrix products: 202 us -> 170 us  [the longest x3 42.9 us: return_units(): jnp.einsum('td,tf->df', left, right, preferred_element_type=jnp.float32)]
  transfers between devices with their start and end apart: 21 -> 23, of which waited for: 18 -> 19; matrix products, arithmetic and copies ran while one was open for 5% -> 14% of each run, Pallas kernels for 0% -> 0%
where the time goes in v1:
time: 1690 us; the launch traced here: 1680 us
  waiting for transfers between devices  1200 us (71%)
  matrix products  238 us (14%)
  local copies, waits for them, and re-layouts  87.3 us (5%)
  other arithmetic  71.2 us (4%)
  blocking collectives  49.9 us (3%)
    reduce_scatter x3, waiting for transfers between devices, return_units(): lax.psum_scatter(term.astype(jnp.bfloat16).reshape(fsdp, ctx * shard, uni...  200 us
    all_gather x3, waiting for transfers between devices, spread_units(): lax.all_gather(swapped.reshape(fsdp, shard, units), 'ctx', axis=1, tiled=...  184 us
    reduce_scatter x2, waiting for transfers between devices, gather_sum(): lax.psum_scatter(part.astype(jnp.bfloat16), 'fsdp', scatter_dimension=0,...  166 us
    reduce_scatter x1, waiting for transfers between devices, local(): lax.psum_scatter(qkv_term.astype(jnp.bfloat16), ('fsdp', 'ctx'), scatter_...  149 us
    all_gather x1, waiting for transfers between devices, local(): lax.all_gather(jnp.concatenate([w_query, w_key, w_value, gains], 1), ('fs...  97.9 us
    all_gather x1, waiting for transfers between devices, local(): lax.all_gather(second_normed.reshape(tokens, model_width), 'fsdp', axis=0...  83.8 us
    reduce_scatter x1, waiting for transfers between devices, local(): lax.psum_scatter(out_term.astype(jnp.bfloat16), ('fsdp', 'ctx'), scatter_...  74.2 us
    unnamed x21, waiting for transfers between devices  68.6 us
  transfers between devices with their start and end apart: 23, of which 19 were waited for; matrix products, arithmetic and copies ran while one was open for 14% of the time, Pallas kernels for 0%

profile of v1, /device:TPU:16, one launch (start us, length us, event | category | flops | bytes accessed | tf_op | source)
XLA Modules:
  0.0 1678.1 jit_solution(14416432343850530562)
XLA Ops:
  12.5 97.9 %all-gather.9.cloned.1.call-done = bf16[2048,1664]{1,0:T(8,128)(2,1)} async-done(((bf16[128,1664]{1,0:T(8,128)(2,1)}), bf16[2048,1664]{1,0:T(8,128)(2,1)}) %all-gather.9.cloned.1.call-update) | async-done | bytes 6815760 | tf_op jit(solution)/shard_map/all_gather | solution.py:137
  136.8 32.6 %all-gather.11.cloned.1.call-done = bf16[2,1024,512]{2,1,0:T(8,128)(2,1)} async-done(((bf16[2,256,512]{2,1,0:T(8,128)(2,1)}), bf16[2,1024,512]{2,1,0:T(8,128)(2,1)}) %all-gather.11.cloned.1.call-update) | async-done | bytes 2097168 | tf_op jit(solution)/shard_map/all_gather | solution.py:191
  181.6 36.7 %while.28 = (s32[]{:T(128)}, bf16[4,2,256,4,64]{2,4,3,1,0:T(8,128)(2,1)}, f32[4,2,4,256,1]{3,2,1,4,0:T(4,128)}, bf16[4,2,1024,64]{2,3,1,0:T(8,128)(2,1)}, bf16[4...) while((s32[]{:T(128)}, ...), condition=%wide.region_4.5_spmd.clone, body=%wide.region_1.4_spmd.clone.sunk | while | flops 562690048 | bytes 28643932 | solution.py:203
  221.8 25.9 %all-gather.13.cloned.1.call-done = bf16[2048,1024]{1,0:T(8,128)(2,1)} async-done(((bf16[128,1024]{1,0:T(8,128)(2,1)}), bf16[2048,1024]{1,0:T(8,128)(2,1)}) %all-gather.13.cloned.1.call-update) | async-done | bytes 4194320 | tf_op jit(solution)/shard_map/all_gather | solution.py:140
  256.3 18.0 %all_to_all.78 = bf16[128,4,1024]{0,2,1:T(8,128)(2,1)} all-to-all(bf16[128,4,1024]{0,2,1:T(8,128)(2,1)} %bitcast.347), channel_id=1, replica_groups=mesh['fsdp'=4,'ctx'=4,'tp'=2] {'fsdp'}, dimensions={1} | all-to-all | bytes 2097152 | tf_op jit(solution)/shard_map/all_to_all | solution.py:149
  276.6 16.6 all_to_all.79
  320.1 35.8 %all-gather.17.cloned.1.call-done = bf16[4,512,1024]{1,2,0:T(8,128)(2,1)} async-done(((bf16[4,128,1024]{1,2,0:T(8,128)(2,1)}), bf16[4,512,1024]{1,2,0:T(8,128)(2,1)}) %all-gather.17.cloned.1.call-update) | async-done | bytes 4194320 | tf_op jit(solution)/shard_map/all_gather | solution.py:151
  362.2 74.0 %all-gather.19.cloned.1.call-done = bf16[4,512,1024]{1,2,0:T(8,128)(2,1)} async-done(((bf16[4,128,1024]{1,2,0:T(8,128)(2,1)}), bf16[4,512,1024]{1,2,0:T(8,128)(2,1)}) %all-gather.19.cloned.1.call-update) | async-done | bytes 4194320 | tf_op jit(solution)/shard_map/all_gather | solution.py:151
  442.5 74.1 %all-gather.21.cloned.1.call-done = bf16[4,512,1024]{1,2,0:T(8,128)(2,1)} async-done(((bf16[4,128,1024]{1,2,0:T(8,128)(2,1)}), bf16[4,512,1024]{1,2,0:T(8,128)(2,1)}) %all-gather.21.cloned.1.call-update) | async-done | bytes 4194320 | tf_op jit(solution)/shard_map/all_gather | solution.py:151
  522.9 83.8 %all-gather.15.cloned.1.call-done = bf16[2048,2048]{1,0:T(8,128)(2,1)} async-done(((bf16[512,2048]{1,0:T(8,128)(2,1)}), bf16[2048,2048]{1,0:T(8,128)(2,1)}) %all-gather.15.cloned.1.call-update) | async-done | bytes 8388624 | tf_op jit(solution)/shard_map/all_gather | solution.py:213
  632.3 64.6 %all-gather.23.cloned.1.call-done = bf16[2048,2048]{1,0:T(8,128)(2,1)} async-done(((bf16[512,2048]{1,0:T(8,128)(2,1)}), bf16[2048,2048]{1,0:T(8,128)(2,1)}) %all-gather.23.cloned.1.call-update) | async-done | bytes 8388624 | tf_op jit(solution)/shard_map/all_gather | solution.py:161
  697.0 21.8 %multiply_convert_fusion = (bf16[2048,1024]{1,0:T(8,128)(2,1)}, bf16[2048,1024]{1,0:T(8,128)(2,1)}, bf16[2048,1024]{1,0:T(8,128)(2,1)}) fusion(f32[2048,1024]{1,0:T(8,128)} %fusion.100, f32[2048,1024]{1,0:T(8,128)} %fusion.101, bf16[2048,2048]{1,0:T(8,128)(2,1)} %all-gather.23.cloned.1.call-done, bf16[2048,1024]{1,0:T(8,128)(2,1)} %bitcast.332), kind=kOutput, calls=%fused_computation.73 | convolution fusion | flops 8621391872 | bytes 41943040 | tf_op jit(solution)/shard_map/dot_general | solution.py:222
  733.0 16.4 add_convert_fusion
  749.5 86.5 %reduce-scatter.14.cloned.1.call-done = bf16[512,2048]{1,0:T(8,128)(2,1)} async-done(((bf16[2048,2048]{1,0:T(8,128)(2,1)}), bf16[512,2048]{1,0:T(8,128)(2,1)}) %reduce-scatter.14.cloned.1.call-update) | async-done | bytes 2097168 | tf_op jit(solution)/shard_map/reduce_scatter | solution.py:232
  836.1 23.8 %all-reduce.8.cloned.1.call-done = bf16[2,256,2048]{2,1,0:T(8,128)(2,1)} async-done(((bf16[2,256,2048]{2,1,0:T(8,128)(2,1)}), bf16[2,256,2048]{2,1,0:T(8,128)(2,1)}) %all-reduce.8.cloned.1.call-update) | async-done | bytes 2097168 | tf_op jit(solution)/shard_map/psum | solution.py:235
  873.5 61.5 %while.29 = (s32[]{:T(128)}, f32[4,2,256,4,64]{2,4,3,1,0:T(8,128)}, bf16[4,2,1024,64]{2,3,0,1:T(8,128)(2,1)}, bf16[4,2,1024,64]{2,3,0,1:T(8,128)(2,1)}, bf16[4,2...) while((s32[]{:T(128)}, f32[4,2,256,4,64]{2,4,3,1,0:T(8,128)}, ...), condition=%wide.region_14.15_spmd.clone, body=%wide.region_12.14_spmd.clone.sunk | while | flops 1374418944 | bytes 77658296 | solution.py:273
  960.0 22.3 %reduce-scatter.16.cloned.1.call-done = bf16[2,256,512]{1,2,0:T(8,128)(2,1)} async-done(((bf16[2,1024,512]{1,2,0:T(8,128)(2,1)}), bf16[2,256,512]{1,2,0:T(8,128)(2,1)}) %reduce-scatter.16.cloned.1.call-update) | async-done | bytes 524304 | tf_op jit(solution)/shard_map/reduce_scatter | solution.py:283
  992.1 79.7 %reduce-scatter.12.cloned.1.call-done = bf16[512,2048]{1,0:T(8,128)(2,1)} async-done(((bf16[2048,2048]{1,0:T(8,128)(2,1)}), bf16[512,2048]{1,0:T(8,128)(2,1)}) %reduce-scatter.12.cloned.1.call-update) | async-done | bytes 2097168 | tf_op jit(solution)/shard_map/reduce_scatter | solution.py:232
  1135.4 48.8 %reduce-scatter.22.cloned.1.call-done = bf16[4,128,1024]{2,1,0:T(8,128)(2,1)} async-done(((bf16[4,512,1024]{2,1,0:T(8,128)(2,1)}), bf16[4,128,1024]{2,1,0:T(8,128)(2,1)}) %reduce-scatter.22.cloned.1.call-update) | async-done | bytes 1048592 | tf_op jit(solution)/shard_map/reduce_scatter | solution.py:241
  1187.8 75.9 %reduce-scatter.24.cloned.1.call-done = bf16[4,128,1024]{2,1,0:T(8,128)(2,1)} async-done(((bf16[4,512,1024]{2,1,0:T(8,128)(2,1)}), bf16[4,128,1024]{2,1,0:T(8,128)(2,1)}) %reduce-scatter.24.cloned.1.call-update) | async-done | bytes 1048592 | tf_op jit(solution)/shard_map/reduce_scatter | solution.py:241
  1267.9 75.2 %reduce-scatter.26.cloned.1.call-done = bf16[4,128,1024]{2,1,0:T(8,128)(2,1)} async-done(((bf16[4,512,1024]{2,1,0:T(8,128)(2,1)}), bf16[4,128,1024]{2,1,0:T(8,128)(2,1)}) %reduce-scatter.26.cloned.1.call-update) | async-done | bytes 1048592 | tf_op jit(solution)/shard_map/reduce_scatter | solution.py:241
  1364.4 74.2 %reduce-scatter.20.cloned.1.call-done = bf16[128,1024]{1,0:T(8,128)(2,1)} async-done(((bf16[2048,1024]{1,0:T(8,128)(2,1)}), bf16[128,1024]{1,0:T(8,128)(2,1)}) %reduce-scatter.20.cloned.1.call-update) | async-done | bytes 262160 | tf_op jit(solution)/shard_map/reduce_scatter | solution.py:264
  1449.1 67.6 %reduce-scatter.28.cloned.1.call-done = f32[128,2]{1,0:T(8,128)} async-done(((f32[2048,2]{1,0:T(8,128)}), f32[128,2]{1,0:T(8,128)}) %reduce-scatter.28.cloned.1.call-update) | async-done | bytes 1040
  1518.8 148.9 %reduce-scatter.18.cloned.1.call-done = bf16[128,1536]{1,0:T(8,128)(2,1)} async-done(((bf16[2048,1536]{1,0:T(8,128)(2,1)}), bf16[128,1536]{1,0:T(8,128)(2,1)}) %reduce-scatter.18.cloned.1.call-update) | async-done | bytes 393232 | tf_op jit(solution)/shard_map/reduce_scatter | solution.py:316
  (323 shorter events, 398.0 us)
Async XLA Ops:
  7.2 103.2 %all-gather.9.cloned.1.call-start = ((), (), s32[]{:S(2)}) async-start(), calls=%async_computation.15 | async-start | bytes 7241728 | tf_op jit(solution)/shard_map/all_gather | solution.py:137
  10.0 159.4 %all-gather.11.cloned.1.call-start = ((), (), s32[]{:S(2)}) async-start(), calls=%async_computation.16 | async-start | bytes 2621440 | tf_op jit(solution)/shard_map/all_gather | solution.py:191
  112.3 752.5 %copy-start.27 = (f32[2048]{0:T(1024)}, f32[2048]{0:T(1024)S(1)}, u32[]{:S(2)}) copy-start(f32[2048]{0:T(1024)S(1)} %get-tuple-element.211) | copy-start | bytes 24580
  125.6 122.1 %all-gather.13.cloned.1.call-start = ((), (), s32[]{:S(2)}) async-start(), calls=%async_computation.17 | async-start | bytes 4456448 | tf_op jit(solution)/shard_map/all_gather | solution.py:140
  126.3 184.6 %all-reduce.6.cloned.1.call-start = ((), (), s32[]{:S(2)}) async-start(), calls=%async_computation.18 | async-start | bytes 4194304 | tf_op jit(solution)/shard_map/psum | solution.py:208
  253.9 101.9 %all-gather.17.cloned.1.call-start = ((), (), s32[]{:S(2)}) async-start(), calls=%async_computation.20 | async-start | bytes 5242880 | tf_op jit(solution)/shard_map/all_gather | solution.py:151
  274.3 161.9 %all-gather.19.cloned.1.call-start = ((), (), s32[]{:S(2)}) async-start(), calls=%async_computation.21 | async-start | bytes 5242880 | tf_op jit(solution)/shard_map/all_gather | solution.py:151
  293.2 223.4 %all-gather.21.cloned.1.call-start = ((), (), s32[]{:S(2)}) async-start(), calls=%async_computation.22 | async-start | bytes 5242880 | tf_op jit(solution)/shard_map/all_gather | solution.py:151
  310.9 295.9 %all-gather.15.cloned.1.call-start = ((), (), s32[]{:S(2)}) async-start(), calls=%async_computation.19 | async-start | bytes 10485760 | tf_op jit(solution)/shard_map/all_gather | solution.py:213
  317.5 379.4 %all-gather.23.cloned.1.call-start = ((), (), s32[]{:S(2)}) async-start(), calls=%async_computation.24 | async-start | bytes 10485760 | tf_op jit(solution)/shard_map/all_gather | solution.py:161
  319.9 516.1 %reduce-scatter.14.cloned.1.call-start = ((), (), s32[]{:S(2)}) async-start(), calls=%async_computation.25 | async-start | bytes 10485760 | tf_op jit(solution)/shard_map/reduce_scatter | solution.py:232
  749.4 110.4 %all-reduce.8.cloned.1.call-start = ((), (), s32[]{:S(2)}) async-start(), calls=%async_computation.26 | async-start | bytes 4194304 | tf_op jit(solution)/shard_map/psum | solution.py:235
  836.0 146.3 %reduce-scatter.16.cloned.1.call-start = ((), (), s32[]{:S(2)}) async-start(), calls=%async_computation.27 | async-start | bytes 2621440 | tf_op jit(solution)/shard_map/reduce_scatter | solution.py:283
  938.1 133.7 %reduce-scatter.12.cloned.1.call-start = ((), (), s32[]{:S(2)}) async-start(), calls=%async_computation.23 | async-start | bytes 10485760 | tf_op jit(solution)/shard_map/reduce_scatter | solution.py:232
  952.5 168.8 %all-reduce.10.cloned.1.call-start = ((), (), s32[]{:S(2)}) async-start(), calls=%async_computation.34 | async-start | bytes 8388608 | tf_op jit(solution)/shard_map/psum | solution.py:235
  1071.8 112.3 %reduce-scatter.22.cloned.1.call-start = ((), (), s32[]{:S(2)}) async-start(), calls=%async_computation.30 | async-start | bytes 5242880 | tf_op jit(solution)/shard_map/reduce_scatter | solution.py:241
  1085.9 177.8 %reduce-scatter.24.cloned.1.call-start = ((), (), s32[]{:S(2)}) async-start(), calls=%async_computation.31 | async-start | bytes 5242880 | tf_op jit(solution)/shard_map/reduce_scatter | solution.py:241
  1100.1 243.0 %reduce-scatter.26.cloned.1.call-start = ((), (), s32[]{:S(2)}) async-start(), calls=%async_computation.32 | async-start | bytes 5242880 | tf_op jit(solution)/shard_map/reduce_scatter | solution.py:241
  1115.0 323.6 %reduce-scatter.20.cloned.1.call-start = ((), (), s32[]{:S(2)}) async-start(), calls=%async_computation.29 | async-start | bytes 4456448 | tf_op jit(solution)/shard_map/reduce_scatter | solution.py:264
  1121.2 395.5 %reduce-scatter.28.cloned.1.call-start = ((), (), s32[]{:S(2)}) async-start(), calls=%async_computation.33 | async-start | bytes 1114112
  1127.3 540.3 %reduce-scatter.18.cloned.1.call-start = ((), (), s32[]{:S(2)}) async-start(), calls=%async_computation.28 | async-start | bytes 6684672 | tf_op jit(solution)/shard_map/reduce_scatter | solution.py:316
  1184.1 79.5 %all-to-all-start.3 = ((bf16[4,128,1024]{2,1,0:T(8,128)(2,1)}), bf16[4,128,1024]{2,1,0:T(8,128)(2,1)S(1)}, u32[]{:S(2)}, u32[]{:S(2)}) async-start(bf16[4,128,1024]{2,1,0:T(8,128)(2,1)} %reduce-scatter.22.cloned.1.call-done), calls=%async_computation.9 | async-start | bytes 2097152 | tf_op jit(solution)/shard_map/all_to_all | solution.py:247
  1263.7 79.4 %all-to-all-start.4 = ((bf16[4,128,1024]{2,1,0:T(8,128)(2,1)}), bf16[4,128,1024]{2,1,0:T(8,128)(2,1)}, u32[]{:S(2)}, u32[]{:S(2)}) async-start(bf16[4,128,1024]{2,1,0:T(8,128)(2,1)} %reduce-scatter.24.cloned.1.call-done), calls=%async_computation.11 | async-start | bytes 2097152 | tf_op jit(solution)/shard_map/all_to_all | solution.py:247
  1343.1 18.3 %all-to-all-start.5 = ((bf16[4,128,1024]{2,1,0:T(8,128)(2,1)}), bf16[4,128,1024]{2,1,0:T(8,128)(2,1)}, u32[]{:S(2)}, u32[]{:S(2)}) async-start(bf16[4,128,1024]{2,1,0:T(8,128)(2,1)} %reduce-scatter.26.cloned.1.call-done), calls=%async_computation.13 | async-start | bytes 2097152 | tf_op jit(solution)/shard_map/all_to_all | solution.py:247
  (51 other events, 2644.5 us)
Sparse Core Ops, SparseCore 0:
  11.3 99.0 all-gather.8
  125.7 43.6 all-gather.10
  172.2 75.4 all-gather.12
  254.1 20.5 all-reduce.5
  276.1 79.7 all-gather.16
  357.4 78.7 all-gather.18
  437.8 78.7 all-gather.20
  519.1 87.5 all-gather.14
  609.3 87.6 all-gather.22
  749.5 86.3 reduce-scatter.13
  838.3 21.4 all-reduce.7
  938.2 44.0 reduce-scatter.15
  985.4 86.3 reduce-scatter.11
  1074.9 28.7 all-reduce.9
  1105.9 78.1 reduce-scatter.21
  1186.4 77.2 reduce-scatter.23
  1265.8 77.2 reduce-scatter.25
  1345.4 93.1 reduce-scatter.19
  1440.9 75.6 reduce-scatter.27
  1521.7 145.8 reduce-scatter.17

commit v2 on v1

v2 whole, which is shorter than its diff:
```python
from functools import partial

import jax
import jax.numpy as jnp
from jax import lax
from jax.experimental import pallas as pl
from jax.experimental.pallas import tpu as pltpu
from jax.sharding import PartitionSpec as P

HD = 64


norm_eps = 1e-05
residual_scale = 0.22
score_scale = 1.0 / 64.0
rope_base = 10000000.0
masked_score = -1e30


def rope_tables(positions, head_dim):
    half_dim = head_dim // 2
    frequency = rope_base ** (-(jnp.arange(half_dim, dtype=jnp.float32) * 2.0) / head_dim)
    angles = positions.astype(jnp.float32)[:, None] * frequency[None, :]
    return (
        jnp.concatenate([jnp.cos(angles), jnp.cos(angles)], -1),
        jnp.concatenate([jnp.sin(angles), jnp.sin(angles)], -1),
    )


def rotate(values_in, cosines, sines):
    half_dim = values_in.shape[-1] // 2
    turned = jnp.concatenate([-values_in[..., half_dim:], values_in[..., :half_dim]], -1)
    return values_in * cosines + turned * sines


def unrotate(grad_in, cosines, sines):
    half_dim = grad_in.shape[-1] // 2
    scaled = grad_in * sines
    return grad_in * cosines + jnp.concatenate(
        [scaled[..., half_dim:], -scaled[..., :half_dim]], -1
    )


def rms_scale(values_in):
    return lax.rsqrt(jnp.mean(values_in * values_in, -1, keepdims=True) + norm_eps)


def norm_back(grad_normed, values_in, scale, gain):
    scaled_grad = grad_normed * gain
    return scale * scaled_grad - values_in * scale**3 * jnp.mean(
        scaled_grad * values_in, -1, keepdims=True
    )


def masked_scores(grouped_query_rows, key_row_block, key_mask):
    scores = (
        jnp.einsum(
            "sqgd,skd->sgqk", grouped_query_rows, key_row_block, preferred_element_type=jnp.float32
        )
        * score_scale
    )
    return jnp.where(key_mask[:, None], scores, masked_score)


def attend_forward(block_item, key_mask):
    grouped_query_rows, key_row_block, value_row_block = block_item
    scores = masked_scores(grouped_query_rows, key_row_block, key_mask)
    top_score = jnp.max(scores, -1, keepdims=True)
    exp_scores = jnp.exp(scores - top_score)
    total_mass = jnp.sum(exp_scores, -1, keepdims=True)
    probs_low = (exp_scores / total_mass).astype(jnp.bfloat16)
    head_output = jnp.einsum(
        "sgqk,skd->sqgd", probs_low, value_row_block, preferred_element_type=jnp.float32
    )
    return (head_output.astype(jnp.bfloat16), top_score + jnp.log(total_mass))


def attend_backward(block_item, key_mask):
    grouped_query_rows, key_row_block, value_row_block, out_grad, log_mass = block_item
    scores = masked_scores(grouped_query_rows, key_row_block, key_mask)
    attention_probabilities = jnp.exp(scores - log_mass)
    probs_low = attention_probabilities.astype(jnp.bfloat16)
    value_grad = jnp.einsum(
        "sgqk,sqgd->skd", probs_low, out_grad, preferred_element_type=jnp.float32
    )
    probs_grad = jnp.einsum(
        "sqgd,skd->sgqk", out_grad, value_row_block, preferred_element_type=jnp.float32
    )
    score_grad = (
        attention_probabilities
        * (probs_grad - jnp.sum(attention_probabilities * probs_grad, -1, keepdims=True))
    ).astype(jnp.bfloat16)
    query_grad = (
        jnp.einsum("sgqk,skd->sqgd", score_grad, key_row_block, preferred_element_type=jnp.float32)
        * score_scale
    )
    key_grad = (
        jnp.einsum(
            "sgqk,sqgd->skd", score_grad, grouped_query_rows, preferred_element_type=jnp.float32
        )
        * score_scale
    )
    return (query_grad, key_grad, value_grad)


MESH_ID = pl.DeviceIdType.MESH


def low_bit(k):
    return k & -k


def high_bit(k):
    return 1 << (k.bit_length() - 1)


def fsdp_order(fsdp):
    return sorted(range(1, fsdp), key=lambda k: (bin(k).count("1"), k))


def flip_index(me, k, fsdp):
    out = me
    for i in range(fsdp.bit_length() - 1):
        b = 1 << i
        if k & b:
            out = out + b - 2 * b * lax.rem(me // b, 2)
    return out


def line_neighbours(me, count):
    return (me > 0).astype(jnp.int32) + (me < count - 1).astype(jnp.int32)


def line_kernel(fsdp, ctx, group, lines, swaps, spots, *refs):
    line_in = refs[:lines]
    swap_in = refs[lines : lines + swaps]
    line_out = refs[lines + swaps : 2 * lines + swaps]
    swap_out = refs[2 * lines + swaps : -5]
    own_sem, z_send, z_recv, f_send, f_recv = refs[-5:]
    me_f = lax.axis_index("fsdp")
    me_c = lax.axis_index("ctx")
    me_t = lax.axis_index("tp")

    def along(step, act):
        there = me_c + step

        @pl.when((there >= 0) & (there < ctx))
        def _():
            act(there)

    barrier = pltpu.get_barrier_semaphore()
    for k in range(1, group):
        pl.semaphore_signal(
            barrier, inc=1, device_id=(flip_index(me_f, k, fsdp), me_c, me_t), device_id_type=MESH_ID
        )
    for step in (-1, 1):
        along(
            step,
            lambda there: pl.semaphore_signal(
                barrier, inc=1, device_id=(me_f, there, me_t), device_id_type=MESH_ID
            ),
        )
    pl.semaphore_wait(barrier, group - 1 + line_neighbours(me_c, ctx))

    def z_copy(i, shard, step, src=None):
        place = line_out[i].at[shard]
        way = 0 if step > 0 else 1
        return pltpu.make_async_remote_copy(
            src_ref=place if src is None else src,
            dst_ref=place,
            send_sem=z_send.at[i, way, shard],
            recv_sem=z_recv.at[i, way, shard],
            device_id=(me_f, me_c + step, me_t),
            device_id_type=MESH_ID,
        )

    def landing(i, f):
        out, start = spots[i]
        width = swap_in[i].shape[1] // group
        return swap_out[out].at[lax.rem(f, group), :, pl.ds(start, width)]

    def columns(i, f):
        width = swap_in[i].shape[1] // group
        return swap_in[i].at[:, pl.ds(pl.multiple_of(lax.rem(f, group) * width, 128), width)]

    def f_copy(i, k):
        there = flip_index(me_f, k, fsdp)
        return pltpu.make_async_remote_copy(
            src_ref=columns(i, there),
            dst_ref=landing(i, me_f),
            send_sem=f_send.at[i, k],
            recv_sem=f_recv.at[i, k],
            device_id=(there, me_c, me_t),
            device_id_type=MESH_ID,
        )

    def f_arrival(i, k):
        there = flip_index(me_f, k, fsdp)
        return pltpu.make_async_remote_copy(
            src_ref=landing(i, there),
            dst_ref=landing(i, there),
            send_sem=f_send.at[i, k],
            recv_sem=f_recv.at[i, k],
            device_id=(there, me_c, me_t),
            device_id_type=MESH_ID,
        )

    for i in range(lines):
        for step in (1, -1):
            along(step, lambda there: z_copy(i, me_c, step, line_in[i]).start())
    order = fsdp_order(group)
    for i in range(swaps):
        for k in order:
            f_copy(i, k).start()
    own = [
        pltpu.make_async_copy(line_in[i], line_out[i].at[me_c], own_sem.at[i])
        for i in range(lines)
    ] + [
        pltpu.make_async_copy(columns(i, me_f), landing(i, me_f), own_sem.at[lines + i])
        for i in range(swaps)
    ]
    for copy in own:
        copy.start()
    for i in range(lines):
        for distance in range(1, ctx):
            for step in (1, -1):
                shard = me_c - step * distance

                @pl.when((shard >= 0) & (shard < ctx))
                def _():
                    z_copy(i, shard, step).wait_recv()
                    along(step, lambda there: z_copy(i, shard, step).start())

    for i in range(swaps):
        for k in order:
            f_arrival(i, k).wait_recv()
            f_copy(i, k).wait_send()
    for copy in own:
        copy.wait()
    for i in range(lines):
        for step in (1, -1):
            along(step, lambda there: z_copy(i, me_c, step, line_in[i]).wait_send())
            for distance in range(1, ctx - 1):
                shard = me_c - step * distance

                @pl.when((shard >= 0) & (shard < ctx))
                def _():
                    along(step, lambda there: z_copy(i, shard, step).wait_send())


def start_exchange(fsdp, ctx, group, lines, swap_sets):
    sems = pltpu.SemaphoreType.DMA
    out_shape = [jax.ShapeDtypeStruct((ctx,) + v.shape, v.dtype) for v in lines]
    swaps, spots = [], []
    for out, arrays in enumerate(swap_sets):
        start = 0
        for v in arrays:
            spots.append((out, start))
            swaps.append(v)
            start += v.shape[1] // group
        out_shape.append(
            jax.ShapeDtypeStruct((group, arrays[0].shape[0], start), arrays[0].dtype)
        )
    count = len(lines) + len(swaps)
    outs = pl.pallas_call(
        partial(line_kernel, fsdp, ctx, group, len(lines), len(swaps), spots),
        out_shape=out_shape,
        in_specs=[pl.BlockSpec(memory_space=pl.ANY)] * count,
        out_specs=[pl.BlockSpec(memory_space=pl.ANY)] * len(out_shape),
        scratch_shapes=[
            sems((count,)),
            sems((len(lines), 2, ctx)),
            sems((len(lines), 2, ctx)),
            sems((len(swaps), group)),
            sems((len(swaps), group)),
        ],
        compiler_params=pltpu.CompilerParams(collective_id=0, has_side_effects=True),
    )(*lines, *swaps)
    return outs[: len(lines)], outs[len(lines) :]


def spread_kernel(fsdp, ctx, count, *refs):
    ins = refs[:count]
    outs = refs[count : 2 * count]
    own_sem, f_send, f_recv = refs[2 * count :]
    me_f = lax.axis_index("fsdp")
    me_c = lax.axis_index("ctx")
    me_t = lax.axis_index("tp")
    bits = [1 << i for i in range(fsdp.bit_length() - 1)]
    order = fsdp_order(fsdp)

    def peer(k):
        return (flip_index(me_f, k, fsdp), me_c, me_t)

    barrier = pltpu.get_barrier_semaphore()
    for b in bits:
        pl.semaphore_signal(barrier, inc=1, device_id=peer(b), device_id_type=MESH_ID)
    pl.semaphore_wait(barrier, len(bits))

    def place(i, shard, have, k, part):
        block = outs[i].at[flip_index(me_f, have, fsdp), shard]
        half = ins[i].shape[1] // 2
        return block if k == low_bit(k) else block.at[pl.ds(part * half, half)]

    def f_copy(i, shard, have, b):
        k = have | b
        part = 1 if have and b == high_bit(k) else 0
        block = place(i, shard, have, k, part)
        return pltpu.make_async_remote_copy(
            src_ref=block if have else ins[i].at[shard],
            dst_ref=block,
            send_sem=f_send.at[i, shard, k, part],
            recv_sem=f_recv.at[i, shard, k, part],
            device_id=peer(b),
            device_id_type=MESH_ID,
        )

    def ways(have):
        return [
            b
            for b in bits
            if not have & b and (not have or b in (low_bit(have | b), high_bit(have | b)))
        ]

    own = [
        pltpu.make_async_copy(ins[i], outs[i].at[me_f], own_sem.at[i]) for i in range(count)
    ]
    for i in range(count):
        for shard in range(ctx):
            for b in ways(0):
                f_copy(i, shard, 0, b).start()
        own[i].start()
    for i in range(count):
        for k in order:
            parts = [(0, k)] if k == low_bit(k) else [(0, low_bit(k)), (1, high_bit(k))]
            for shard in range(ctx):
                for part, b in parts:
                    block = place(i, shard, k, k, part)
                    pltpu.make_async_remote_copy(
                        src_ref=block,
                        dst_ref=block,
                        send_sem=f_send.at[i, shard, k, part],
                        recv_sem=f_recv.at[i, shard, k, part],
                        device_id=peer(b),
                        device_id_type=MESH_ID,
                    ).wait_recv()
                for b in ways(k):
                    f_copy(i, shard, k, b).start()
    for i in range(count):
        own[i].wait()
        for have in [0] + order:
            for shard in range(ctx):
                for b in ways(have):
                    f_copy(i, shard, have, b).wait_send()


def spread_weights(fsdp, ctx, arrays):
    count = len(arrays)
    sems = pltpu.SemaphoreType.DMA
    outs = pl.pallas_call(
        partial(spread_kernel, fsdp, ctx, count),
        out_shape=[jax.ShapeDtypeStruct((fsdp,) + v.shape, v.dtype) for v in arrays],
        in_specs=[pl.BlockSpec(memory_space=pl.ANY)] * count,
        out_specs=[pl.BlockSpec(memory_space=pl.ANY)] * count,
        scratch_shapes=[
            sems((count,)),
            sems((count, ctx, fsdp, 2)),
            sems((count, ctx, fsdp, 2)),
        ],
        compiler_params=pltpu.CompilerParams(collective_id=1, has_side_effects=True),
    )(*arrays)
    return [o.reshape(-1, v.shape[-1]) for o, v in zip(outs, arrays)]


def sum_kernel(fsdp, ctx, count, *refs):
    ins = refs[:count]
    outs = refs[count : 2 * count]
    held = refs[2 * count : 3 * count]
    got = refs[3 * count : 4 * count]
    line = refs[4 * count : 5 * count]
    in_sem, f_send, f_recv, z_send, z_recv = refs[5 * count :]
    me_f = lax.axis_index("fsdp")
    me_c = lax.axis_index("ctx")
    me_t = lax.axis_index("tp")
    bits = [1 << i for i in range(fsdp.bit_length() - 1)]
    order = fsdp_order(fsdp)

    def peer(k):
        return (flip_index(me_f, k, fsdp), me_c, me_t)

    def along(step, act):
        there = me_c + step

        @pl.when((there >= 0) & (there < ctx))
        def _():
            act(there)

    loads = {}
    for i in range(count):
        for k in reversed([0] + order):
            loads[i, k] = pltpu.make_async_copy(
                ins[i].at[flip_index(me_f, k, fsdp)], held[i].at[k], in_sem.at[i, k]
            )
            loads[i, k].start()

    barrier = pltpu.get_barrier_semaphore()
    for b in bits:
        pl.semaphore_signal(barrier, inc=1, device_id=peer(b), device_id_type=MESH_ID)
    for step in (-1, 1):
        along(
            step,
            lambda there: pl.semaphore_signal(
                barrier, inc=1, device_id=(me_f, there, me_t), device_id_type=MESH_ID
            ),
        )
    pl.semaphore_wait(barrier, len(bits) + line_neighbours(me_c, ctx))

    def ways(k):
        return [(0, k)] if k == low_bit(k) else [(0, low_bit(k)), (1, high_bit(k))]

    def piece(i, k, part):
        rows = ins[i].shape[2]
        return pl.ds(0, rows) if k == low_bit(k) else pl.ds(part * (rows // 2), rows // 2)

    def f_copy(i, shard, k, part, b):
        span = piece(i, k, part)
        return pltpu.make_async_remote_copy(
            src_ref=held[i].at[k, shard, span],
            dst_ref=got[i].at[k, shard, span],
            send_sem=f_send.at[i, shard, k, part],
            recv_sem=f_recv.at[i, shard, k, part],
            device_id=peer(b),
            device_id_type=MESH_ID,
        )

    def add(into, other):
        rows = into.shape[0]

        def body(r, _):
            span = pl.ds(pl.multiple_of(r * 16, 16), 16)
            into[span] = (
                into[span].astype(jnp.float32) + other[span].astype(jnp.float32)
            ).astype(into.dtype)
            return 0

        lax.fori_loop(0, rows // 16, body, 0)

    def collect(i, shard, k):
        for far in order:
            for part, b in ways(far):
                if far ^ b == k:
                    f_copy(i, shard, far, part, b).wait_recv()
                    span = piece(i, far, part)
                    add(held[i].at[k, shard, span], got[i].at[far, shard, span])

    def z_copy(i, shard, step):
        way = 0 if step > 0 else 1
        return pltpu.make_async_remote_copy(
            src_ref=held[i].at[0, shard],
            dst_ref=line[i].at[way, shard],
            send_sem=z_send.at[i, way, shard],
            recv_sem=z_recv.at[i, way, shard],
            device_id=(me_f, me_c + step, me_t),
            device_id_type=MESH_ID,
        )

    def on_line(i, shard):
        for step in (1, -1):
            way = 0 if step > 0 else 1

            @pl.when((step * (shard - me_c) >= 0) & (me_c - step >= 0) & (me_c - step < ctx))
            def _():
                z_copy(i, shard, step).wait_recv()
                add(held[i].at[0, shard], line[i].at[way, shard])

            @pl.when(step * (shard - me_c) > 0)
            def _():
                z_copy(i, shard, step).start()

        @pl.when(shard == me_c)
        def _():
            rows = outs[i].shape[0]

            def body(r, _):
                span = pl.ds(pl.multiple_of(r * 16, 16), 16)
                outs[i][span] = held[i][0, shard, span].astype(outs[i].dtype)
                return 0

            lax.fori_loop(0, rows // 16, body, 0)

    shards = sorted(range(ctx), key=lambda c: -abs(2 * c - ctx + 1))
    work = [(i, shard) for i in range(count) for shard in shards]
    levels = sorted({bin(k).count("1") for k in order}, reverse=True)
    for level in levels:
        ks = [k for k in order if bin(k).count("1") == level]
        for i in range(count):
            for k in ks:
                loads[i, k].wait()
            for shard in shards:
                for k in ks:
                    collect(i, shard, k)
                    for part, b in ways(k):
                        f_copy(i, shard, k, part, b).start()
    for i in range(count):
        loads[i, 0].wait()
    late = None
    for item in work + [None]:
        if item is not None:
            collect(item[0], item[1], 0)
        if late is not None:
            on_line(*late)
        late = item
    for i, shard in work:
        for k in order:
            for part, b in ways(k):
                f_copy(i, shard, k, part, b).wait_send()
        for step in (1, -1):

            @pl.when(step * (shard - me_c) > 0)
            def _():
                z_copy(i, shard, step).wait_send()


def sum_weights(fsdp, ctx, arrays):
    count = len(arrays)
    sems = pltpu.SemaphoreType.DMA
    shards = [v.reshape(fsdp, ctx, -1, v.shape[-1]) for v in arrays]
    vmem = pltpu.VMEM
    return pl.pallas_call(
        partial(sum_kernel, fsdp, ctx, count),
        out_shape=[jax.ShapeDtypeStruct(v.shape[2:], jnp.float32) for v in shards],
        in_specs=[pl.BlockSpec(memory_space=pl.ANY)] * count,
        out_specs=[pl.BlockSpec(memory_space=pltpu.VMEM)] * count,
        scratch_shapes=[vmem(v.shape, v.dtype) for v in shards]
        + [vmem(v.shape, v.dtype) for v in shards]
        + [vmem((2,) + v.shape[1:], v.dtype) for v in shards]
        + [
            sems((count, fsdp)),
            sems((count, ctx, fsdp, 2)),
            sems((count, ctx, fsdp, 2)),
            sems((count, 2, ctx)),
            sems((count, 2, ctx)),
        ],
        compiler_params=pltpu.CompilerParams(
            collective_id=2, has_side_effects=True, vmem_limit_bytes=50 * 1024 * 1024
        ),
    )(*shards)


def local(
    inputs,
    lengths,
    cotangent,
    norm1_gain,
    w_query,
    w_key,
    w_value,
    w_out,
    norm2_gain,
    w_gate,
    w_up,
    w_down,
):
    seq_count, local_rows, model_width = inputs.shape
    tokens = seq_count * local_rows
    half = tokens // 2
    fsdp = lax.axis_size("fsdp")
    ctx = lax.axis_size("ctx")
    shard = w_query.shape[0]
    query_width = w_query.shape[1]
    kv_width = w_key.shape[1]
    kv_end = query_width + 2 * kv_width
    group = min(fsdp, 4)
    far = fsdp // group
    units = w_gate.shape[1] // group
    me_f = lax.axis_index("fsdp")
    me_c = lax.axis_index("ctx")
    me_t = lax.axis_index("tp")
    order = fsdp_order(group)
    low = jnp.bfloat16
    wide = jnp.float32

    def hop(v, k):
        return lax.ppermute(v, "fsdp", [(i, i ^ k) for i in range(fsdp)])

    def swap(v):
        return lax.ppermute(v, "tp", [(0, 1), (1, 0)])

    def up_line(v):
        return lax.ppermute(v, "ctx", [(i, i + 1) for i in range(ctx - 1)])

    def down_line(v):
        return lax.ppermute(v, "ctx", [(i + 1, i) for i in range(ctx - 1)])

    def pair_sum(part):
        part = part.astype(low)
        return part.astype(wide) + swap(part).astype(wide)

    def by_ctx(v):
        rest = v.shape[:-1]
        return v.reshape(*rest, fsdp, ctx, shard).swapaxes(-3, -2).reshape(*rest, model_width)

    def by_fsdp(v):
        rest = v.shape[:-1]
        return v.reshape(*rest, ctx, fsdp, shard).swapaxes(-3, -2).reshape(*rest, model_width)

    def gather_tokens(v):
        mine = lax.dynamic_slice_in_dim(v, me_t * half, half)
        other = lax.dynamic_slice_in_dim(v, (1 - me_t) * half, half)
        got = {0: mine}
        for k in order:
            lo, hi = low_bit(k), high_bit(k)
            if lo == hi:
                got[k] = hop(mine, k)
            else:
                cut = half // 2
                got[k] = jnp.concatenate(
                    [hop(got[k ^ lo][:cut], lo), hop(got[k ^ hi][cut:], hi)]
                )
        return [(mine, other)] + [(got[k], swap(got[k])) for k in range(1, group)]

    def scatter_tokens(blocks):
        total = {}
        for k in reversed([0] + order):
            mine, other = blocks[k]
            total[k] = mine.astype(wide) + swap(other.astype(low)).astype(wide)
        for k in reversed(order):
            lo, hi = low_bit(k), high_bit(k)
            sent = total[k].astype(low)
            if lo == hi:
                total[0] = total[0] + hop(sent, k).astype(wide)
            else:
                cut = half // 2
                for there, first, b in ((k ^ lo, True, lo), (k ^ hi, False, hi)):
                    piece = hop(sent[:cut] if first else sent[cut:], b).astype(wide)
                    base = total[there]
                    total[there] = jnp.concatenate(
                        [base[:cut] + piece, base[cut:]]
                        if first
                        else [base[:cut], base[cut:] + piece]
                    )
        own = total[0].astype(low)
        other = swap(own)
        return jnp.where(
            me_t == 0, jnp.concatenate([own, other]), jnp.concatenate([other, own])
        ).astype(wide)

    positions = me_c * local_rows + jnp.arange(local_rows, dtype=jnp.int32)
    key_places = (
        (me_c - jnp.arange(ctx, dtype=jnp.int32))[:, None] * local_rows
        + jnp.arange(local_rows, dtype=jnp.int32)[None, :]
    ).reshape(-1)
    valid_rows = (positions[None, :] < lengths[:, None]).astype(wide)[..., None]
    key_mask = (
        (key_places[None, None, :] <= positions[None, :, None])
        & (key_places[None, None, :] < lengths[:, None, None])
        & (key_places >= 0)[None, None, :]
    )
    cosines, sines = rope_tables(positions, HD)
    head_cos = cosines[None, :, None, :]
    head_sin = sines[None, :, None, :]

    gains = jnp.pad(jnp.stack([norm1_gain, norm2_gain], 1), ((0, 0), (0, 126)))
    lined, held = start_exchange(
        fsdp,
        ctx,
        group,
        [jnp.concatenate([w_query, w_key, w_value, gains], 1), w_out],
        [[w_gate, w_up], [w_down]],
    )
    far_groups = [[h * group + g for h in range(far)] for g in range(group)]
    near_groups = [[h * group + g for g in range(group)] for h in range(far)]

    def whole_width(v):
        if far > 1:
            v = lax.all_gather(v, "fsdp", axis=0, tiled=False, axis_index_groups=far_groups)
        return lax.all_gather(v, "ctx", axis=0, tiled=False).reshape(model_width, -1)

    both_full, down_full = [whole_width(v) for v in held]
    qkv_full, out_full = spread_weights(fsdp, ctx, lined)
    gain_one = qkv_full[:, kv_end].astype(wide)
    gain_two = qkv_full[:, kv_end + 1].astype(wide)

    back = cotangent.astype(wide) * valid_rows
    ff_grad = by_ctx((residual_scale * back).astype(low).reshape(tokens, model_width))
    ff_grad_blocks = gather_tokens(ff_grad)

    query_heads = query_width // HD
    kv_heads = kv_width // HD
    group_size = query_heads // kv_heads
    layer_in = inputs.astype(wide)
    first_rms = rms_scale(layer_in)
    first_normed = (layer_in * first_rms * gain_one).astype(low)
    qkv_lin = jnp.dot(
        first_normed.reshape(tokens, model_width),
        qkv_full[:, :kv_end],
        preferred_element_type=wide,
    ).reshape(seq_count, local_rows, kv_end)
    query_rot = rotate(
        qkv_lin[..., :query_width].reshape(seq_count, local_rows, query_heads, HD),
        head_cos,
        head_sin,
    ).astype(low)
    key_rot = (
        rotate(
            qkv_lin[..., query_width : query_width + kv_width].reshape(
                seq_count, local_rows, kv_heads, HD
            ),
            head_cos,
            head_sin,
        )
        .astype(low)
        .reshape(seq_count, local_rows, kv_width)
    )
    value_low = qkv_lin[..., query_width + kv_width :].astype(low)
    kv_blocks = [jnp.concatenate([key_rot, value_low], -1)]
    for _ in range(ctx - 1):
        kv_blocks.append(up_line(kv_blocks[-1]))
    kv_all = jnp.concatenate(kv_blocks, 1)
    full_rows = kv_all.shape[1]
    key_split = jnp.moveaxis(
        kv_all[..., :kv_width].reshape(seq_count, full_rows, kv_heads, HD), 2, 0
    )
    value_split = jnp.moveaxis(
        kv_all[..., kv_width:].reshape(seq_count, full_rows, kv_heads, HD), 2, 0
    )
    query_split = jnp.moveaxis(
        query_rot.reshape(seq_count, local_rows, kv_heads, group_size, HD), 2, 0
    )
    head_output, log_mass = lax.map(
        partial(attend_forward, key_mask=key_mask), (query_split, key_split, value_split)
    )
    attended = jnp.moveaxis(head_output, 0, 2).reshape(tokens, query_width)
    attn_part = jnp.einsum("tj,dj->td", attended, out_full, preferred_element_type=wide)
    attn_branch = pair_sum(attn_part)
    middle = layer_in + residual_scale * attn_branch.reshape(layer_in.shape)

    second_rms = rms_scale(middle)
    second_normed = (middle * second_rms * gain_two).astype(low)
    normed_blocks = gather_tokens(by_ctx(second_normed.reshape(tokens, model_width)))
    normed_all = jnp.concatenate([jnp.concatenate(b) for b in normed_blocks])
    ff_grad_all = jnp.concatenate([jnp.concatenate(b) for b in ff_grad_blocks])

    both_lin = jnp.dot(normed_all, both_full, preferred_element_type=wide)
    gate_lin = both_lin[:, :units]
    up_lin = both_lin[:, units:]
    gate_sig = jax.nn.sigmoid(gate_lin)
    gate_act = gate_lin * gate_sig
    hidden = (gate_act * up_lin).astype(low)
    hidden_grad = jnp.dot(ff_grad_all, down_full, preferred_element_type=wide)
    gate_grad = (hidden_grad * up_lin * gate_sig * (1.0 + gate_lin * (1.0 - gate_sig))).astype(low)
    up_grad = (hidden_grad * gate_act).astype(low)

    def sum_blocks(left, right):
        blocks = [None] * group
        for k in reversed([0] + order):
            rows = slice(k * tokens, (k + 1) * tokens)
            part = jnp.einsum(
                "tf,df->td", left[rows], right, preferred_element_type=wide
            ).astype(low)
            blocks[k] = (part[:half], part[half:])
        return by_fsdp(scatter_tokens(blocks)).reshape(layer_in.shape)

    def unit_term(left, right):
        return jnp.einsum("td,tf->df", left, right, preferred_element_type=wide).astype(low)

    def return_units(term):
        own = lax.psum_scatter(
            term.reshape(ctx, fsdp, shard, units), "ctx", scatter_dimension=0, tiled=False
        )
        if far > 1:
            own = lax.psum_scatter(
                own.reshape(far, group, shard, units),
                "fsdp",
                scatter_dimension=0,
                tiled=False,
                axis_index_groups=far_groups,
            )
        return lax.all_to_all(
            own.reshape(group * shard, units),
            "fsdp",
            0,
            1,
            tiled=True,
            axis_index_groups=near_groups if far > 1 else None,
        ).astype(wide)

    second_grad = sum_blocks(jnp.concatenate([gate_grad, up_grad], 1), both_full)
    ff_branch = sum_blocks(hidden, down_full)
    down_term = unit_term(ff_grad_all, hidden)
    gate_term = unit_term(normed_all, gate_grad)
    up_term = unit_term(normed_all, up_grad)
    second_grad, ff_branch, _, _, _ = lax.optimization_barrier(
        (second_grad, ff_branch, down_term, gate_term, up_term)
    )
    w_down_grad = return_units(down_term)
    w_gate_grad = return_units(gate_term)
    w_up_grad = return_units(up_term)
    output = (valid_rows * (middle + residual_scale * ff_branch)).astype(low)

    gain_two_term = jnp.sum(second_grad * middle * second_rms, axis=(0, 1))
    middle_grad = back + norm_back(second_grad, middle, second_rms, gain_two)

    attn_grad = (residual_scale * middle_grad).astype(low).reshape(tokens, model_width)
    out_term = jnp.einsum("td,tj->dj", attn_grad, attended, preferred_element_type=wide)
    attended_grad = jnp.dot(attn_grad, out_full, preferred_element_type=wide).astype(low)
    grad_split = jnp.moveaxis(
        attended_grad.reshape(seq_count, local_rows, kv_heads, group_size, HD), 2, 0
    )
    query_back, key_back, value_back = lax.map(
        partial(attend_backward, key_mask=key_mask),
        (query_split, key_split, value_split, grad_split, log_mass),
    )
    query_back = jnp.moveaxis(query_back, 0, 2).reshape(seq_count, local_rows, query_heads, HD)
    query_grad = (
        unrotate(query_back, head_cos, head_sin).astype(low).reshape(tokens, query_width)
    )
    key_spread = jnp.moveaxis(key_back, 0, 2).reshape(seq_count, full_rows, kv_width)
    value_spread = jnp.moveaxis(value_back, 0, 2).reshape(seq_count, full_rows, kv_width)
    kv_spread = jnp.concatenate([key_spread, value_spread], -1).reshape(
        seq_count, ctx, local_rows, 2 * kv_width
    )
    kv_own = kv_spread[:, ctx - 1]
    for s in reversed(range(ctx - 1)):
        kv_own = kv_spread[:, s] + down_line(kv_own.astype(low)).astype(wide)
    key_grad = (
        unrotate(
            kv_own[..., :kv_width].reshape(seq_count, local_rows, kv_heads, HD), head_cos, head_sin
        )
        .astype(low)
        .reshape(tokens, kv_width)
    )
    value_grad = kv_own[..., kv_width:].astype(low).reshape(tokens, kv_width)
    qkv_grad = jnp.concatenate([query_grad, key_grad, value_grad], -1)
    qkv_term = jnp.einsum(
        "td,tj->dj",
        first_normed.reshape(tokens, model_width),
        qkv_grad,
        preferred_element_type=wide,
    )
    first_part = jnp.einsum(
        "tj,dj->td", qkv_grad, qkv_full[:, :kv_end], preferred_element_type=wide
    )
    first_grad = pair_sum(first_part).reshape(layer_in.shape)
    gain_one_term = jnp.sum(first_grad * layer_in * first_rms, axis=(0, 1))
    input_grad = (middle_grad + norm_back(first_grad, layer_in, first_rms, gain_one)).astype(low)
    gain_terms = jnp.pad(jnp.stack([gain_one_term, gain_two_term], 1), ((0, 0), (0, 126)))
    qkv_term = jnp.concatenate([qkv_term, gain_terms], 1).astype(low)
    qkv_term, w_down_grad, w_gate_grad, w_up_grad = lax.optimization_barrier(
        (qkv_term, w_down_grad, w_gate_grad, w_up_grad)
    )
    w_out_grad, qkv_own = sum_weights(fsdp, ctx, [out_term.astype(low), qkv_term])
    return (
        output,
        input_grad,
        qkv_own[:, kv_end],
        qkv_own[:, :query_width],
        qkv_own[:, query_width : query_width + kv_width],
        qkv_own[:, query_width + kv_width : kv_end],
        w_out_grad,
        qkv_own[:, kv_end + 1],
        w_gate_grad,
        w_up_grad,
        w_down_grad,
    )


def solution(mesh):
    placed = (
        P("fsdp", "ctx", None),
        P("fsdp"),
        P("fsdp", "ctx", None),
        P(("fsdp", "ctx")),
        P(("fsdp", "ctx"), "tp"),
        P(("fsdp", "ctx"), "tp"),
        P(("fsdp", "ctx"), "tp"),
        P(("fsdp", "ctx"), "tp"),
        P(("fsdp", "ctx")),
        P(("fsdp", "ctx"), "tp"),
        P(("fsdp", "ctx"), "tp"),
        P(("fsdp", "ctx"), "tp"),
    )
    return jax.shard_map(
        local,
        mesh=mesh,
        in_specs=placed,
        out_specs=(
            P("fsdp", "ctx", None),
            P("fsdp", "ctx", None),
            P(("fsdp", "ctx")),
            P(("fsdp", "ctx"), "tp"),
            P(("fsdp", "ctx"), "tp"),
            P(("fsdp", "ctx"), "tp"),
            P(("fsdp", "ctx"), "tp"),
            P(("fsdp", "ctx")),
            P(("fsdp", "ctx"), "tp"),
            P(("fsdp", "ctx"), "tp"),
            P(("fsdp", "ctx"), "tp"),
        ),
        check_vma=False,
    )
```

time: 1690 us -> 1130 us (0.67)
  waiting for transfers between devices: 1200 us -> 256 us
  Pallas kernels: 0 us -> 303 us
  local copies, waits for them, and re-layouts: 87.3 us -> 158 us
  blocking collectives: 49.9 us -> 0 us
  starting transfers between devices: 13.8 us -> 51.1 us
  other arithmetic: 71.2 us -> 103 us
    reduce_scatter x8 -> x3, waiting for transfers between devices: 611 us -> 0.02 us  [return_units(): lax.psum_scatter(term.reshape(ctx, fsdp, shard, units), 'ctx', scatter_di...]
    all_gather x8 -> x2, waiting for transfers between devices: 489 us -> 0.01 us  [whole_width(): lax.all_gather(v, 'ctx', axis=0, tiled=False).reshape(model_width, -1)]
    pallas_call x0 -> x3, Pallas kernels: none -> 303 us  [the longest x1 162 us: sum_weights(): pl.pallas_call(partial(sum_kernel, fsdp, ctx, count), out_shape=[jax.Shap...]
    ppermute x0 -> x40, waiting for transfers between devices: none -> 241 us  [the longest x16 89.6 us: hop(): return lax.ppermute(v, 'fsdp', [(i, i ^ k) for i in range(fsdp)])]
    unnamed x21 -> x5, waiting for transfers between devices: 68.6 us -> 0.08 us
    all_to_all x3 -> x0, blocking collectives: 49.9 us -> none  [spread_units(): swapped = lax.all_to_all(weight, 'fsdp', 1, 0, tiled=True)]
    ppermute x0 -> x40, starting transfers between devices: none -> 38.8 us  [the longest x16 17 us: hop(): return lax.ppermute(v, 'fsdp', [(i, i ^ k) for i in range(fsdp)])]
    another operation x0 -> x8, local copies, waits for them, and re-layouts: none -> 24.4 us  [the longest x4 17.3 us: sum_blocks(): return by_fsdp(scatter_tokens(blocks)).reshape(layer_in.shape)]
  transfers between devices with their start and end apart: 23 -> 48, of which waited for: 19 -> 19; matrix products, arithmetic and copies ran while one was open for 14% -> 33% of each run, Pallas kernels for 0% -> 0%
where the time goes in v2:
time: 1130 us; the launch traced here: 1120 us
  Pallas kernels  303 us (27%)
  waiting for transfers between devices  256 us (23%)
  matrix products  236 us (21%)
  local copies, waits for them, and re-layouts  158 us (14%)
  other arithmetic  103 us (9%)
  starting transfers between devices  51.1 us (5%)
  between operations  16 us (1%)
    pallas_call x1, Pallas kernels, sum_weights(): pl.pallas_call(partial(sum_kernel, fsdp, ctx, count), out_shape=[jax.Shap...  162 us
    pallas_call x1, Pallas kernels, spread_weights(): pl.pallas_call(partial(spread_kernel, fsdp, ctx, count), out_shape=[jax.S...  92.7 us
    ppermute x16, waiting for transfers between devices, hop(): return lax.ppermute(v, 'fsdp', [(i, i ^ k) for i in range(fsdp)])  89.6 us
    ppermute x3, waiting for transfers between devices, up_line(): return lax.ppermute(v, 'ctx', [(i, i + 1) for i in range(ctx - 1)])  77.4 us
    ppermute x3, waiting for transfers between devices, down_line(): return lax.ppermute(v, 'ctx', [(i + 1, i) for i in range(ctx - 1)])  74.1 us
    dot_general x8, matrix products, sum_blocks(): jnp.einsum('tf,df->td', left[rows], right, preferred_element_type=wide)  53.6 us
    pallas_call x1, Pallas kernels, start_exchange(): pl.pallas_call(partial(line_kernel, fsdp, ctx, group, len(lines), len(swa...  48.8 us
    unnamed x198, local copies, waits for them, and re-layouts  44.4 us
  transfers between devices with their start and end apart: 48, of which 19 were waited for; matrix products, arithmetic and copies ran while one was open for 33% of the time, Pallas kernels for 0%

profile of v2, /device:TPU:16, one launch (start us, length us, event | category | flops | bytes accessed | tf_op | source)
XLA Modules:
  0.0 1123.6 jit_solution(16416162248083966504)
XLA Ops:
  10.0 48.8 %shard_map.203 = (bf16[4,128,1664]{2,1,0:T(8,128)(2,1)}, bf16[4,128,1024]{2,1,0:T(8,128)(2,1)}, bf16[4,128,2048]{2,1,0:T(8,128)(2,1)}, bf16[4,128,1024]{2,1,0:T(8,128)(2,1)}) custom-call(bf16[128,1664]{1,0:T(8,128)(2,1)} %fusion.104.refs_0_, bf16[128,1024]{1,0:T(8,128)(2,1)} %refs_1_.1, bf16[128,4096]{1,0:T(8,128)(2,1)} %refs_2_.1, ...), custom_call_target="tpu_custom_call" | custom-call | tf_op jit(solution)/shard_map/pallas_call | solution.py:265
  58.8 92.7 %shard_map.204 = (bf16[4,4,128,1664]{3,2,1,0:T(8,128)(2,1)}, bf16[4,4,128,1024]{3,2,1,0:T(8,128)(2,1)}) custom-call(bf16[4,128,1664]{2,1,0:T(8,128)(2,1)} %get-tuple-element.117.refs_0_, bf16[4,128,1024]{2,1,0:T(8,128)(2,1)} %get-tuple-element.118.refs_1_), custom_call_target="tpu_custom_call" | custom-call | tf_op jit(solution)/shard_map/pallas_call | solution.py:360
  186.6 35.7 %collective-permute-done.1 = bf16[2,256,512]{2,1,0:T(8,128)(2,1)} collective-permute-done((bf16[2,256,512]{2,1,0:T(8,128)(2,1)S(1)}, bf16[2,256,512]{2,1,0:T(8,128)(2,1)}, u32[]{:S(2)}, u32[]{:S(2)}) %collective-permute-start.1) | collective-permute-done | bytes 524320 | tf_op jit(solution)/shard_map/ppermute | solution.py:590
  227.9 36.9 %collective-permute-done.2 = bf16[2,256,512]{2,1,0:T(8,128)(2,1)} collective-permute-done((bf16[2,256,512]{2,1,0:T(8,128)(2,1)}, bf16[2,256,512]{2,1,0:T(8,128)(2,1)}, u32[]{:S(2)}, u32[]{:S(2)}) %collective-permute-start.2) | collective-permute-done | bytes 524320 | tf_op jit(solution)/shard_map/ppermute | solution.py:590
  277.0 37.6 %while.28 = (s32[]{:T(128)}, bf16[4,2,256,4,64]{2,4,3,1,0:T(8,128)(2,1)}, f32[4,2,4,256,1]{3,2,1,4,0:T(4,128)}, bf16[4,2,1024,64]{2,3,1,0:T(8,128)(2,1)}, bf16[4...) while((s32[]{:T(128)}, ...), condition=%wide.region_4.5_spmd.clone, body=%wide.region_1.4_spmd.clone.sunk | while | flops 563214336 | bytes 28644964 | solution.py:730
  337.7 22.9 %collective-permute-done.6 = bf16[256,2048]{0,1:T(8,128)(2,1)S(1)} collective-permute-done((bf16[256,2048]{0,1:T(8,128)(2,1)}, bf16[256,2048]{0,1:T(8,128)(2,1)S(1)}, u32[]{:S(2)}, u32[]{:S(2)}) %collective-permute-start.6) | collective-permute-done | bytes 1048608 | tf_op jit(solution)/shard_map/ppermute | solution.py:584
  392.5 12.8 %collective-permute-done.11 = bf16[256,2048]{0,1:T(8,128)(2,1)S(1)} collective-permute-done((bf16[256,2048]{0,1:T(8,128)(2,1)S(1)}, bf16[256,2048]{0,1:T(8,128)(2,1)S(1)}, u32[]{:S(2)}, u32[]{:S(2)}) %collective-permute-start.11) | collective-permute-done | bytes 1048608 | tf_op jit(solution)/shard_map/ppermute | solution.py:584
  429.3 24.4 %fusion.120 = f32[2048,2048]{0,1:T(8,128)} fusion(bf16[2048,2048]{0,1:T(8,128)(2,1)} %constant_dynamic-update-slice_fusion.8, bf16[2048,2048]{1,0:T(8,128)(2,1)} %bitcast.403), kind=kOutput, calls=%fused_computation.266 | convolution fusion | flops 17179869184 | bytes 33554432 | tf_op jit(solution)/shard_map/dot_general | solution.py:744
  453.7 23.4 %multiply_convert_fusion.2 = (bf16[2048,1024]{0,1:T(8,128)(2,1)}, bf16[2048,1024]{0,1:T(8,128)(2,1)}, bf16[2048,1024]{0,1:T(8,128)(2,1)}) fusion(f32[2048,2048]{0,1:T(8,128)} %fusion.120, bf16[2048,2048]{0,1:T(8,128)(2,1)} %constant_dynamic-update-slice_fusion, bf16[2048,1024]{1,0:T(8,128)(2,1)} %bitcast.410), kind=kOutput, calls=%fused_computation.80 | convolution fusion | flops 8621391872 | bytes 41943040 | tf_op jit(solution)/shard_map/dot_general | solution.py:750
  486.6 13.7 %convolution_convert_fusion.2 = bf16[2048,1024]{1,0:T(8,128)(2,1)} fusion(bf16[2048,2048]{0,1:T(8,128)(2,1)} %constant_dynamic-update-slice_fusion.8, bf16[2048,1024]{0,1:T(8,128)(2,1)S(1)} %copy-done.79), kind=kOutput, calls=%fused_computation.114 | convolution fusion | flops 8592031744 | bytes 16777216 | tf_op jit(solution)/shard_map/td,tf->df/dot_general | solution.py:765
  508.6 9.3 convolution_convert_fusion.12
  518.0 9.5 convolution_convert_fusion.11
  527.5 9.3 convolution_convert_fusion.10
  566.8 9.3 collective-permute-done.30
  594.3 13.5 %convolution_convert_fusion.3 = bf16[2048,1024]{1,0:T(8,128)(2,1)} fusion(bf16[2048,2048]{0,1:T(8,128)(2,1)} %constant_dynamic-update-slice_fusion.8, bf16[2048,1024]{0,1:T(8,128)(2,1)S(1)} %copy-done.78), kind=kOutput, calls=%fused_computation.115 | convolution fusion | flops 8592031744 | bytes 16777216 | tf_op jit(solution)/shard_map/td,tf->df/dot_general | solution.py:765
  615.4 18.5 %collective-permute-done.22 = bf16[256,2048]{1,0:T(8,128)(2,1)S(1)} collective-permute-done((bf16[256,2048]{1,0:T(8,128)(2,1)S(1)}, bf16[256,2048]{1,0:T(8,128)(2,1)S(1)}, u32[]{:S(2)}, u32[]{:S(2)}) %collective-permute-start.22) | collective-permute-done | bytes 1048608 | tf_op jit(solution)/shard_map/ppermute | solution.py:584
  636.0 10.6 convolution_convert_fusion.4
  690.1 62.2 %while.29 = (s32[]{:T(128)}, f32[4,2,256,4,64]{2,4,3,1,0:T(8,128)}, f32[4,2,1024,64]{2,3,1,0:T(8,128)}, f32[4,2,1024,64]{2,3,1,0:T(8,128)}, bf16[4,2,1024,64]{2,...) while((s32[]{:T(128)}, f32[4,2,256,4,64]{2,4,3,1,0:T(8,128)}, ...), condition=%wide.region_9.10_spmd.clone, body=%wide.region_7.9_spmd.clone.sunk | while | flops 1374943232 | bytes 69270656 | solution.py:810
  775.9 10.3 collective-permute-done.36
  792.4 33.8 %collective-permute-done.37 = bf16[2,256,512]{1,2,0:T(8,128)(2,1)S(1)} collective-permute-done((bf16[2,256,512]{1,2,0:T(8,128)(2,1)S(1)}, bf16[2,256,512]{1,2,0:T(8,128)(2,1)S(1)}, u32[]{:S(2)}, u32[]{:S(2)}) %collective-permute-start.37) | collective-permute-done | bytes 524320 | tf_op jit(solution)/shard_map/ppermute | solution.py:593
  835.4 30.0 %collective-permute-done.38 = bf16[2,256,512]{1,2,0:T(8,128)(2,1)S(1)} collective-permute-done((bf16[2,256,512]{1,2,0:T(8,128)(2,1)S(1)}, bf16[2,256,512]{1,2,0:T(8,128)(2,1)S(1)}, u32[]{:S(2)}, u32[]{:S(2)}) %collective-permute-start.38) | collective-permute-done | bytes 524320 | tf_op jit(solution)/shard_map/ppermute | solution.py:593
  909.5 9.6 fusion.71
  942.1 9.7 copy.169
  951.8 162.0 %shard_map.205 = (f32[128,1024]{1,0:T(8,128)S(1)}, f32[128,1664]{1,0:T(8,128)S(1)}) custom-call(bf16[4,4,128,1024]{3,2,1,0:T(8,128)(2,1)} %bitcast.362, bf16[4,4,128,1664]{3,2,1,0:T(8,128)(2,1)} %bitcast.339), custom_call_target="tpu_custom_call" | custom-call | tf_op jit(solution)/shard_map/pallas_call | solution.py:529
  (508 shorter events, 460.5 us)
Async XLA Ops:
  7.2 422.1 %all-gather.7.cloned.1.call-start = ((), (), s32[]{:S(2)}) async-start(), calls=%async_computation.10 | async-start | bytes 10485760 | tf_op jit(solution)/shard_map/all_gather | solution.py:677
  169.9 283.7 %all-gather.5.cloned.1.call-start = ((), (), s32[]{:S(2)}) async-start(), calls=%async_computation.9 | async-start | bytes 5242880 | tf_op jit(solution)/shard_map/all_gather | solution.py:677
  183.1 39.1 %collective-permute-start.1 = (bf16[2,256,512]{2,1,0:T(8,128)(2,1)S(1)}, bf16[2,256,512]{2,1,0:T(8,128)(2,1)}, u32[]{:S(2)}, u32[]{:S(2)}) collective-permute-start(bf16[2,256,512]{2,1,0:T(8,128)(2,1)S(1)} %collective-permute-done), channel_id=1, source_target_pairs={{0,2},{2,4},{4,6},{1,3},{3,5},{5,7},{8,10},{10,12},{12,14},{9,11},... | collective-permute-start | bytes 1572872 | tf_op jit(solution)/shard_map/ppermute | solution.py:590
  222.2 42.6 %collective-permute-start.2 = (bf16[2,256,512]{2,1,0:T(8,128)(2,1)}, bf16[2,256,512]{2,1,0:T(8,128)(2,1)}, u32[]{:S(2)}, u32[]{:S(2)}) collective-permute-start(bf16[2,256,512]{2,1,0:T(8,128)(2,1)} %collective-permute-done.1), channel_id=1, source_target_pairs={{0,2},{2,4},{4,6},{1,3},{3,5},{5,7},{8,10},{10,12},{12,14},{9,11},... | collective-permute-start | bytes 1572872 | tf_op jit(solution)/shard_map/ppermute | solution.py:590
  321.5 45.7 %collective-permute-start.3 = (bf16[512,2048]{1,0:T(8,128)(2,1)}, bf16[512,2048]{1,0:T(8,128)(2,1)}, u32[]{:S(2)}, u32[]{:S(2)}) collective-permute-start(bf16[512,2048]{1,0:T(8,128)(2,1)} %convolution_convert_fusion.9), channel_id=1, source_target_pairs={{0,1},{1,0},{2,3},{3,2},{4,5},{5,4},{6,7},{7,6},{8,9},{9,8},{10,11... | collective-permute-start | bytes 6291464 | tf_op jit(solution)/shard_map/ppermute | solution.py:587
  334.8 25.8 %collective-permute-start.6 = (bf16[256,2048]{0,1:T(8,128)(2,1)}, bf16[256,2048]{0,1:T(8,128)(2,1)S(1)}, u32[]{:S(2)}, u32[]{:S(2)}) collective-permute-start(bf16[256,2048]{0,1:T(8,128)(2,1)} %get-tuple-element.306), channel_id=1, source_target_pairs={{0,16},{8,24},{16,0},{24,8},{1,17},{9,25},{17,1},{25,9},{2,18},{10... | collective-permute-start | bytes 3145736 | tf_op jit(solution)/shard_map/ppermute | solution.py:584
  334.8 26.6 %collective-permute-start.4 = (bf16[256,2048]{0,1:T(8,128)(2,1)}, bf16[256,2048]{0,1:T(8,128)(2,1)}, u32[]{:S(2)}, u32[]{:S(2)}) collective-permute-start(bf16[256,2048]{0,1:T(8,128)(2,1)} %get-tuple-element.306), channel_id=1, source_target_pairs={{0,8},{8,0},{16,24},{24,16},{1,9},{9,1},{17,25},{25,17},{2,10},{10... | collective-permute-start | bytes 3145736 | tf_op jit(solution)/shard_map/ppermute | solution.py:584
  334.9 551.7 %reduce-scatter.8.cloned.1.call-start = ((), (), s32[]{:S(2)}) async-start(), calls=%async_computation.8 | async-start | bytes 5242880 | tf_op jit(solution)/shard_map/reduce_scatter | solution.py:768
  364.3 23.9 %collective-permute-start.7 = (bf16[256,2048]{0,1:T(8,128)(2,1)S(1)}, bf16[256,2048]{0,1:T(8,128)(2,1)}, u32[]{:S(2)}, u32[]{:S(2)}) collective-permute-start(bf16[256,2048]{0,1:T(8,128)(2,1)S(1)} %collective-permute-done.6), channel_id=1, source_target_pairs={{0,1},{1,0},{2,3},{3,2},{4,5},{5,4},{6,7},{7,6},{8,9},{9,8},{10,11... | collective-permute-start | bytes 3145736 | tf_op jit(solution)/shard_map/ppermute | solution.py:587
  380.2 25.1 %collective-permute-start.11 = (bf16[256,2048]{0,1:T(8,128)(2,1)S(1)}, bf16[256,2048]{0,1:T(8,128)(2,1)S(1)}, u32[]{:S(2)}, u32[]{:S(2)}) collective-permute-start(bf16[256,2048]{0,1:T(8,128)(2,1)S(1)} %get-tuple-element.302), channel_id=1, source_target_pairs={{0,8},{8,0},{16,24},{24,16},{1,9},{9,1},{17,25},{25,17},{2,10},{10... | collective-permute-start | bytes 3145736 | tf_op jit(solution)/shard_map/ppermute | solution.py:584
  382.9 27.6 %collective-permute-start.10 = (bf16[256,2048]{0,1:T(8,128)(2,1)S(1)}, bf16[256,2048]{0,1:T(8,128)(2,1)S(1)}, u32[]{:S(2)}, u32[]{:S(2)}) collective-permute-start(bf16[256,2048]{0,1:T(8,128)(2,1)S(1)} %pad_maximum_fusion.6), channel_id=1, source_target_pairs={{0,1},{1,0},{2,3},{3,2},{4,5},{5,4},{6,7},{7,6},{8,9},{9,8},{10,11... | collective-permute-start | bytes 3145736 | tf_op jit(solution)/shard_map/ppermute | solution.py:587
  382.9 25.6 %collective-permute-start.13 = (bf16[256,2048]{0,1:T(8,128)(2,1)S(1)}, bf16[256,2048]{0,1:T(8,128)(2,1)S(1)}, u32[]{:S(2)}, u32[]{:S(2)}) collective-permute-start(bf16[256,2048]{0,1:T(8,128)(2,1)S(1)} %get-tuple-element.302), channel_id=1, source_target_pairs={{0,16},{8,24},{16,0},{24,8},{1,17},{9,25},{17,1},{25,9},{2,18},{10... | collective-permute-start | bytes 3145736 | tf_op jit(solution)/shard_map/ppermute | solution.py:584
  550.0 42.9 %collective-permute-start.27 = (bf16[256,2048]{1,0:T(8,128)(2,1)}, bf16[256,2048]{1,0:T(8,128)(2,1)S(1)}, u32[]{:S(2)}, u32[]{:S(2)}) collective-permute-start(bf16[256,2048]{1,0:T(8,128)(2,1)} %slice.324), channel_id=1, source_target_pairs={{0,1},{1,0},{2,3},{3,2},{4,5},{5,4},{6,7},{7,6},{8,9},{9,8},{10,11... | collective-permute-start | bytes 3145736 | tf_op jit(solution)/shard_map/ppermute | solution.py:587
  551.1 64.3 %collective-permute-start.18 = (bf16[256,2048]{1,0:T(8,128)(2,1)}, bf16[256,2048]{1,0:T(8,128)(2,1)}, u32[]{:S(2)}, u32[]{:S(2)}) collective-permute-start(bf16[256,2048]{1,0:T(8,128)(2,1)} %slice.305), channel_id=1, source_target_pairs={{0,1},{1,0},{2,3},{3,2},{4,5},{5,4},{6,7},{7,6},{8,9},{9,8},{10,11... | collective-permute-start | bytes 3145736 | tf_op jit(solution)/shard_map/ppermute | solution.py:587
  554.8 341.6 %reduce-scatter.6.cloned.1.call-start = ((), (), s32[]{:S(2)}) async-start(), calls=%async_computation.7 | async-start | bytes 5242880 | tf_op jit(solution)/shard_map/reduce_scatter | solution.py:768
  578.1 35.4 %collective-permute-start.31 = (bf16[256,2048]{1,0:T(8,128)(2,1)S(1)}, bf16[256,2048]{1,0:T(8,128)(2,1)S(1)}, u32[]{:S(2)}, u32[]{:S(2)}) collective-permute-start(bf16[256,2048]{1,0:T(8,128)(2,1)S(1)} %pad_maximum_fusion.10), channel_id=1, source_target_pairs={{0,16},{8,24},{16,0},{24,8},{1,17},{9,25},{17,1},{25,9},{2,18},{10... | collective-permute-start | bytes 3145736 | tf_op jit(solution)/shard_map/ppermute | solution.py:584
  586.8 26.7 %collective-permute-start.34 = (bf16[256,2048]{1,0:T(8,128)(2,1)S(1)}, bf16[256,2048]{1,0:T(8,128)(2,1)S(1)}, u32[]{:S(2)}, u32[]{:S(2)}) collective-permute-start(bf16[256,2048]{1,0:T(8,128)(2,1)S(1)} %pad_maximum_fusion.11), channel_id=1, source_target_pairs={{0,8},{8,0},{16,24},{24,16},{1,9},{9,1},{17,25},{25,17},{2,10},{10... | collective-permute-start | bytes 3145736 | tf_op jit(solution)/shard_map/ppermute | solution.py:584
  591.0 43.0 %collective-permute-start.22 = (bf16[256,2048]{1,0:T(8,128)(2,1)S(1)}, bf16[256,2048]{1,0:T(8,128)(2,1)S(1)}, u32[]{:S(2)}, u32[]{:S(2)}) collective-permute-start(bf16[256,2048]{1,0:T(8,128)(2,1)S(1)} %pad_maximum_fusion.8), channel_id=1, source_target_pairs={{0,16},{8,24},{16,0},{24,8},{1,17},{9,25},{17,1},{25,9},{2,18},{10... | collective-permute-start | bytes 3145736 | tf_op jit(solution)/shard_map/ppermute | solution.py:584
  592.9 41.1 %collective-permute-start.25 = (bf16[256,2048]{1,0:T(8,128)(2,1)S(1)}, bf16[256,2048]{1,0:T(8,128)(2,1)S(1)}, u32[]{:S(2)}, u32[]{:S(2)}) collective-permute-start(bf16[256,2048]{1,0:T(8,128)(2,1)S(1)} %pad_maximum_fusion.9), channel_id=1, source_target_pairs={{0,8},{8,0},{16,24},{24,16},{1,9},{9,1},{17,25},{25,17},{2,10},{10... | collective-permute-start | bytes 3145736 | tf_op jit(solution)/shard_map/ppermute | solution.py:584
  615.4 33.9 %collective-permute-start.35 = (bf16[256,2048]{1,0:T(8,128)(2,1)S(1)}, bf16[256,2048]{1,0:T(8,128)(2,1)}, u32[]{:S(2)}, u32[]{:S(2)}) collective-permute-start(bf16[256,2048]{1,0:T(8,128)(2,1)S(1)} %add_convert_fusion.1), channel_id=1, source_target_pairs={{0,1},{1,0},{2,3},{3,2},{4,5},{5,4},{6,7},{7,6},{8,9},{9,8},{10,11... | collective-permute-start | bytes 3145736 | tf_op jit(solution)/shard_map/ppermute | solution.py:587
  635.9 27.1 %collective-permute-start.26 = (bf16[256,2048]{1,0:T(8,128)(2,1)S(1)}, bf16[256,2048]{1,0:T(8,128)(2,1)}, u32[]{:S(2)}, u32[]{:S(2)}) collective-permute-start(bf16[256,2048]{1,0:T(8,128)(2,1)S(1)} %add_convert_fusion.3), channel_id=1, source_target_pairs={{0,1},{1,0},{2,3},{3,2},{4,5},{5,4},{6,7},{7,6},{8,9},{9,8},{10,11... | collective-permute-start | bytes 3145736 | tf_op jit(solution)/shard_map/ppermute | solution.py:587
  646.7 272.4 %reduce-scatter.4.cloned.1.call-start = ((), (), s32[]{:S(2)}) async-start(), calls=%async_computation.6 | async-start | bytes 5242880 | tf_op jit(solution)/shard_map/reduce_scatter | solution.py:768
  787.3 38.8 %collective-permute-start.37 = (bf16[2,256,512]{1,2,0:T(8,128)(2,1)S(1)}, bf16[2,256,512]{1,2,0:T(8,128)(2,1)S(1)}, u32[]{:S(2)}, u32[]{:S(2)}) collective-permute-start(bf16[2,256,512]{1,2,0:T(8,128)(2,1)S(1)} %fusion.101), channel_id=1, source_target_pairs={{2,0},{4,2},{6,4},{3,1},{5,3},{7,5},{10,8},{12,10},{14,12},{11,9},... | collective-permute-start | bytes 1572872 | tf_op jit(solution)/shard_map/ppermute | solution.py:593
  826.3 39.1 %collective-permute-start.38 = (bf16[2,256,512]{1,2,0:T(8,128)(2,1)S(1)}, bf16[2,256,512]{1,2,0:T(8,128)(2,1)S(1)}, u32[]{:S(2)}, u32[]{:S(2)}) collective-permute-start(bf16[2,256,512]{1,2,0:T(8,128)(2,1)S(1)} %fusion.99), channel_id=1, source_target_pairs={{2,0},{4,2},{6,4},{3,1},{5,3},{7,5},{10,8},{12,10},{14,12},{11,9},... | collective-permute-start | bytes 1572872 | tf_op jit(solution)/shard_map/ppermute | solution.py:593
  (108 other events, 1729.5 us)
Sparse Core Ops, SparseCore 0:
  170.1 162.5 all-gather.6
  335.0 85.3 all-gather.4
  554.9 77.3 reduce-scatter.7
  646.8 77.4 reduce-scatter.5
  771.0 103.9 reduce-scatter.3

commit v3 on v2

--- a/solution.py
+++ b/solution.py
@@ -52,58 +52,324 @@
     )
 
 
-def masked_scores(grouped_query_rows, key_row_block, key_mask):
-    scores = (
-        jnp.einsum(
-            "sqgd,skd->sgqk", grouped_query_rows, key_row_block, preferred_element_type=jnp.float32
-        )
-        * score_scale
-    )
-    return jnp.where(key_mask[:, None], scores, masked_score)
-
-
-def attend_forward(block_item, key_mask):
-    grouped_query_rows, key_row_block, value_row_block = block_item
-    scores = masked_scores(grouped_query_rows, key_row_block, key_mask)
-    top_score = jnp.max(scores, -1, keepdims=True)
-    exp_scores = jnp.exp(scores - top_score)
-    total_mass = jnp.sum(exp_scores, -1, keepdims=True)
-    probs_low = (exp_scores / total_mass).astype(jnp.bfloat16)
-    head_output = jnp.einsum(
-        "sgqk,skd->sqgd", probs_low, value_row_block, preferred_element_type=jnp.float32
-    )
-    return (head_output.astype(jnp.bfloat16), top_score + jnp.log(total_mass))
-
-
-def attend_backward(block_item, key_mask):
-    grouped_query_rows, key_row_block, value_row_block, out_grad, log_mass = block_item
-    scores = masked_scores(grouped_query_rows, key_row_block, key_mask)
-    attention_probabilities = jnp.exp(scores - log_mass)
-    probs_low = attention_probabilities.astype(jnp.bfloat16)
-    value_grad = jnp.einsum(
-        "sgqk,sqgd->skd", probs_low, out_grad, preferred_element_type=jnp.float32
-    )
-    probs_grad = jnp.einsum(
-        "sqgd,skd->sgqk", out_grad, value_row_block, preferred_element_type=jnp.float32
-    )
-    score_grad = (
-        attention_probabilities
-        * (probs_grad - jnp.sum(attention_probabilities * probs_grad, -1, keepdims=True))
-    ).astype(jnp.bfloat16)
-    query_grad = (
-        jnp.einsum("sgqk,skd->sqgd", score_grad, key_row_block, preferred_element_type=jnp.float32)
-        * score_scale
-    )
-    key_grad = (
-        jnp.einsum(
-            "sgqk,sqgd->skd", score_grad, grouped_query_rows, preferred_element_type=jnp.float32
-        )
-        * score_scale
-    )
-    return (query_grad, key_grad, value_grad)
-
-
 MESH_ID = pl.DeviceIdType.MESH
+NT = (((1,), (1,)), ((), ()))
+TN = (((0,), (0,)), ((), ()))
+SMEM = pltpu.SMEM
+
+
+def mul(left, right, dims=(((1,), (0,)), ((), ()))):
+    return lax.dot_general(left, right, dims, preferred_element_type=jnp.float32)
+
+
+def reorder(v, first, second, width):
+    if width % 128:
+        return v
+    pieces = []
+    for b in range(second):
+        for a in range(first):
+            start = (a * second + b) * width
+            pieces.append(v[:, start : start + width])
+    return jnp.concatenate(pieces, 1)
+
+
+def turn(t, sign):
+    lane = lax.broadcasted_iota(jnp.int32, t.shape, 1)
+    ahead = pltpu.roll(t, 128 - HD // 2, 1)
+    behind = pltpu.roll(t, HD // 2, 1)
+    return jnp.where(lax.rem(lane, HD) < HD // 2, -sign * ahead, sign * behind)
+
+
+def row_valid(len_ref, rows, local_rows):
+    step = pl.program_id(0)
+    start = step * rows
+    seq = start // local_rows
+    place = (
+        lax.axis_index("ctx") * local_rows
+        + lax.rem(start, local_rows)
+        + lax.broadcasted_iota(jnp.int32, (rows, 1), 0)
+    )
+    return (place < len_ref[seq]).astype(jnp.float32)
+
+
+def qkv_kernel(dims, x_ref, w_ref, gain_ref, cos_ref, sin_ref, normed_ref, q_ref, kv_ref):
+    x = reorder(x_ref[...].astype(jnp.float32), *dims)
+    normed = (x * rms_scale(x) * gain_ref[...]).astype(jnp.bfloat16)
+    normed_ref[...] = normed
+    lin = mul(normed, w_ref[...])
+    cosines, sines = cos_ref[...], sin_ref[...]
+    width = q_ref.shape[1]
+    half = kv_ref.shape[1] // 2
+    for start in range(0, width + half, 128):
+        t = lin[:, start : start + 128]
+        t = (t * cosines + turn(t, 1.0) * sines).astype(jnp.bfloat16)
+        if start < width:
+            q_ref[:, start : start + 128] = t
+        else:
+            kv_ref[:, start - width : start - width + 128] = t
+    kv_ref[:, half:] = lin[:, width + half :].astype(jnp.bfloat16)
+
+
+def key_biases(len_ref, rows, ctx):
+    length = len_ref[pl.program_id(0)]
+    me = lax.axis_index("ctx")
+    row = lax.broadcasted_iota(jnp.int32, (rows, rows), 0)
+    col = lax.broadcasted_iota(jnp.int32, (rows, rows), 1)
+    first = jnp.where((col <= row) & (me * rows + col < length), 0.0, masked_score)
+    out = [first]
+    for s in range(1, ctx):
+        place = (me - s) * rows + lax.broadcasted_iota(jnp.int32, (1, rows), 1)
+        out.append(jnp.where((place >= 0) & (place < length), 0.0, masked_score))
+    return out
+
+
+def attend_kernel(ctx, len_ref, q_ref, *refs):
+    keys, values = refs[:ctx], refs[ctx : 2 * ctx]
+    o_ref, lse_ref = refs[2 * ctx :]
+    rows = q_ref.shape[0]
+    biases = key_biases(len_ref, rows, ctx)
+    lane = lax.broadcasted_iota(jnp.int32, (rows, 128), 1)
+    lse_all = jnp.zeros((rows, 128), jnp.float32)
+    for j in range(q_ref.shape[1] // 128):
+        q_pair = q_ref[:, j * 128 : (j + 1) * 128] * jnp.bfloat16(score_scale)
+        outs = []
+        for g in range(2):
+            mine = (lane < HD) if g == 0 else (lane >= HD)
+            q_head = jnp.where(mine, q_pair, jnp.zeros_like(q_pair))
+            scores = [mul(q_head, k[...], NT) + b for k, b in zip(keys, biases)]
+            top = scores[0].max(-1, keepdims=True)
+            for s in scores[1:]:
+                top = jnp.maximum(top, s.max(-1, keepdims=True))
+            mass, out = 0.0, 0.0
+            for s, v in zip(scores, values):
+                p = jnp.exp(s - top)
+                mass = mass + p.sum(-1, keepdims=True)
+                out = out + mul(p.astype(jnp.bfloat16), v[...])
+            outs.append(out / mass)
+            lse_all = jnp.where(lane == 2 * j + g, top + jnp.log(mass), lse_all)
+        o_ref[:, j * 128 : (j + 1) * 128] = jnp.where(lane < HD, outs[0], outs[1]).astype(
+            jnp.bfloat16
+        )
+    lse_ref[...] = lse_all
+
+
+def attend_back_kernel(ctx, len_ref, q_ref, do_ref, lse_ref, cos_ref, sin_ref, *refs):
+    keys, values = refs[:ctx], refs[ctx : 2 * ctx]
+    dq_ref, dkv_ref, dk_sum, dv_sum = refs[2 * ctx :]
+    rows = q_ref.shape[0]
+    biases = key_biases(len_ref, rows, ctx)
+    lane = lax.broadcasted_iota(jnp.int32, (rows, 128), 1)
+    dk_sum[...] = jnp.zeros_like(dk_sum)
+    dv_sum[...] = jnp.zeros_like(dv_sum)
+    lse_all = lse_ref[...]
+    for j in range(q_ref.shape[1] // 128):
+        q_pair = q_ref[:, j * 128 : (j + 1) * 128] * jnp.bfloat16(score_scale)
+        do_pair = do_ref[:, j * 128 : (j + 1) * 128]
+        dqs = []
+        for g in range(2):
+            mine = (lane < HD) if g == 0 else (lane >= HD)
+            q_head = jnp.where(mine, q_pair, jnp.zeros_like(q_pair))
+            do_head = jnp.where(mine, do_pair, jnp.zeros_like(do_pair))
+            h = 2 * j + g
+            lse = lse_all[:, h : h + 1]
+            probs, grads, total = [], [], 0.0
+            for s in range(ctx):
+                p = jnp.exp(mul(q_head, keys[s][...], NT) + (biases[s] - lse))
+                dp = mul(do_head, values[s][...], NT)
+                total = total + (p * dp).sum(-1, keepdims=True)
+                probs.append(p)
+                grads.append(dp)
+            dq = 0.0
+            for s in range(ctx):
+                ds = (probs[s] * (grads[s] - total)).astype(jnp.bfloat16)
+                dv_sum[s] += mul(probs[s].astype(jnp.bfloat16), do_head, TN)
+                dk_sum[s] += mul(ds, q_head, TN)
+                dq = dq + mul(ds, keys[s][...])
+            dqs.append(dq)
+        dq = jnp.where(lane < HD, dqs[0], dqs[1]) * score_scale
+        dq = dq * cos_ref[...] + turn(dq * sin_ref[...], -1.0)
+        dq_ref[:, j * 128 : (j + 1) * 128] = dq.astype(jnp.bfloat16)
+    for s in range(ctx):
+        dkv_ref[s, 0] = dk_sum[s].astype(dkv_ref.dtype)
+        dkv_ref[s, 1] = dv_sum[s].astype(dkv_ref.dtype)
+
+
+def cot_kernel(dims, local_rows, len_ref, cot_ref, ff_ref):
+    rows = cot_ref.shape[0]
+    back = cot_ref[...].astype(jnp.float32) * row_valid(len_ref, rows, local_rows)
+    ff_ref[...] = reorder((residual_scale * back).astype(jnp.bfloat16), *dims)
+
+
+def middle_kernel(dims, x_ref, part_ref, other_ref, gain_ref, middle_ref, normed_ref):
+    branch = part_ref[...].astype(jnp.float32) + other_ref[...].astype(jnp.float32)
+    middle = reorder(x_ref[...].astype(jnp.float32), *dims) + residual_scale * branch
+    middle_ref[...] = middle
+    normed_ref[...] = (middle * rms_scale(middle) * gain_ref[...]).astype(jnp.bfloat16)
+
+
+def swiglu_kernel(n_ref, g_ref, both_ref, down_ref, hidden_ref, grads_ref, second_ref, ff_ref):
+    units = hidden_ref.shape[1]
+    lin = mul(n_ref[...], both_ref[...])
+    gate, up = lin[:, :units], lin[:, units:]
+    sig = jax.nn.sigmoid(gate)
+    act = gate * sig
+    hidden = (act * up).astype(jnp.bfloat16)
+    hidden_ref[...] = hidden
+    hidden_grad = mul(g_ref[...], down_ref[...])
+    grads_ref[:, :units] = (hidden_grad * up * sig * (1.0 + gate * (1.0 - sig))).astype(
+        jnp.bfloat16
+    )
+    grads_ref[:, units:] = (hidden_grad * act).astype(jnp.bfloat16)
+    second_ref[...] = mul(grads_ref[...], both_ref[...], NT).astype(jnp.bfloat16)
+    ff_ref[...] = mul(hidden, down_ref[...], NT).astype(jnp.bfloat16)
+
+
+def middle_back_kernel(
+    dims, local_rows, len_ref, cot_ref, middle_ref, grad_ref, gain_ref, back_ref, attn_ref, gain_sum
+):
+    rows = cot_ref.shape[0]
+    back = cot_ref[...].astype(jnp.float32) * row_valid(len_ref, rows, local_rows)
+    middle = middle_ref[...]
+    grad = grad_ref[...].astype(jnp.float32)
+    scale = rms_scale(middle)
+    out = reorder(back, *dims) + norm_back(grad, middle, scale, gain_ref[...])
+    back_ref[...] = out
+    attn_ref[...] = (residual_scale * out).astype(jnp.bfloat16)
+
+    @pl.when(pl.program_id(0) == 0)
+    def _():
+        gain_sum[...] = jnp.zeros_like(gain_sum)
+
+    gain_sum[...] += (grad * middle * scale).sum(0, keepdims=True)
+
+
+def output_kernel(dims, local_rows, len_ref, middle_ref, ff_ref, out_ref):
+    rows = middle_ref.shape[0]
+    out = middle_ref[...] + residual_scale * ff_ref[...].astype(jnp.float32)
+    out = (out * row_valid(len_ref, rows, local_rows)).astype(jnp.bfloat16)
+    out_ref[...] = reorder(out, *dims)
+
+
+def input_back_kernel(
+    dims, x_ref, part_ref, other_ref, back_ref, gain_ref, out_ref, gain_sum
+):
+    first, second, width = dims
+    x = reorder(x_ref[...].astype(jnp.float32), *dims)
+    grad = (part_ref[...].astype(jnp.float32) + other_ref[...].astype(jnp.float32))
+    scale = rms_scale(x)
+    out = back_ref[...] + norm_back(grad, x, scale, gain_ref[...])
+    out_ref[...] = reorder(out.astype(jnp.bfloat16), second, first, width)
+
+    @pl.when(pl.program_id(0) == 0)
+    def _():
+        gain_sum[...] = jnp.zeros_like(gain_sum)
+
+    gain_sum[...] += (grad * x * scale).sum(0, keepdims=True)
+
+
+def by_rows(kernel, rows, ins, outs, flops=0, limit=40):
+    total = max(v.shape[0] for v, kind in ins if kind == "rows")
+    in_specs = []
+    moved = 0
+    for v, kind in ins:
+        moved += v.size * v.dtype.itemsize
+        if kind == "rows":
+            in_specs.append(pl.BlockSpec((rows, v.shape[1]), lambda i: (i, 0)))
+        elif kind == "cycle":
+            period = v.shape[0] // rows
+            in_specs.append(
+                pl.BlockSpec((rows, v.shape[1]), lambda i, period=period: (lax.rem(i, period), 0))
+            )
+        elif kind == "smem":
+            in_specs.append(pl.BlockSpec(memory_space=SMEM))
+        else:
+            in_specs.append(
+                pl.BlockSpec(v.shape, lambda i: (0, 0), pipeline_mode=pl.Buffered(1))
+            )
+    out_specs = []
+    for shape, dtype in outs:
+        moved += shape[0] * shape[1] * jnp.dtype(dtype).itemsize
+        if shape[0] == 1:
+            out_specs.append(pl.BlockSpec(shape, lambda i: (0, 0)))
+        else:
+            out_specs.append(pl.BlockSpec((rows, shape[1]), lambda i: (i, 0)))
+    return pl.pallas_call(
+        kernel,
+        grid=(total // rows,),
+        in_specs=in_specs,
+        out_specs=out_specs,
+        out_shape=[jax.ShapeDtypeStruct(shape, dtype) for shape, dtype in outs],
+        compiler_params=pltpu.CompilerParams(vmem_limit_bytes=limit * 1024 * 1024),
+        cost_estimate=pl.CostEstimate(flops=flops, bytes_accessed=moved, transcendentals=0),
+    )(*[v for v, _ in ins])
+
+
+def kv_specs(ctx, rows, pairs):
+    def spec(slot, start):
+        return pl.BlockSpec((None, rows, 128), lambda s, p: (slot, s, start + p))
+
+    return [spec(slot, start) for start in (0, pairs) for slot in range(ctx)]
+
+
+def attend(lengths, query, kv_all):
+    ctx = kv_all.shape[0]
+    seqs = lengths.shape[0]
+    rows = query.shape[0] // seqs
+    pairs = kv_all.shape[2] // 256
+    wide = query.shape[1] // pairs
+    flops = 4 * query.shape[0] * query.shape[1] * rows * ctx
+    return pl.pallas_call(
+        partial(attend_kernel, ctx),
+        grid=(seqs, pairs),
+        in_specs=[
+            pl.BlockSpec(memory_space=SMEM),
+            pl.BlockSpec((rows, wide), lambda s, p: (s, p)),
+        ]
+        + kv_specs(ctx, rows, pairs),
+        out_specs=[
+            pl.BlockSpec((rows, wide), lambda s, p: (s, p)),
+            pl.BlockSpec((rows, 128), lambda s, p: (s, p)),
+        ],
+        out_shape=[
+            jax.ShapeDtypeStruct(query.shape, jnp.bfloat16),
+            jax.ShapeDtypeStruct((query.shape[0], 128 * pairs), jnp.float32),
+        ],
+        compiler_params=pltpu.CompilerParams(vmem_limit_bytes=40 * 1024 * 1024),
+        cost_estimate=pl.CostEstimate(flops=4 * flops, bytes_accessed=6 << 20, transcendentals=0),
+    )(lengths, query, *[kv_all] * (2 * ctx))
+
+
+def attend_back(lengths, query, out_grad, lse, cosines, sines, kv_all):
+    ctx = kv_all.shape[0]
+    seqs = lengths.shape[0]
+    rows = query.shape[0] // seqs
+    pairs = kv_all.shape[2] // 256
+    wide = query.shape[1] // pairs
+    flops = 10 * query.shape[0] * query.shape[1] * rows * ctx
+    return pl.pallas_call(
+        partial(attend_back_kernel, ctx),
+        grid=(seqs, pairs),
+        in_specs=[
+            pl.BlockSpec(memory_space=SMEM),
+            pl.BlockSpec((rows, wide), lambda s, p: (s, p)),
+            pl.BlockSpec((rows, wide), lambda s, p: (s, p)),
+            pl.BlockSpec((rows, 128), lambda s, p: (s, p)),
+            pl.BlockSpec((rows, 128), lambda s, p: (0, 0)),
+            pl.BlockSpec((rows, 128), lambda s, p: (0, 0)),
+        ]
+        + kv_specs(ctx, rows, pairs),
+        out_specs=[
+            pl.BlockSpec((rows, wide), lambda s, p: (s, p)),
+            pl.BlockSpec((ctx, 2, rows, 128), lambda s, p: (0, 0, s, p)),
+        ],
+        out_shape=[
+            jax.ShapeDtypeStruct(query.shape, jnp.bfloat16),
+            jax.ShapeDtypeStruct((ctx, 2, query.shape[0], 128 * pairs), jnp.bfloat16),
+        ],
+        scratch_shapes=[pltpu.VMEM((ctx, rows, 128), jnp.float32)] * 2,
+        compiler_params=pltpu.CompilerParams(vmem_limit_bytes=40 * 1024 * 1024),
+        cost_estimate=pl.CostEstimate(flops=4 * flops, bytes_accessed=10 << 20, transcendentals=0),
+    )(lengths, query, out_grad, lse, cosines, sines, *[kv_all] * (2 * ctx))
 
 
 def low_bit(k):
@@ -279,10 +545,10 @@
     return outs[: len(lines)], outs[len(lines) :]
 
 
-def spread_kernel(fsdp, ctx, count, *refs):
+def spread_kernel(fsdp, ctx, count, chain, *refs):
     ins = refs[:count]
-    outs = refs[count : 2 * count]
-    own_sem, f_send, f_recv = refs[2 * count :]
+    outs = refs[count + chain : 2 * count + chain]
+    own_sem, f_send, f_recv, c_own, c_send, c_recv = refs[2 * (count + chain) :]
     me_f = lax.axis_index("fsdp")
     me_c = lax.axis_index("ctx")
     me_t = lax.axis_index("tp")
@@ -295,10 +561,64 @@
     barrier = pltpu.get_barrier_semaphore()
     for b in bits:
         pl.semaphore_signal(barrier, inc=1, device_id=peer(b), device_id_type=MESH_ID)
-    pl.semaphore_wait(barrier, len(bits))
+    if chain:
+        chain_in, chain_out = refs[count], refs[2 * count + 1]
+        for step in (-1, 1):
+            there = me_c + step
+
+            @pl.when((there >= 0) & (there < ctx))
+            def _():
+                pl.semaphore_signal(
+                    barrier, inc=1, device_id=(me_f, there, me_t), device_id_type=MESH_ID
+                )
+
+        pl.semaphore_wait(barrier, len(bits) + line_neighbours(me_c, ctx))
+    else:
+        pl.semaphore_wait(barrier, len(bits))
+
+    def climb(s):
+        return pltpu.make_async_remote_copy(
+            src_ref=chain_out.at[s] if s else chain_in,
+            dst_ref=chain_out.at[s + 1],
+            send_sem=c_send.at[s],
+            recv_sem=c_recv.at[s + 1],
+            device_id=(me_f, me_c + 1, me_t),
+            device_id_type=MESH_ID,
+        )
+
+    def keep(s):
+        return pltpu.make_async_copy(chain_in, chain_out.at[s], c_own.at[s])
+
+    def send_up(s):
+        @pl.when((me_c >= s) & (me_c < ctx - 1))
+        def _():
+            climb(s).start()
+
+    def take_up(s):
+        @pl.when(me_c >= s)
+        def _():
+            pltpu.make_async_remote_copy(
+                src_ref=chain_out.at[s],
+                dst_ref=chain_out.at[s],
+                send_sem=c_send.at[s - 1],
+                recv_sem=c_recv.at[s],
+                device_id=(me_f, me_c - 1, me_t),
+                device_id_type=MESH_ID,
+            ).wait_recv()
+
+        if s < ctx - 1:
+            send_up(s)
+
+    if chain:
+        send_up(0)
+        keep(0).start()
+        for s in range(1, ctx):
+            @pl.when(me_c < s)
+            def _():
+                keep(s).start()
 
     def place(i, shard, have, k, part):
-        block = outs[i].at[flip_index(me_f, have, fsdp), shard]
+        block = outs[i].at[shard, flip_index(me_f, have, fsdp)]
         half = ins[i].shape[1] // 2
         return block if k == low_bit(k) else block.at[pl.ds(part * half, half)]
 
@@ -323,15 +643,19 @@
         ]
 
     own = [
-        pltpu.make_async_copy(ins[i], outs[i].at[me_f], own_sem.at[i]) for i in range(count)
+        pltpu.make_async_copy(ins[i], outs[i].at[:, me_f], own_sem.at[i]) for i in range(count)
     ]
     for i in range(count):
         for shard in range(ctx):
             for b in ways(0):
                 f_copy(i, shard, 0, b).start()
         own[i].start()
+    climbed = 1
     for i in range(count):
         for k in order:
+            if chain and climbed < ctx:
+                take_up(climbed)
+                climbed += 1
             parts = [(0, k)] if k == low_bit(k) else [(0, low_bit(k)), (1, high_bit(k))]
             for shard in range(ctx):
                 for part, b in parts:
@@ -346,6 +670,23 @@
                     ).wait_recv()
                 for b in ways(k):
                     f_copy(i, shard, k, b).start()
+    if chain:
+        for s in range(climbed, ctx):
+            take_up(s)
+        keep(0).wait()
+        for s in range(ctx):
+            if s:
+
+                @pl.when(me_c < s)
+                def _():
+                    keep(s).wait()
+
+            if s < ctx - 1:
+
+                @pl.when((me_c >= s) & (me_c < ctx - 1))
+                def _():
+                    climb(s).wait_send()
+
     for i in range(count):
         own[i].wait()
         for have in [0] + order:
@@ -354,31 +695,47 @@
                     f_copy(i, shard, have, b).wait_send()
 
 
-def spread_weights(fsdp, ctx, arrays):
+def spread_weights(fsdp, ctx, arrays, chain=None):
     count = len(arrays)
     sems = pltpu.SemaphoreType.DMA
+    extra = [] if chain is None else [chain]
     outs = pl.pallas_call(
-        partial(spread_kernel, fsdp, ctx, count),
-        out_shape=[jax.ShapeDtypeStruct((fsdp,) + v.shape, v.dtype) for v in arrays],
-        in_specs=[pl.BlockSpec(memory_space=pl.ANY)] * count,
-        out_specs=[pl.BlockSpec(memory_space=pl.ANY)] * count,
+        partial(spread_kernel, fsdp, ctx, count, len(extra)),
+        out_shape=[
+            jax.ShapeDtypeStruct((ctx, fsdp) + v.shape[1:], v.dtype) for v in arrays
+        ]
+        + [jax.ShapeDtypeStruct((ctx,) + v.shape, v.dtype) for v in extra],
+        in_specs=[pl.BlockSpec(memory_space=pl.ANY)] * (count + len(extra)),
+        out_specs=[pl.BlockSpec(memory_space=pl.ANY)] * (count + len(extra)),
         scratch_shapes=[
             sems((count,)),
             sems((count, ctx, fsdp, 2)),
             sems((count, ctx, fsdp, 2)),
+            sems((ctx,)),
+            sems((ctx,)),
+            sems((ctx,)),
         ],
-        compiler_params=pltpu.CompilerParams(collective_id=1, has_side_effects=True),
-    )(*arrays)
-    return [o.reshape(-1, v.shape[-1]) for o, v in zip(outs, arrays)]
-
-
-def sum_kernel(fsdp, ctx, count, *refs):
+        compiler_params=pltpu.CompilerParams(
+            collective_id=1 if chain is None else 3, has_side_effects=True
+        ),
+    )(*arrays, *extra)
+    return [o.reshape(-1, v.shape[-1]) for o, v in zip(outs, arrays)] + list(outs[count:])
+
+
+def sum_kernel(fsdp, ctx, count, chain, *refs):
     ins = refs[:count]
+    if chain:
+        parts_ref, cos_ref, sin_ref = refs[count : count + 3]
+        refs = refs[:count] + refs[count + 3 :]
+        kv_ref = refs[2 * count]
+        refs = refs[: 2 * count] + refs[2 * count + 1 :]
     outs = refs[count : 2 * count]
     held = refs[2 * count : 3 * count]
     got = refs[3 * count : 4 * count]
     line = refs[4 * count : 5 * count]
-    in_sem, f_send, f_recv, z_send, z_recv = refs[5 * count :]
+    in_sem, f_send, f_recv, z_send, z_recv = refs[5 * count : 5 * count + 5]
+    if chain:
+        kv_parts, kv_got, kv_sem, c_send, c_recv = refs[5 * count + 5 :]
     me_f = lax.axis_index("fsdp")
     me_c = lax.axis_index("ctx")
     me_t = lax.axis_index("tp")
@@ -396,10 +753,13 @@
             act(there)
 
     loads = {}
+    if chain:
+        kv_load = pltpu.make_async_copy(parts_ref, kv_parts, kv_sem.at[0])
+        kv_load.start()
     for i in range(count):
         for k in reversed([0] + order):
             loads[i, k] = pltpu.make_async_copy(
-                ins[i].at[flip_index(me_f, k, fsdp)], held[i].at[k], in_sem.at[i, k]
+                ins[i].at[:, flip_index(me_f, k, fsdp)], held[i].at[k], in_sem.at[i, k]
             )
             loads[i, k].start()
 
@@ -434,16 +794,16 @@
         )
 
     def add(into, other):
-        rows = into.shape[0]
+        tile = 16 if into.dtype == jnp.bfloat16 else 8
 
         def body(r, _):
-            span = pl.ds(pl.multiple_of(r * 16, 16), 16)
+            span = pl.ds(pl.multiple_of(r * tile, tile), tile)
             into[span] = (
                 into[span].astype(jnp.float32) + other[span].astype(jnp.float32)
             ).astype(into.dtype)
             return 0
 
-        lax.fori_loop(0, rows // 16, body, 0)
+        lax.fori_loop(0, into.shape[0] // tile, body, 0)
 
     def collect(i, shard, k):
         for far in order:
@@ -488,6 +848,62 @@
 
             lax.fori_loop(0, rows // 16, body, 0)
 
+    def descend(s):
+        return pltpu.make_async_remote_copy(
+            src_ref=kv_parts.at[s],
+            dst_ref=kv_got.at[s - 1],
+            send_sem=c_send.at[s],
+            recv_sem=c_recv.at[s - 1],
+            device_id=(me_f, me_c - 1, me_t),
+            device_id_type=MESH_ID,
+        )
+
+    def chain_step(s):
+        if s < ctx - 1:
+
+            @pl.when((me_c >= s) & (me_c < ctx - 1))
+            def _():
+                pltpu.make_async_remote_copy(
+                    src_ref=kv_got.at[s],
+                    dst_ref=kv_got.at[s],
+                    send_sem=c_send.at[s + 1],
+                    recv_sem=c_recv.at[s],
+                    device_id=(me_f, me_c + 1, me_t),
+                    device_id_type=MESH_ID,
+                ).wait_recv()
+                for side in range(2):
+                    add(kv_parts.at[s, side], kv_got.at[s, side])
+
+        if s:
+
+            @pl.when(me_c >= s)
+            def _():
+                descend(s).start()
+
+    def chain_result():
+        width = kv_parts.shape[3]
+        rows = cos_ref.shape[0]
+        for seq in range(kv_parts.shape[2] // rows):
+            span = pl.ds(seq * rows, rows)
+            for start in range(0, width, 128):
+                cols = slice(start, start + 128)
+                t = kv_parts[0, 0, span, cols].astype(jnp.float32)
+                t = t * cos_ref[...] + turn(t * sin_ref[...], -1.0)
+                kv_ref[span, cols] = t.astype(kv_ref.dtype)
+            kv_ref[span, width:] = kv_parts[0, 1, span]
+
+    steps = list(reversed(range(ctx))) if chain else []
+
+    def next_step():
+        if steps:
+            s = steps.pop(0)
+            chain_step(s)
+            if s == 0:
+                chain_result()
+
+    if chain:
+        kv_load.wait()
+        next_step()
     shards = sorted(range(ctx), key=lambda c: -abs(2 * c - ctx + 1))
     work = [(i, shard) for i in range(count) for shard in shards]
     levels = sorted({bin(k).count("1") for k in order}, reverse=True)
@@ -501,9 +917,12 @@
                     collect(i, shard, k)
                     for part, b in ways(k):
                         f_copy(i, shard, k, part, b).start()
+        next_step()
     for i in range(count):
         loads[i, 0].wait()
     late = None
+    while steps:
+        next_step()
     for item in work + [None]:
         if item is not None:
             collect(item[0], item[1], 0)
@@ -520,31 +939,54 @@
             def _():
                 z_copy(i, shard, step).wait_send()
 
-
-def sum_weights(fsdp, ctx, arrays):
+    if chain:
+        for s in range(1, ctx):
+
+            @pl.when(me_c >= s)
+            def _():
+                descend(s).wait_send()
+
+
+def sum_weights(fsdp, ctx, arrays, chain=()):
     count = len(arrays)
     sems = pltpu.SemaphoreType.DMA
-    shards = [v.reshape(fsdp, ctx, -1, v.shape[-1]) for v in arrays]
+    shards = [v.reshape(ctx, fsdp, -1, v.shape[-1]) for v in arrays]
     vmem = pltpu.VMEM
+    blocks = [(fsdp, ctx) + v.shape[2:] for v in shards]
     return pl.pallas_call(
-        partial(sum_kernel, fsdp, ctx, count),
-        out_shape=[jax.ShapeDtypeStruct(v.shape[2:], jnp.float32) for v in shards],
-        in_specs=[pl.BlockSpec(memory_space=pl.ANY)] * count,
-        out_specs=[pl.BlockSpec(memory_space=pltpu.VMEM)] * count,
-        scratch_shapes=[vmem(v.shape, v.dtype) for v in shards]
-        + [vmem(v.shape, v.dtype) for v in shards]
-        + [vmem((2,) + v.shape[1:], v.dtype) for v in shards]
+        partial(sum_kernel, fsdp, ctx, count, bool(chain)),
+        out_shape=[jax.ShapeDtypeStruct(v.shape[2:], jnp.float32) for v in shards]
+        + [jax.ShapeDtypeStruct((v.shape[2], 2 * v.shape[3]), v.dtype) for v in chain[:1]],
+        in_specs=[pl.BlockSpec(memory_space=pl.ANY)] * (count + len(chain[:1]))
+        + [pl.BlockSpec(memory_space=pltpu.VMEM)] * len(chain[1:]),
+        out_specs=[pl.BlockSpec(memory_space=pltpu.VMEM)] * (count + len(chain[:1])),
+        scratch_shapes=[vmem(b, v.dtype) for b, v in zip(blocks, shards)]
+        + [vmem(b, v.dtype) for b, v in zip(blocks, shards)]
+        + [vmem((2,) + b[1:], v.dtype) for b, v in zip(blocks, shards)]
         + [
             sems((count, fsdp)),
             sems((count, ctx, fsdp, 2)),
             sems((count, ctx, fsdp, 2)),
             sems((count, 2, ctx)),
             sems((count, 2, ctx)),
+        ]
+        + [
+            scratch
+            for v in chain[:1]
+            for scratch in (
+                vmem(v.shape, v.dtype),
+                vmem((ctx - 1,) + v.shape[1:], v.dtype),
+                sems((1,)),
+                sems((ctx,)),
+                sems((ctx,)),
+            )
         ],
         compiler_params=pltpu.CompilerParams(
-            collective_id=2, has_side_effects=True, vmem_limit_bytes=50 * 1024 * 1024
+            collective_id=4 if chain else 2,
+            has_side_effects=True,
+            vmem_limit_bytes=50 * 1024 * 1024,
         ),
-    )(*shards)
+    )(*shards, *chain)
 
 
 def local(
@@ -570,10 +1012,11 @@
     query_width = w_query.shape[1]
     kv_width = w_key.shape[1]
     kv_end = query_width + 2 * kv_width
+    pairs = kv_width // (2 * HD)
+    group_size = query_width // kv_width
     group = min(fsdp, 4)
     far = fsdp // group
     units = w_gate.shape[1] // group
-    me_f = lax.axis_index("fsdp")
     me_c = lax.axis_index("ctx")
     me_t = lax.axis_index("tp")
     order = fsdp_order(group)
@@ -586,23 +1029,33 @@
     def swap(v):
         return lax.ppermute(v, "tp", [(0, 1), (1, 0)])
 
-    def up_line(v):
-        return lax.ppermute(v, "ctx", [(i, i + 1) for i in range(ctx - 1)])
-
-    def down_line(v):
-        return lax.ppermute(v, "ctx", [(i + 1, i) for i in range(ctx - 1)])
-
-    def pair_sum(part):
-        part = part.astype(low)
-        return part.astype(wide) + swap(part).astype(wide)
+    inside = shard % 128 == 0
+    dims = (fsdp, ctx, shard)
+    back_dims = (ctx, fsdp, shard)
 
     def by_ctx(v):
-        rest = v.shape[:-1]
-        return v.reshape(*rest, fsdp, ctx, shard).swapaxes(-3, -2).reshape(*rest, model_width)
+        if inside:
+            return v
+        rows = v.shape[0]
+        return v.reshape(rows, fsdp, ctx, shard).swapaxes(1, 2).reshape(rows, model_width)
 
     def by_fsdp(v):
-        rest = v.shape[:-1]
-        return v.reshape(*rest, ctx, fsdp, shard).swapaxes(-3, -2).reshape(*rest, model_width)
+        if inside:
+            return v
+        rows = v.shape[0]
+        return v.reshape(rows, ctx, fsdp, shard).swapaxes(1, 2).reshape(rows, model_width)
+
+    def pair_heads(v):
+        rows = v.shape[0]
+        return (
+            v.reshape(rows, pairs, 2, group_size, HD).swapaxes(2, 3).reshape(rows, query_width)
+        )
+
+    def plain_heads(v):
+        rows = v.shape[0]
+        return (
+            v.reshape(rows, pairs, group_size, 2, HD).swapaxes(2, 3).reshape(rows, query_width)
+        )
 
     def gather_tokens(v):
         mine = lax.dynamic_slice_in_dim(v, me_t * half, half)
@@ -617,20 +1070,23 @@
                 got[k] = jnp.concatenate(
                     [hop(got[k ^ lo][:cut], lo), hop(got[k ^ hi][cut:], hi)]
                 )
-        return [(mine, other)] + [(got[k], swap(got[k])) for k in range(1, group)]
-
-    def scatter_tokens(blocks):
+        return jnp.concatenate(
+            [mine, other] + [v for k in range(1, group) for v in (got[k], swap(got[k]))]
+        )
+
+    def scatter_tokens(v):
+        cut = half // 2
         total = {}
         for k in reversed([0] + order):
-            mine, other = blocks[k]
-            total[k] = mine.astype(wide) + swap(other.astype(low)).astype(wide)
+            start = 2 * k * half
+            mine, other = v[start : start + half], v[start + half : start + 2 * half]
+            total[k] = mine.astype(wide) + swap(other).astype(wide)
         for k in reversed(order):
             lo, hi = low_bit(k), high_bit(k)
             sent = total[k].astype(low)
             if lo == hi:
                 total[0] = total[0] + hop(sent, k).astype(wide)
             else:
-                cut = half // 2
                 for there, first, b in ((k ^ lo, True, lo), (k ^ hi, False, hi)):
                     piece = hop(sent[:cut] if first else sent[cut:], b).astype(wide)
                     base = total[there]
@@ -643,29 +1099,24 @@
         other = swap(own)
         return jnp.where(
             me_t == 0, jnp.concatenate([own, other]), jnp.concatenate([other, own])
-        ).astype(wide)
-
+        )
+
+    x = by_ctx(inputs.reshape(tokens, model_width))
+    cot = by_ctx(cotangent.reshape(tokens, model_width))
     positions = me_c * local_rows + jnp.arange(local_rows, dtype=jnp.int32)
-    key_places = (
-        (me_c - jnp.arange(ctx, dtype=jnp.int32))[:, None] * local_rows
-        + jnp.arange(local_rows, dtype=jnp.int32)[None, :]
-    ).reshape(-1)
-    valid_rows = (positions[None, :] < lengths[:, None]).astype(wide)[..., None]
-    key_mask = (
-        (key_places[None, None, :] <= positions[None, :, None])
-        & (key_places[None, None, :] < lengths[:, None, None])
-        & (key_places >= 0)[None, None, :]
-    )
     cosines, sines = rope_tables(positions, HD)
-    head_cos = cosines[None, :, None, :]
-    head_sin = sines[None, :, None, :]
-
-    gains = jnp.pad(jnp.stack([norm1_gain, norm2_gain], 1), ((0, 0), (0, 126)))
+    cosines, sines = jnp.tile(cosines, (1, 2)), jnp.tile(sines, (1, 2))
+
+    gains = jnp.pad(jnp.stack([norm1_gain, norm2_gain]).astype(wide), ((0, 14), (0, 0)))
     lined, held = start_exchange(
         fsdp,
         ctx,
         group,
-        [jnp.concatenate([w_query, w_key, w_value, gains], 1), w_out],
+        [
+            gains,
+            jnp.concatenate([pair_heads(w_query), w_key, w_value], 1),
+            pair_heads(w_out),
+        ],
         [[w_gate, w_up], [w_down]],
     )
     far_groups = [[h * group + g for h in range(far)] for g in range(group)]
@@ -677,89 +1128,69 @@
         return lax.all_gather(v, "ctx", axis=0, tiled=False).reshape(model_width, -1)
 
     both_full, down_full = [whole_width(v) for v in held]
-    qkv_full, out_full = spread_weights(fsdp, ctx, lined)
-    gain_one = qkv_full[:, kv_end].astype(wide)
-    gain_two = qkv_full[:, kv_end + 1].astype(wide)
-
-    back = cotangent.astype(wide) * valid_rows
-    ff_grad = by_ctx((residual_scale * back).astype(low).reshape(tokens, model_width))
-    ff_grad_blocks = gather_tokens(ff_grad)
-
-    query_heads = query_width // HD
-    kv_heads = kv_width // HD
-    group_size = query_heads // kv_heads
-    layer_in = inputs.astype(wide)
-    first_rms = rms_scale(layer_in)
-    first_normed = (layer_in * first_rms * gain_one).astype(low)
-    qkv_lin = jnp.dot(
-        first_normed.reshape(tokens, model_width),
-        qkv_full[:, :kv_end],
-        preferred_element_type=wide,
-    ).reshape(seq_count, local_rows, kv_end)
-    query_rot = rotate(
-        qkv_lin[..., :query_width].reshape(seq_count, local_rows, query_heads, HD),
-        head_cos,
-        head_sin,
+    gain_rows, qkv_full = spread_weights(fsdp, ctx, lined[:2])
+    gain_rows = gain_rows.reshape(ctx * fsdp, 16, shard)
+    gain_one = gain_rows[:, 0].reshape(1, model_width)
+    gain_two = gain_rows[:, 1].reshape(1, model_width)
+
+    (ff_grad,) = by_rows(
+        partial(cot_kernel, dims, local_rows),
+        128,
+        [(lengths, "smem"), (cot, "rows")],
+        [((tokens, model_width), low)],
+    )
+    ff_grad, gain_one = lax.optimization_barrier((ff_grad, gain_one))
+    ff_grad_all = gather_tokens(ff_grad)
+
+    first_normed, query, kv_own = by_rows(
+        partial(qkv_kernel, dims),
+        128,
+        [
+            (x, "rows"),
+            (qkv_full, "whole"),
+            (gain_one, "whole"),
+            (cosines, "cycle"),
+            (sines, "cycle"),
+        ],
+        [
+            ((tokens, model_width), low),
+            ((tokens, query_width), low),
+            ((tokens, 2 * kv_width), low),
+        ],
+        flops=2 * tokens * model_width * kv_end,
+    )
+    out_full, kv_all = spread_weights(fsdp, ctx, lined[2:], kv_own)
+    attended, lse = attend(lengths, query, kv_all)
+    attn_part = jnp.einsum(
+        "tj,dj->td", attended, out_full, preferred_element_type=wide
     ).astype(low)
-    key_rot = (
-        rotate(
-            qkv_lin[..., query_width : query_width + kv_width].reshape(
-                seq_count, local_rows, kv_heads, HD
-            ),
-            head_cos,
-            head_sin,
-        )
-        .astype(low)
-        .reshape(seq_count, local_rows, kv_width)
-    )
-    value_low = qkv_lin[..., query_width + kv_width :].astype(low)
-    kv_blocks = [jnp.concatenate([key_rot, value_low], -1)]
-    for _ in range(ctx - 1):
-        kv_blocks.append(up_line(kv_blocks[-1]))
-    kv_all = jnp.concatenate(kv_blocks, 1)
-    full_rows = kv_all.shape[1]
-    key_split = jnp.moveaxis(
-        kv_all[..., :kv_width].reshape(seq_count, full_rows, kv_heads, HD), 2, 0
-    )
-    value_split = jnp.moveaxis(
-        kv_all[..., kv_width:].reshape(seq_count, full_rows, kv_heads, HD), 2, 0
-    )
-    query_split = jnp.moveaxis(
-        query_rot.reshape(seq_count, local_rows, kv_heads, group_size, HD), 2, 0
-    )
-    head_output, log_mass = lax.map(
-        partial(attend_forward, key_mask=key_mask), (query_split, key_split, value_split)
-    )
-    attended = jnp.moveaxis(head_output, 0, 2).reshape(tokens, query_width)
-    attn_part = jnp.einsum("tj,dj->td", attended, out_full, preferred_element_type=wide)
-    attn_branch = pair_sum(attn_part)
-    middle = layer_in + residual_scale * attn_branch.reshape(layer_in.shape)
-
-    second_rms = rms_scale(middle)
-    second_normed = (middle * second_rms * gain_two).astype(low)
-    normed_blocks = gather_tokens(by_ctx(second_normed.reshape(tokens, model_width)))
-    normed_all = jnp.concatenate([jnp.concatenate(b) for b in normed_blocks])
-    ff_grad_all = jnp.concatenate([jnp.concatenate(b) for b in ff_grad_blocks])
-
-    both_lin = jnp.dot(normed_all, both_full, preferred_element_type=wide)
-    gate_lin = both_lin[:, :units]
-    up_lin = both_lin[:, units:]
-    gate_sig = jax.nn.sigmoid(gate_lin)
-    gate_act = gate_lin * gate_sig
-    hidden = (gate_act * up_lin).astype(low)
-    hidden_grad = jnp.dot(ff_grad_all, down_full, preferred_element_type=wide)
-    gate_grad = (hidden_grad * up_lin * gate_sig * (1.0 + gate_lin * (1.0 - gate_sig))).astype(low)
-    up_grad = (hidden_grad * gate_act).astype(low)
-
-    def sum_blocks(left, right):
-        blocks = [None] * group
-        for k in reversed([0] + order):
-            rows = slice(k * tokens, (k + 1) * tokens)
-            part = jnp.einsum(
-                "tf,df->td", left[rows], right, preferred_element_type=wide
-            ).astype(low)
-            blocks[k] = (part[:half], part[half:])
-        return by_fsdp(scatter_tokens(blocks)).reshape(layer_in.shape)
+    middle, second_normed = by_rows(
+        partial(middle_kernel, dims),
+        128,
+        [(x, "rows"), (attn_part, "rows"), (swap(attn_part), "rows"), (gain_two, "whole")],
+        [((tokens, model_width), wide), ((tokens, model_width), low)],
+    )
+    normed_all = gather_tokens(second_normed)
+
+    many = group * tokens
+    hidden, both_grad, second_part, ff_part = by_rows(
+        swiglu_kernel,
+        256,
+        [
+            (normed_all, "rows"),
+            (ff_grad_all, "rows"),
+            (both_full, "whole"),
+            (down_full, "whole"),
+        ],
+        [
+            ((many, units), low),
+            ((many, 2 * units), low),
+            ((many, model_width), low),
+            ((many, model_width), low),
+        ],
+        flops=12 * many * model_width * units,
+        limit=56,
+    )
 
     def unit_term(left, right):
         return jnp.einsum("td,tf->df", left, right, preferred_element_type=wide).astype(low)
@@ -785,80 +1216,78 @@
             axis_index_groups=near_groups if far > 1 else None,
         ).astype(wide)
 
-    second_grad = sum_blocks(jnp.concatenate([gate_grad, up_grad], 1), both_full)
-    ff_branch = sum_blocks(hidden, down_full)
     down_term = unit_term(ff_grad_all, hidden)
-    gate_term = unit_term(normed_all, gate_grad)
-    up_term = unit_term(normed_all, up_grad)
-    second_grad, ff_branch, _, _, _ = lax.optimization_barrier(
-        (second_grad, ff_branch, down_term, gate_term, up_term)
-    )
+    second_grad = scatter_tokens(second_part)
+    gate_term = unit_term(normed_all, both_grad[:, :units])
+    up_term = unit_term(normed_all, both_grad[:, units:])
+    second_grad, ff_part, _, _, _ = lax.optimization_barrier(
+        (second_grad, ff_part, down_term, gate_term, up_term)
+    )
+    ff_branch = scatter_tokens(ff_part)
     w_down_grad = return_units(down_term)
     w_gate_grad = return_units(gate_term)
     w_up_grad = return_units(up_term)
-    output = (valid_rows * (middle + residual_scale * ff_branch)).astype(low)
-
-    gain_two_term = jnp.sum(second_grad * middle * second_rms, axis=(0, 1))
-    middle_grad = back + norm_back(second_grad, middle, second_rms, gain_two)
-
-    attn_grad = (residual_scale * middle_grad).astype(low).reshape(tokens, model_width)
+    (output,) = by_rows(
+        partial(output_kernel, back_dims, local_rows),
+        128,
+        [(lengths, "smem"), (middle, "rows"), (ff_branch, "rows")],
+        [((tokens, model_width), low)],
+    )
+
+    middle_grad, attn_grad, gain_two_term = by_rows(
+        partial(middle_back_kernel, dims, local_rows),
+        128,
+        [
+            (lengths, "smem"),
+            (cot, "rows"),
+            (middle, "rows"),
+            (second_grad, "rows"),
+            (gain_two, "whole"),
+        ],
+        [((tokens, model_width), wide), ((tokens, model_width), low), ((1, model_width), wide)],
+    )
+    attended_grad = jnp.dot(attn_grad, out_full, preferred_element_type=wide).astype(low)
+    query_grad, kv_parts = attend_back(
+        lengths, query, attended_grad, lse, cosines, sines, kv_all
+    )
     out_term = jnp.einsum("td,tj->dj", attn_grad, attended, preferred_element_type=wide)
-    attended_grad = jnp.dot(attn_grad, out_full, preferred_element_type=wide).astype(low)
-    grad_split = jnp.moveaxis(
-        attended_grad.reshape(seq_count, local_rows, kv_heads, group_size, HD), 2, 0
-    )
-    query_back, key_back, value_back = lax.map(
-        partial(attend_backward, key_mask=key_mask),
-        (query_split, key_split, value_split, grad_split, log_mass),
-    )
-    query_back = jnp.moveaxis(query_back, 0, 2).reshape(seq_count, local_rows, query_heads, HD)
-    query_grad = (
-        unrotate(query_back, head_cos, head_sin).astype(low).reshape(tokens, query_width)
-    )
-    key_spread = jnp.moveaxis(key_back, 0, 2).reshape(seq_count, full_rows, kv_width)
-    value_spread = jnp.moveaxis(value_back, 0, 2).reshape(seq_count, full_rows, kv_width)
-    kv_spread = jnp.concatenate([key_spread, value_spread], -1).reshape(
-        seq_count, ctx, local_rows, 2 * kv_width
-    )
-    kv_own = kv_spread[:, ctx - 1]
-    for s in reversed(range(ctx - 1)):
-        kv_own = kv_spread[:, s] + down_line(kv_own.astype(low)).astype(wide)
-    key_grad = (
-        unrotate(
-            kv_own[..., :kv_width].reshape(seq_count, local_rows, kv_heads, HD), head_cos, head_sin
-        )
-        .astype(low)
-        .reshape(tokens, kv_width)
-    )
-    value_grad = kv_own[..., kv_width:].astype(low).reshape(tokens, kv_width)
-    qkv_grad = jnp.concatenate([query_grad, key_grad, value_grad], -1)
-    qkv_term = jnp.einsum(
-        "td,tj->dj",
-        first_normed.reshape(tokens, model_width),
-        qkv_grad,
-        preferred_element_type=wide,
-    )
+    w_out_grad, kv_grad = sum_weights(
+        fsdp, ctx, [out_term.astype(low)], (kv_parts, cosines, sines)
+    )
+    qkv_grad = jnp.concatenate([query_grad, kv_grad], -1)
+    qkv_term = jnp.einsum("td,tj->dj", first_normed, qkv_grad, preferred_element_type=wide)
     first_part = jnp.einsum(
-        "tj,dj->td", qkv_grad, qkv_full[:, :kv_end], preferred_element_type=wide
-    )
-    first_grad = pair_sum(first_part).reshape(layer_in.shape)
-    gain_one_term = jnp.sum(first_grad * layer_in * first_rms, axis=(0, 1))
-    input_grad = (middle_grad + norm_back(first_grad, layer_in, first_rms, gain_one)).astype(low)
-    gain_terms = jnp.pad(jnp.stack([gain_one_term, gain_two_term], 1), ((0, 0), (0, 126)))
-    qkv_term = jnp.concatenate([qkv_term, gain_terms], 1).astype(low)
+        "tj,dj->td", qkv_grad, qkv_full, preferred_element_type=wide
+    ).astype(low)
+    input_grad, gain_one_term = by_rows(
+        partial(input_back_kernel, dims),
+        128,
+        [
+            (x, "rows"),
+            (first_part, "rows"),
+            (swap(first_part), "rows"),
+            (middle_grad, "rows"),
+            (gain_one, "whole"),
+        ],
+        [((tokens, model_width), low), ((1, model_width), wide)],
+    )
+    gain_terms = jnp.stack(
+        [gain_one_term.reshape(-1, shard), gain_two_term.reshape(-1, shard)], 1
+    )
+    gain_terms = jnp.pad(gain_terms, ((0, 0), (0, 14), (0, 0))).reshape(-1, shard)
     qkv_term, w_down_grad, w_gate_grad, w_up_grad = lax.optimization_barrier(
-        (qkv_term, w_down_grad, w_gate_grad, w_up_grad)
-    )
-    w_out_grad, qkv_own = sum_weights(fsdp, ctx, [out_term.astype(low), qkv_term])
+        (qkv_term.astype(low), w_down_grad, w_gate_grad, w_up_grad)
+    )
+    gain_own, qkv_own = sum_weights(fsdp, ctx, [gain_terms, qkv_term])
     return (
-        output,
-        input_grad,
-        qkv_own[:, kv_end],
-        qkv_own[:, :query_width],
+        by_fsdp(output).reshape(inputs.shape),
+        by_fsdp(input_grad).reshape(inputs.shape),
+        gain_own[0],
+        plain_heads(qkv_own[:, :query_width]),
         qkv_own[:, query_width : query_width + kv_width],
-        qkv_own[:, query_width + kv_width : kv_end],
-        w_out_grad,
-        qkv_own[:, kv_end + 1],
+        qkv_own[:, query_width + kv_width :],
+        plain_heads(w_out_grad),
+        gain_own[1],
         w_gate_grad,
         w_up_grad,
         w_down_grad,

time: 1130 us -> 928 us (0.82)
  Pallas kernels: 303 us -> 596 us
  matrix products: 236 us -> 66.1 us
  waiting for transfers between devices: 256 us -> 118 us
  local copies, waits for them, and re-layouts: 158 us -> 57.4 us
  other arithmetic: 103 us -> 33.1 us
  starting transfers between devices: 51.1 us -> 37.7 us
    pallas_call x2 -> x13, Pallas kernels: 255 us -> 548 us  [the longest x2 260 us: sum_weights(): pl.pallas_call(partial(sum_kernel, fsdp, ctx, count, bool(chain)), out_sh...]
    dot_general x41 -> x2, matrix products: 187 us -> 12.9 us  [the longest x1 8.26 us: local(): jnp.einsum('td,tj->dj', first_normed, qkv_grad, preferred_element_type=wide)]
    ppermute x6 -> x0, waiting for transfers between devices: 151 us -> none  [the longest x3 77.4 us: up_line(): return lax.ppermute(v, 'ctx', [(i, i + 1) for i in range(ctx - 1)])]
    convert_element_type x18 -> x1, other arithmetic: 31.2 us -> 0.01 us  [rope_tables(): angles = positions.astype(jnp.float32)[:, None] * frequency[None, :]]
    another operation x9 -> x5, local copies, waits for them, and re-layouts: 24.6 us -> 1.13 us  [the longest x1 0.93 us: local(): gain_two = gain_rows[:, 1].reshape(1, model_width)]
    ppermute x16, waiting for transfers between devices: 89.6 us -> 108 us  [hop(): return lax.ppermute(v, 'fsdp', [(i, i ^ k) for i in range(fsdp)])]
    ppermute x6 -> x0, starting transfers between devices: 18.4 us -> none  [the longest x3 11.3 us: down_line(): return lax.ppermute(v, 'ctx', [(i + 1, i) for i in range(ctx - 1)])]
    reduce_sum x8 -> x0, other arithmetic: 18.2 us -> none  [the longest x4 7.28 us: attend_forward(): total_mass = jnp.sum(exp_scores, -1, keepdims=True)]
  transfers between devices with their start and end apart: 48 -> 42, of which waited for: 19 -> 17; matrix products, arithmetic and copies ran while one was open for 33% -> 13% of each run, Pallas kernels for 0% -> 41%
where the time goes in v3:
time: 928 us; the launch traced here: 924 us
  Pallas kernels  596 us (64%)
  waiting for transfers between devices  118 us (13%)
  matrix products  66.1 us (7%)
  local copies, waits for them, and re-layouts  57.4 us (6%)
  starting transfers between devices  37.7 us (4%)
  other arithmetic  33.1 us (4%)
  between operations  15 us (2%)
    pallas_call x2, Pallas kernels, sum_weights(): pl.pallas_call(partial(sum_kernel, fsdp, ctx, count, bool(chain)), out_sh...  260 us
    pallas_call x2, Pallas kernels, spread_weights(): pl.pallas_call(partial(spread_kernel, fsdp, ctx, count, len(extra)), out_...  150 us
    ppermute x16, waiting for transfers between devices, hop(): return lax.ppermute(v, 'fsdp', [(i, i ^ k) for i in range(fsdp)])  108 us
    pallas_call x7, Pallas kernels, by_rows(): pl.pallas_call(kernel, grid=(total // rows,), in_specs=in_specs, out_spec...  87.5 us
    pallas_call x1, Pallas kernels, start_exchange(): pl.pallas_call(partial(line_kernel, fsdp, ctx, group, len(lines), len(swa...  48.3 us
    dot_general x3, matrix products, unit_term(): jnp.einsum('td,tf->df', left, right, preferred_element_type=wide)  42.8 us
    unnamed x77, local copies, waits for them, and re-layouts  36.9 us
    pallas_call x1, Pallas kernels, attend_back(): pl.pallas_call(partial(attend_back_kernel, ctx), grid=(seqs, pairs), in_s...  33.2 us
  transfers between devices with their start and end apart: 42, of which 17 were waited for; matrix products, arithmetic and copies ran while one was open for 13% of the time, Pallas kernels for 41%

profile of v3, /device:TPU:16, one launch (start us, length us, event | category | flops | bytes accessed | tf_op | source)
XLA Modules:
  0.0 923.6 jit_solution(4390264755102311661)
XLA Ops:
  13.5 48.3 %shard_map.203 = (f32[4,16,128]{2,1,0:T(8,128)}, bf16[4,128,1536]{2,1,0:T(8,128)(2,1)}, bf16[4,128,1024]{2,1,0:T(8,128)(2,1)}, bf16[4,128,2048]{2,1,0:T(8,128)(2,1)}, bf16[4,128,1024]{2,1,0:T(8,128)(2,1)}) custom-call(f32[16,128]{1,0:T(8,128)} %fusion.17.refs_0_, bf16[128,1536]{1,0:T(8,128)(2,1)} %pad_maximum_fusion.6.refs_1_, ...), custom_call_target="tpu_custom_call" | custom-call | tf_op jit(solution)/shard_map/pallas_call | solution.py:531
  65.6 55.9 %shard_map.204 = (f32[4,4,16,128]{3,2,1,0:T(8,128)}, bf16[4,4,128,1536]{3,2,1,0:T(8,128)(2,1)}) custom-call(f32[4,16,128]{2,1,0:T(8,128)} %get-tuple-element.50.refs_0_, bf16[4,128,1536]{2,1,0:T(8,128)(2,1)} %get-tuple-element.51.refs_1_), custom_call_target="tpu_custom_call" | custom-call | tf_op jit(solution)/shard_map/pallas_call | solution.py:702
  126.8 5.3 shard_map.206
  134.3 94.3 %shard_map.207 = (bf16[4,4,128,1024]{3,2,1,0:T(8,128)(2,1)}, bf16[4,512,512]{2,1,0:T(8,128)(2,1)}) custom-call(bf16[4,128,1024]{2,1,0:T(8,128)(2,1)} %get-tuple-element.56.refs_0_, bf16[512,512]{1,0:T(8,128)(2,1)} %copy-done.9), custom_call_target="tpu_custom_call" | custom-call | tf_op jit(solution)/shard_map/pallas_call | solution.py:702
  230.2 17.4 %shard_map.208 = (bf16[512,1024]{1,0:T(8,128)(2,1)S(1)}, f32[512,256]{1,0:T(8,128)S(1)}) custom-call(s32[2]{0:T(128)S(1)} %copy-done.12, bf16[512,1024]{1,0:T(8,128)(2,1)S(1)} %get-tuple-element.55.q_ref, bf16[4,512,512]{2,1,0:T(8,128)(2,1)S(1)} %copy-done.14, bf16[4,512,512]{2,1,0:T(8,128)(2,1)S(1)} %copy-done.14, bf16[4,512,512]{2,1,0:T(8,128)(2,1)S(1)} %copy-done.14, ...), custom_call_target="tpu_custom_call" | custom-call | flops 8589934592 | bytes 6291456 | tf_op jit(solution)/shard_map/pallas_call | solution.py:321
  257.3 22.7 %collective-permute-done.8 = bf16[256,2048]{1,0:T(8,128)(2,1)} collective-permute-done((bf16[256,2048]{1,0:T(8,128)(2,1)}, bf16[256,2048]{1,0:T(8,128)(2,1)}, u32[]{:S(2)}, u32[]{:S(2)}) %collective-permute-start.8) | collective-permute-done | bytes 1048608 | tf_op jit(solution)/shard_map/ppermute | solution.py:1027
  307.6 13.5 %collective-permute-done.1 = bf16[256,2048]{1,0:T(8,128)(2,1)S(1)} collective-permute-done((bf16[256,2048]{1,0:T(8,128)(2,1)S(1)}, bf16[256,2048]{1,0:T(8,128)(2,1)S(1)}, u32[]{:S(2)}, u32[]{:S(2)}) %collective-permute-start.1) | collective-permute-done | bytes 1048608 | tf_op jit(solution)/shard_map/ppermute | solution.py:1027
  331.4 8.3 collective-permute-done.5
  346.1 62.3 %shard_map.210 = (bf16[2048,1024]{1,0:T(8,128)(2,1)}, bf16[2048,2048]{1,0:T(8,128)(2,1)}, bf16[2048,2048]{1,0:T(8,128)(2,1)}, bf16[2048,2048]{1,0:T(8,128)(2,1)}) custom-call(bf16[2048,2048]{1,0:T(8,128)(2,1)} %constant_dynamic-update-slice_fusion.n_ref, bf16[2048,2048]{1,0:T(8,128)(2,1)} %constant_dynamic-update-slice_fusion.8.g_ref, ...), custom_call_target="tpu_custom_call" | custom-call | flops 51539607552 | bytes 58720256 | tf_op jit(solution)/shard_map/pallas_call | solution.py:296
  408.4 14.1 %convolution_convert_fusion.2 = bf16[2048,1024]{1,0:T(8,128)(2,1)} fusion(bf16[2048,2048]{1,0:T(8,128)(2,1)} %constant_dynamic-update-slice_fusion.8.g_ref, bf16[2048,1024]{1,0:T(8,128)(2,1)} %get-tuple-element.68), kind=kOutput, calls=%fused_computation.8 | convolution fusion | flops 8592031744 | bytes 16777216 | tf_op jit(solution)/shard_map/td,tf->df/dot_general | solution.py:1196
  422.5 14.5 %fusion.7 = bf16[2048,1024]{1,0:T(8,128)(2,1)} fusion(bf16[2048,2048]{1,0:T(8,128)(2,1)} %constant_dynamic-update-slice_fusion.n_ref, bf16[2048,2048]{1,0:T(8,128)(2,1)} %get-tuple-element.69), kind=kOutput, calls=%fused_computation.6 | convolution fusion | flops 8592031744 | bytes 16777216 | tf_op jit(solution)/shard_map/td,tf->df/dot_general | solution.py:1196
  453.0 10.7 %collective-permute-done.21 = bf16[128,2048]{1,0:T(8,128)(2,1)S(1)} collective-permute-done((bf16[128,2048]{1,0:T(8,128)(2,1)S(1)}, bf16[128,2048]{1,0:T(8,128)(2,1)S(1)}, u32[]{:S(2)}, u32[]{:S(2)}) %collective-permute-start.21) | collective-permute-done | bytes 524320 | tf_op jit(solution)/shard_map/ppermute | solution.py:1027
  469.3 20.6 %collective-permute-done.22 = bf16[256,2048]{1,0:T(8,128)(2,1)} collective-permute-done((bf16[256,2048]{1,0:T(8,128)(2,1)}, bf16[256,2048]{1,0:T(8,128)(2,1)}, u32[]{:S(2)}, u32[]{:S(2)}) %collective-permute-start.22) | collective-permute-done | bytes 1048608 | tf_op jit(solution)/shard_map/ppermute | solution.py:1027
  496.5 14.2 %fusion.4 = bf16[2048,1024]{1,0:T(8,128)(2,1)} fusion(bf16[2048,2048]{1,0:T(8,128)(2,1)} %constant_dynamic-update-slice_fusion.n_ref, bf16[2048,2048]{1,0:T(8,128)(2,1)} %get-tuple-element.69), kind=kOutput, calls=%fused_computation.5 | convolution fusion | flops 8592031744 | bytes 16777216 | tf_op jit(solution)/shard_map/td,tf->df/dot_general | solution.py:1196
  519.0 5.9 shard_map.212
  528.2 33.2 %shard_map.213 = (bf16[512,1024]{1,0:T(8,128)(2,1)S(1)}, bf16[4,2,512,256]{3,2,1,0:T(8,128)(2,1)S(1)}) custom-call(s32[2]{0:T(128)S(1)} %copy-done.12, bf16[512,1024]{1,0:T(8,128)(2,1)S(1)} %get-tuple-element.55.q_ref, bf16[512,1024]{1,0:T(8,128)(2,1)S(1)} %convolution_convert_fusion.5.do_ref, f32[512,256]{1,0:T(8,128)S(1)} %copy-done.20, ...), custom_call_target="tpu_custom_call" | custom-call | flops 21474836480 | bytes 10485760 | tf_op jit(solution)/shard_map/pallas_call | solution.py:349
  566.6 4.4 convolution_convert_fusion.1
  571.0 148.6 %shard_map.214 = (f32[128,1024]{1,0:T(8,128)S(1)}, bf16[512,512]{1,0:T(8,128)(2,1)S(1)}) custom-call(bf16[4,4,128,1024]{3,2,1,0:T(8,128)(2,1)} %bitcast.98, bf16[4,2,512,256]{3,2,1,0:T(8,128)(2,1)S(1)} %get-tuple-element.75.refs_1_, f32[256,128]{1,0:T(8,128)S(1)} %copy.66.cos_ref.refs_2_, f32[256,128]{1,0:T(8,128)S(1)} %copy.67.sin_ref.refs_3_), custom_call_target="tpu_custom_call" | custom-call | tf_op jit(solution)/shard_map/pallas_call | solution.py:956
  725.1 8.1 collective-permute-done.27
  735.9 4.6 convolution_convert_fusion.4.part_ref
  744.5 12.7 %collective-permute-done.28 = bf16[256,2048]{1,0:T(8,128)(2,1)} collective-permute-done((bf16[256,2048]{1,0:T(8,128)(2,1)}, bf16[256,2048]{1,0:T(8,128)(2,1)}, u32[]{:S(2)}, u32[]{:S(2)}) %collective-permute-start.28) | collective-permute-done | bytes 1048608 | tf_op jit(solution)/shard_map/ppermute | solution.py:1027
  766.4 8.3 convolution_convert_fusion
  774.7 6.1 shard_map.215
  802.9 111.2 %shard_map.216 = (f32[16,128]{1,0:T(8,128)S(1)}, f32[128,1536]{1,0:T(8,128)S(1)}) custom-call(f32[4,4,16,128]{3,2,1,0:T(8,128)S(1)} %bitcast.87, bf16[4,4,128,1536]{3,2,1,0:T(8,128)(2,1)} %bitcast.94), custom_call_target="tpu_custom_call" | custom-call | tf_op jit(solution)/shard_map/pallas_call | solution.py:956
  (225 shorter events, 163.4 us)
Async XLA Ops:
  7.2 338.9 %all-gather.7.cloned.1.call-start = ((), (), s32[]{:S(2)}) async-start(), calls=%async_computation.10 | async-start | bytes 5242880 | tf_op jit(solution)/shard_map/all_gather | solution.py:1128
  61.8 284.3 %all-gather.5.cloned.1.call-start = ((), (), s32[]{:S(2)}) async-start(), calls=%async_computation.9 | async-start | bytes 10485760 | tf_op jit(solution)/shard_map/all_gather | solution.py:1128
  62.5 678.1 %reduce-scatter.4.cloned.1.call-start = ((), (), s32[]{:S(2)}) async-start(), calls=%async_computation.6 | async-start | bytes 5242880 | tf_op jit(solution)/shard_map/reduce_scatter | solution.py:1199
  251.3 38.8 %collective-permute-start = (bf16[512,2048]{1,0:T(8,128)(2,1)}, bf16[512,2048]{1,0:T(8,128)(2,1)}, u32[]{:S(2)}, u32[]{:S(2)}) collective-permute-start(bf16[512,2048]{1,0:T(8,128)(2,1)} %convolution_convert_fusion.3.part_ref), channel_id=1, source_target_pairs={{0,1},{1,0},{2,3},{3,2},{4,5},{5,4},{6,7},{7,6},{8,9},{9,8},{10,11... | collective-permute-start | bytes 6291464 | tf_op jit(solution)/shard_map/ppermute | solution.py:1030
  254.1 25.9 %collective-permute-start.8 = (bf16[256,2048]{1,0:T(8,128)(2,1)}, bf16[256,2048]{1,0:T(8,128)(2,1)}, u32[]{:S(2)}, u32[]{:S(2)}) collective-permute-start(bf16[256,2048]{1,0:T(8,128)(2,1)} %get-tuple-element.112), channel_id=1, source_target_pairs={{0,8},{8,0},{16,24},{24,16},{1,9},{9,1},{17,25},{25,17},{2,10},{10... | collective-permute-start | bytes 3145736 | tf_op jit(solution)/shard_map/ppermute | solution.py:1027
  255.8 26.5 %collective-permute-start.10 = (bf16[256,2048]{1,0:T(8,128)(2,1)}, bf16[256,2048]{1,0:T(8,128)(2,1)}, u32[]{:S(2)}, u32[]{:S(2)}) collective-permute-start(bf16[256,2048]{1,0:T(8,128)(2,1)} %get-tuple-element.112), channel_id=1, source_target_pairs={{0,16},{8,24},{16,0},{24,8},{1,17},{9,25},{17,1},{25,9},{2,18},{10... | collective-permute-start | bytes 3145736 | tf_op jit(solution)/shard_map/ppermute | solution.py:1027
  280.0 23.1 %collective-permute-start.9 = (bf16[256,2048]{1,0:T(8,128)(2,1)}, bf16[256,2048]{1,0:T(8,128)(2,1)S(1)}, u32[]{:S(2)}, u32[]{:S(2)}) collective-permute-start(bf16[256,2048]{1,0:T(8,128)(2,1)} %collective-permute-done.8), channel_id=1, source_target_pairs={{0,1},{1,0},{2,3},{3,2},{4,5},{5,4},{6,7},{7,6},{8,9},{9,8},{10,11... | collective-permute-start | bytes 3145736 | tf_op jit(solution)/shard_map/ppermute | solution.py:1030
  295.6 25.6 %collective-permute-start.1 = (bf16[256,2048]{1,0:T(8,128)(2,1)S(1)}, bf16[256,2048]{1,0:T(8,128)(2,1)S(1)}, u32[]{:S(2)}, u32[]{:S(2)}) collective-permute-start(bf16[256,2048]{1,0:T(8,128)(2,1)S(1)} %get-tuple-element.114), channel_id=1, source_target_pairs={{0,8},{8,0},{16,24},{24,16},{1,9},{9,1},{17,25},{25,17},{2,10},{10... | collective-permute-start | bytes 3145736 | tf_op jit(solution)/shard_map/ppermute | solution.py:1027
  300.5 28.8 %collective-permute-start.14 = (bf16[256,2048]{1,0:T(8,128)(2,1)S(1)}, bf16[256,2048]{1,0:T(8,128)(2,1)S(1)}, u32[]{:S(2)}, u32[]{:S(2)}) collective-permute-start(bf16[256,2048]{1,0:T(8,128)(2,1)S(1)} %pad_maximum_fusion.1), channel_id=1, source_target_pairs={{0,1},{1,0},{2,3},{3,2},{4,5},{5,4},{6,7},{7,6},{8,9},{9,8},{10,11... | collective-permute-start | bytes 3145736 | tf_op jit(solution)/shard_map/ppermute | solution.py:1030
  300.5 25.6 %collective-permute-start.3 = (bf16[256,2048]{1,0:T(8,128)(2,1)S(1)}, bf16[256,2048]{1,0:T(8,128)(2,1)S(1)}, u32[]{:S(2)}, u32[]{:S(2)}) collective-permute-start(bf16[256,2048]{1,0:T(8,128)(2,1)S(1)} %get-tuple-element.114), channel_id=1, source_target_pairs={{0,16},{8,24},{16,0},{24,8},{1,17},{9,25},{17,1},{25,9},{2,18},{10... | collective-permute-start | bytes 3145736 | tf_op jit(solution)/shard_map/ppermute | solution.py:1027
  422.4 338.2 %reduce-scatter.8.cloned.1.call-start = ((), (), s32[]{:S(2)}) async-start(), calls=%async_computation.8 | async-start | bytes 5242880 | tf_op jit(solution)/shard_map/reduce_scatter | solution.py:1199
  437.0 343.8 %reduce-scatter.6.cloned.1.call-start = ((), (), s32[]{:S(2)}) async-start(), calls=%async_computation.7 | async-start | bytes 5242880 | tf_op jit(solution)/shard_map/reduce_scatter | solution.py:1199
  464.9 25.0 %collective-permute-start.22 = (bf16[256,2048]{1,0:T(8,128)(2,1)}, bf16[256,2048]{1,0:T(8,128)(2,1)}, u32[]{:S(2)}, u32[]{:S(2)}) collective-permute-start(bf16[256,2048]{1,0:T(8,128)(2,1)} %pad_maximum_fusion.3), channel_id=1, source_target_pairs={{0,8},{8,0},{16,24},{24,16},{1,9},{9,1},{17,25},{25,17},{2,10},{10... | collective-permute-start | bytes 3145736 | tf_op jit(solution)/shard_map/ppermute | solution.py:1027
  467.8 24.8 %collective-permute-start.19 = (bf16[256,2048]{1,0:T(8,128)(2,1)}, bf16[256,2048]{1,0:T(8,128)(2,1)}, u32[]{:S(2)}, u32[]{:S(2)}) collective-permute-start(bf16[256,2048]{1,0:T(8,128)(2,1)} %pad_maximum_fusion.2), channel_id=1, source_target_pairs={{0,16},{8,24},{16,0},{24,8},{1,17},{9,25},{17,1},{25,9},{2,18},{10... | collective-permute-start | bytes 3145736 | tf_op jit(solution)/shard_map/ppermute | solution.py:1027
  518.0 226.1 %collective-permute-start.24 = (bf16[256,2048]{1,0:T(8,128)(2,1)}, bf16[256,2048]{1,0:T(8,128)(2,1)}, u32[]{:S(2)}, u32[]{:S(2)}) collective-permute-start(bf16[256,2048]{1,0:T(8,128)(2,1)} %get-tuple-element.115), channel_id=1, source_target_pairs={{0,1},{1,0},{2,3},{3,2},{4,5},{5,4},{6,7},{7,6},{8,9},{9,8},{10,11... | collective-permute-start | bytes 3145736 | tf_op jit(solution)/shard_map/ppermute | solution.py:1030
  518.4 43.0 %collective-permute-start.29 = (bf16[256,2048]{1,0:T(8,128)(2,1)S(1)}, bf16[256,2048]{1,0:T(8,128)(2,1)S(1)}, u32[]{:S(2)}, u32[]{:S(2)}) collective-permute-start(bf16[256,2048]{1,0:T(8,128)(2,1)S(1)} %get-tuple-element.116), channel_id=1, source_target_pairs={{0,1},{1,0},{2,3},{3,2},{4,5},{5,4},{6,7},{7,6},{8,9},{9,8},{10,11... | collective-permute-start | bytes 3145736 | tf_op jit(solution)/shard_map/ppermute | solution.py:1030
  518.5 42.9 %collective-permute-start.26 = (bf16[256,2048]{1,0:T(8,128)(2,1)S(1)}, bf16[256,2048]{1,0:T(8,128)(2,1)S(1)}, u32[]{:S(2)}, u32[]{:S(2)}) collective-permute-start(bf16[256,2048]{1,0:T(8,128)(2,1)S(1)} %get-tuple-element.117), channel_id=1, source_target_pairs={{0,1},{1,0},{2,3},{3,2},{4,5},{5,4},{6,7},{7,6},{8,9},{9,8},{10,11... | collective-permute-start | bytes 3145736 | tf_op jit(solution)/shard_map/ppermute | solution.py:1030
  518.9 42.5 %collective-permute-start.25 = (bf16[256,2048]{1,0:T(8,128)(2,1)S(1)}, bf16[256,2048]{1,0:T(8,128)(2,1)}, u32[]{:S(2)}, u32[]{:S(2)}) collective-permute-start(bf16[256,2048]{1,0:T(8,128)(2,1)S(1)} %get-tuple-element.118), channel_id=1, source_target_pairs={{0,1},{1,0},{2,3},{3,2},{4,5},{5,4},{6,7},{7,6},{8,9},{9,8},{10,11... | collective-permute-start | bytes 3145736 | tf_op jit(solution)/shard_map/ppermute | solution.py:1030
  565.0 156.4 %collective-permute-start.30 = (bf16[128,2048]{1,0:T(8,128)(2,1)S(1)}, bf16[128,2048]{1,0:T(8,128)(2,1)}, u32[]{:S(2)}, u32[]{:S(2)}) collective-permute-start(bf16[128,2048]{1,0:T(8,128)(2,1)S(1)} %get-tuple-element.130), channel_id=1, source_target_pairs={{0,16},{8,24},{16,0},{24,8},{1,17},{9,25},{17,1},{25,9},{2,18},{10... | collective-permute-start | bytes 1572872 | tf_op jit(solution)/shard_map/ppermute | solution.py:1027
  723.9 20.6 %collective-permute-start.31 = (bf16[256,2048]{1,0:T(8,128)(2,1)}, bf16[256,2048]{1,0:T(8,128)(2,1)S(1)}, u32[]{:S(2)}, u32[]{:S(2)}) collective-permute-start(bf16[256,2048]{1,0:T(8,128)(2,1)} %pad_maximum_fusion.5), channel_id=1, source_target_pairs={{0,8},{8,0},{16,24},{24,16},{1,9},{9,1},{17,25},{25,17},{2,10},{10... | collective-permute-start | bytes 3145736 | tf_op jit(solution)/shard_map/ppermute | solution.py:1027
  734.5 22.7 %collective-permute-start.28 = (bf16[256,2048]{1,0:T(8,128)(2,1)}, bf16[256,2048]{1,0:T(8,128)(2,1)}, u32[]{:S(2)}, u32[]{:S(2)}) collective-permute-start(bf16[256,2048]{1,0:T(8,128)(2,1)} %pad_maximum_fusion.4), channel_id=1, source_target_pairs={{0,16},{8,24},{16,0},{24,8},{1,17},{9,25},{17,1},{25,9},{2,18},{10... | collective-permute-start | bytes 3145736 | tf_op jit(solution)/shard_map/ppermute | solution.py:1027
  740.6 34.1 %collective-permute-start.33 = (bf16[512,2048]{1,0:T(8,128)(2,1)}, bf16[512,2048]{1,0:T(8,128)(2,1)}, u32[]{:S(2)}, u32[]{:S(2)}) collective-permute-start(bf16[512,2048]{1,0:T(8,128)(2,1)} %convolution_convert_fusion.4.part_ref), channel_id=1, source_target_pairs={{0,1},{1,0},{2,3},{3,2},{4,5},{5,4},{6,7},{7,6},{8,9},{9,8},{10,11... | collective-permute-start | bytes 6291464 | tf_op jit(solution)/shard_map/ppermute | solution.py:1030
  740.6 20.1 %all-to-all-start = ((bf16[4,128,1024]{2,1,0:T(8,128)(2,1)}), bf16[4,128,1024]{2,1,0:T(8,128)(2,1)S(1)}, u32[]{:S(2)}, u32[]{:S(2)}) async-start(bf16[4,128,1024]{2,1,0:T(8,128)(2,1)} %bitcast.108), calls=%async_computation.1 | async-start | bytes 2097152 | tf_op jit(solution)/shard_map/all_to_all | solution.py:1210
  760.6 24.4 %collective-permute-start.32 = (bf16[256,2048]{1,0:T(8,128)(2,1)}, bf16[256,2048]{1,0:T(8,128)(2,1)}, u32[]{:S(2)}, u32[]{:S(2)}) collective-permute-start(bf16[256,2048]{1,0:T(8,128)(2,1)} %add_convert_fusion), channel_id=1, source_target_pairs={{0,1},{1,0},{2,3},{3,2},{4,5},{5,4},{6,7},{7,6},{8,9},{9,8},{10,11... | collective-permute-start | bytes 3145736 | tf_op jit(solution)/shard_map/ppermute | solution.py:1030
  (46 other events, 677.1 us)
Sparse Core Ops, SparseCore 0:
  61.9 79.7 all-gather.6
  143.2 165.9 all-gather.4
  422.6 79.5 reduce-scatter.3
  504.4 82.3 reduce-scatter.7
  589.0 100.1 reduce-scatter.5

commit v4 on v3

--- a/solution.py
+++ b/solution.py
@@ -207,23 +207,6 @@
     normed_ref[...] = (middle * rms_scale(middle) * gain_ref[...]).astype(jnp.bfloat16)
 
 
-def swiglu_kernel(n_ref, g_ref, both_ref, down_ref, hidden_ref, grads_ref, second_ref, ff_ref):
-    units = hidden_ref.shape[1]
-    lin = mul(n_ref[...], both_ref[...])
-    gate, up = lin[:, :units], lin[:, units:]
-    sig = jax.nn.sigmoid(gate)
-    act = gate * sig
-    hidden = (act * up).astype(jnp.bfloat16)
-    hidden_ref[...] = hidden
-    hidden_grad = mul(g_ref[...], down_ref[...])
-    grads_ref[:, :units] = (hidden_grad * up * sig * (1.0 + gate * (1.0 - sig))).astype(
-        jnp.bfloat16
-    )
-    grads_ref[:, units:] = (hidden_grad * act).astype(jnp.bfloat16)
-    second_ref[...] = mul(grads_ref[...], both_ref[...], NT).astype(jnp.bfloat16)
-    ff_ref[...] = mul(hidden, down_ref[...], NT).astype(jnp.bfloat16)
-
-
 def middle_back_kernel(
     dims, local_rows, len_ref, cot_ref, middle_ref, grad_ref, gain_ref, back_ref, attn_ref, gain_sum
 ):
@@ -487,8 +470,8 @@
     ]
     for copy in own:
         copy.start()
-    for i in range(lines):
-        for distance in range(1, ctx):
+    for distance in range(1, ctx):
+        for i in range(lines):
             for step in (1, -1):
                 shard = me_c - step * distance
 
@@ -531,7 +514,7 @@
     outs = pl.pallas_call(
         partial(line_kernel, fsdp, ctx, group, len(lines), len(swaps), spots),
         out_shape=out_shape,
-        in_specs=[pl.BlockSpec(memory_space=pl.ANY)] * count,
+        in_specs=[pl.BlockSpec(memory_space=pltpu.VMEM)] * count,
         out_specs=[pl.BlockSpec(memory_space=pl.ANY)] * len(out_shape),
         scratch_shapes=[
             sems((count,)),
@@ -540,15 +523,357 @@
             sems((len(swaps), group)),
             sems((len(swaps), group)),
         ],
-        compiler_params=pltpu.CompilerParams(collective_id=0, has_side_effects=True),
+        compiler_params=pltpu.CompilerParams(
+            collective_id=0, has_side_effects=True, vmem_limit_bytes=24 * 1024 * 1024
+        ),
     )(*lines, *swaps)
     return outs[: len(lines)], outs[len(lines) :]
 
 
-def spread_kernel(fsdp, ctx, count, chain, *refs):
+class TokenGather:
+    def __init__(self, group, fsdp, v_ref, out_ref, own_sem, f_send, f_recv, t_send, t_recv):
+        self.order = fsdp_order(group)
+        self.bits = [1 << i for i in range(group.bit_length() - 1)]
+        self.out_ref = out_ref
+        self.sems = (f_send, f_recv, t_send, t_recv)
+        self.fsdp = fsdp
+        half = out_ref.shape[2]
+        self.half = half
+        me_t = lax.axis_index("tp")
+        self.mine = v_ref.at[pl.ds(pl.multiple_of(me_t * half, half), half)]
+        other = v_ref.at[pl.ds(pl.multiple_of((1 - me_t) * half, half), half)]
+        self.own = [
+            pltpu.make_async_copy(self.mine, out_ref.at[0, 0], own_sem.at[0]),
+            pltpu.make_async_copy(other, out_ref.at[0, 1], own_sem.at[1]),
+        ]
+
+    def peer(self, k):
+        me_f = lax.axis_index("fsdp")
+        return (flip_index(me_f, k, self.fsdp), lax.axis_index("ctx"), lax.axis_index("tp"))
+
+    def rows(self, k, part):
+        if k == low_bit(k):
+            return pl.ds(0, self.half)
+        return pl.ds(part * (self.half // 2), self.half // 2)
+
+    def f_copy(self, have, b):
+        k = have | b
+        part = 1 if have and b == high_bit(k) else 0
+        place = self.out_ref.at[k, 0, self.rows(k, part)]
+        src = self.out_ref.at[have, 0, self.rows(k, part)] if have else self.mine
+        return pltpu.make_async_remote_copy(
+            src_ref=src,
+            dst_ref=place,
+            send_sem=self.sems[0].at[k, part],
+            recv_sem=self.sems[1].at[k, part],
+            device_id=self.peer(b),
+            device_id_type=MESH_ID,
+        )
+
+    def ways(self, have):
+        return [
+            b
+            for b in self.bits
+            if not have & b and (not have or b in (low_bit(have | b), high_bit(have | b)))
+        ]
+
+    def swap(self, k):
+        me_f, me_c, me_t = self.peer(0)
+        return pltpu.make_async_remote_copy(
+            src_ref=self.out_ref.at[k, 0],
+            dst_ref=self.out_ref.at[k, 1],
+            send_sem=self.sems[2].at[k],
+            recv_sem=self.sems[3].at[k],
+            device_id=(me_f, me_c, 1 - me_t),
+            device_id_type=MESH_ID,
+        )
+
+    def start(self):
+        for b in self.ways(0):
+            self.f_copy(0, b).start()
+        for copy in self.own:
+            copy.start()
+
+    def relay(self, k):
+        parts = [(0, k)] if k == low_bit(k) else [(0, low_bit(k)), (1, high_bit(k))]
+        for part, b in parts:
+            place = self.out_ref.at[k, 0, self.rows(k, part)]
+            pltpu.make_async_remote_copy(
+                src_ref=place,
+                dst_ref=place,
+                send_sem=self.sems[0].at[k, part],
+                recv_sem=self.sems[1].at[k, part],
+                device_id=self.peer(b),
+                device_id_type=MESH_ID,
+            ).wait_recv()
+        for b in self.ways(k):
+            self.f_copy(k, b).start()
+        self.swap(k).start()
+
+    def finish(self):
+        for copy in self.own:
+            copy.wait()
+        for have in [0] + self.order:
+            for b in self.ways(have):
+                self.f_copy(have, b).wait_send()
+        me_f, me_c, me_t = self.peer(0)
+        for k in self.order:
+            pltpu.make_async_remote_copy(
+                src_ref=self.out_ref.at[k, 1],
+                dst_ref=self.out_ref.at[k, 1],
+                send_sem=self.sems[2].at[k],
+                recv_sem=self.sems[3].at[k],
+                device_id=(me_f, me_c, 1 - me_t),
+                device_id_type=MESH_ID,
+            ).wait_recv()
+            self.swap(k).wait_send()
+
+
+def token_sems(group):
+    sems = pltpu.SemaphoreType.DMA
+    return [sems((2,)), sems((group, 2)), sems((group, 2)), sems((group,)), sems((group,))]
+
+
+def token_shape(group, v):
+    return jax.ShapeDtypeStruct((group, 2, v.shape[0] // 2, v.shape[1]), v.dtype)
+
+
+def tokens_kernel(group, fsdp, v_ref, out_ref, *sems):
+    gather = TokenGather(group, fsdp, v_ref, out_ref, *sems)
+    me_f, me_c, me_t = gather.peer(0)
+    barrier = pltpu.get_barrier_semaphore()
+    for b in gather.bits:
+        pl.semaphore_signal(barrier, inc=1, device_id=gather.peer(b), device_id_type=MESH_ID)
+    pl.semaphore_signal(
+        barrier, inc=1, device_id=(me_f, me_c, 1 - me_t), device_id_type=MESH_ID
+    )
+    pl.semaphore_wait(barrier, len(gather.bits) + 1)
+    gather.start()
+    for k in gather.order:
+        gather.relay(k)
+    gather.finish()
+
+
+def gather_tokens(group, fsdp, v):
+    out = pl.pallas_call(
+        partial(tokens_kernel, group, fsdp),
+        out_shape=token_shape(group, v),
+        in_specs=[pl.BlockSpec(memory_space=pltpu.VMEM)],
+        out_specs=pl.BlockSpec(memory_space=pl.ANY),
+        scratch_shapes=token_sems(group),
+        compiler_params=pltpu.CompilerParams(
+            collective_id=5, has_side_effects=True, vmem_limit_bytes=24 * 1024 * 1024
+        ),
+    )(v)
+    return out.reshape(-1, v.shape[1])
+
+
+def swiglu_kernel(
+    fsdp,
+    group,
+    n_ref,
+    g_ref,
+    both_ref,
+    down_ref,
+    hidden_ref,
+    grads_ref,
+    ff_ref,
+    own_ref,
+    s_out,
+    f_out,
+    s_in,
+    f_in,
+    total,
+    got,
+    t_send,
+    t_recv,
+    f_send,
+    f_recv,
+    own_sem,
+):
+    half = n_ref.shape[0]
+    units = hidden_ref.shape[1]
+    step = pl.program_id(0)
+    me_f = lax.axis_index("fsdp")
+    me_c = lax.axis_index("ctx")
+    me_t = lax.axis_index("tp")
+    bits = [1 << i for i in range(group.bit_length() - 1)]
+    order = fsdp_order(group)
+    core = (me_f, me_c, 1 - me_t)
+
+    def peer(k):
+        return (flip_index(me_f, k, fsdp), me_c, me_t)
+
+    @pl.when(step == 0)
+    def _():
+        barrier = pltpu.get_barrier_semaphore()
+        for b in bits:
+            pl.semaphore_signal(barrier, inc=1, device_id=peer(b), device_id_type=MESH_ID)
+        pl.semaphore_signal(barrier, inc=1, device_id=core, device_id_type=MESH_ID)
+        pl.semaphore_wait(barrier, len(bits) + 1)
+
+    def core_copies(k):
+        slot = k % 2
+        return [
+            pltpu.make_async_remote_copy(
+                src_ref=out.at[slot],
+                dst_ref=into.at[slot],
+                send_sem=t_send.at[which, k],
+                recv_sem=t_recv.at[which, k],
+                device_id=core,
+                device_id_type=MESH_ID,
+            )
+            for which, (out, into) in enumerate(((s_out, s_in), (f_out, f_in)))
+        ]
+
+    def ways(k):
+        return [(0, k)] if k == low_bit(k) else [(0, low_bit(k)), (1, high_bit(k))]
+
+    def span(k, part):
+        return pl.ds(0, half) if k == low_bit(k) else pl.ds(part * (half // 2), half // 2)
+
+    def f_copy(k, part, b):
+        return pltpu.make_async_remote_copy(
+            src_ref=total.at[k, span(k, part)],
+            dst_ref=got.at[k, span(k, part)],
+            send_sem=f_send.at[k, part],
+            recv_sem=f_recv.at[k, part],
+            device_id=peer(b),
+            device_id_type=MESH_ID,
+        )
+
+    def own_copy():
+        return pltpu.make_async_remote_copy(
+            src_ref=total.at[0],
+            dst_ref=own_ref.at[me_t],
+            send_sem=own_sem.at[0],
+            recv_sem=own_sem.at[1],
+            device_id=core,
+            device_id_type=MESH_ID,
+        )
+
+    lin = mul(n_ref[...], both_ref[...])
+    gate, up = lin[:, :units], lin[:, units:]
+    sig = jax.nn.sigmoid(gate)
+    act = gate * sig
+    hidden = (act * up).astype(jnp.bfloat16)
+    hidden_ref[...] = hidden
+    hidden_grad = mul(g_ref[...], down_ref[...])
+    grads_ref[:, :units] = (hidden_grad * up * sig * (1.0 + gate * (1.0 - sig))).astype(
+        jnp.bfloat16
+    )
+    grads_ref[:, units:] = (hidden_grad * act).astype(jnp.bfloat16)
+    second = mul(grads_ref[...], both_ref[...], NT)
+    ff = mul(hidden, down_ref[...], NT)
+
+    for k in reversed(range(group)):
+        slot = k % 2
+
+        @pl.when(step == 2 * (group - 1 - k))
+        def _():
+            if k + 2 < group:
+                for copy in core_copies(k + 2):
+                    copy.wait_send()
+            s_out[slot] = second.astype(jnp.bfloat16)
+            f_out[slot] = ff.astype(jnp.bfloat16)
+            for copy in core_copies(k):
+                copy.start()
+
+        @pl.when(step == 2 * (group - 1 - k) + 1)
+        def _():
+            for copy in core_copies(k):
+                copy.wait_recv()
+            ff_ref[...] = (ff + f_in[slot].astype(jnp.float32)).astype(jnp.bfloat16)
+            total[k] = (second + s_in[slot].astype(jnp.float32)).astype(jnp.bfloat16)
+            for far in order:
+                for part, b in ways(far):
+                    if far ^ b == k:
+                        f_copy(far, part, b).wait_recv()
+                        rows = span(far, part)
+                        total[k, rows] = (
+                            total[k, rows].astype(jnp.float32)
+                            + got[far, rows].astype(jnp.float32)
+                        ).astype(jnp.bfloat16)
+            if k:
+                for part, b in ways(k):
+                    f_copy(k, part, b).start()
+            else:
+                own_copy().start()
+                local = pltpu.make_async_copy(total.at[0], own_ref.at[me_t], own_sem.at[2])
+                local.start()
+                local.wait()
+                other = own_ref.at[1 - me_t]
+                pltpu.make_async_remote_copy(
+                    src_ref=other,
+                    dst_ref=other,
+                    send_sem=own_sem.at[0],
+                    recv_sem=own_sem.at[1],
+                    device_id=core,
+                    device_id_type=MESH_ID,
+                ).wait_recv()
+                own_copy().wait_send()
+                for far in order:
+                    for part, b in ways(far):
+                        f_copy(far, part, b).wait_send()
+                for late in range(min(2, group)):
+                    for copy in core_copies(late):
+                        copy.wait_send()
+
+
+def swiglu(fsdp, group, normed, grads, both, down):
+    many, width = normed.shape
+    half = many // (2 * group)
+    units = down.shape[1]
+    low = jnp.bfloat16
+    last = 2 * group - 1
+    sems = pltpu.SemaphoreType.DMA
+    block = (half, width)
+
+    def rows(cols):
+        return pl.BlockSpec((half, cols), lambda i: (last - i, 0))
+
+    def whole(v):
+        return pl.BlockSpec(v.shape, lambda i: (0, 0), pipeline_mode=pl.Buffered(1))
+
+    return pl.pallas_call(
+        partial(swiglu_kernel, fsdp, group),
+        grid=(2 * group,),
+        in_specs=[rows(width), rows(width), whole(both), whole(down)],
+        out_specs=[
+            rows(units),
+            rows(2 * units),
+            pl.BlockSpec(block, lambda i: (group - 1 - i // 2, 0)),
+            pl.BlockSpec(memory_space=pl.ANY),
+        ],
+        out_shape=[
+            jax.ShapeDtypeStruct((many, units), low),
+            jax.ShapeDtypeStruct((many, 2 * units), low),
+            jax.ShapeDtypeStruct((group * half, width), low),
+            jax.ShapeDtypeStruct((2,) + block, low),
+        ],
+        scratch_shapes=[pltpu.VMEM((2,) + block, low)] * 4
+        + [pltpu.VMEM((group,) + block, low)] * 2
+        + [
+            sems((2, group)),
+            sems((2, group)),
+            sems((group, 2)),
+            sems((group, 2)),
+            sems((3,)),
+        ],
+        compiler_params=pltpu.CompilerParams(
+            collective_id=6, has_side_effects=True, vmem_limit_bytes=58 * 1024 * 1024
+        ),
+        cost_estimate=pl.CostEstimate(
+            flops=12 * many * width * units, bytes_accessed=50 << 20, transcendentals=0
+        ),
+    )(normed, grads, both, down)
+
+
+def spread_kernel(fsdp, ctx, group, count, chain, *refs):
     ins = refs[:count]
     outs = refs[count + chain : 2 * count + chain]
-    own_sem, f_send, f_recv, c_own, c_send, c_recv = refs[2 * (count + chain) :]
+    sems = refs[2 * (count + chain) :]
+    own_sem, f_send, f_recv, c_own, c_send, c_recv = sems[:6]
     me_f = lax.axis_index("fsdp")
     me_c = lax.axis_index("ctx")
     me_t = lax.axis_index("tp")
@@ -562,7 +887,13 @@
     for b in bits:
         pl.semaphore_signal(barrier, inc=1, device_id=peer(b), device_id_type=MESH_ID)
     if chain:
-        chain_in, chain_out = refs[count], refs[2 * count + 1]
+        chain_in, chain_out = refs[count], refs[2 * count + chain]
+        gather = TokenGather(
+            group, fsdp, refs[count + 1], refs[2 * count + chain + 1], *sems[6:]
+        )
+        pl.semaphore_signal(
+            barrier, inc=1, device_id=(me_f, me_c, 1 - me_t), device_id_type=MESH_ID
+        )
         for step in (-1, 1):
             there = me_c + step
 
@@ -572,19 +903,25 @@
                     barrier, inc=1, device_id=(me_f, there, me_t), device_id_type=MESH_ID
                 )
 
-        pl.semaphore_wait(barrier, len(bits) + line_neighbours(me_c, ctx))
+        pl.semaphore_wait(barrier, len(bits) + 1 + line_neighbours(me_c, ctx))
     else:
         pl.semaphore_wait(barrier, len(bits))
 
+    def quarters(rows):
+        return [pl.ds(i * (rows // 4), rows // 4) for i in range(4)]
+
     def climb(s):
-        return pltpu.make_async_remote_copy(
-            src_ref=chain_out.at[s] if s else chain_in,
-            dst_ref=chain_out.at[s + 1],
-            send_sem=c_send.at[s],
-            recv_sem=c_recv.at[s + 1],
-            device_id=(me_f, me_c + 1, me_t),
-            device_id_type=MESH_ID,
-        )
+        return [
+            pltpu.make_async_remote_copy(
+                src_ref=chain_out.at[s, part] if s else chain_in.at[part],
+                dst_ref=chain_out.at[s + 1, part],
+                send_sem=c_send.at[s, i],
+                recv_sem=c_recv.at[s + 1, i],
+                device_id=(me_f, me_c + 1, me_t),
+                device_id_type=MESH_ID,
+            )
+            for i, part in enumerate(quarters(chain_in.shape[0]))
+        ]
 
     def keep(s):
         return pltpu.make_async_copy(chain_in, chain_out.at[s], c_own.at[s])
@@ -592,19 +929,21 @@
     def send_up(s):
         @pl.when((me_c >= s) & (me_c < ctx - 1))
         def _():
-            climb(s).start()
+            for copy in climb(s):
+                copy.start()
 
     def take_up(s):
         @pl.when(me_c >= s)
         def _():
-            pltpu.make_async_remote_copy(
-                src_ref=chain_out.at[s],
-                dst_ref=chain_out.at[s],
-                send_sem=c_send.at[s - 1],
-                recv_sem=c_recv.at[s],
-                device_id=(me_f, me_c - 1, me_t),
-                device_id_type=MESH_ID,
-            ).wait_recv()
+            for i, part in enumerate(quarters(chain_in.shape[0])):
+                pltpu.make_async_remote_copy(
+                    src_ref=chain_out.at[s, part],
+                    dst_ref=chain_out.at[s, part],
+                    send_sem=c_send.at[s - 1, i],
+                    recv_sem=c_recv.at[s, i],
+                    device_id=(me_f, me_c - 1, me_t),
+                    device_id_type=MESH_ID,
+                ).wait_recv()
 
         if s < ctx - 1:
             send_up(s)
@@ -650,12 +989,16 @@
             for b in ways(0):
                 f_copy(i, shard, 0, b).start()
         own[i].start()
+    if chain:
+        gather.start()
     climbed = 1
     for i in range(count):
         for k in order:
             if chain and climbed < ctx:
                 take_up(climbed)
                 climbed += 1
+            if chain and k < group and i == 0:
+                gather.relay(k)
             parts = [(0, k)] if k == low_bit(k) else [(0, low_bit(k)), (1, high_bit(k))]
             for shard in range(ctx):
                 for part, b in parts:
@@ -673,6 +1016,7 @@
     if chain:
         for s in range(climbed, ctx):
             take_up(s)
+        gather.finish()
         keep(0).wait()
         for s in range(ctx):
             if s:
@@ -685,7 +1029,8 @@
 
                 @pl.when((me_c >= s) & (me_c < ctx - 1))
                 def _():
-                    climb(s).wait_send()
+                    for copy in climb(s):
+                        copy.wait_send()
 
     for i in range(count):
         own[i].wait()
@@ -695,34 +1040,42 @@
                     f_copy(i, shard, have, b).wait_send()
 
 
-def spread_weights(fsdp, ctx, arrays, chain=None):
+def spread_weights(fsdp, ctx, group, arrays, chain=()):
     count = len(arrays)
     sems = pltpu.SemaphoreType.DMA
-    extra = [] if chain is None else [chain]
     outs = pl.pallas_call(
-        partial(spread_kernel, fsdp, ctx, count, len(extra)),
+        partial(spread_kernel, fsdp, ctx, group, count, len(chain)),
         out_shape=[
             jax.ShapeDtypeStruct((ctx, fsdp) + v.shape[1:], v.dtype) for v in arrays
         ]
-        + [jax.ShapeDtypeStruct((ctx,) + v.shape, v.dtype) for v in extra],
-        in_specs=[pl.BlockSpec(memory_space=pl.ANY)] * (count + len(extra)),
-        out_specs=[pl.BlockSpec(memory_space=pl.ANY)] * (count + len(extra)),
+        + [jax.ShapeDtypeStruct((ctx,) + v.shape, v.dtype) for v in chain[:1]]
+        + [token_shape(group, v) for v in chain[1:]],
+        in_specs=[pl.BlockSpec(memory_space=pltpu.VMEM)] * (count + len(chain)),
+        out_specs=[pl.BlockSpec(memory_space=pl.ANY)] * (count + len(chain)),
         scratch_shapes=[
             sems((count,)),
             sems((count, ctx, fsdp, 2)),
             sems((count, ctx, fsdp, 2)),
             sems((ctx,)),
-            sems((ctx,)),
-            sems((ctx,)),
-        ],
+            sems((ctx, 4)),
+            sems((ctx, 4)),
+        ]
+        + (token_sems(group) if chain else []),
         compiler_params=pltpu.CompilerParams(
-            collective_id=1 if chain is None else 3, has_side_effects=True
+            collective_id=3 if chain else 1,
+            has_side_effects=True,
+            vmem_limit_bytes=24 * 1024 * 1024,
         ),
-    )(*arrays, *extra)
-    return [o.reshape(-1, v.shape[-1]) for o, v in zip(outs, arrays)] + list(outs[count:])
-
-
-def sum_kernel(fsdp, ctx, count, chain, *refs):
+    )(*arrays, *chain)
+    return (
+        [o.reshape(-1, v.shape[-1]) for o, v in zip(outs, arrays)]
+        + list(outs[count : count + 1])
+        + [o.reshape(-1, o.shape[-1]) for o in outs[count + 1 :]]
+    )
+
+
+def sum_kernel(fsdp, ctx, group, count, chain, *refs):
+    weights = count - 1 if chain else count
     ins = refs[:count]
     if chain:
         parts_ref, cos_ref, sin_ref = refs[count : count + 3]
@@ -732,15 +1085,23 @@
     outs = refs[count : 2 * count]
     held = refs[2 * count : 3 * count]
     got = refs[3 * count : 4 * count]
-    line = refs[4 * count : 5 * count]
-    in_sem, f_send, f_recv, z_send, z_recv = refs[5 * count : 5 * count + 5]
+    line = refs[4 * count : 4 * count + weights]
+    refs = refs[4 * count + weights :]
+    in_sem, f_send, f_recv, z_send, z_recv = refs[:5]
     if chain:
-        kv_parts, kv_got, kv_sem, c_send, c_recv = refs[5 * count + 5 :]
+        kv_parts, kv_got, kv_sem, c_send, c_recv = refs[5:]
     me_f = lax.axis_index("fsdp")
     me_c = lax.axis_index("ctx")
     me_t = lax.axis_index("tp")
     bits = [1 << i for i in range(fsdp.bit_length() - 1)]
     order = fsdp_order(fsdp)
+    near = fsdp_order(group)
+
+    def steps_of(i):
+        return order if i < weights else near
+
+    def shards_of(i):
+        return shards if i < weights else [0]
 
     def peer(k):
         return (flip_index(me_f, k, fsdp), me_c, me_t)
@@ -757,10 +1118,9 @@
         kv_load = pltpu.make_async_copy(parts_ref, kv_parts, kv_sem.at[0])
         kv_load.start()
     for i in range(count):
-        for k in reversed([0] + order):
-            loads[i, k] = pltpu.make_async_copy(
-                ins[i].at[:, flip_index(me_f, k, fsdp)], held[i].at[k], in_sem.at[i, k]
-            )
+        for k in reversed([0] + steps_of(i)):
+            block = ins[i].at[:, flip_index(me_f, k, fsdp)] if i < weights else ins[i].at[k]
+            loads[i, k] = pltpu.make_async_copy(block, held[i].at[k], in_sem.at[i, k])
             loads[i, k].start()
 
     barrier = pltpu.get_barrier_semaphore()
@@ -806,7 +1166,7 @@
         lax.fori_loop(0, into.shape[0] // tile, body, 0)
 
     def collect(i, shard, k):
-        for far in order:
+        for far in steps_of(i):
             for part, b in ways(far):
                 if far ^ b == k:
                     f_copy(i, shard, far, part, b).wait_recv()
@@ -824,61 +1184,65 @@
             device_id_type=MESH_ID,
         )
 
-    def on_line(i, shard):
-        for step in (1, -1):
-            way = 0 if step > 0 else 1
-
-            @pl.when((step * (shard - me_c) >= 0) & (me_c - step >= 0) & (me_c - step < ctx))
-            def _():
-                z_copy(i, shard, step).wait_recv()
-                add(held[i].at[0, shard], line[i].at[way, shard])
-
-            @pl.when(step * (shard - me_c) > 0)
-            def _():
-                z_copy(i, shard, step).start()
-
-        @pl.when(shard == me_c)
+    def give(i, shard):
+        def body(r, _):
+            span = pl.ds(pl.multiple_of(r * 16, 16), 16)
+            outs[i][span] = held[i][0, shard, span].astype(outs[i].dtype)
+            return 0
+
+        lax.fori_loop(0, outs[i].shape[0] // 16, body, 0)
+
+    def on_line(i, shard, step):
+        way = 0 if step > 0 else 1
+
+        @pl.when((me_c - step >= 0) & (me_c - step < ctx))
         def _():
-            rows = outs[i].shape[0]
-
-            def body(r, _):
-                span = pl.ds(pl.multiple_of(r * 16, 16), 16)
-                outs[i][span] = held[i][0, shard, span].astype(outs[i].dtype)
-                return 0
-
-            lax.fori_loop(0, rows // 16, body, 0)
+            z_copy(i, shard, step).wait_recv()
+            add(held[i].at[0, shard], line[i].at[way, shard])
+
+        @pl.when(step * (shard - me_c) > 0)
+        def _():
+            z_copy(i, shard, step).start()
+
+    def quarters():
+        rows = kv_parts.shape[2] // 2
+        return [(side, pl.ds(i * rows, rows)) for side in range(2) for i in range(2)]
 
     def descend(s):
-        return pltpu.make_async_remote_copy(
-            src_ref=kv_parts.at[s],
-            dst_ref=kv_got.at[s - 1],
-            send_sem=c_send.at[s],
-            recv_sem=c_recv.at[s - 1],
-            device_id=(me_f, me_c - 1, me_t),
-            device_id_type=MESH_ID,
-        )
+        return [
+            pltpu.make_async_remote_copy(
+                src_ref=kv_parts.at[s, side, part],
+                dst_ref=kv_got.at[s - 1, side, part],
+                send_sem=c_send.at[s, i],
+                recv_sem=c_recv.at[s - 1, i],
+                device_id=(me_f, me_c - 1, me_t),
+                device_id_type=MESH_ID,
+            )
+            for i, (side, part) in enumerate(quarters())
+        ]
 
     def chain_step(s):
         if s < ctx - 1:
 
             @pl.when((me_c >= s) & (me_c < ctx - 1))
             def _():
-                pltpu.make_async_remote_copy(
-                    src_ref=kv_got.at[s],
-                    dst_ref=kv_got.at[s],
-                    send_sem=c_send.at[s + 1],
-                    recv_sem=c_recv.at[s],
-                    device_id=(me_f, me_c + 1, me_t),
-                    device_id_type=MESH_ID,
-                ).wait_recv()
-                for side in range(2):
-                    add(kv_parts.at[s, side], kv_got.at[s, side])
+                for i, (side, part) in enumerate(quarters()):
+                    pltpu.make_async_remote_copy(
+                        src_ref=kv_got.at[s, side, part],
+                        dst_ref=kv_got.at[s, side, part],
+                        send_sem=c_send.at[s + 1, i],
+                        recv_sem=c_recv.at[s, i],
+                        device_id=(me_f, me_c + 1, me_t),
+                        device_id_type=MESH_ID,
+                    ).wait_recv()
+                    add(kv_parts.at[s, side, part], kv_got.at[s, side, part])
 
         if s:
 
             @pl.when(me_c >= s)
             def _():
-                descend(s).start()
+                for copy in descend(s):
+                    copy.start()
 
     def chain_result():
         width = kv_parts.shape[3]
@@ -905,35 +1269,65 @@
         kv_load.wait()
         next_step()
     shards = sorted(range(ctx), key=lambda c: -abs(2 * c - ctx + 1))
-    work = [(i, shard) for i in range(count) for shard in shards]
+    work = [[(i, shard) for i in range(weights)] for shard in shards]
+    work += [[(i, 0)] for i in range(weights, count)]
     levels = sorted({bin(k).count("1") for k in order}, reverse=True)
-    for level in levels:
-        ks = [k for k in order if bin(k).count("1") == level]
-        for i in range(count):
-            for k in ks:
-                loads[i, k].wait()
-            for shard in shards:
-                for k in ks:
+    waited = set()
+
+    def loaded(i, k):
+        if (i, k) not in waited:
+            waited.add((i, k))
+            loads[i, k].wait()
+
+    def advance(stage, item):
+        for i, shard in item:
+            if stage == len(levels):
+                loaded(i, 0)
+                collect(i, shard, 0)
+                if i >= weights:
+                    give(i, shard)
+                continue
+            for k in steps_of(i):
+                if bin(k).count("1") == levels[stage]:
+                    loaded(i, k)
                     collect(i, shard, k)
                     for part, b in ways(k):
                         f_copy(i, shard, k, part, b).start()
+
+    def line_tick(item, hops):
+        for i, shard in item:
+            if i >= weights:
+                continue
+            for step, there in ((1, hops), (-1, ctx - 1 - hops)):
+                if step * (shard - there) >= 0:
+
+                    @pl.when(me_c == there)
+                    def _():
+                        on_line(i, shard, step)
+
+            if hops == max(shard, ctx - 1 - shard):
+
+                @pl.when(me_c == shard)
+                def _():
+                    give(i, shard)
+
+    stages = len(levels) + 1
+    for tick in range(len(work) + stages + ctx - 2):
+        for stage in range(stages):
+            if 0 <= tick - stage < len(work):
+                advance(stage, work[tick - stage])
+        for hops in range(ctx):
+            place = tick - stages + 1 - hops
+            if 0 <= place < len(work):
+                line_tick(work[place], hops)
         next_step()
-    for i in range(count):
-        loads[i, 0].wait()
-    late = None
     while steps:
         next_step()
-    for item in work + [None]:
-        if item is not None:
-            collect(item[0], item[1], 0)
-        if late is not None:
-            on_line(*late)
-        late = item
-    for i, shard in work:
-        for k in order:
+    for i, shard in [pair for item in work for pair in item]:
+        for k in steps_of(i):
             for part, b in ways(k):
                 f_copy(i, shard, k, part, b).wait_send()
-        for step in (1, -1):
+        for step in (1, -1) if i < weights else ():
 
             @pl.when(step * (shard - me_c) > 0)
             def _():
@@ -944,25 +1338,42 @@
 
             @pl.when(me_c >= s)
             def _():
-                descend(s).wait_send()
-
-
-def sum_weights(fsdp, ctx, arrays, chain=()):
-    count = len(arrays)
+                for copy in descend(s):
+                    copy.wait_send()
+
+
+def sum_weights(fsdp, ctx, group, arrays, chain=()):
     sems = pltpu.SemaphoreType.DMA
+    vmem = pltpu.VMEM
     shards = [v.reshape(ctx, fsdp, -1, v.shape[-1]) for v in arrays]
-    vmem = pltpu.VMEM
     blocks = [(fsdp, ctx) + v.shape[2:] for v in shards]
+    out_shape = [jax.ShapeDtypeStruct(v.shape[2:], jnp.float32) for v in shards]
+    lines = [vmem((2,) + b[1:], v.dtype) for b, v in zip(blocks, shards)]
+    extra = []
+    if chain:
+        rows, parts, cosines, sines = chain
+        shards.append(rows[:, None])
+        blocks.append(shards[-1].shape)
+        out_shape.append(jax.ShapeDtypeStruct(rows.shape[1:], rows.dtype))
+        out_shape.append(jax.ShapeDtypeStruct((parts.shape[2], 2 * parts.shape[3]), parts.dtype))
+        extra = [
+            vmem(parts.shape, parts.dtype),
+            vmem((ctx - 1,) + parts.shape[1:], parts.dtype),
+            sems((1,)),
+            sems((ctx, 4)),
+            sems((ctx, 4)),
+        ]
+    count = len(shards)
+    held = [vmem(b, v.dtype) for b, v in zip(blocks, shards)]
     return pl.pallas_call(
-        partial(sum_kernel, fsdp, ctx, count, bool(chain)),
-        out_shape=[jax.ShapeDtypeStruct(v.shape[2:], jnp.float32) for v in shards]
-        + [jax.ShapeDtypeStruct((v.shape[2], 2 * v.shape[3]), v.dtype) for v in chain[:1]],
-        in_specs=[pl.BlockSpec(memory_space=pl.ANY)] * (count + len(chain[:1]))
-        + [pl.BlockSpec(memory_space=pltpu.VMEM)] * len(chain[1:]),
-        out_specs=[pl.BlockSpec(memory_space=pltpu.VMEM)] * (count + len(chain[:1])),
-        scratch_shapes=[vmem(b, v.dtype) for b, v in zip(blocks, shards)]
-        + [vmem(b, v.dtype) for b, v in zip(blocks, shards)]
-        + [vmem((2,) + b[1:], v.dtype) for b, v in zip(blocks, shards)]
+        partial(sum_kernel, fsdp, ctx, group, count, bool(chain)),
+        out_shape=out_shape,
+        in_specs=[pl.BlockSpec(memory_space=pl.ANY)] * (count + len(chain[1:2]))
+        + [pl.BlockSpec(memory_space=pltpu.VMEM)] * len(chain[2:]),
+        out_specs=[pl.BlockSpec(memory_space=pltpu.VMEM)] * len(out_shape),
+        scratch_shapes=held
+        + held
+        + lines
         + [
             sems((count, fsdp)),
             sems((count, ctx, fsdp, 2)),
@@ -970,23 +1381,13 @@
             sems((count, 2, ctx)),
             sems((count, 2, ctx)),
         ]
-        + [
-            scratch
-            for v in chain[:1]
-            for scratch in (
-                vmem(v.shape, v.dtype),
-                vmem((ctx - 1,) + v.shape[1:], v.dtype),
-                sems((1,)),
-                sems((ctx,)),
-                sems((ctx,)),
-            )
-        ],
+        + extra,
         compiler_params=pltpu.CompilerParams(
             collective_id=4 if chain else 2,
             has_side_effects=True,
-            vmem_limit_bytes=50 * 1024 * 1024,
+            vmem_limit_bytes=52 * 1024 * 1024,
         ),
-    )(*shards, *chain)
+    )(*shards, *chain[1:])
 
 
 def local(
@@ -1019,12 +1420,8 @@
     units = w_gate.shape[1] // group
     me_c = lax.axis_index("ctx")
     me_t = lax.axis_index("tp")
-    order = fsdp_order(group)
     low = jnp.bfloat16
     wide = jnp.float32
-
-    def hop(v, k):
-        return lax.ppermute(v, "fsdp", [(i, i ^ k) for i in range(fsdp)])
 
     def swap(v):
         return lax.ppermute(v, "tp", [(0, 1), (1, 0)])
@@ -1057,45 +1454,7 @@
             v.reshape(rows, pairs, group_size, 2, HD).swapaxes(2, 3).reshape(rows, query_width)
         )
 
-    def gather_tokens(v):
-        mine = lax.dynamic_slice_in_dim(v, me_t * half, half)
-        other = lax.dynamic_slice_in_dim(v, (1 - me_t) * half, half)
-        got = {0: mine}
-        for k in order:
-            lo, hi = low_bit(k), high_bit(k)
-            if lo == hi:
-                got[k] = hop(mine, k)
-            else:
-                cut = half // 2
-                got[k] = jnp.concatenate(
-                    [hop(got[k ^ lo][:cut], lo), hop(got[k ^ hi][cut:], hi)]
-                )
-        return jnp.concatenate(
-            [mine, other] + [v for k in range(1, group) for v in (got[k], swap(got[k]))]
-        )
-
-    def scatter_tokens(v):
-        cut = half // 2
-        total = {}
-        for k in reversed([0] + order):
-            start = 2 * k * half
-            mine, other = v[start : start + half], v[start + half : start + 2 * half]
-            total[k] = mine.astype(wide) + swap(other).astype(wide)
-        for k in reversed(order):
-            lo, hi = low_bit(k), high_bit(k)
-            sent = total[k].astype(low)
-            if lo == hi:
-                total[0] = total[0] + hop(sent, k).astype(wide)
-            else:
-                for there, first, b in ((k ^ lo, True, lo), (k ^ hi, False, hi)):
-                    piece = hop(sent[:cut] if first else sent[cut:], b).astype(wide)
-                    base = total[there]
-                    total[there] = jnp.concatenate(
-                        [base[:cut] + piece, base[cut:]]
-                        if first
-                        else [base[:cut], base[cut:] + piece]
-                    )
-        own = total[0].astype(low)
+    def both_halves(own):
         other = swap(own)
         return jnp.where(
             me_t == 0, jnp.concatenate([own, other]), jnp.concatenate([other, own])
@@ -1113,8 +1472,8 @@
         ctx,
         group,
         [
+            jnp.concatenate([pair_heads(w_query), w_key, w_value], 1),
             gains,
-            jnp.concatenate([pair_heads(w_query), w_key, w_value], 1),
             pair_heads(w_out),
         ],
         [[w_gate, w_up], [w_down]],
@@ -1128,7 +1487,7 @@
         return lax.all_gather(v, "ctx", axis=0, tiled=False).reshape(model_width, -1)
 
     both_full, down_full = [whole_width(v) for v in held]
-    gain_rows, qkv_full = spread_weights(fsdp, ctx, lined[:2])
+    qkv_full, gain_rows = spread_weights(fsdp, ctx, group, lined[:2])
     gain_rows = gain_rows.reshape(ctx * fsdp, 16, shard)
     gain_one = gain_rows[:, 0].reshape(1, model_width)
     gain_two = gain_rows[:, 1].reshape(1, model_width)
@@ -1139,9 +1498,6 @@
         [(lengths, "smem"), (cot, "rows")],
         [((tokens, model_width), low)],
     )
-    ff_grad, gain_one = lax.optimization_barrier((ff_grad, gain_one))
-    ff_grad_all = gather_tokens(ff_grad)
-
     first_normed, query, kv_own = by_rows(
         partial(qkv_kernel, dims),
         128,
@@ -1159,7 +1515,9 @@
         ],
         flops=2 * tokens * model_width * kv_end,
     )
-    out_full, kv_all = spread_weights(fsdp, ctx, lined[2:], kv_own)
+    out_full, kv_all, ff_grad_all = spread_weights(
+        fsdp, ctx, group, lined[2:], (kv_own, ff_grad)
+    )
     attended, lse = attend(lengths, query, kv_all)
     attn_part = jnp.einsum(
         "tj,dj->td", attended, out_full, preferred_element_type=wide
@@ -1170,32 +1528,17 @@
         [(x, "rows"), (attn_part, "rows"), (swap(attn_part), "rows"), (gain_two, "whole")],
         [((tokens, model_width), wide), ((tokens, model_width), low)],
     )
-    normed_all = gather_tokens(second_normed)
-
-    many = group * tokens
-    hidden, both_grad, second_part, ff_part = by_rows(
-        swiglu_kernel,
-        256,
-        [
-            (normed_all, "rows"),
-            (ff_grad_all, "rows"),
-            (both_full, "whole"),
-            (down_full, "whole"),
-        ],
-        [
-            ((many, units), low),
-            ((many, 2 * units), low),
-            ((many, model_width), low),
-            ((many, model_width), low),
-        ],
-        flops=12 * many * model_width * units,
-        limit=56,
-    )
+    normed_all = gather_tokens(group, fsdp, second_normed)
+
+    hidden, both_grad, ff_sums, second_grad = swiglu(
+        fsdp, group, normed_all, ff_grad_all, both_full, down_full
+    )
+    second_grad = second_grad.reshape(tokens, model_width)
 
     def unit_term(left, right):
         return jnp.einsum("td,tf->df", left, right, preferred_element_type=wide).astype(low)
 
-    def return_units(term):
+    def own_units(term):
         own = lax.psum_scatter(
             term.reshape(ctx, fsdp, shard, units), "ctx", scatter_dimension=0, tiled=False
         )
@@ -1207,6 +1550,9 @@
                 tiled=False,
                 axis_index_groups=far_groups,
             )
+        return own
+
+    def return_units(own):
         return lax.all_to_all(
             own.reshape(group * shard, units),
             "fsdp",
@@ -1217,22 +1563,8 @@
         ).astype(wide)
 
     down_term = unit_term(ff_grad_all, hidden)
-    second_grad = scatter_tokens(second_part)
-    gate_term = unit_term(normed_all, both_grad[:, :units])
-    up_term = unit_term(normed_all, both_grad[:, units:])
-    second_grad, ff_part, _, _, _ = lax.optimization_barrier(
-        (second_grad, ff_part, down_term, gate_term, up_term)
-    )
-    ff_branch = scatter_tokens(ff_part)
-    w_down_grad = return_units(down_term)
-    w_gate_grad = return_units(gate_term)
-    w_up_grad = return_units(up_term)
-    (output,) = by_rows(
-        partial(output_kernel, back_dims, local_rows),
-        128,
-        [(lengths, "smem"), (middle, "rows"), (ff_branch, "rows")],
-        [((tokens, model_width), low)],
-    )
+    second_grad, down_after = lax.optimization_barrier((second_grad, down_term))
+    w_down_grad = return_units(own_units(down_term))
 
     middle_grad, attn_grad, gain_two_term = by_rows(
         partial(middle_back_kernel, dims, local_rows),
@@ -1250,10 +1582,26 @@
     query_grad, kv_parts = attend_back(
         lengths, query, attended_grad, lse, cosines, sines, kv_all
     )
+    query_grad, normed_all, both_grad = lax.optimization_barrier(
+        (query_grad, normed_all, both_grad)
+    )
+    gate_term = unit_term(normed_all, both_grad[:, :units])
+    w_gate_grad = return_units(own_units(gate_term))
+    ff_sums = ff_sums.reshape(group, half, model_width)
     out_term = jnp.einsum("td,tj->dj", attn_grad, attended, preferred_element_type=wide)
-    w_out_grad, kv_grad = sum_weights(
-        fsdp, ctx, [out_term.astype(low)], (kv_parts, cosines, sines)
-    )
+    kv_parts, gate_after = lax.optimization_barrier((kv_parts, gate_term))
+    w_out_grad, ff_own, kv_grad = sum_weights(
+        fsdp, ctx, group, [out_term.astype(low)], (ff_sums, kv_parts, cosines, sines)
+    )
+    (output,) = by_rows(
+        partial(output_kernel, back_dims, local_rows),
+        128,
+        [(lengths, "smem"), (middle, "rows"), (both_halves(ff_own), "rows")],
+        [((tokens, model_width), low)],
+    )
+    kv_grad, normed_all, both_grad = lax.optimization_barrier((kv_grad, normed_all, both_grad))
+    up_term = unit_term(normed_all, both_grad[:, units:])
+    up_own = own_units(up_term)
     qkv_grad = jnp.concatenate([query_grad, kv_grad], -1)
     qkv_term = jnp.einsum("td,tj->dj", first_normed, qkv_grad, preferred_element_type=wide)
     first_part = jnp.einsum(
@@ -1275,10 +1623,12 @@
         [gain_one_term.reshape(-1, shard), gain_two_term.reshape(-1, shard)], 1
     )
     gain_terms = jnp.pad(gain_terms, ((0, 0), (0, 14), (0, 0))).reshape(-1, shard)
-    qkv_term, w_down_grad, w_gate_grad, w_up_grad = lax.optimization_barrier(
-        (qkv_term.astype(low), w_down_grad, w_gate_grad, w_up_grad)
-    )
-    gain_own, qkv_own = sum_weights(fsdp, ctx, [gain_terms, qkv_term])
+    qkv_term, w_down_grad, w_gate_grad, up_after = lax.optimization_barrier(
+        (qkv_term.astype(low), w_down_grad, w_gate_grad, up_term)
+    )
+    qkv_own, gain_own = sum_weights(fsdp, ctx, group, [qkv_term, gain_terms])
+    up_own, qkv_own = lax.optimization_barrier((up_own, qkv_own))
+    w_up_grad = return_units(up_own)
     return (
         by_fsdp(output).reshape(inputs.shape),
         by_fsdp(input_grad).reshape(inputs.shape),

time: 928 us -> 780 us (0.84)
  waiting for transfers between devices: 118 us -> 31 us
  starting transfers between devices: 37.7 us -> 12.9 us
  other arithmetic: 33.1 us -> 8.41 us
  local copies, waits for them, and re-layouts: 57.4 us -> 34.2 us
    ppermute x16 -> x0, waiting for transfers between devices: 108 us -> none  [hop(): return lax.ppermute(v, 'fsdp', [(i, i ^ k) for i in range(fsdp)])]
    pallas_call x4 -> x6, Pallas kernels: 410 us -> 484 us  [the longest x2 211 us: sum_weights(): pl.pallas_call(partial(sum_kernel, fsdp, ctx, group, count, bool(chain)),...]
    pallas_call x7 -> x6, Pallas kernels: 87.5 us -> 22.5 us  [by_rows(): pl.pallas_call(kernel, grid=(total // rows,), in_specs=in_specs, out_spec...]
    ppermute x16 -> x0, starting transfers between devices: 23 us -> none  [hop(): return lax.ppermute(v, 'fsdp', [(i, i ^ k) for i in range(fsdp)])]
    all_to_all x3, waiting for transfers between devices: 4.19 us -> 15.2 us  [return_units(): lax.all_to_all(own.reshape(group * shard, units), 'fsdp', 0, 1, tiled=Tru...]
    unnamed x77 -> x79, local copies, waits for them, and re-layouts: 36.9 us -> 25.9 us
    all_gather x2, waiting for transfers between devices: 0.01 us -> 10.8 us  [whole_width(): lax.all_gather(v, 'ctx', axis=0, tiled=False).reshape(model_width, -1)]
    slice x12 -> x0, local copies, waits for them, and re-layouts: 10.1 us -> none  [the longest x2 7.47 us: scatter_tokens(): mine, other = (v[start:start + half], v[start + half:start + 2 * half])]
  transfers between devices with their start and end apart: 42 -> 11, of which waited for: 17 -> 4; matrix products, arithmetic and copies ran while one was open for 13% -> 9% of each run, Pallas kernels for 41% -> 62%
where the time goes in v4:
time: 780 us; the launch traced here: 771 us
  Pallas kernels  602 us (77%)
  matrix products  67.1 us (9%)
  local copies, waits for them, and re-layouts  34.2 us (4%)
  waiting for transfers between devices  31 us (4%)
  between operations  15 us (2%)
  starting transfers between devices  12.9 us (2%)
  other arithmetic  8.41 us (1%)
    pallas_call x2, Pallas kernels, sum_weights(): pl.pallas_call(partial(sum_kernel, fsdp, ctx, group, count, bool(chain)),...  211 us
    pallas_call x2, Pallas kernels, spread_weights(): pl.pallas_call(partial(spread_kernel, fsdp, ctx, group, count, len(chain)...  152 us
    pallas_call x1, Pallas kernels, swiglu(): pl.pallas_call(partial(swiglu_kernel, fsdp, group), grid=(2 * group,), in...  80.6 us
    pallas_call x1, Pallas kernels, start_exchange(): pl.pallas_call(partial(line_kernel, fsdp, ctx, group, len(lines), len(swa...  45.8 us
    dot_general x3, matrix products, unit_term(): jnp.einsum('td,tf->df', left, right, preferred_element_type=wide)  41.3 us
    pallas_call x1, Pallas kernels, gather_tokens(): pl.pallas_call(partial(tokens_kernel, group, fsdp), out_shape=token_shape...  40.7 us
    pallas_call x1, Pallas kernels, attend_back(): pl.pallas_call(partial(attend_back_kernel, ctx), grid=(seqs, pairs), in_s...  32.9 us
    unnamed x79, local copies, waits for them, and re-layouts  25.9 us
  transfers between devices with their start and end apart: 11, of which 4 were waited for; matrix products, arithmetic and copies ran while one was open for 9% of the time, Pallas kernels for 62%

profile of v4, /device:TPU:16, one launch (start us, length us, event | category | flops | bytes accessed | tf_op | source)
XLA Modules:
  0.0 770.9 jit_solution(5763883621022449763)
XLA Ops:
  15.1 45.8 %shard_map.203 = (bf16[4,128,1536]{2,1,0:T(8,128)(2,1)S(1)}, f32[4,16,128]{2,1,0:T(8,128)S(1)}, bf16[4,128,1024]{2,1,0:T(8,128)(2,1)S(1)}, bf16[4,128,2048]{2,1,0:T(8,128)(2,1)S(1)}, bf16[4,128,1024]{2,1,0:T(8,128)(2,1)S(1)}) custom-call(bf16[128,1536]{1,0:T(8,128)(2,1)S(1)} %pad_maximum_fusion.refs_0_, f32[16,128]{1,0:T(8,128)S(1)} %fusion.13.refs_1_, ...), custom_call_target="tpu_custom_call" | custom-call | tf_op jit(solution)/shard_map/pallas_call | solution.py:514
  68.6 56.7 %shard_map.204 = (bf16[4,4,128,1536]{3,2,1,0:T(8,128)(2,1)S(1)}, f32[4,4,16,128]{3,2,1,0:T(8,128)S(1)}) custom-call(bf16[4,128,1536]{2,1,0:T(8,128)(2,1)S(1)} %copy-done.12, f32[4,16,128]{2,1,0:T(8,128)S(1)} %get-tuple-element.58.refs_1_), custom_call_target="tpu_custom_call" | custom-call | tf_op jit(solution)/shard_map/pallas_call | solution.py:1046
  125.4 5.1 shard_map.205
  130.5 95.0 %shard_map.207 = (bf16[4,4,128,1024]{3,2,1,0:T(8,128)(2,1)S(1)}, bf16[4,512,512]{2,1,0:T(8,128)(2,1)S(1)}, bf16[4,2,256,2048]{3,2,1,0:T(8,128)(2,1)S(1)}) custom-call(bf16[4,128,1024]{2,1,0:T(8,128)(2,1)S(1)} %get-tuple-element.62.refs_0_, bf16[512,512]{1,0:T(8,128)(2,1)S(1)} %get-tuple-element.63.refs_1_, bf16[512,2048]{1,0:T(8,128)(2,1)S(1)} %shard_map.206.refs_2_), custom_call_target="tpu_custom_call" | custom-call | tf_op jit(solution)/shard_map/pallas_call | solution.py:1046
  228.8 17.4 %shard_map.208 = (bf16[512,1024]{1,0:T(8,128)(2,1)S(1)}, f32[512,256]{1,0:T(8,128)S(1)}) custom-call(s32[2]{0:T(128)S(1)} %copy-done.19, bf16[512,1024]{1,0:T(8,128)(2,1)S(1)} %get-tuple-element.61.q_ref, bf16[4,512,512]{2,1,0:T(8,128)(2,1)S(1)} %get-tuple-element.64.refs_0_.refs_1_.refs_2_.refs_3_.refs_4_.refs_5_.refs_6_.refs_7_, ...), custom_call_target="tpu_custom_call" | custom-call | flops 8589934592 | bytes 6291456 | tf_op jit(solution)/shard_map/pallas_call | solution.py:304
  249.4 4.1 collective-permute-done.other_ref
  257.6 40.7 %shard_map.210 = bf16[4,2,256,2048]{3,2,1,0:T(8,128)(2,1)S(1)} custom-call(bf16[512,2048]{1,0:T(8,128)(2,1)S(1)} %get-tuple-element.68.v_ref), custom_call_target="tpu_custom_call" | custom-call | tf_op jit(solution)/shard_map/pallas_call | solution.py:658
  301.6 10.8 %all-gather.5.cloned.1.call-done = bf16[16,128,2048]{2,1,0:T(8,128)(2,1)} async-done(((bf16[4,128,2048]{2,1,0:T(8,128)(2,1)}), bf16[16,128,2048]{2,1,0:T(8,128)(2,1)}) %all-gather.5.cloned.1.call-update) | async-done | bytes 8388624 | tf_op jit(solution)/shard_map/all_gather | solution.py:1487
  312.4 80.6 %shard_map.211 = (bf16[2048,1024]{1,0:T(8,128)(2,1)}, bf16[2048,2048]{1,0:T(8,128)(2,1)}, bf16[1024,2048]{1,0:T(8,128)(2,1)}, bf16[2,256,2048]{2,1,0:T(8,128)(2,1)}) custom-call(bf16[2048,2048]{1,0:T(8,128)(2,1)} %bitcast.86, bf16[2048,2048]{1,0:T(8,128)(2,1)} %bitcast.101, bf16[2048,2048]{1,0:T(8,128)(2,1)} %bitcast.132, bf16[2048,1024]{1,0:T(8,128)(2,1)} %bitcast.133), custom_call_target="tpu_custom_call" | custom-call | flops 51539607552 | bytes 52428800 | tf_op jit(solution)/shard_map/pallas_call | solution.py:838
  392.9 14.0 %convolution_convert_fusion.2 = bf16[2048,1024]{1,0:T(8,128)(2,1)} fusion(bf16[2048,2048]{1,0:T(8,128)(2,1)} %bitcast.102, bf16[2048,1024]{1,0:T(8,128)(2,1)} %get-tuple-element.73), kind=kOutput, calls=%fused_computation.8 | convolution fusion | flops 8592031744 | bytes 16777216 | tf_op jit(solution)/shard_map/td,tf->df/dot_general | solution.py:1539
  408.6 6.0 shard_map.212
  418.9 32.9 %shard_map.213 = (bf16[512,1024]{1,0:T(8,128)(2,1)S(1)}, bf16[4,2,512,256]{3,2,1,0:T(8,128)(2,1)S(1)}) custom-call(s32[2]{0:T(128)S(1)} %copy-done.19, bf16[512,1024]{1,0:T(8,128)(2,1)S(1)} %copy-done.30, bf16[512,1024]{1,0:T(8,128)(2,1)S(1)} %convolution_convert_fusion.5.do_ref, f32[512,256]{1,0:T(8,128)S(1)} %copy-done.33, ...), custom_call_target="tpu_custom_call" | custom-call | flops 21474836480 | bytes 10485760 | tf_op jit(solution)/shard_map/pallas_call | solution.py:332
  451.8 12.9 %fusion.4 = bf16[2048,1024]{1,0:T(8,128)(2,1)} fusion(bf16[2048,2048]{1,0:T(8,128)(2,1)S(1)} %bitcast.90, bf16[2048,2048]{1,0:T(8,128)(2,1)} %get-tuple-element.92), kind=kOutput, calls=%fused_computation.5 | convolution fusion | flops 8592031744 | bytes 16777216 | tf_op jit(solution)/shard_map/td,tf->df/dot_general | solution.py:1539
  466.3 5.7 convolution_convert_fusion.1
  472.0 139.0 %shard_map.214 = (f32[128,1024]{1,0:T(8,128)S(1)}, bf16[256,2048]{1,0:T(8,128)(2,1)}, bf16[512,512]{1,0:T(8,128)(2,1)S(1)}) custom-call(bf16[4,4,128,1024]{3,2,1,0:T(8,128)(2,1)} %bitcast.112, bf16[4,1,256,2048]{3,2,1,0:T(8,128)(2,1)} %bitcast.111, bf16[4,2,512,256]{3,2,1,0:T(8,128)(2,1)} %copy-done.10, f32[256,128]{1,0:T(8,128)S(1)} %copy.66.cos_ref.refs_3_, ...), custom_call_target="tpu_custom_call" | custom-call | tf_op jit(solution)/shard_map/pallas_call | solution.py:1368
  611.0 14.4 %fusion.7 = bf16[2048,1024]{1,0:T(8,128)(2,1)} fusion(bf16[2048,2048]{1,0:T(8,128)(2,1)} %bitcast.87, bf16[2048,2048]{1,0:T(8,128)(2,1)} %get-tuple-element.92), kind=kOutput, calls=%fused_computation.6 | convolution fusion | flops 8592031744 | bytes 16777216 | tf_op jit(solution)/shard_map/td,tf->df/dot_general | solution.py:1539
  625.5 7.1 convolution_convert_fusion.4.part_ref
  632.7 4.3 all-to-all-start
  637.5 14.1 %all-to-all-done = bf16[4,128,1024]{2,1,0:T(8,128)(2,1)} async-done(((bf16[4,128,1024]{2,1,0:T(8,128)(2,1)}), bf16[4,128,1024]{2,1,0:T(8,128)(2,1)}, u32[]{:S(2)}, u32[]{:S(2)}) %all-to-all-start) | async-done | bytes 1048608 | tf_op jit(solution)/shard_map/all_to_all | solution.py:1556
  651.6 4.2 all-to-all-start.1
  655.9 8.3 %convolution_convert_fusion = bf16[2048,1536]{1,0:T(8,128)(2,1)} fusion(bf16[512,2048]{1,0:T(8,128)(2,1)} %copy-done.28, bf16[512,1536]{1,0:T(8,128)(2,1)} %copy-done.34), kind=kOutput, calls=%fused_computation | convolution fusion | flops 3224371200 | bytes 9961472 | tf_op jit(solution)/shard_map/td,tj->dj/dot_general | solution.py:1606
  664.2 5.6 shard_map.216
  675.7 71.9 %shard_map.217 = (f32[128,1536]{1,0:T(8,128)S(1)}, f32[16,128]{1,0:T(8,128)S(1)}) custom-call(bf16[4,4,128,1536]{3,2,1,0:T(8,128)(2,1)} %bitcast.107, f32[4,4,16,128]{3,2,1,0:T(8,128)S(1)} %bitcast.97), custom_call_target="tpu_custom_call" | custom-call | tf_op jit(solution)/shard_map/pallas_call | solution.py:1368
  747.6 3.5 all-to-all-start.2
  (137 shorter events, 56.0 us)
Async XLA Ops:
  7.2 294.4 %all-gather.7.cloned.1.call-start = ((), (), s32[]{:S(2)}) async-start(), calls=%async_computation.10 | async-start | bytes 5242880 | tf_op jit(solution)/shard_map/all_gather | solution.py:1487
  15.1 52.1 %copy-start.3 = (bf16[2,256,2048]{2,1,0:T(8,128)(2,1)S(1)}, bf16[2,256,2048]{2,1,0:T(8,128)(2,1)}, u32[]{:S(2)}) copy-start(bf16[2,256,2048]{2,1,0:T(8,128)(2,1)} %param.14) | copy-start | bytes 6291460
  15.1 52.1 %copy-start.19 = (s32[2]{0:T(128)S(1)}, s32[2]{0:T(128)}, u32[]{:S(2)}) copy-start(s32[2]{0:T(128)} %len_ref.9) | copy-start | bytes 28
  64.3 248.0 %all-gather.5.cloned.1.call-start = ((), (), s32[]{:S(2)}) async-start(), calls=%async_computation.9 | async-start | bytes 10485760 | tf_op jit(solution)/shard_map/all_gather | solution.py:1487
  65.1 567.7 %reduce-scatter.4.cloned.1.call-start = ((), (), s32[]{:S(2)}) async-start(), calls=%async_computation.6 | async-start | bytes 5242880 | tf_op jit(solution)/shard_map/reduce_scatter | solution.py:1542
  67.2 58.2 %copy-start.4 = (bf16[2,256,2048]{2,1,0:T(8,128)(2,1)S(1)}, bf16[2,256,2048]{2,1,0:T(8,128)(2,1)}, u32[]{:S(2)}) copy-start(bf16[2,256,2048]{2,1,0:T(8,128)(2,1)} %param.12) | copy-start | bytes 6291460
  130.4 98.3 %copy-start.28 = (bf16[512,2048]{1,0:T(8,128)(2,1)}, bf16[512,2048]{1,0:T(8,128)(2,1)S(1)}, u32[]{:S(2)}) copy-start(bf16[512,2048]{1,0:T(8,128)(2,1)S(1)} %get-tuple-element.90) | copy-start | bytes 6291460
  130.5 115.7 %copy-start.29 = (bf16[512,1024]{1,0:T(8,128)(2,1)}, bf16[512,1024]{1,0:T(8,128)(2,1)S(1)}, u32[]{:S(2)}) copy-start(bf16[512,1024]{1,0:T(8,128)(2,1)S(1)} %get-tuple-element.61.q_ref) | copy-start | bytes 3145732
  228.7 17.4 %copy-start.24 = (bf16[4,512,512]{2,1,0:T(8,128)(2,1)}, bf16[4,512,512]{2,1,0:T(8,128)(2,1)S(1)}, u32[]{:S(2)}) copy-start(bf16[4,512,512]{2,1,0:T(8,128)(2,1)S(1)} %get-tuple-element.64.refs_0_.refs_1_.refs_2_.refs_3_.refs_4_.refs_5_.refs_6_.refs_7_) | copy-start | bytes 6291460
  228.7 18.2 %copy-start.22 = (bf16[4,4,128,1024]{3,2,1,0:T(8,128)(2,1)}, bf16[4,4,128,1024]{3,2,1,0:T(8,128)(2,1)S(1)}, u32[]{:S(2)}) copy-start(bf16[4,4,128,1024]{3,2,1,0:T(8,128)(2,1)S(1)} %get-tuple-element.66) | copy-start | bytes 12582916
  249.3 4.2 collective-permute-start
  407.0 230.5 %reduce-scatter.6.cloned.1.call-start = ((), (), s32[]{:S(2)}) async-start(), calls=%async_computation.7 | async-start | bytes 5242880 | tf_op jit(solution)/shard_map/reduce_scatter | solution.py:1542
  414.7 37.1 %slice-start = ((s8[8388608]{0:T(1024)(128)(4,1)}), s8[4194304]{0:T(1024)(128)(4,1)S(1)}, s32[]{:S(2)}) async-start(s8[8388608]{0:T(1024)(128)(4,1)} %bitcast.88), calls=%async_computation.11 | async-start | bytes 8388608
  418.9 32.9 %slice-start.1 = ((s8[8388608]{0:T(1024)(128)(4,1)}), s8[4194304]{0:T(1024)(128)(4,1)S(1)}, s32[]{:S(2)}) async-start(s8[8388608]{0:T(1024)(128)(4,1)} %bitcast.88), calls=%async_computation.12 | async-start | bytes 8388608
  451.8 13.0 %copy-start.10 = (bf16[4,2,512,256]{3,2,1,0:T(8,128)(2,1)}, bf16[4,2,512,256]{3,2,1,0:T(8,128)(2,1)S(1)}, u32[]{:S(2)}) copy-start(bf16[4,2,512,256]{3,2,1,0:T(8,128)(2,1)S(1)} %get-tuple-element.83.refs_2_) | copy-start | bytes 6291460
  464.8 282.8 %reduce-scatter.8.cloned.1.call-start = ((), (), s32[]{:S(2)}) async-start(), calls=%async_computation.8 | async-start | bytes 5242880 | tf_op jit(solution)/shard_map/reduce_scatter | solution.py:1542
  632.6 31.5 %collective-permute-start.2 = (bf16[512,2048]{1,0:T(8,128)(2,1)S(1)}, bf16[512,2048]{1,0:T(8,128)(2,1)}, u32[]{:S(2)}, u32[]{:S(2)}) collective-permute-start(bf16[512,2048]{1,0:T(8,128)(2,1)S(1)} %convolution_convert_fusion.4.part_ref), channel_id=1, source_target_pairs={{0,1},{1,0},{2,3},{3,2},{4,5},{5,4},{6,7},{7,6},{8,9},{9,8},{10,11... | collective-permute-start | bytes 6291464 | tf_op jit(solution)/shard_map/ppermute | solution.py:1427
  632.7 18.9 %all-to-all-start = ((bf16[4,128,1024]{2,1,0:T(8,128)(2,1)}), bf16[4,128,1024]{2,1,0:T(8,128)(2,1)}, u32[]{:S(2)}, u32[]{:S(2)}) async-start(bf16[4,128,1024]{2,1,0:T(8,128)(2,1)} %bitcast.123), calls=%async_computation.1 | async-start | bytes 2097152 | tf_op jit(solution)/shard_map/all_to_all | solution.py:1556
  637.0 115.4 %collective-permute-start.1 = (bf16[256,2048]{1,0:T(8,128)(2,1)}, bf16[256,2048]{1,0:T(8,128)(2,1)}, u32[]{:S(2)}, u32[]{:S(2)}) collective-permute-start(bf16[256,2048]{1,0:T(8,128)(2,1)} %get-tuple-element.84), channel_id=1, source_target_pairs={{0,1},{1,0},{2,3},{3,2},{4,5},{5,4},{6,7},{7,6},{8,9},{9,8},{10,11... | collective-permute-start | bytes 3145736 | tf_op jit(solution)/shard_map/ppermute | solution.py:1427
  651.6 21.1 %all-to-all-start.1 = ((bf16[4,128,1024]{2,1,0:T(8,128)(2,1)}), bf16[4,128,1024]{2,1,0:T(8,128)(2,1)}, u32[]{:S(2)}, u32[]{:S(2)}) async-start(bf16[4,128,1024]{2,1,0:T(8,128)(2,1)} %bitcast.122), calls=%async_computation.3 | async-start | bytes 2097152 | tf_op jit(solution)/shard_map/all_to_all | solution.py:1556
  655.8 8.3 %copy-start.5 = (bf16[2,256,2048]{2,1,0:T(8,128)(2,1)S(1)}, bf16[2,256,2048]{2,1,0:T(8,128)(2,1)}, u32[]{:S(2)}) copy-start(bf16[2,256,2048]{2,1,0:T(8,128)(2,1)} %param.12) | copy-start | bytes 6291460
  655.9 8.3 %copy-start.7 = (f32[512,2048]{1,0:T(8,128)S(1)}, f32[512,2048]{1,0:T(8,128)}, u32[]{:S(2)}) copy-start(f32[512,2048]{1,0:T(8,128)} %copy-done.6) | copy-start | bytes 12582916
  655.9 8.3 %copy-start.18 = (f32[1,2048]{1,0:T(1,128)S(1)}, f32[1,2048]{1,0:T(1,128)}, u32[]{:S(2)}) copy-start(f32[1,2048]{1,0:T(1,128)} %copy-done.17) | copy-start | bytes 24580
  747.6 14.5 %all-to-all-start.2 = ((bf16[4,128,1024]{2,1,0:T(8,128)(2,1)}), bf16[4,128,1024]{2,1,0:T(8,128)(2,1)S(1)}, u32[]{:S(2)}, u32[]{:S(2)}) async-start(bf16[4,128,1024]{2,1,0:T(8,128)(2,1)} %bitcast.121), calls=%async_computation.5 | async-start | bytes 2097152 | tf_op jit(solution)/shard_map/all_to_all | solution.py:1556
  (24 other events, 67.4 us)
Sparse Core Ops, SparseCore 0:
  64.4 82.1 all-gather.6
  148.7 163.5 all-gather.4
  407.1 82.8 reduce-scatter.3
  492.3 111.5 reduce-scatter.5
  625.5 79.5 reduce-scatter.7

commit v5 on v4

--- a/solution.py
+++ b/solution.py
@@ -53,6 +53,7 @@
 
 
 MESH_ID = pl.DeviceIdType.MESH
+FIRST_EIGHTHS = 4
 NT = (((1,), (1,)), ((), ()))
 TN = (((0,), (0,)), ((), ()))
 SMEM = pltpu.SMEM
@@ -153,9 +154,118 @@
     lse_ref[...] = lse_all
 
 
-def attend_back_kernel(ctx, len_ref, q_ref, do_ref, lse_ref, cos_ref, sin_ref, *refs):
+class RowSum:
+    def __init__(
+        self, group, fsdp, rows_ref, own_ref, held, got, in_sem, f_send, f_recv, own_sem
+    ):
+        self.group, self.fsdp = group, fsdp
+        self.order = fsdp_order(group)
+        self.bits = [1 << i for i in range(group.bit_length() - 1)]
+        self.own_ref, self.held, self.got = own_ref, held, got
+        self.f_send, self.f_recv, self.own_sem = f_send, f_recv, own_sem
+        self.half = rows_ref.shape[1]
+        self.loads = [
+            pltpu.make_async_copy(rows_ref.at[k], held.at[k], in_sem.at[k]) for k in range(group)
+        ]
+
+    def peer(self, k):
+        me_f = lax.axis_index("fsdp")
+        return (flip_index(me_f, k, self.fsdp), lax.axis_index("ctx"), lax.axis_index("tp"))
+
+    def core(self):
+        me_f, me_c, me_t = self.peer(0)
+        return (me_f, me_c, 1 - me_t)
+
+    def ways(self, k):
+        return [(0, k)] if k == low_bit(k) else [(0, low_bit(k)), (1, high_bit(k))]
+
+    def span(self, k, part):
+        half = self.half
+        return pl.ds(0, half) if k == low_bit(k) else pl.ds(part * (half // 2), half // 2)
+
+    def copy(self, k, part, b):
+        return pltpu.make_async_remote_copy(
+            src_ref=self.held.at[k, self.span(k, part)],
+            dst_ref=self.got.at[k, self.span(k, part)],
+            send_sem=self.f_send.at[k, part],
+            recv_sem=self.f_recv.at[k, part],
+            device_id=self.peer(b),
+            device_id_type=MESH_ID,
+        )
+
+    def own_copy(self, place):
+        return pltpu.make_async_remote_copy(
+            src_ref=self.held.at[0],
+            dst_ref=self.own_ref.at[place],
+            send_sem=self.own_sem.at[0],
+            recv_sem=self.own_sem.at[1],
+            device_id=self.core(),
+            device_id_type=MESH_ID,
+        )
+
+    def collect(self, k):
+        for far in self.order:
+            for part, b in self.ways(far):
+                if far ^ b == k:
+                    self.copy(far, part, b).wait_recv()
+                    rows = self.span(far, part)
+                    self.held[k, rows] = (
+                        self.held[k, rows].astype(jnp.float32)
+                        + self.got[far, rows].astype(jnp.float32)
+                    ).astype(self.held.dtype)
+
+    def send(self, k):
+        for part, b in self.ways(k):
+            self.copy(k, part, b).start()
+
+    def start(self):
+        barrier = pltpu.get_barrier_semaphore()
+        for b in self.bits:
+            pl.semaphore_signal(barrier, inc=1, device_id=self.peer(b), device_id_type=MESH_ID)
+        pl.semaphore_signal(barrier, inc=1, device_id=self.core(), device_id_type=MESH_ID)
+        for load in self.loads:
+            load.start()
+        pl.semaphore_wait(barrier, len(self.bits) + 1)
+        for load in self.loads:
+            load.wait()
+        for k in self.order:
+            if k != low_bit(k):
+                self.send(k)
+
+    def relay(self):
+        for k in self.order:
+            if k == low_bit(k):
+                self.collect(k)
+                self.send(k)
+
+    def finish(self):
+        self.collect(0)
+        me_t = lax.axis_index("tp")
+        self.own_copy(me_t).start()
+        local = pltpu.make_async_copy(
+            self.held.at[0], self.own_ref.at[me_t], self.own_sem.at[2]
+        )
+        local.start()
+        local.wait()
+        self.own_copy(1 - me_t).wait_recv()
+        self.own_copy(me_t).wait_send()
+        for k in self.order:
+            for part, b in self.ways(k):
+                self.copy(k, part, b).wait_send()
+
+
+def attend_back_kernel(
+    ctx, fsdp, group, len_ref, q_ref, do_ref, lse_ref, cos_ref, sin_ref, rows_ref, *refs
+):
     keys, values = refs[:ctx], refs[ctx : 2 * ctx]
-    dq_ref, dkv_ref, dk_sum, dv_sum = refs[2 * ctx :]
+    dq_ref, dkv_ref, own_ref, dk_sum, dv_sum = refs[2 * ctx : 2 * ctx + 5]
+    step = pl.program_id(0) * pl.num_programs(1) + pl.program_id(1)
+    sums = RowSum(group, fsdp, rows_ref, own_ref, *refs[2 * ctx + 5 :])
+
+    @pl.when(step == 0)
+    def _():
+        sums.start()
+
     rows = q_ref.shape[0]
     biases = key_biases(len_ref, rows, ctx)
     lane = lax.broadcasted_iota(jnp.int32, (rows, 128), 1)
@@ -189,9 +299,19 @@
         dq = jnp.where(lane < HD, dqs[0], dqs[1]) * score_scale
         dq = dq * cos_ref[...] + turn(dq * sin_ref[...], -1.0)
         dq_ref[:, j * 128 : (j + 1) * 128] = dq.astype(jnp.bfloat16)
+        if j == 1:
+
+            @pl.when(step == 1)
+            def _():
+                sums.relay()
+
     for s in range(ctx):
         dkv_ref[s, 0] = dk_sum[s].astype(dkv_ref.dtype)
         dkv_ref[s, 1] = dv_sum[s].astype(dkv_ref.dtype)
+
+    @pl.when(step == pl.num_programs(0) * pl.num_programs(1) - 1)
+    def _():
+        sums.finish()
 
 
 def cot_kernel(dims, local_rows, len_ref, cot_ref, ff_ref):
@@ -322,15 +442,18 @@
     )(lengths, query, *[kv_all] * (2 * ctx))
 
 
-def attend_back(lengths, query, out_grad, lse, cosines, sines, kv_all):
+def attend_back(fsdp, group, lengths, query, out_grad, lse, cosines, sines, kv_all, row_blocks):
     ctx = kv_all.shape[0]
+    block = row_blocks.shape[1:]
+    low = jnp.bfloat16
+    sems = pltpu.SemaphoreType.DMA
     seqs = lengths.shape[0]
     rows = query.shape[0] // seqs
     pairs = kv_all.shape[2] // 256
     wide = query.shape[1] // pairs
     flops = 10 * query.shape[0] * query.shape[1] * rows * ctx
     return pl.pallas_call(
-        partial(attend_back_kernel, ctx),
+        partial(attend_back_kernel, ctx, fsdp, group),
         grid=(seqs, pairs),
         in_specs=[
             pl.BlockSpec(memory_space=SMEM),
@@ -339,20 +462,27 @@
             pl.BlockSpec((rows, 128), lambda s, p: (s, p)),
             pl.BlockSpec((rows, 128), lambda s, p: (0, 0)),
             pl.BlockSpec((rows, 128), lambda s, p: (0, 0)),
+            pl.BlockSpec(memory_space=pl.ANY),
         ]
         + kv_specs(ctx, rows, pairs),
         out_specs=[
             pl.BlockSpec((rows, wide), lambda s, p: (s, p)),
             pl.BlockSpec((ctx, 2, rows, 128), lambda s, p: (0, 0, s, p)),
+            pl.BlockSpec(memory_space=pl.ANY),
         ],
         out_shape=[
             jax.ShapeDtypeStruct(query.shape, jnp.bfloat16),
-            jax.ShapeDtypeStruct((ctx, 2, query.shape[0], 128 * pairs), jnp.bfloat16),
+            jax.ShapeDtypeStruct((ctx, 2, query.shape[0], 128 * pairs), low),
+            jax.ShapeDtypeStruct((2,) + block, low),
         ],
-        scratch_shapes=[pltpu.VMEM((ctx, rows, 128), jnp.float32)] * 2,
-        compiler_params=pltpu.CompilerParams(vmem_limit_bytes=40 * 1024 * 1024),
+        scratch_shapes=[pltpu.VMEM((ctx, rows, 128), jnp.float32)] * 2
+        + [pltpu.VMEM((group,) + block, low)] * 2
+        + [sems((group,)), sems((group, 2)), sems((group, 2)), sems((3,))],
+        compiler_params=pltpu.CompilerParams(
+            collective_id=7, has_side_effects=True, vmem_limit_bytes=44 * 1024 * 1024
+        ),
         cost_estimate=pl.CostEstimate(flops=4 * flops, bytes_accessed=10 << 20, transcendentals=0),
-    )(lengths, query, out_grad, lse, cosines, sines, *[kv_all] * (2 * ctx))
+    )(lengths, query, out_grad, lse, cosines, sines, row_blocks, *[kv_all] * (2 * ctx))
 
 
 def low_bit(k):
@@ -380,12 +510,13 @@
     return (me > 0).astype(jnp.int32) + (me < count - 1).astype(jnp.int32)
 
 
-def line_kernel(fsdp, ctx, group, lines, swaps, spots, *refs):
+def line_kernel(fsdp, ctx, group, lines, swaps, widths, *refs):
     line_in = refs[:lines]
     swap_in = refs[lines : lines + swaps]
     line_out = refs[lines + swaps : 2 * lines + swaps]
     swap_out = refs[2 * lines + swaps : -5]
     own_sem, z_send, z_recv, f_send, f_recv = refs[-5:]
+    parts = len(widths)
     me_f = lax.axis_index("fsdp")
     me_c = lax.axis_index("ctx")
     me_t = lax.axis_index("tp")
@@ -423,50 +554,54 @@
             device_id_type=MESH_ID,
         )
 
-    def landing(i, f):
-        out, start = spots[i]
-        width = swap_in[i].shape[1] // group
-        return swap_out[out].at[lax.rem(f, group), :, pl.ds(start, width)]
-
-    def columns(i, f):
-        width = swap_in[i].shape[1] // group
-        return swap_in[i].at[:, pl.ds(pl.multiple_of(lax.rem(f, group) * width, 128), width)]
-
-    def f_copy(i, k):
+    def landing(i, part, f):
+        width = widths[part]
+        return swap_out[part].at[lax.rem(f, group), :, pl.ds(i * width, width)]
+
+    def columns(i, part, f):
+        start = lax.rem(f, group) * sum(widths) + sum(widths[:part])
+        return swap_in[i].at[:, pl.ds(pl.multiple_of(start, 128), widths[part])]
+
+    def f_copy(i, part, k):
         there = flip_index(me_f, k, fsdp)
         return pltpu.make_async_remote_copy(
-            src_ref=columns(i, there),
-            dst_ref=landing(i, me_f),
-            send_sem=f_send.at[i, k],
-            recv_sem=f_recv.at[i, k],
+            src_ref=columns(i, part, there),
+            dst_ref=landing(i, part, me_f),
+            send_sem=f_send.at[i * parts + part, k],
+            recv_sem=f_recv.at[i * parts + part, k],
             device_id=(there, me_c, me_t),
             device_id_type=MESH_ID,
         )
 
-    def f_arrival(i, k):
+    def f_arrival(i, part, k):
         there = flip_index(me_f, k, fsdp)
         return pltpu.make_async_remote_copy(
-            src_ref=landing(i, there),
-            dst_ref=landing(i, there),
-            send_sem=f_send.at[i, k],
-            recv_sem=f_recv.at[i, k],
+            src_ref=landing(i, part, there),
+            dst_ref=landing(i, part, there),
+            send_sem=f_send.at[i * parts + part, k],
+            recv_sem=f_recv.at[i * parts + part, k],
             device_id=(there, me_c, me_t),
             device_id_type=MESH_ID,
         )
 
+    pieces = [(i, part) for part in range(parts) for i in range(swaps)]
     for i in range(lines):
         for step in (1, -1):
             along(step, lambda there: z_copy(i, me_c, step, line_in[i]).start())
     order = fsdp_order(group)
-    for i in range(swaps):
+    for i, part in pieces:
         for k in order:
-            f_copy(i, k).start()
+            f_copy(i, part, k).start()
     own = [
         pltpu.make_async_copy(line_in[i], line_out[i].at[me_c], own_sem.at[i])
         for i in range(lines)
     ] + [
-        pltpu.make_async_copy(columns(i, me_f), landing(i, me_f), own_sem.at[lines + i])
-        for i in range(swaps)
+        pltpu.make_async_copy(
+            columns(i, part, me_f),
+            landing(i, part, me_f),
+            own_sem.at[lines + i * parts + part],
+        )
+        for i, part in pieces
     ]
     for copy in own:
         copy.start()
@@ -480,10 +615,10 @@
                     z_copy(i, shard, step).wait_recv()
                     along(step, lambda there: z_copy(i, shard, step).start())
 
-    for i in range(swaps):
+    for i, part in pieces:
         for k in order:
-            f_arrival(i, k).wait_recv()
-            f_copy(i, k).wait_send()
+            f_arrival(i, part, k).wait_recv()
+            f_copy(i, part, k).wait_send()
     for copy in own:
         copy.wait()
     for i in range(lines):
@@ -497,31 +632,26 @@
                     along(step, lambda there: z_copy(i, shard, step).wait_send())
 
 
-def start_exchange(fsdp, ctx, group, lines, swap_sets):
+def start_exchange(fsdp, ctx, group, lines, swaps, widths):
+    parts = len(widths)
     sems = pltpu.SemaphoreType.DMA
+    rows = swaps[0].shape[0]
     out_shape = [jax.ShapeDtypeStruct((ctx,) + v.shape, v.dtype) for v in lines]
-    swaps, spots = [], []
-    for out, arrays in enumerate(swap_sets):
-        start = 0
-        for v in arrays:
-            spots.append((out, start))
-            swaps.append(v)
-            start += v.shape[1] // group
-        out_shape.append(
-            jax.ShapeDtypeStruct((group, arrays[0].shape[0], start), arrays[0].dtype)
-        )
+    out_shape += [
+        jax.ShapeDtypeStruct((group, rows, len(swaps) * w), swaps[0].dtype) for w in widths
+    ]
     count = len(lines) + len(swaps)
     outs = pl.pallas_call(
-        partial(line_kernel, fsdp, ctx, group, len(lines), len(swaps), spots),
+        partial(line_kernel, fsdp, ctx, group, len(lines), len(swaps), tuple(widths)),
         out_shape=out_shape,
         in_specs=[pl.BlockSpec(memory_space=pltpu.VMEM)] * count,
         out_specs=[pl.BlockSpec(memory_space=pl.ANY)] * len(out_shape),
         scratch_shapes=[
-            sems((count,)),
+            sems((len(lines) + len(swaps) * parts,)),
             sems((len(lines), 2, ctx)),
             sems((len(lines), 2, ctx)),
-            sems((len(swaps), group)),
-            sems((len(swaps), group)),
+            sems((len(swaps) * parts, group)),
+            sems((len(swaps) * parts, group)),
         ],
         compiler_params=pltpu.CompilerParams(
             collective_id=0, has_side_effects=True, vmem_limit_bytes=24 * 1024 * 1024
@@ -668,13 +798,38 @@
     return out.reshape(-1, v.shape[1])
 
 
+def swiglu_parts(n_ref, g_ref, w_ref, hidden_ref, grads_ref):
+    units = hidden_ref.shape[1]
+    both = w_ref[:, : 2 * units]
+    down = w_ref[:, 2 * units :]
+    lin = mul(n_ref[...], both)
+    gate, up = lin[:, :units], lin[:, units:]
+    sig = jax.nn.sigmoid(gate)
+    act = gate * sig
+    hidden = (act * up).astype(jnp.bfloat16)
+    hidden_ref[...] = hidden
+    hidden_grad = mul(g_ref[...], down)
+    grads_ref[:, :units] = (hidden_grad * up * sig * (1.0 + gate * (1.0 - sig))).astype(
+        jnp.bfloat16
+    )
+    grads_ref[:, units:] = (hidden_grad * act).astype(jnp.bfloat16)
+    return mul(grads_ref[...], both, NT), mul(hidden, down, NT)
+
+
+def swiglu_first_kernel(n_ref, g_ref, w_ref, hidden_ref, grads_ref, second_ref, ff_ref):
+    second, ff = swiglu_parts(n_ref, g_ref, w_ref, hidden_ref, grads_ref)
+    second_ref[...] = second.astype(jnp.bfloat16)
+    ff_ref[...] = ff.astype(jnp.bfloat16)
+
+
 def swiglu_kernel(
     fsdp,
     group,
     n_ref,
     g_ref,
-    both_ref,
-    down_ref,
+    w_ref,
+    second_ref,
+    ff_first_ref,
     hidden_ref,
     grads_ref,
     ff_ref,
@@ -692,7 +847,6 @@
     own_sem,
 ):
     half = n_ref.shape[0]
-    units = hidden_ref.shape[1]
     step = pl.program_id(0)
     me_f = lax.axis_index("fsdp")
     me_c = lax.axis_index("ctx")
@@ -752,19 +906,9 @@
             device_id_type=MESH_ID,
         )
 
-    lin = mul(n_ref[...], both_ref[...])
-    gate, up = lin[:, :units], lin[:, units:]
-    sig = jax.nn.sigmoid(gate)
-    act = gate * sig
-    hidden = (act * up).astype(jnp.bfloat16)
-    hidden_ref[...] = hidden
-    hidden_grad = mul(g_ref[...], down_ref[...])
-    grads_ref[:, :units] = (hidden_grad * up * sig * (1.0 + gate * (1.0 - sig))).astype(
-        jnp.bfloat16
-    )
-    grads_ref[:, units:] = (hidden_grad * act).astype(jnp.bfloat16)
-    second = mul(grads_ref[...], both_ref[...], NT)
-    ff = mul(hidden, down_ref[...], NT)
+    second, ff = swiglu_parts(n_ref, g_ref, w_ref, hidden_ref, grads_ref)
+    second = second + second_ref[...].astype(jnp.float32)
+    ff = ff + ff_first_ref[...].astype(jnp.float32)
 
     for k in reversed(range(group)):
         slot = k % 2
@@ -820,10 +964,10 @@
                         copy.wait_send()
 
 
-def swiglu(fsdp, group, normed, grads, both, down):
+def swiglu(fsdp, group, normed, grads, weights, second, ff):
     many, width = normed.shape
     half = many // (2 * group)
-    units = down.shape[1]
+    units = weights.shape[1] // 3
     low = jnp.bfloat16
     last = 2 * group - 1
     sems = pltpu.SemaphoreType.DMA
@@ -838,7 +982,7 @@
     return pl.pallas_call(
         partial(swiglu_kernel, fsdp, group),
         grid=(2 * group,),
-        in_specs=[rows(width), rows(width), whole(both), whole(down)],
+        in_specs=[rows(width), rows(width), whole(weights), rows(width), rows(width)],
         out_specs=[
             rows(units),
             rows(2 * units),
@@ -866,7 +1010,7 @@
         cost_estimate=pl.CostEstimate(
             flops=12 * many * width * units, bytes_accessed=50 << 20, transcendentals=0
         ),
-    )(normed, grads, both, down)
+    )(normed, grads, weights, second, ff)
 
 
 def spread_kernel(fsdp, ctx, group, count, chain, *refs):
@@ -1074,8 +1218,7 @@
     )
 
 
-def sum_kernel(fsdp, ctx, group, count, chain, *refs):
-    weights = count - 1 if chain else count
+def sum_kernel(fsdp, ctx, count, chain, *refs):
     ins = refs[:count]
     if chain:
         parts_ref, cos_ref, sin_ref = refs[count : count + 3]
@@ -1085,8 +1228,8 @@
     outs = refs[count : 2 * count]
     held = refs[2 * count : 3 * count]
     got = refs[3 * count : 4 * count]
-    line = refs[4 * count : 4 * count + weights]
-    refs = refs[4 * count + weights :]
+    line = refs[4 * count : 5 * count]
+    refs = refs[5 * count :]
     in_sem, f_send, f_recv, z_send, z_recv = refs[:5]
     if chain:
         kv_parts, kv_got, kv_sem, c_send, c_recv = refs[5:]
@@ -1095,13 +1238,6 @@
     me_t = lax.axis_index("tp")
     bits = [1 << i for i in range(fsdp.bit_length() - 1)]
     order = fsdp_order(fsdp)
-    near = fsdp_order(group)
-
-    def steps_of(i):
-        return order if i < weights else near
-
-    def shards_of(i):
-        return shards if i < weights else [0]
 
     def peer(k):
         return (flip_index(me_f, k, fsdp), me_c, me_t)
@@ -1118,8 +1254,8 @@
         kv_load = pltpu.make_async_copy(parts_ref, kv_parts, kv_sem.at[0])
         kv_load.start()
     for i in range(count):
-        for k in reversed([0] + steps_of(i)):
-            block = ins[i].at[:, flip_index(me_f, k, fsdp)] if i < weights else ins[i].at[k]
+        for k in reversed([0] + order):
+            block = ins[i].at[:, flip_index(me_f, k, fsdp)]
             loads[i, k] = pltpu.make_async_copy(block, held[i].at[k], in_sem.at[i, k])
             loads[i, k].start()
 
@@ -1166,7 +1302,7 @@
         lax.fori_loop(0, into.shape[0] // tile, body, 0)
 
     def collect(i, shard, k):
-        for far in steps_of(i):
+        for far in order:
             for part, b in ways(far):
                 if far ^ b == k:
                     f_copy(i, shard, far, part, b).wait_recv()
@@ -1269,8 +1405,7 @@
         kv_load.wait()
         next_step()
     shards = sorted(range(ctx), key=lambda c: -abs(2 * c - ctx + 1))
-    work = [[(i, shard) for i in range(weights)] for shard in shards]
-    work += [[(i, 0)] for i in range(weights, count)]
+    work = [[(i, shard) for i in range(count)] for shard in shards]
     levels = sorted({bin(k).count("1") for k in order}, reverse=True)
     waited = set()
 
@@ -1284,10 +1419,8 @@
             if stage == len(levels):
                 loaded(i, 0)
                 collect(i, shard, 0)
-                if i >= weights:
-                    give(i, shard)
                 continue
-            for k in steps_of(i):
+            for k in order:
                 if bin(k).count("1") == levels[stage]:
                     loaded(i, k)
                     collect(i, shard, k)
@@ -1296,8 +1429,6 @@
 
     def line_tick(item, hops):
         for i, shard in item:
-            if i >= weights:
-                continue
             for step, there in ((1, hops), (-1, ctx - 1 - hops)):
                 if step * (shard - there) >= 0:
 
@@ -1324,10 +1455,10 @@
     while steps:
         next_step()
     for i, shard in [pair for item in work for pair in item]:
-        for k in steps_of(i):
+        for k in order:
             for part, b in ways(k):
                 f_copy(i, shard, k, part, b).wait_send()
-        for step in (1, -1) if i < weights else ():
+        for step in (1, -1):
 
             @pl.when(step * (shard - me_c) > 0)
             def _():
@@ -1342,7 +1473,7 @@
                     copy.wait_send()
 
 
-def sum_weights(fsdp, ctx, group, arrays, chain=()):
+def sum_weights(fsdp, ctx, arrays, chain=()):
     sems = pltpu.SemaphoreType.DMA
     vmem = pltpu.VMEM
     shards = [v.reshape(ctx, fsdp, -1, v.shape[-1]) for v in arrays]
@@ -1351,10 +1482,7 @@
     lines = [vmem((2,) + b[1:], v.dtype) for b, v in zip(blocks, shards)]
     extra = []
     if chain:
-        rows, parts, cosines, sines = chain
-        shards.append(rows[:, None])
-        blocks.append(shards[-1].shape)
-        out_shape.append(jax.ShapeDtypeStruct(rows.shape[1:], rows.dtype))
+        parts = chain[0]
         out_shape.append(jax.ShapeDtypeStruct((parts.shape[2], 2 * parts.shape[3]), parts.dtype))
         extra = [
             vmem(parts.shape, parts.dtype),
@@ -1366,10 +1494,10 @@
     count = len(shards)
     held = [vmem(b, v.dtype) for b, v in zip(blocks, shards)]
     return pl.pallas_call(
-        partial(sum_kernel, fsdp, ctx, group, count, bool(chain)),
+        partial(sum_kernel, fsdp, ctx, count, bool(chain)),
         out_shape=out_shape,
-        in_specs=[pl.BlockSpec(memory_space=pl.ANY)] * (count + len(chain[1:2]))
-        + [pl.BlockSpec(memory_space=pltpu.VMEM)] * len(chain[2:]),
+        in_specs=[pl.BlockSpec(memory_space=pl.ANY)] * (count + len(chain[:1]))
+        + [pl.BlockSpec(memory_space=pltpu.VMEM)] * len(chain[1:]),
         out_specs=[pl.BlockSpec(memory_space=pltpu.VMEM)] * len(out_shape),
         scratch_shapes=held
         + held
@@ -1387,7 +1515,35 @@
             has_side_effects=True,
             vmem_limit_bytes=52 * 1024 * 1024,
         ),
-    )(*shards, *chain[1:])
+    )(*shards, *chain)
+
+
+def place_kernel(group, count, *refs):
+    parts, outs = refs[:count], refs[count:]
+    span = sum(v.shape[3] for v in parts)
+    for i, out in enumerate(outs):
+        for f in range(group):
+            start = f * span
+            for v in parts:
+                width = v.shape[3]
+                out[:, start : start + width] = v[f, i].astype(out.dtype)
+                start += width
+
+
+def place_units(parts):
+    group, arrays, rows, _ = parts[0].shape
+    cols = group * sum(v.shape[3] for v in parts)
+    vmem = pl.BlockSpec(memory_space=pltpu.VMEM)
+    return pl.pallas_call(
+        partial(place_kernel, group, len(parts)),
+        out_shape=[jax.ShapeDtypeStruct((rows, cols), jnp.float32)] * arrays,
+        in_specs=[vmem] * len(parts),
+        out_specs=[vmem] * arrays,
+        compiler_params=pltpu.CompilerParams(vmem_limit_bytes=24 * 1024 * 1024),
+        cost_estimate=pl.CostEstimate(
+            flops=0, bytes_accessed=6 * rows * cols * arrays, transcendentals=0
+        ),
+    )(*parts)
 
 
 def local(
@@ -1417,7 +1573,9 @@
     group_size = query_width // kv_width
     group = min(fsdp, 4)
     far = fsdp // group
-    units = w_gate.shape[1] // group
+    own = w_gate.shape[1] // group
+    first_units = own * FIRST_EIGHTHS // 8
+    widths = (first_units, own - first_units)
     me_c = lax.axis_index("ctx")
     me_t = lax.axis_index("tp")
     low = jnp.bfloat16
@@ -1452,12 +1610,6 @@
         rows = v.shape[0]
         return (
             v.reshape(rows, pairs, group_size, 2, HD).swapaxes(2, 3).reshape(rows, query_width)
-        )
-
-    def both_halves(own):
-        other = swap(own)
-        return jnp.where(
-            me_t == 0, jnp.concatenate([own, other]), jnp.concatenate([other, own])
         )
 
     x = by_ctx(inputs.reshape(tokens, model_width))
@@ -1476,7 +1628,8 @@
             gains,
             pair_heads(w_out),
         ],
-        [[w_gate, w_up], [w_down]],
+        [w_gate, w_up, w_down],
+        widths,
     )
     far_groups = [[h * group + g for h in range(far)] for g in range(group)]
     near_groups = [[h * group + g for g in range(group)] for h in range(far)]
@@ -1486,8 +1639,10 @@
             v = lax.all_gather(v, "fsdp", axis=0, tiled=False, axis_index_groups=far_groups)
         return lax.all_gather(v, "ctx", axis=0, tiled=False).reshape(model_width, -1)
 
-    both_full, down_full = [whole_width(v) for v in held]
+    first_full = whole_width(held[0])
     qkv_full, gain_rows = spread_weights(fsdp, ctx, group, lined[:2])
+    late_held, gain_rows = lax.optimization_barrier((held[1], gain_rows))
+    late_full = whole_width(late_held)
     gain_rows = gain_rows.reshape(ctx * fsdp, 16, shard)
     gain_one = gain_rows[:, 0].reshape(1, model_width)
     gain_two = gain_rows[:, 1].reshape(1, model_width)
@@ -1530,21 +1685,17 @@
     )
     normed_all = gather_tokens(group, fsdp, second_normed)
 
-    hidden, both_grad, ff_sums, second_grad = swiglu(
-        fsdp, group, normed_all, ff_grad_all, both_full, down_full
-    )
-    second_grad = second_grad.reshape(tokens, model_width)
-
     def unit_term(left, right):
         return jnp.einsum("td,tf->df", left, right, preferred_element_type=wide).astype(low)
 
     def own_units(term):
+        width = term.shape[1]
         own = lax.psum_scatter(
-            term.reshape(ctx, fsdp, shard, units), "ctx", scatter_dimension=0, tiled=False
+            term.reshape(ctx, fsdp, shard, width), "ctx", scatter_dimension=0, tiled=False
         )
         if far > 1:
             own = lax.psum_scatter(
-                own.reshape(far, group, shard, units),
+                own.reshape(far, group, shard, width),
                 "fsdp",
                 scatter_dimension=0,
                 tiled=False,
@@ -1552,19 +1703,43 @@
             )
         return own
 
-    def return_units(own):
-        return lax.all_to_all(
-            own.reshape(group * shard, units),
+    def return_units(both, down):
+        units = down.shape[-1]
+        pieces = jnp.concatenate([both[..., :units], both[..., units:], down], 1)
+        back = lax.all_to_all(
+            pieces.reshape(group * 3 * shard, units),
             "fsdp",
             0,
-            1,
+            0,
             tiled=True,
             axis_index_groups=near_groups if far > 1 else None,
-        ).astype(wide)
-
-    down_term = unit_term(ff_grad_all, hidden)
-    second_grad, down_after = lax.optimization_barrier((second_grad, down_term))
-    w_down_grad = return_units(own_units(down_term))
+        )
+        return back.reshape(group, 3, shard, units)
+
+    many = group * tokens
+    first_hidden, first_grads, second_part, ff_part = by_rows(
+        swiglu_first_kernel,
+        256,
+        [(normed_all, "rows"), (ff_grad_all, "rows"), (first_full, "whole")],
+        [
+            ((many, first_units), low),
+            ((many, 2 * first_units), low),
+            ((many, model_width), low),
+            ((many, model_width), low),
+        ],
+        flops=12 * many * model_width * first_units,
+        limit=56,
+    )
+    first_both = unit_term(normed_all, first_grads)
+    first_down = unit_term(ff_grad_all, first_hidden)
+    first_own = (own_units(first_both), own_units(first_down))
+    second_part, ff_part, _, _ = lax.optimization_barrier(
+        (second_part, ff_part, first_both, first_down)
+    )
+    hidden, both_grad, ff_sums, second_grad = swiglu(
+        fsdp, group, normed_all, ff_grad_all, late_full, second_part, ff_part
+    )
+    second_grad = second_grad.reshape(tokens, model_width)
 
     middle_grad, attn_grad, gain_two_term = by_rows(
         partial(middle_back_kernel, dims, local_rows),
@@ -1579,29 +1754,37 @@
         [((tokens, model_width), wide), ((tokens, model_width), low), ((1, model_width), wide)],
     )
     attended_grad = jnp.dot(attn_grad, out_full, preferred_element_type=wide).astype(low)
-    query_grad, kv_parts = attend_back(
-        lengths, query, attended_grad, lse, cosines, sines, kv_all
-    )
-    query_grad, normed_all, both_grad = lax.optimization_barrier(
-        (query_grad, normed_all, both_grad)
-    )
-    gate_term = unit_term(normed_all, both_grad[:, :units])
-    w_gate_grad = return_units(own_units(gate_term))
-    ff_sums = ff_sums.reshape(group, half, model_width)
+    query_grad, kv_parts, ff_branch = attend_back(
+        fsdp,
+        group,
+        lengths,
+        query,
+        attended_grad,
+        lse,
+        cosines,
+        sines,
+        kv_all,
+        ff_sums.reshape(group, half, model_width),
+    )
+    query_grad, normed_all, ff_grad_all, both_grad, hidden = lax.optimization_barrier(
+        (query_grad, normed_all, ff_grad_all, both_grad, hidden)
+    )
+    late_down = unit_term(ff_grad_all, hidden)
+    late_down_own = own_units(late_down)
     out_term = jnp.einsum("td,tj->dj", attn_grad, attended, preferred_element_type=wide)
-    kv_parts, gate_after = lax.optimization_barrier((kv_parts, gate_term))
-    w_out_grad, ff_own, kv_grad = sum_weights(
-        fsdp, ctx, group, [out_term.astype(low)], (ff_sums, kv_parts, cosines, sines)
+    kv_parts, _ = lax.optimization_barrier((kv_parts, late_down))
+    w_out_grad, kv_grad = sum_weights(
+        fsdp, ctx, [out_term.astype(low)], (kv_parts, cosines, sines)
     )
     (output,) = by_rows(
         partial(output_kernel, back_dims, local_rows),
         128,
-        [(lengths, "smem"), (middle, "rows"), (both_halves(ff_own), "rows")],
+        [(lengths, "smem"), (middle, "rows"), (ff_branch.reshape(tokens, model_width), "rows")],
         [((tokens, model_width), low)],
     )
     kv_grad, normed_all, both_grad = lax.optimization_barrier((kv_grad, normed_all, both_grad))
-    up_term = unit_term(normed_all, both_grad[:, units:])
-    up_own = own_units(up_term)
+    late_both = unit_term(normed_all, both_grad)
+    late_both_own = own_units(late_both)
     qkv_grad = jnp.concatenate([query_grad, kv_grad], -1)
     qkv_term = jnp.einsum("td,tj->dj", first_normed, qkv_grad, preferred_element_type=wide)
     first_part = jnp.einsum(
@@ -1623,12 +1806,16 @@
         [gain_one_term.reshape(-1, shard), gain_two_term.reshape(-1, shard)], 1
     )
     gain_terms = jnp.pad(gain_terms, ((0, 0), (0, 14), (0, 0))).reshape(-1, shard)
-    qkv_term, w_down_grad, w_gate_grad, up_after = lax.optimization_barrier(
-        (qkv_term.astype(low), w_down_grad, w_gate_grad, up_term)
-    )
-    qkv_own, gain_own = sum_weights(fsdp, ctx, group, [qkv_term, gain_terms])
-    up_own, qkv_own = lax.optimization_barrier((up_own, qkv_own))
-    w_up_grad = return_units(up_own)
+    first_back = return_units(*first_own)
+    qkv_term, first_back, _ = lax.optimization_barrier(
+        (qkv_term.astype(low), first_back, late_both)
+    )
+    qkv_own, gain_own = sum_weights(fsdp, ctx, [qkv_term, gain_terms])
+    late_both_own, late_down_own, qkv_own = lax.optimization_barrier(
+        (late_both_own, late_down_own, qkv_own)
+    )
+    late_back = return_units(late_both_own, late_down_own)
+    w_gate_grad, w_up_grad, w_down_grad = place_units([first_back, late_back])
     return (
         by_fsdp(output).reshape(inputs.shape),
         by_fsdp(input_grad).reshape(inputs.shape),

time: 780 us -> 757 us (0.971)
  local copies, waits for them, and re-layouts: 34.2 us -> 54.7 us
  waiting for transfers between devices: 31 us -> 10.7 us
  Pallas kernels: 602 us -> 585 us
    pallas_call x6 -> x7, Pallas kernels: 22.5 us -> 56.4 us  [by_rows(): pl.pallas_call(kernel, grid=(total // rows,), in_specs=in_specs, out_spec...]
    pallas_call x3 -> x4, Pallas kernels: 244 us -> 217 us  [the longest x2 169 us: sum_weights(): pl.pallas_call(partial(sum_kernel, fsdp, ctx, count, bool(chain)), out_sh...]
    pallas_call x1, Pallas kernels: 80.6 us -> 64.6 us  [swiglu(): pl.pallas_call(partial(swiglu_kernel, fsdp, group), grid=(2 * group,), in...]
    unnamed x79 -> x101, local copies, waits for them, and re-layouts: 25.9 us -> 37.1 us
    all_gather x2, waiting for transfers between devices: 10.8 us -> 0.02 us  [whole_width(): lax.all_gather(v, 'ctx', axis=0, tiled=False).reshape(model_width, -1)]
    all_to_all x3 -> x2, waiting for transfers between devices: 15.2 us -> 6.35 us  [return_units(): lax.all_to_all(pieces.reshape(group * 3 * shard, units), 'fsdp', 0, 0, ti...]
    pallas_call x2, Pallas kernels: 152 us -> 143 us  [spread_weights(): pl.pallas_call(partial(spread_kernel, fsdp, ctx, group, count, len(chain)...]
    dot_general x3 -> x4, matrix products: 41.3 us -> 45.9 us  [unit_term(): jnp.einsum('td,tf->df', left, right, preferred_element_type=wide)]
  transfers between devices with their start and end apart: 11 -> 10, of which waited for: 4 -> 2; matrix products, arithmetic and copies ran while one was open for 9% -> 13% of each run, Pallas kernels for 62% -> 71%
where the time goes in v5:
time: 757 us; the launch traced here: 751 us
  Pallas kernels  585 us (77%)
  matrix products  72.9 us (10%)
  local copies, waits for them, and re-layouts  54.7 us (7%)
  between operations  15.2 us (2%)
  waiting for transfers between devices  10.7 us (1%)
  starting transfers between devices  8.98 us (1%)
    pallas_call x2, Pallas kernels, sum_weights(): pl.pallas_call(partial(sum_kernel, fsdp, ctx, count, bool(chain)), out_sh...  169 us
    pallas_call x2, Pallas kernels, spread_weights(): pl.pallas_call(partial(spread_kernel, fsdp, ctx, group, count, len(chain)...  143 us
    pallas_call x1, Pallas kernels, swiglu(): pl.pallas_call(partial(swiglu_kernel, fsdp, group), grid=(2 * group,), in...  64.6 us
    pallas_call x7, Pallas kernels, by_rows(): pl.pallas_call(kernel, grid=(total // rows,), in_specs=in_specs, out_spec...  56.4 us
    pallas_call x1, Pallas kernels, start_exchange(): pl.pallas_call(partial(line_kernel, fsdp, ctx, group, len(lines), len(swa...  46 us
    dot_general x4, matrix products, unit_term(): jnp.einsum('td,tf->df', left, right, preferred_element_type=wide)  45.9 us
    pallas_call x1, Pallas kernels, attend_back(): pl.pallas_call(partial(attend_back_kernel, ctx, fsdp, group), grid=(seqs,...  44.7 us
    pallas_call x1, Pallas kernels, gather_tokens(): pl.pallas_call(partial(tokens_kernel, group, fsdp), out_shape=token_shape...  40.7 us
  transfers between devices with their start and end apart: 10, of which 2 were waited for; matrix products, arithmetic and copies ran while one was open for 13% of the time, Pallas kernels for 71%

profile of v5, /device:TPU:16, one launch (start us, length us, event | category | flops | bytes accessed | tf_op | source)
XLA Modules:
  0.0 751.1 jit_solution(10295357686419067076)
XLA Ops:
  11.4 46.0 %shard_map.203 = (bf16[4,128,1536]{2,1,0:T(8,128)(2,1)S(1)}, f32[4,16,128]{2,1,0:T(8,128)S(1)}, bf16[4,128,1024]{2,1,0:T(8,128)(2,1)S(1)}, bf16[4,128,1536]{2,1,0:T(8,128)(2,1)}, bf16[4,128,1536]{2,1,0:T(8,128)(2,1)S(1)}) custom-call(bf16[128,1536]{1,0:T(8,128)(2,1)S(1)} %pad_maximum_fusion.2.refs_0_, f32[16,128]{1,0:T(8,128)S(1)} %fusion.3.refs_1_, ...), custom_call_target="tpu_custom_call" | custom-call | tf_op jit(solution)/shard_map/pallas_call | solution.py:644
  61.2 56.7 %shard_map.204 = (bf16[4,4,128,1536]{3,2,1,0:T(8,128)(2,1)S(1)}, f32[4,4,16,128]{3,2,1,0:T(8,128)S(1)}) custom-call(bf16[4,128,1536]{2,1,0:T(8,128)(2,1)S(1)} %copy-done.14, f32[4,16,128]{2,1,0:T(8,128)S(1)} %get-tuple-element.70.refs_1_), custom_call_target="tpu_custom_call" | custom-call | tf_op jit(solution)/shard_map/pallas_call | solution.py:1190
  127.9 5.0 shard_map.205
  134.3 86.4 %shard_map.207 = (bf16[4,4,128,1024]{3,2,1,0:T(8,128)(2,1)S(1)}, bf16[4,512,512]{2,1,0:T(8,128)(2,1)S(1)}, bf16[4,2,256,2048]{3,2,1,0:T(8,128)(2,1)S(1)}) custom-call(bf16[4,128,1024]{2,1,0:T(8,128)(2,1)S(1)} %get-tuple-element.76.refs_0_, bf16[512,512]{1,0:T(8,128)(2,1)S(1)} %get-tuple-element.77.refs_1_, bf16[512,2048]{1,0:T(8,128)(2,1)S(1)} %shard_map.206.refs_2_), custom_call_target="tpu_custom_call" | custom-call | tf_op jit(solution)/shard_map/pallas_call | solution.py:1190
  224.0 17.4 %shard_map.208 = (bf16[512,1024]{1,0:T(8,128)(2,1)S(1)}, f32[512,256]{1,0:T(8,128)S(1)}) custom-call(s32[2]{0:T(128)S(1)} %copy-done.22, bf16[512,1024]{1,0:T(8,128)(2,1)S(1)} %get-tuple-element.75.q_ref, bf16[4,512,512]{2,1,0:T(8,128)(2,1)S(1)} %get-tuple-element.78.refs_0_.refs_1_.refs_2_.refs_3_.refs_4_.refs_5_.refs_6_.refs_7_, ...), custom_call_target="tpu_custom_call" | custom-call | flops 8589934592 | bytes 6291456 | tf_op jit(solution)/shard_map/pallas_call | solution.py:424
  244.7 4.1 collective-permute-done.other_ref
  252.8 40.7 %shard_map.210 = bf16[4,2,256,2048]{3,2,1,0:T(8,128)(2,1)S(1)} custom-call(bf16[512,2048]{1,0:T(8,128)(2,1)S(1)} %get-tuple-element.82.v_ref), custom_call_target="tpu_custom_call" | custom-call | tf_op jit(solution)/shard_map/pallas_call | solution.py:788
  296.9 33.7 %shard_map.211 = (bf16[2048,512]{1,0:T(8,128)(2,1)}, bf16[2048,1024]{1,0:T(8,128)(2,1)}, bf16[2048,2048]{1,0:T(8,128)(2,1)}, bf16[2048,2048]{1,0:T(8,128)(2,1)}) custom-call(bf16[2048,2048]{1,0:T(8,128)(2,1)} %bitcast.80, bf16[2048,2048]{1,0:T(8,128)(2,1)} %bitcast.97, bf16[2048,1536]{1,0:T(8,128)(2,1)} %bitcast.131), custom_call_target="tpu_custom_call" | custom-call | flops 25769803776 | bytes 46137344 | tf_op jit(solution)/shard_map/pallas_call | solution.py:399
  330.6 14.2 %convolution_convert_fusion.3 = bf16[2048,1024]{1,0:T(8,128)(2,1)} fusion(bf16[2048,2048]{1,0:T(8,128)(2,1)} %bitcast.81, bf16[2048,1024]{1,0:T(8,128)(2,1)} %get-tuple-element.88), kind=kOutput, calls=%fused_computation.3 | convolution fusion | flops 8592031744 | bytes 16777216 | tf_op jit(solution)/shard_map/td,tf->df/dot_general | solution.py:1689
  344.8 9.9 %convolution_convert_fusion.7 = bf16[2048,512]{1,0:T(8,128)(2,1)} fusion(bf16[2048,2048]{1,0:T(8,128)(2,1)} %bitcast.98, bf16[2048,512]{1,0:T(8,128)(2,1)} %get-tuple-element.89), kind=kOutput, calls=%fused_computation.7 | convolution fusion | flops 4296015872 | bytes 12582912 | tf_op jit(solution)/shard_map/td,tf->df/dot_general | solution.py:1689
  354.8 64.6 %shard_map.212 = (bf16[2048,512]{1,0:T(8,128)(2,1)}, bf16[2048,1024]{1,0:T(8,128)(2,1)}, bf16[1024,2048]{1,0:T(8,128)(2,1)}, bf16[2,256,2048]{2,1,0:T(8,128)(2,1)}) custom-call(bf16[2048,2048]{1,0:T(8,128)(2,1)} %bitcast.82, bf16[2048,2048]{1,0:T(8,128)(2,1)} %bitcast.99, bf16[2048,1536]{1,0:T(8,128)(2,1)} %bitcast.130, ...), custom_call_target="tpu_custom_call" | custom-call | flops 25769803776 | bytes 52428800 | tf_op jit(solution)/shard_map/pallas_call | solution.py:982
  421.0 5.9 shard_map.213
  431.2 44.7 %shard_map.214 = (bf16[512,1024]{1,0:T(8,128)(2,1)S(1)}, bf16[4,2,512,256]{3,2,1,0:T(8,128)(2,1)S(1)}, bf16[2,256,2048]{2,1,0:T(8,128)(2,1)S(1)}) custom-call(s32[2]{0:T(128)S(1)} %copy-done.22, bf16[512,1024]{1,0:T(8,128)(2,1)S(1)} %copy-done.34, bf16[512,1024]{1,0:T(8,128)(2,1)S(1)} %convolution_convert_fusion.8.do_ref, f32[512,256]{1,0:T(8,128)S(1)} %copy-done.38, ...), custom_call_target="tpu_custom_call" | custom-call | flops 21474836480 | bytes 10485760 | tf_op jit(solution)/shard_map/pallas_call | solution.py:455
  476.0 8.8 %convolution_convert_fusion.6 = bf16[2048,512]{1,0:T(8,128)(2,1)} fusion(bf16[2048,2048]{1,0:T(8,128)(2,1)S(1)} %bitcast.102, bf16[2048,512]{1,0:T(8,128)(2,1)} %get-tuple-element.103), kind=kOutput, calls=%fused_computation.6 | convolution fusion | flops 4296015872 | bytes 12582912 | tf_op jit(solution)/shard_map/td,tf->df/dot_general | solution.py:1689
  486.0 5.9 convolution_convert_fusion.1
  492.0 94.1 %shard_map.216 = (f32[128,1024]{1,0:T(8,128)S(1)}, bf16[512,512]{1,0:T(8,128)(2,1)S(1)}) custom-call(bf16[4,4,128,1024]{3,2,1,0:T(8,128)(2,1)} %bitcast.110, bf16[4,2,512,256]{3,2,1,0:T(8,128)(2,1)} %copy-done.8, f32[256,128]{1,0:T(8,128)S(1)} %copy.55.cos_ref.refs_2_, f32[256,128]{1,0:T(8,128)S(1)} %copy.56.sin_ref.refs_3_), custom_call_target="tpu_custom_call" | custom-call | tf_op jit(solution)/shard_map/pallas_call | solution.py:1496
  586.1 13.0 %convolution_convert_fusion.2 = bf16[2048,1024]{1,0:T(8,128)(2,1)} fusion(bf16[2048,2048]{1,0:T(8,128)(2,1)} %bitcast.83, bf16[2048,1024]{1,0:T(8,128)(2,1)S(1)} %copy-done.45), kind=kOutput, calls=%fused_computation.2 | convolution fusion | flops 8592031744 | bytes 16777216 | tf_op jit(solution)/shard_map/td,tf->df/dot_general | solution.py:1689
  599.3 8.1 %convolution_convert_fusion.5.part_ref = bf16[512,2048]{1,0:T(8,128)(2,1)} fusion(bf16[512,1536]{1,0:T(8,128)(2,1)S(1)} %constant_dynamic-update-slice_fusion, bf16[2048,1536]{1,0:T(8,128)(2,1)} %bitcast.103), kind=kOutput, calls=%fused_computation.5 | convolution fusion | flops 3222274048 | bytes 9961472 | tf_op jit(solution)/shard_map/tj,dj->td/dot_general | solution.py:1790
  611.0 4.3 all-to-all-start
  615.4 8.3 %convolution_convert_fusion = bf16[2048,1536]{1,0:T(8,128)(2,1)} fusion(bf16[512,2048]{1,0:T(8,128)(2,1)} %copy-done.32, bf16[512,1536]{1,0:T(8,128)(2,1)} %copy-done.39), kind=kOutput, calls=%fused_computation | convolution fusion | flops 3224371200 | bytes 9961472 | tf_op jit(solution)/shard_map/td,tj->dj/dot_general | solution.py:1789
  623.7 6.0 shard_map.217
  629.7 6.3 all-to-all-done
  636.0 74.9 %shard_map.218 = (f32[128,1536]{1,0:T(8,128)S(1)}, f32[16,128]{1,0:T(8,128)S(1)}) custom-call(bf16[4,4,128,1536]{3,2,1,0:T(8,128)(2,1)} %bitcast.107, f32[4,4,16,128]{3,2,1,0:T(8,128)S(1)} %bitcast.93), custom_call_target="tpu_custom_call" | custom-call | tf_op jit(solution)/shard_map/pallas_call | solution.py:1496
  714.4 4.1 all-to-all-start.1
  (158 shorter events, 72.8 us)
Async XLA Ops:
  7.2 289.7 %all-gather.7.cloned.1.call-start = ((), (), s32[]{:S(2)}) async-start(), calls=%async_computation.11 | async-start | bytes 7864320 | tf_op jit(solution)/shard_map/all_gather | solution.py:1640
  59.7 295.1 %all-gather.5.cloned.1.call-start = ((), (), s32[]{:S(2)}) async-start(), calls=%async_computation.10 | async-start | bytes 7864320 | tf_op jit(solution)/shard_map/all_gather | solution.py:1640
  61.2 61.8 %copy-start.3 = (bf16[2,256,2048]{2,1,0:T(8,128)(2,1)S(1)}, bf16[2,256,2048]{2,1,0:T(8,128)(2,1)}, u32[]{:S(2)}) copy-start(bf16[2,256,2048]{2,1,0:T(8,128)(2,1)} %param.14) | copy-start | bytes 6291460
  61.2 61.8 %copy-start.22 = (s32[2]{0:T(128)S(1)}, s32[2]{0:T(128)}, u32[]{:S(2)}) copy-start(s32[2]{0:T(128)} %len_ref.9) | copy-start | bytes 28
  120.5 486.8 %reduce-scatter.5.cloned.1.call-start = ((), (), s32[]{:S(2)}) async-start(), calls=%async_computation.6 | async-start | bytes 5242880 | tf_op jit(solution)/shard_map/reduce_scatter | solution.py:1693
  134.3 107.1 %copy-start.33 = (bf16[512,1024]{1,0:T(8,128)(2,1)}, bf16[512,1024]{1,0:T(8,128)(2,1)S(1)}, u32[]{:S(2)}) copy-start(bf16[512,1024]{1,0:T(8,128)(2,1)S(1)} %get-tuple-element.75.q_ref) | copy-start | bytes 3145732
  224.0 17.4 %copy-start.29 = (bf16[4,512,512]{2,1,0:T(8,128)(2,1)}, bf16[4,512,512]{2,1,0:T(8,128)(2,1)S(1)}, u32[]{:S(2)}) copy-start(bf16[4,512,512]{2,1,0:T(8,128)(2,1)S(1)} %get-tuple-element.78.refs_0_.refs_1_.refs_2_.refs_3_.refs_4_.refs_5_.refs_6_.refs_7_) | copy-start | bytes 6291460
  224.0 18.2 %copy-start.27 = (bf16[4,4,128,1024]{3,2,1,0:T(8,128)(2,1)}, bf16[4,4,128,1024]{3,2,1,0:T(8,128)(2,1)S(1)}, u32[]{:S(2)}) copy-start(bf16[4,4,128,1024]{3,2,1,0:T(8,128)(2,1)S(1)} %get-tuple-element.80) | copy-start | bytes 12582916
  244.6 4.2 collective-permute-start
  344.8 263.9 %reduce-scatter.7.cloned.1.call-start = ((), (), s32[]{:S(2)}) async-start(), calls=%async_computation.7 | async-start | bytes 2621440 | tf_op jit(solution)/shard_map/reduce_scatter | solution.py:1693
  354.7 357.1 %reduce-scatter.11.cloned.1.call-start = ((), (), s32[]{:S(2)}) async-start(), calls=%async_computation.9 | async-start | bytes 2621440 | tf_op jit(solution)/shard_map/reduce_scatter | solution.py:1693
  426.9 49.1 %slice-start = ((s8[8388608]{0:T(1024)(128)(4,1)}), s8[4194304]{0:T(1024)(128)(4,1)S(1)}, s32[]{:S(2)}) async-start(s8[8388608]{0:T(1024)(128)(4,1)} %bitcast.100), calls=%async_computation.12 | async-start | bytes 8388608
  431.2 44.8 %slice-start.1 = ((s8[8388608]{0:T(1024)(128)(4,1)}), s8[4194304]{0:T(1024)(128)(4,1)S(1)}, s32[]{:S(2)}) async-start(s8[8388608]{0:T(1024)(128)(4,1)} %bitcast.100), calls=%async_computation.13 | async-start | bytes 8388608
  475.9 8.9 %copy-start.8 = (bf16[4,2,512,256]{3,2,1,0:T(8,128)(2,1)}, bf16[4,2,512,256]{3,2,1,0:T(8,128)(2,1)S(1)}, u32[]{:S(2)}) copy-start(bf16[4,2,512,256]{3,2,1,0:T(8,128)(2,1)S(1)} %get-tuple-element.104.refs_1_) | copy-start | bytes 6291460
  476.0 8.8 %copy-start.10 = (bf16[2,256,2048]{2,1,0:T(8,128)(2,1)}, bf16[2,256,2048]{2,1,0:T(8,128)(2,1)S(1)}, u32[]{:S(2)}) copy-start(bf16[2,256,2048]{2,1,0:T(8,128)(2,1)S(1)} %get-tuple-element.96) | copy-start | bytes 6291460
  484.8 227.0 %reduce-scatter.9.cloned.1.call-start = ((), (), s32[]{:S(2)}) async-start(), calls=%async_computation.8 | async-start | bytes 5242880 | tf_op jit(solution)/shard_map/reduce_scatter | solution.py:1693
  492.0 94.1 %copy-start.45 = (bf16[2048,1024]{1,0:T(8,128)(2,1)S(1)}, bf16[2048,1024]{1,0:T(8,128)(2,1)}, u32[]{:S(2)}) copy-start(bf16[2048,1024]{1,0:T(8,128)(2,1)} %get-tuple-element.113) | copy-start | bytes 12582916
  586.1 13.0 %copy-start.19 = (f32[128,1024]{1,0:T(8,128)}, f32[128,1024]{1,0:T(8,128)S(1)}, u32[]{:S(2)}) copy-start(f32[128,1024]{1,0:T(8,128)S(1)} %get-tuple-element.120) | copy-start | bytes 1572868
  607.3 16.3 %collective-permute-start.1 = (bf16[512,2048]{1,0:T(8,128)(2,1)}, bf16[512,2048]{1,0:T(8,128)(2,1)}, u32[]{:S(2)}, u32[]{:S(2)}) collective-permute-start(bf16[512,2048]{1,0:T(8,128)(2,1)} %convolution_convert_fusion.5.part_ref), channel_id=1, source_target_pairs={{0,1},{1,0},{2,3},{3,2},{4,5},{5,4},{6,7},{7,6},{8,9},{9,8},{10,11... | collective-permute-start | bytes 6291464 | tf_op jit(solution)/shard_map/ppermute | solution.py:1585
  611.0 25.0 %all-to-all-start = ((bf16[4,384,512]{2,1,0:T(8,128)(2,1)}), bf16[4,384,512]{2,1,0:T(8,128)(2,1)S(1)}, u32[]{:S(2)}, u32[]{:S(2)}) async-start(bf16[4,384,512]{2,1,0:T(8,128)(2,1)} %pad_maximum_fusion), calls=%async_computation.2 | async-start | bytes 3145728 | tf_op jit(solution)/shard_map/all_to_all | solution.py:1709
  615.4 8.3 %copy-start.5 = (bf16[2,256,2048]{2,1,0:T(8,128)(2,1)S(1)}, bf16[2,256,2048]{2,1,0:T(8,128)(2,1)}, u32[]{:S(2)}) copy-start(bf16[2,256,2048]{2,1,0:T(8,128)(2,1)} %param.12) | copy-start | bytes 6291460
  615.4 8.3 %copy-start.7 = (f32[512,2048]{1,0:T(8,128)S(1)}, f32[512,2048]{1,0:T(8,128)}, u32[]{:S(2)}) copy-start(f32[512,2048]{1,0:T(8,128)} %copy-done.6) | copy-start | bytes 12582916
  615.4 8.3 %copy-start.21 = (f32[1,2048]{1,0:T(1,128)S(1)}, f32[1,2048]{1,0:T(1,128)}, u32[]{:S(2)}) copy-start(f32[1,2048]{1,0:T(1,128)} %copy-done.20) | copy-start | bytes 24580
  714.4 26.6 %all-to-all-start.1 = ((bf16[4,384,512]{2,1,0:T(8,128)(2,1)}), bf16[4,384,512]{2,1,0:T(8,128)(2,1)S(1)}, u32[]{:S(2)}, u32[]{:S(2)}) async-start(bf16[4,384,512]{2,1,0:T(8,128)(2,1)} %pad_maximum_fusion.1), calls=%async_computation.5 | async-start | bytes 3145728 | tf_op jit(solution)/shard_map/all_to_all | solution.py:1709
  (34 other events, 91.4 us)
Sparse Core Ops, SparseCore 0:
  59.8 123.7 all-gather.6
  185.8 124.3 all-gather.4
  344.9 76.7 reduce-scatter.4
  424.6 43.1 reduce-scatter.6
  485.0 71.8 reduce-scatter.10
  599.2 86.7 reduce-scatter.8

commit v6 on v5

--- a/solution.py
+++ b/solution.py
@@ -1218,7 +1218,16 @@
     )
 
 
-def sum_kernel(fsdp, ctx, count, chain, *refs):
+def sum_kernel(fsdp, ctx, count, chain, products, *refs):
+    inner = []
+    if products:
+        first = count + 3
+        pairs = refs[first : first + 2 * products]
+        place = first + 2 * products + count + 1
+        results = refs[place : place + products]
+        inner = refs[-2 * products - 1 :]
+        refs = refs[:first] + refs[first + 2 * products : place] + refs[place + products :]
+        refs = refs[: -2 * products - 1]
     ins = refs[:count]
     if chain:
         parts_ref, cos_ref, sin_ref = refs[count : count + 3]
@@ -1253,6 +1262,9 @@
     if chain:
         kv_load = pltpu.make_async_copy(parts_ref, kv_parts, kv_sem.at[0])
         kv_load.start()
+    inner_loads = [
+        pltpu.make_async_copy(pairs[i], inner[i], inner[-1].at[i]) for i in range(2 * products)
+    ]
     for i in range(count):
         for k in reversed([0] + order):
             block = ins[i].at[:, flip_index(me_f, k, fsdp)]
@@ -1401,9 +1413,29 @@
             if s == 0:
                 chain_result()
 
+    turns = 4
+
+    def make_products(turn):
+        if turn == 0:
+            for load in inner_loads:
+                load.wait()
+        for i in range(products):
+            left, right, result = inner[2 * i], inner[2 * i + 1], results[i]
+            tiles = left.shape[1] // 256
+            per = -(-tiles // turns)
+
+            def body(t, _):
+                cols = pl.ds(pl.multiple_of(t * 256, 256), 256)
+                result[cols, :] = mul(left[:, cols], right[...], TN).astype(result.dtype)
+                return 0
+
+            lax.fori_loop(min(turn * per, tiles), min((turn + 1) * per, tiles), body, 0)
+
     if chain:
         kv_load.wait()
         next_step()
+    for load in inner_loads:
+        load.start()
     shards = sorted(range(ctx), key=lambda c: -abs(2 * c - ctx + 1))
     work = [[(i, shard) for i in range(count)] for shard in shards]
     levels = sorted({bin(k).count("1") for k in order}, reverse=True)
@@ -1451,6 +1483,8 @@
             place = tick - stages + 1 - hops
             if 0 <= place < len(work):
                 line_tick(work[place], hops)
+        if products and tick < turns:
+            make_products(tick)
         next_step()
     while steps:
         next_step()
@@ -1473,7 +1507,7 @@
                     copy.wait_send()
 
 
-def sum_weights(fsdp, ctx, arrays, chain=()):
+def sum_weights(fsdp, ctx, arrays, chain=(), products=()):
     sems = pltpu.SemaphoreType.DMA
     vmem = pltpu.VMEM
     shards = [v.reshape(ctx, fsdp, -1, v.shape[-1]) for v in arrays]
@@ -1492,12 +1526,18 @@
             sems((ctx, 4)),
         ]
     count = len(shards)
+    flat = [v for pair in products for v in pair]
+    for left, right in products:
+        out_shape.append(jax.ShapeDtypeStruct((left.shape[1], right.shape[1]), left.dtype))
+    if products:
+        extra = extra + [vmem(v.shape, v.dtype) for v in flat] + [sems((len(flat),))]
     held = [vmem(b, v.dtype) for b, v in zip(blocks, shards)]
     return pl.pallas_call(
-        partial(sum_kernel, fsdp, ctx, count, bool(chain)),
+        partial(sum_kernel, fsdp, ctx, count, bool(chain), len(products)),
         out_shape=out_shape,
         in_specs=[pl.BlockSpec(memory_space=pl.ANY)] * (count + len(chain[:1]))
-        + [pl.BlockSpec(memory_space=pltpu.VMEM)] * len(chain[1:]),
+        + [pl.BlockSpec(memory_space=pltpu.VMEM)] * len(chain[1:])
+        + [pl.BlockSpec(memory_space=pl.ANY)] * len(flat),
         out_specs=[pl.BlockSpec(memory_space=pltpu.VMEM)] * len(out_shape),
         scratch_shapes=held
         + held
@@ -1513,9 +1553,43 @@
         compiler_params=pltpu.CompilerParams(
             collective_id=4 if chain else 2,
             has_side_effects=True,
-            vmem_limit_bytes=52 * 1024 * 1024,
+            vmem_limit_bytes=58 * 1024 * 1024,
         ),
-    )(*shards, *chain)
+    )(*shards, *chain, *flat)
+
+
+def heads_kernel(group_size, qkv_ref, out_ref, *outs):
+    width = outs[0].shape[1]
+    for source, target in ((qkv_ref, outs[0]), (out_ref, outs[3])):
+        for block in range(width // 128):
+            pair, rest = divmod(2 * block, 2 * group_size)
+            g, j = divmod(rest, group_size)
+            start = (pair * group_size + j) * 128
+            left = source[:, start : start + 128]
+            right = source[:, start + 128 : start + 256]
+            if g:
+                left = pltpu.roll(left, HD, 1)
+            else:
+                right = pltpu.roll(right, HD, 1)
+            lane = lax.broadcasted_iota(jnp.int32, left.shape, 1)
+            target[:, block * 128 : (block + 1) * 128] = jnp.where(lane < HD, left, right)
+    kv_width = outs[1].shape[1]
+    outs[1][...] = qkv_ref[:, width : width + kv_width]
+    outs[2][...] = qkv_ref[:, width + kv_width :]
+
+
+def plain_grads(group_size, qkv, out, kv_width):
+    rows, width = out.shape
+    vmem = pl.BlockSpec(memory_space=pltpu.VMEM)
+    return pl.pallas_call(
+        partial(heads_kernel, group_size),
+        out_shape=[
+            jax.ShapeDtypeStruct((rows, w), out.dtype) for w in (width, kv_width, kv_width, width)
+        ],
+        in_specs=[vmem] * 2,
+        out_specs=[vmem] * 4,
+        cost_estimate=pl.CostEstimate(flops=0, bytes_accessed=4 << 20, transcendentals=0),
+    )(qkv, out)
 
 
 def place_kernel(group, count, *refs):
@@ -1606,12 +1680,6 @@
             v.reshape(rows, pairs, 2, group_size, HD).swapaxes(2, 3).reshape(rows, query_width)
         )
 
-    def plain_heads(v):
-        rows = v.shape[0]
-        return (
-            v.reshape(rows, pairs, group_size, 2, HD).swapaxes(2, 3).reshape(rows, query_width)
-        )
-
     x = by_ctx(inputs.reshape(tokens, model_width))
     cot = by_ctx(cotangent.reshape(tokens, model_width))
     positions = me_c * local_rows + jnp.arange(local_rows, dtype=jnp.int32)
@@ -1766,25 +1834,22 @@
         kv_all,
         ff_sums.reshape(group, half, model_width),
     )
-    query_grad, normed_all, ff_grad_all, both_grad, hidden = lax.optimization_barrier(
-        (query_grad, normed_all, ff_grad_all, both_grad, hidden)
-    )
-    late_down = unit_term(ff_grad_all, hidden)
+    out_term = jnp.einsum("td,tj->dj", attn_grad, attended, preferred_element_type=wide)
+    w_out_grad, kv_grad, late_both, late_down = sum_weights(
+        fsdp,
+        ctx,
+        [out_term.astype(low)],
+        (kv_parts, cosines, sines),
+        ((normed_all, both_grad), (ff_grad_all, hidden)),
+    )
+    late_both_own = own_units(late_both)
     late_down_own = own_units(late_down)
-    out_term = jnp.einsum("td,tj->dj", attn_grad, attended, preferred_element_type=wide)
-    kv_parts, _ = lax.optimization_barrier((kv_parts, late_down))
-    w_out_grad, kv_grad = sum_weights(
-        fsdp, ctx, [out_term.astype(low)], (kv_parts, cosines, sines)
-    )
     (output,) = by_rows(
         partial(output_kernel, back_dims, local_rows),
         128,
         [(lengths, "smem"), (middle, "rows"), (ff_branch.reshape(tokens, model_width), "rows")],
         [((tokens, model_width), low)],
     )
-    kv_grad, normed_all, both_grad = lax.optimization_barrier((kv_grad, normed_all, both_grad))
-    late_both = unit_term(normed_all, both_grad)
-    late_both_own = own_units(late_both)
     qkv_grad = jnp.concatenate([query_grad, kv_grad], -1)
     qkv_term = jnp.einsum("td,tj->dj", first_normed, qkv_grad, preferred_element_type=wide)
     first_part = jnp.einsum(
@@ -1811,6 +1876,9 @@
         (qkv_term.astype(low), first_back, late_both)
     )
     qkv_own, gain_own = sum_weights(fsdp, ctx, [qkv_term, gain_terms])
+    w_query_grad, w_key_grad, w_value_grad, w_out_grad = plain_grads(
+        group_size, qkv_own, w_out_grad, kv_width
+    )
     late_both_own, late_down_own, qkv_own = lax.optimization_barrier(
         (late_both_own, late_down_own, qkv_own)
     )
@@ -1820,10 +1888,10 @@
         by_fsdp(output).reshape(inputs.shape),
         by_fsdp(input_grad).reshape(inputs.shape),
         gain_own[0],
-        plain_heads(qkv_own[:, :query_width]),
-        qkv_own[:, query_width : query_width + kv_width],
-        qkv_own[:, query_width + kv_width :],
-        plain_heads(w_out_grad),
+        w_query_grad,
+        w_key_grad,
+        w_value_grad,
+        w_out_grad,
         gain_own[1],
         w_gate_grad,
         w_up_grad,

time: 757 us -> 742 us (0.980)
  matrix products: 72.9 us -> 49.5 us
  local copies, waits for them, and re-layouts: 54.7 us -> 39.2 us
  waiting for transfers between devices: 10.7 us -> 23.9 us
  Pallas kernels: 585 us -> 597 us
    dot_general x4 -> x2, matrix products: 45.9 us -> 24 us  [unit_term(): jnp.einsum('td,tf->df', left, right, preferred_element_type=wide)]
    pallas_call x2 -> x3, Pallas kernels: 169 us -> 182 us  [the longest x2 179 us: sum_weights(): pl.pallas_call(partial(sum_kernel, fsdp, ctx, count, bool(chain), len(pro...]
    all_to_all x2, waiting for transfers between devices: 6.35 us -> 14.4 us  [return_units(): lax.all_to_all(pieces.reshape(group * 3 * shard, units), 'fsdp', 0, 0, ti...]
    unnamed x101 -> x93, local copies, waits for them, and re-layouts: 37.1 us -> 32.3 us
  transfers between devices with their start and end apart: 10 -> 10, of which waited for: 2 -> 4; matrix products, arithmetic and copies ran while one was open for 13% -> 8% of each run, Pallas kernels for 71% -> 74%
where the time goes in v6:
time: 742 us; the launch traced here: 737 us
  Pallas kernels  597 us (80%)
  matrix products  49.5 us (7%)
  local copies, waits for them, and re-layouts  39.2 us (5%)
  waiting for transfers between devices  23.9 us (3%)
  between operations  15.1 us (2%)
  starting transfers between devices  7.79 us (1%)
    pallas_call x2, Pallas kernels, sum_weights(): pl.pallas_call(partial(sum_kernel, fsdp, ctx, count, bool(chain), len(pro...  179 us
    pallas_call x2, Pallas kernels, spread_weights(): pl.pallas_call(partial(spread_kernel, fsdp, ctx, group, count, len(chain)...  143 us
    pallas_call x1, Pallas kernels, swiglu(): pl.pallas_call(partial(swiglu_kernel, fsdp, group), grid=(2 * group,), in...  64.6 us
    pallas_call x7, Pallas kernels, by_rows(): pl.pallas_call(kernel, grid=(total // rows,), in_specs=in_specs, out_spec...  56.4 us
    pallas_call x1, Pallas kernels, start_exchange(): pl.pallas_call(partial(line_kernel, fsdp, ctx, group, len(lines), len(swa...  46 us
    pallas_call x1, Pallas kernels, attend_back(): pl.pallas_call(partial(attend_back_kernel, ctx, fsdp, group), grid=(seqs,...  44.1 us
    pallas_call x1, Pallas kernels, gather_tokens(): pl.pallas_call(partial(tokens_kernel, group, fsdp), out_shape=token_shape...  40.7 us
    unnamed x93, local copies, waits for them, and re-layouts  32.3 us
  transfers between devices with their start and end apart: 10, of which 4 were waited for; matrix products, arithmetic and copies ran while one was open for 8% of the time, Pallas kernels for 74%

profile of v6, /device:TPU:16, one launch (start us, length us, event | category | flops | bytes accessed | tf_op | source)
XLA Modules:
  0.0 737.2 jit_solution(262455046354427727)
XLA Ops:
  11.4 46.0 %shard_map.203 = (bf16[4,128,1536]{2,1,0:T(8,128)(2,1)S(1)}, f32[4,16,128]{2,1,0:T(8,128)S(1)}, bf16[4,128,1024]{2,1,0:T(8,128)(2,1)S(1)}, bf16[4,128,1536]{2,1,0:T(8,128)(2,1)}, bf16[4,128,1536]{2,1,0:T(8,128)(2,1)S(1)}) custom-call(bf16[128,1536]{1,0:T(8,128)(2,1)S(1)} %pad_maximum_fusion.2.refs_0_, f32[16,128]{1,0:T(8,128)S(1)} %fusion.3.refs_1_, ...), custom_call_target="tpu_custom_call" | custom-call | tf_op jit(solution)/shard_map/pallas_call | solution.py:644
  61.2 56.7 %shard_map.204 = (bf16[4,4,128,1536]{3,2,1,0:T(8,128)(2,1)S(1)}, f32[4,4,16,128]{3,2,1,0:T(8,128)S(1)}) custom-call(bf16[4,128,1536]{2,1,0:T(8,128)(2,1)S(1)} %copy-done.15, f32[4,16,128]{2,1,0:T(8,128)S(1)} %get-tuple-element.66.refs_1_), custom_call_target="tpu_custom_call" | custom-call | tf_op jit(solution)/shard_map/pallas_call | solution.py:1190
  128.0 5.0 shard_map.205
  134.3 86.4 %shard_map.207 = (bf16[4,4,128,1024]{3,2,1,0:T(8,128)(2,1)S(1)}, bf16[4,512,512]{2,1,0:T(8,128)(2,1)S(1)}, bf16[4,2,256,2048]{3,2,1,0:T(8,128)(2,1)S(1)}) custom-call(bf16[4,128,1024]{2,1,0:T(8,128)(2,1)S(1)} %get-tuple-element.72.refs_0_, bf16[512,512]{1,0:T(8,128)(2,1)S(1)} %get-tuple-element.73.refs_1_, bf16[512,2048]{1,0:T(8,128)(2,1)S(1)} %shard_map.206.refs_2_), custom_call_target="tpu_custom_call" | custom-call | tf_op jit(solution)/shard_map/pallas_call | solution.py:1190
  224.1 17.4 %shard_map.208 = (bf16[512,1024]{1,0:T(8,128)(2,1)S(1)}, f32[512,256]{1,0:T(8,128)S(1)}) custom-call(s32[2]{0:T(128)S(1)} %copy-done.23, bf16[512,1024]{1,0:T(8,128)(2,1)S(1)} %get-tuple-element.71.q_ref, bf16[4,512,512]{2,1,0:T(8,128)(2,1)S(1)} %get-tuple-element.74.refs_0_.refs_1_.refs_2_.refs_3_.refs_4_.refs_5_.refs_6_.refs_7_, ...), custom_call_target="tpu_custom_call" | custom-call | flops 8589934592 | bytes 6291456 | tf_op jit(solution)/shard_map/pallas_call | solution.py:424
  244.0 4.1 collective-permute-done.other_ref
  252.1 40.7 %shard_map.210 = bf16[4,2,256,2048]{3,2,1,0:T(8,128)(2,1)S(1)} custom-call(bf16[512,2048]{1,0:T(8,128)(2,1)S(1)} %get-tuple-element.78.v_ref), custom_call_target="tpu_custom_call" | custom-call | tf_op jit(solution)/shard_map/pallas_call | solution.py:788
  296.1 33.7 %shard_map.211 = (bf16[2048,512]{1,0:T(8,128)(2,1)}, bf16[2048,1024]{1,0:T(8,128)(2,1)}, bf16[2048,2048]{1,0:T(8,128)(2,1)}, bf16[2048,2048]{1,0:T(8,128)(2,1)}) custom-call(bf16[2048,2048]{1,0:T(8,128)(2,1)} %bitcast.68, bf16[2048,2048]{1,0:T(8,128)(2,1)} %bitcast.72, bf16[2048,1536]{1,0:T(8,128)(2,1)} %bitcast.113), custom_call_target="tpu_custom_call" | custom-call | flops 25769803776 | bytes 46137344 | tf_op jit(solution)/shard_map/pallas_call | solution.py:399
  329.8 14.2 %convolution_convert_fusion.2 = bf16[2048,1024]{1,0:T(8,128)(2,1)} fusion(bf16[2048,2048]{1,0:T(8,128)(2,1)} %bitcast.69, bf16[2048,1024]{1,0:T(8,128)(2,1)} %get-tuple-element.84), kind=kOutput, calls=%fused_computation.2 | convolution fusion | flops 8592031744 | bytes 16777216 | tf_op jit(solution)/shard_map/td,tf->df/dot_general | solution.py:1757
  344.0 9.9 %convolution_convert_fusion.5 = bf16[2048,512]{1,0:T(8,128)(2,1)} fusion(bf16[2048,2048]{1,0:T(8,128)(2,1)} %bitcast.73, bf16[2048,512]{1,0:T(8,128)(2,1)} %get-tuple-element.85), kind=kOutput, calls=%fused_computation.5 | convolution fusion | flops 4296015872 | bytes 12582912 | tf_op jit(solution)/shard_map/td,tf->df/dot_general | solution.py:1757
  354.0 64.6 %shard_map.212 = (bf16[2048,512]{1,0:T(8,128)(2,1)}, bf16[2048,1024]{1,0:T(8,128)(2,1)}, bf16[1024,2048]{1,0:T(8,128)(2,1)}, bf16[2,256,2048]{2,1,0:T(8,128)(2,1)}) custom-call(bf16[2048,2048]{1,0:T(8,128)(2,1)} %bitcast.70, bf16[2048,2048]{1,0:T(8,128)(2,1)} %bitcast.74, bf16[2048,1536]{1,0:T(8,128)(2,1)} %bitcast.112, ...), custom_call_target="tpu_custom_call" | custom-call | flops 25769803776 | bytes 52428800 | tf_op jit(solution)/shard_map/pallas_call | solution.py:982
  420.2 5.8 shard_map.213
  426.0 4.4 convolution_convert_fusion.1
  433.1 44.1 %shard_map.214 = (bf16[512,1024]{1,0:T(8,128)(2,1)S(1)}, bf16[4,2,512,256]{3,2,1,0:T(8,128)(2,1)S(1)}, bf16[2,256,2048]{2,1,0:T(8,128)(2,1)S(1)}) custom-call(s32[2]{0:T(128)S(1)} %copy-done.23, bf16[512,1024]{1,0:T(8,128)(2,1)S(1)} %copy-done.33, bf16[512,1024]{1,0:T(8,128)(2,1)S(1)} %convolution_convert_fusion.6.do_ref, f32[512,256]{1,0:T(8,128)S(1)} %copy-done.37, ...), custom_call_target="tpu_custom_call" | custom-call | flops 21474836480 | bytes 10485760 | tf_op jit(solution)/shard_map/pallas_call | solution.py:455
  479.8 74.2 %shard_map.216 = (f32[128,1024]{1,0:T(8,128)}, bf16[512,512]{1,0:T(8,128)(2,1)}, bf16[2048,1024]{1,0:T(8,128)(2,1)}, bf16[2048,512]{1,0:T(8,128)(2,1)}) custom-call(bf16[4,4,128,1024]{3,2,1,0:T(8,128)(2,1)} %bitcast.93, bf16[4,2,512,256]{3,2,1,0:T(8,128)(2,1)} %copy-done.9, f32[256,128]{1,0:T(8,128)} %copy-done.19, f32[256,128]{1,0:T(8,128)} %copy-done.20, ...), custom_call_target="tpu_custom_call" | custom-call | tf_op jit(solution)/shard_map/pallas_call | solution.py:1535
  555.7 8.1 %convolution_convert_fusion.4.part_ref = bf16[512,2048]{1,0:T(8,128)(2,1)} fusion(bf16[512,1536]{1,0:T(8,128)(2,1)S(1)} %constant_dynamic-update-slice_fusion, bf16[2048,1536]{1,0:T(8,128)(2,1)} %bitcast.88), kind=kOutput, calls=%fused_computation.4 | convolution fusion | flops 3222274048 | bytes 9961472 | tf_op jit(solution)/shard_map/tj,dj->td/dot_general | solution.py:1855
  567.5 3.8 all-to-all-start
  571.3 8.3 %convolution_convert_fusion = bf16[2048,1536]{1,0:T(8,128)(2,1)} fusion(bf16[512,2048]{1,0:T(8,128)(2,1)} %copy-done.31, bf16[512,1536]{1,0:T(8,128)(2,1)} %copy-done.38), kind=kOutput, calls=%fused_computation | convolution fusion | flops 3224371200 | bytes 9961472 | tf_op jit(solution)/shard_map/td,tj->dj/dot_general | solution.py:1854
  579.7 6.0 shard_map.217
  586.3 5.2 all-to-all-done
  591.5 105.2 %shard_map.218 = (f32[128,1536]{1,0:T(8,128)}, f32[16,128]{1,0:T(8,128)}) custom-call(bf16[4,4,128,1536]{3,2,1,0:T(8,128)(2,1)} %bitcast.92, f32[4,4,16,128]{3,2,1,0:T(8,128)} %bitcast.105), custom_call_target="tpu_custom_call" | custom-call | tf_op jit(solution)/shard_map/pallas_call | solution.py:1535
  696.7 4.7 reduce-scatter.9.cloned.1.call-done
  703.9 3.7 all-to-all-start.1
  717.8 9.3 %all-to-all-done.1 = bf16[4,384,512]{2,1,0:T(8,128)(2,1)S(1)} async-done(((bf16[4,384,512]{2,1,0:T(8,128)(2,1)}), bf16[4,384,512]{2,1,0:T(8,128)(2,1)S(1)}, u32[]{:S(2)}, u32[]{:S(2)}) %all-to-all-start.1) | async-done | bytes 1572896 | tf_op jit(solution)/shard_map/all_to_all | solution.py:1777
  (142 shorter events, 60.8 us)
Async XLA Ops:
  7.2 288.9 %all-gather.7.cloned.1.call-start = ((), (), s32[]{:S(2)}) async-start(), calls=%async_computation.11 | async-start | bytes 7864320 | tf_op jit(solution)/shard_map/all_gather | solution.py:1708
  59.7 294.3 %all-gather.5.cloned.1.call-start = ((), (), s32[]{:S(2)}) async-start(), calls=%async_computation.10 | async-start | bytes 7864320 | tf_op jit(solution)/shard_map/all_gather | solution.py:1708
  61.2 61.8 %copy-start.4 = (bf16[2,256,2048]{2,1,0:T(8,128)(2,1)S(1)}, bf16[2,256,2048]{2,1,0:T(8,128)(2,1)}, u32[]{:S(2)}) copy-start(bf16[2,256,2048]{2,1,0:T(8,128)(2,1)} %param.14) | copy-start | bytes 6291460
  61.2 61.8 %copy-start.23 = (s32[2]{0:T(128)S(1)}, s32[2]{0:T(128)}, u32[]{:S(2)}) copy-start(s32[2]{0:T(128)} %len_ref.9) | copy-start | bytes 28
  120.5 443.3 %reduce-scatter.5.cloned.1.call-start = ((), (), s32[]{:S(2)}) async-start(), calls=%async_computation.6 | async-start | bytes 5242880 | tf_op jit(solution)/shard_map/reduce_scatter | solution.py:1761
  121.2 311.8 %copy-start.19 = (f32[256,128]{1,0:T(8,128)}, f32[256,128]{1,0:T(8,128)S(1)}, u32[]{:S(2)}) copy-start(f32[256,128]{1,0:T(8,128)S(1)} %copy.47.cos_ref.refs_2_) | copy-start | bytes 393220
  122.9 310.1 %copy-start.20 = (f32[256,128]{1,0:T(8,128)}, f32[256,128]{1,0:T(8,128)S(1)}, u32[]{:S(2)}) copy-start(f32[256,128]{1,0:T(8,128)S(1)} %copy.48.sin_ref.refs_3_) | copy-start | bytes 393220
  125.1 7.9 %copy-start.21 = (f32[1,2048]{1,0:T(1,128)}, f32[1,2048]{1,0:T(1,128)S(1)}, u32[]{:S(2)}) copy-start(f32[1,2048]{1,0:T(1,128)S(1)} %get-tuple-element.124.gain_ref) | copy-start | bytes 24580
  134.3 107.1 %copy-start.32 = (bf16[512,1024]{1,0:T(8,128)(2,1)}, bf16[512,1024]{1,0:T(8,128)(2,1)S(1)}, u32[]{:S(2)}) copy-start(bf16[512,1024]{1,0:T(8,128)(2,1)S(1)} %get-tuple-element.71.q_ref) | copy-start | bytes 3145732
  224.1 17.4 %copy-start.29 = (bf16[4,512,512]{2,1,0:T(8,128)(2,1)}, bf16[4,512,512]{2,1,0:T(8,128)(2,1)S(1)}, u32[]{:S(2)}) copy-start(bf16[4,512,512]{2,1,0:T(8,128)(2,1)S(1)} %get-tuple-element.74.refs_0_.refs_1_.refs_2_.refs_3_.refs_4_.refs_5_.refs_6_.refs_7_) | copy-start | bytes 6291460
  224.1 17.4 %copy-start.27 = (bf16[4,4,128,1024]{3,2,1,0:T(8,128)(2,1)}, bf16[4,4,128,1024]{3,2,1,0:T(8,128)(2,1)S(1)}, u32[]{:S(2)}) copy-start(bf16[4,4,128,1024]{3,2,1,0:T(8,128)(2,1)S(1)} %get-tuple-element.76) | copy-start | bytes 12582916
  243.9 4.2 collective-permute-start
  344.0 221.2 %reduce-scatter.7.cloned.1.call-start = ((), (), s32[]{:S(2)}) async-start(), calls=%async_computation.7 | async-start | bytes 2621440 | tf_op jit(solution)/shard_map/reduce_scatter | solution.py:1761
  353.9 342.8 %reduce-scatter.11.cloned.1.call-start = ((), (), s32[]{:S(2)}) async-start(), calls=%async_computation.9 | async-start | bytes 2621440 | tf_op jit(solution)/shard_map/reduce_scatter | solution.py:1761
  420.2 5.8 copy-start.35
  554.0 147.3 %reduce-scatter.9.cloned.1.call-start = ((), (), s32[]{:S(2)}) async-start(), calls=%async_computation.8 | async-start | bytes 5242880 | tf_op jit(solution)/shard_map/reduce_scatter | solution.py:1761
  555.7 8.1 %copy-start.38 = (bf16[512,1536]{1,0:T(8,128)(2,1)}, bf16[512,1536]{1,0:T(8,128)(2,1)S(1)}, u32[]{:S(2)}) copy-start(bf16[512,1536]{1,0:T(8,128)(2,1)S(1)} %constant_dynamic-update-slice_fusion) | copy-start | bytes 4718596
  563.8 15.8 %collective-permute-start.1 = (bf16[512,2048]{1,0:T(8,128)(2,1)}, bf16[512,2048]{1,0:T(8,128)(2,1)}, u32[]{:S(2)}, u32[]{:S(2)}) collective-permute-start(bf16[512,2048]{1,0:T(8,128)(2,1)} %convolution_convert_fusion.4.part_ref), channel_id=1, source_target_pairs={{0,1},{1,0},{2,3},{3,2},{4,5},{5,4},{6,7},{7,6},{8,9},{9,8},{10,11... | collective-permute-start | bytes 6291464 | tf_op jit(solution)/shard_map/ppermute | solution.py:1659
  567.5 24.0 %all-to-all-start = ((bf16[4,384,512]{2,1,0:T(8,128)(2,1)}), bf16[4,384,512]{2,1,0:T(8,128)(2,1)S(1)}, u32[]{:S(2)}, u32[]{:S(2)}) async-start(bf16[4,384,512]{2,1,0:T(8,128)(2,1)} %pad_maximum_fusion), calls=%async_computation.2 | async-start | bytes 3145728 | tf_op jit(solution)/shard_map/all_to_all | solution.py:1777
  571.3 8.3 %copy-start.6 = (bf16[2,256,2048]{2,1,0:T(8,128)(2,1)S(1)}, bf16[2,256,2048]{2,1,0:T(8,128)(2,1)}, u32[]{:S(2)}) copy-start(bf16[2,256,2048]{2,1,0:T(8,128)(2,1)} %param.12) | copy-start | bytes 6291460
  571.3 8.3 %copy-start.8 = (f32[512,2048]{1,0:T(8,128)S(1)}, f32[512,2048]{1,0:T(8,128)}, u32[]{:S(2)}) copy-start(f32[512,2048]{1,0:T(8,128)} %copy-done.7) | copy-start | bytes 12582916
  571.3 8.3 %copy-start.22 = (f32[1,2048]{1,0:T(1,128)S(1)}, f32[1,2048]{1,0:T(1,128)}, u32[]{:S(2)}) copy-start(f32[1,2048]{1,0:T(1,128)} %copy-done.21) | copy-start | bytes 24580
  696.7 6.0 copy-start.40
  703.9 23.1 %all-to-all-start.1 = ((bf16[4,384,512]{2,1,0:T(8,128)(2,1)}), bf16[4,384,512]{2,1,0:T(8,128)(2,1)S(1)}, u32[]{:S(2)}, u32[]{:S(2)}) async-start(bf16[4,384,512]{2,1,0:T(8,128)(2,1)} %pad_maximum_fusion.1), calls=%async_computation.5 | async-start | bytes 3145728 | tf_op jit(solution)/shard_map/all_to_all | solution.py:1777
  (31 other events, 70.5 us)
Sparse Core Ops, SparseCore 0:
  59.8 123.7 all-gather.6
  185.8 124.2 all-gather.4
  344.1 76.7 reduce-scatter.4
  423.7 43.1 reduce-scatter.6
  554.2 42.2 reduce-scatter.10
  598.7 102.6 reduce-scatter.8

commit v7 on v6

--- a/solution.py
+++ b/solution.py
@@ -830,10 +830,13 @@
     w_ref,
     second_ref,
     ff_first_ref,
+    left_ref,
+    right_ref,
     hidden_ref,
     grads_ref,
     ff_ref,
     own_ref,
+    product_ref,
     s_out,
     f_out,
     s_in,
@@ -845,6 +848,10 @@
     f_send,
     f_recv,
     own_sem,
+    left,
+    right,
+    product,
+    inner_sem,
 ):
     half = n_ref.shape[0]
     step = pl.program_id(0)
@@ -865,6 +872,28 @@
             pl.semaphore_signal(barrier, inc=1, device_id=peer(b), device_id_type=MESH_ID)
         pl.semaphore_signal(barrier, inc=1, device_id=core, device_id_type=MESH_ID)
         pl.semaphore_wait(barrier, len(bits) + 1)
+
+    inner = [
+        pltpu.make_async_copy(left_ref, left, inner_sem.at[0]),
+        pltpu.make_async_copy(right_ref, right, inner_sem.at[1]),
+    ]
+
+    @pl.when(step == 1)
+    def _():
+        for copy in inner:
+            copy.start()
+
+    def make_product():
+        for copy in inner:
+            copy.wait()
+
+        def body(t, _):
+            cols = pl.ds(pl.multiple_of(t * 256, 256), 256)
+            product[cols, :] = mul(left[:, cols], right[...], TN).astype(product.dtype)
+            return 0
+
+        lax.fori_loop(0, left.shape[1] // 256, body, 0)
+        pltpu.make_async_copy(product, product_ref, inner_sem.at[2]).start()
 
     def core_copies(k):
         slot = k % 2
@@ -929,6 +958,8 @@
                 copy.wait_recv()
             ff_ref[...] = (ff + f_in[slot].astype(jnp.float32)).astype(jnp.bfloat16)
             total[k] = (second + s_in[slot].astype(jnp.float32)).astype(jnp.bfloat16)
+            if k == 0:
+                make_product()
             for far in order:
                 for part, b in ways(far):
                     if far ^ b == k:
@@ -962,9 +993,10 @@
                 for late in range(min(2, group)):
                     for copy in core_copies(late):
                         copy.wait_send()
-
-
-def swiglu(fsdp, group, normed, grads, weights, second, ff):
+                pltpu.make_async_copy(product, product_ref, inner_sem.at[2]).wait()
+
+
+def swiglu(fsdp, group, normed, grads, weights, second, ff, hidden):
     many, width = normed.shape
     half = many // (2 * group)
     units = weights.shape[1] // 3
@@ -982,11 +1014,13 @@
     return pl.pallas_call(
         partial(swiglu_kernel, fsdp, group),
         grid=(2 * group,),
-        in_specs=[rows(width), rows(width), whole(weights), rows(width), rows(width)],
+        in_specs=[rows(width), rows(width), whole(weights), rows(width), rows(width)]
+        + [pl.BlockSpec(memory_space=pl.ANY)] * 2,
         out_specs=[
             rows(units),
             rows(2 * units),
             pl.BlockSpec(block, lambda i: (group - 1 - i // 2, 0)),
+            pl.BlockSpec(memory_space=pl.ANY),
             pl.BlockSpec(memory_space=pl.ANY),
         ],
         out_shape=[
@@ -994,6 +1028,7 @@
             jax.ShapeDtypeStruct((many, 2 * units), low),
             jax.ShapeDtypeStruct((group * half, width), low),
             jax.ShapeDtypeStruct((2,) + block, low),
+            jax.ShapeDtypeStruct((width, hidden.shape[1]), low),
         ],
         scratch_shapes=[pltpu.VMEM((2,) + block, low)] * 4
         + [pltpu.VMEM((group,) + block, low)] * 2
@@ -1003,6 +1038,10 @@
             sems((group, 2)),
             sems((group, 2)),
             sems((3,)),
+            pltpu.VMEM(grads.shape, low),
+            pltpu.VMEM(hidden.shape, low),
+            pltpu.VMEM((width, hidden.shape[1]), low),
+            sems((3,)),
         ],
         compiler_params=pltpu.CompilerParams(
             collective_id=6, has_side_effects=True, vmem_limit_bytes=58 * 1024 * 1024
@@ -1010,7 +1049,7 @@
         cost_estimate=pl.CostEstimate(
             flops=12 * many * width * units, bytes_accessed=50 << 20, transcendentals=0
         ),
-    )(normed, grads, weights, second, ff)
+    )(normed, grads, weights, second, ff, grads, hidden)
 
 
 def spread_kernel(fsdp, ctx, group, count, chain, *refs):
@@ -1709,8 +1748,6 @@
 
     first_full = whole_width(held[0])
     qkv_full, gain_rows = spread_weights(fsdp, ctx, group, lined[:2])
-    late_held, gain_rows = lax.optimization_barrier((held[1], gain_rows))
-    late_full = whole_width(late_held)
     gain_rows = gain_rows.reshape(ctx * fsdp, 16, shard)
     gain_one = gain_rows[:, 0].reshape(1, model_width)
     gain_two = gain_rows[:, 1].reshape(1, model_width)
@@ -1741,6 +1778,8 @@
     out_full, kv_all, ff_grad_all = spread_weights(
         fsdp, ctx, group, lined[2:], (kv_own, ff_grad)
     )
+    late_held, kv_all = lax.optimization_barrier((held[1], kv_all))
+    late_full = whole_width(late_held)
     attended, lse = attend(lengths, query, kv_all)
     attn_part = jnp.einsum(
         "tj,dj->td", attended, out_full, preferred_element_type=wide
@@ -1799,14 +1838,18 @@
         limit=56,
     )
     first_both = unit_term(normed_all, first_grads)
-    first_down = unit_term(ff_grad_all, first_hidden)
+    second_part, ff_part, _ = lax.optimization_barrier((second_part, ff_part, first_both))
+    hidden, both_grad, ff_sums, second_grad, first_down = swiglu(
+        fsdp,
+        group,
+        normed_all,
+        ff_grad_all,
+        late_full,
+        second_part,
+        ff_part,
+        first_hidden,
+    )
     first_own = (own_units(first_both), own_units(first_down))
-    second_part, ff_part, _, _ = lax.optimization_barrier(
-        (second_part, ff_part, first_both, first_down)
-    )
-    hidden, both_grad, ff_sums, second_grad = swiglu(
-        fsdp, group, normed_all, ff_grad_all, late_full, second_part, ff_part
-    )
     second_grad = second_grad.reshape(tokens, model_width)
 
     middle_grad, attn_grad, gain_two_term = by_rows(

time: 742 us -> 739 us (level)
  matrix products: 49.5 us -> 39.8 us
    dot_general x2 -> x1, matrix products: 24 us -> 14.4 us  [unit_term(): jnp.einsum('td,tf->df', left, right, preferred_element_type=wide)]
    unnamed x93 -> x95, local copies, waits for them, and re-layouts: 32.3 us -> 31.3 us
  transfers between devices with their start and end apart: 10 -> 10, of which waited for: 4 -> 4; matrix products, arithmetic and copies ran while one was open for 8% -> 6% of each run, Pallas kernels for 74% -> 76%
where the time goes in v7:
time: 739 us; the launch traced here: 733 us
  Pallas kernels  604 us (82%)
  matrix products  39.8 us (5%)
  local copies, waits for them, and re-layouts  37.3 us (5%)
  waiting for transfers between devices  23.8 us (3%)
  between operations  15.2 us (2%)
  starting transfers between devices  7.96 us (1%)
    pallas_call x2, Pallas kernels, sum_weights(): pl.pallas_call(partial(sum_kernel, fsdp, ctx, count, bool(chain), len(pro...  180 us
    pallas_call x2, Pallas kernels, spread_weights(): pl.pallas_call(partial(spread_kernel, fsdp, ctx, group, count, len(chain)...  150 us
    pallas_call x1, Pallas kernels, swiglu(): pl.pallas_call(partial(swiglu_kernel, fsdp, group), grid=(2 * group,), in...  64.2 us
    pallas_call x7, Pallas kernels, by_rows(): pl.pallas_call(kernel, grid=(total // rows,), in_specs=in_specs, out_spec...  56.4 us
    pallas_call x1, Pallas kernels, start_exchange(): pl.pallas_call(partial(line_kernel, fsdp, ctx, group, len(lines), len(swa...  46 us
    pallas_call x1, Pallas kernels, attend_back(): pl.pallas_call(partial(attend_back_kernel, ctx, fsdp, group), grid=(seqs,...  44.1 us
    pallas_call x1, Pallas kernels, gather_tokens(): pl.pallas_call(partial(tokens_kernel, group, fsdp), out_shape=token_shape...  40.4 us
    unnamed x95, local copies, waits for them, and re-layouts  31.3 us
  transfers between devices with their start and end apart: 10, of which 4 were waited for; matrix products, arithmetic and copies ran while one was open for 6% of the time, Pallas kernels for 76%

profile of v7, /device:TPU:16, one launch (start us, length us, event | category | flops | bytes accessed | tf_op | source)
XLA Modules:
  0.0 733.0 jit_solution(7374718643211923341)
XLA Ops:
  11.4 46.0 %shard_map.203 = (bf16[4,128,1536]{2,1,0:T(8,128)(2,1)S(1)}, f32[4,16,128]{2,1,0:T(8,128)S(1)}, bf16[4,128,1024]{2,1,0:T(8,128)(2,1)S(1)}, bf16[4,128,1536]{2,1,0:T(8,128)(2,1)S(1)}, bf16[4,128,1536]{2,1,0:T(8,128)(2,1)S(1)}) custom-call(bf16[128,1536]{1,0:T(8,128)(2,1)S(1)} %pad_maximum_fusion.2.refs_0_, f32[16,128]{1,0:T(8,128)S(1)} %fusion.3.refs_1_, ...), custom_call_target="tpu_custom_call" | custom-call | tf_op jit(solution)/shard_map/pallas_call | solution.py:644
  64.4 56.7 %shard_map.204 = (bf16[4,4,128,1536]{3,2,1,0:T(8,128)(2,1)S(1)}, f32[4,4,16,128]{3,2,1,0:T(8,128)S(1)}) custom-call(bf16[4,128,1536]{2,1,0:T(8,128)(2,1)S(1)} %copy-done.17, f32[4,16,128]{2,1,0:T(8,128)S(1)} %get-tuple-element.67.refs_1_), custom_call_target="tpu_custom_call" | custom-call | tf_op jit(solution)/shard_map/pallas_call | solution.py:1229
  121.2 5.1 shard_map.205
  126.3 93.2 %shard_map.207 = (bf16[4,4,128,1024]{3,2,1,0:T(8,128)(2,1)S(1)}, bf16[4,512,512]{2,1,0:T(8,128)(2,1)S(1)}, bf16[4,2,256,2048]{3,2,1,0:T(8,128)(2,1)S(1)}) custom-call(bf16[4,128,1024]{2,1,0:T(8,128)(2,1)S(1)} %get-tuple-element.72.refs_0_, bf16[512,512]{1,0:T(8,128)(2,1)S(1)} %get-tuple-element.73.refs_1_, bf16[512,2048]{1,0:T(8,128)(2,1)S(1)} %shard_map.206.refs_2_), custom_call_target="tpu_custom_call" | custom-call | tf_op jit(solution)/shard_map/pallas_call | solution.py:1229
  219.6 3.3 copy-done.3
  229.3 17.4 %shard_map.208 = (bf16[512,1024]{1,0:T(8,128)(2,1)S(1)}, f32[512,256]{1,0:T(8,128)S(1)}) custom-call(s32[2]{0:T(128)S(1)} %copy-done.25, bf16[512,1024]{1,0:T(8,128)(2,1)S(1)} %copy-done.35, bf16[4,512,512]{2,1,0:T(8,128)(2,1)S(1)} %copy-done.31, bf16[4,512,512]{2,1,0:T(8,128)(2,1)S(1)} %copy-done.31, bf16[4,512,512]{2,1,0:T(8,128)(2,1)S(1)} %copy-done.31, ...), custom_call_target="tpu_custom_call" | custom-call | flops 8589934592 | bytes 6291456 | tf_op jit(solution)/shard_map/pallas_call | solution.py:424
  249.2 4.1 collective-permute-done.other_ref
  257.3 40.4 %shard_map.210 = bf16[4,2,256,2048]{3,2,1,0:T(8,128)(2,1)S(1)} custom-call(bf16[512,2048]{1,0:T(8,128)(2,1)S(1)} %get-tuple-element.79.v_ref), custom_call_target="tpu_custom_call" | custom-call | tf_op jit(solution)/shard_map/pallas_call | solution.py:788
  301.1 33.7 %shard_map.211 = (bf16[2048,512]{1,0:T(8,128)(2,1)}, bf16[2048,1024]{1,0:T(8,128)(2,1)}, bf16[2048,2048]{1,0:T(8,128)(2,1)}, bf16[2048,2048]{1,0:T(8,128)(2,1)}) custom-call(bf16[2048,2048]{1,0:T(8,128)(2,1)} %bitcast.69, bf16[2048,2048]{1,0:T(8,128)(2,1)} %bitcast.73, bf16[2048,1536]{1,0:T(8,128)(2,1)} %bitcast.113), custom_call_target="tpu_custom_call" | custom-call | flops 25769803776 | bytes 46137344 | tf_op jit(solution)/shard_map/pallas_call | solution.py:399
  334.7 14.4 %convolution_convert_fusion.2 = bf16[2048,1024]{1,0:T(8,128)(2,1)} fusion(bf16[2048,2048]{1,0:T(8,128)(2,1)} %bitcast.70, bf16[2048,1024]{1,0:T(8,128)(2,1)} %get-tuple-element.85), kind=kOutput, calls=%fused_computation.2 | convolution fusion | flops 8592031744 | bytes 16777216 | tf_op jit(solution)/shard_map/td,tf->df/dot_general | solution.py:1796
  349.2 64.2 %shard_map.212 = (bf16[2048,512]{1,0:T(8,128)(2,1)}, bf16[2048,1024]{1,0:T(8,128)(2,1)}, bf16[1024,2048]{1,0:T(8,128)(2,1)}, bf16[2,256,2048]{2,1,0:T(8,128)(2,1)}, bf16[2048,512]{1,0:T(8,128)(2,1)}) custom-call(bf16[2048,2048]{1,0:T(8,128)(2,1)} %bitcast.71, bf16[2048,2048]{1,0:T(8,128)(2,1)} %bitcast.74, bf16[2048,1536]{1,0:T(8,128)(2,1)} %bitcast.114, ...), custom_call_target="tpu_custom_call" | custom-call | flops 25769803776 | bytes 52428800 | tf_op jit(solution)/shard_map/pallas_call | solution.py:1014
  415.1 5.8 shard_map.213
  420.9 4.4 convolution_convert_fusion.1
  427.9 44.1 %shard_map.214 = (bf16[512,1024]{1,0:T(8,128)(2,1)S(1)}, bf16[4,2,512,256]{3,2,1,0:T(8,128)(2,1)S(1)}, bf16[2,256,2048]{2,1,0:T(8,128)(2,1)S(1)}) custom-call(s32[2]{0:T(128)S(1)} %copy-done.25, bf16[512,1024]{1,0:T(8,128)(2,1)S(1)} %copy-done.36, bf16[512,1024]{1,0:T(8,128)(2,1)S(1)} %convolution_convert_fusion.5.do_ref, ...), custom_call_target="tpu_custom_call" | custom-call | flops 21474836480 | bytes 10485760 | tf_op jit(solution)/shard_map/pallas_call | solution.py:455
  474.7 75.0 %shard_map.216 = (f32[128,1024]{1,0:T(8,128)}, bf16[512,512]{1,0:T(8,128)(2,1)}, bf16[2048,1024]{1,0:T(8,128)(2,1)}, bf16[2048,512]{1,0:T(8,128)(2,1)}) custom-call(bf16[4,4,128,1024]{3,2,1,0:T(8,128)(2,1)} %bitcast.94, bf16[4,2,512,256]{3,2,1,0:T(8,128)(2,1)} %copy-done.10, f32[256,128]{1,0:T(8,128)} %copy-done.21, f32[256,128]{1,0:T(8,128)} %copy-done.22, ...), custom_call_target="tpu_custom_call" | custom-call | tf_op jit(solution)/shard_map/pallas_call | solution.py:1574
  551.5 8.1 %convolution_convert_fusion.4.part_ref = bf16[512,2048]{1,0:T(8,128)(2,1)} fusion(bf16[512,1536]{1,0:T(8,128)(2,1)S(1)} %constant_dynamic-update-slice_fusion, bf16[2048,1536]{1,0:T(8,128)(2,1)} %bitcast.90), kind=kOutput, calls=%fused_computation.4 | convolution fusion | flops 3222274048 | bytes 9961472 | tf_op jit(solution)/shard_map/tj,dj->td/dot_general | solution.py:1898
  563.2 3.8 all-to-all-start
  567.1 8.3 %convolution_convert_fusion = bf16[2048,1536]{1,0:T(8,128)(2,1)} fusion(bf16[512,2048]{1,0:T(8,128)(2,1)} %copy-done.33, bf16[512,1536]{1,0:T(8,128)(2,1)} %copy-done.39), kind=kOutput, calls=%fused_computation | convolution fusion | flops 3224371200 | bytes 9961472 | tf_op jit(solution)/shard_map/td,tj->dj/dot_general | solution.py:1897
  575.4 6.0 shard_map.217
  582.0 5.1 all-to-all-done
  587.2 105.4 %shard_map.218 = (f32[128,1536]{1,0:T(8,128)}, f32[16,128]{1,0:T(8,128)}) custom-call(bf16[4,4,128,1536]{3,2,1,0:T(8,128)(2,1)} %bitcast.93, f32[4,4,16,128]{3,2,1,0:T(8,128)} %bitcast.106), custom_call_target="tpu_custom_call" | custom-call | tf_op jit(solution)/shard_map/pallas_call | solution.py:1574
  692.7 4.6 reduce-scatter.9.cloned.1.call-done
  699.8 3.6 all-to-all-start.1
  713.7 9.2 %all-to-all-done.1 = bf16[4,384,512]{2,1,0:T(8,128)(2,1)S(1)} async-done(((bf16[4,384,512]{2,1,0:T(8,128)(2,1)}), bf16[4,384,512]{2,1,0:T(8,128)(2,1)S(1)}, u32[]{:S(2)}, u32[]{:S(2)}) %all-to-all-start.1) | async-done | bytes 1572896 | tf_op jit(solution)/shard_map/all_to_all | solution.py:1816
  (143 shorter events, 55.8 us)
Async XLA Ops:
  7.2 293.8 %all-gather.7.cloned.1.call-start = ((), (), s32[]{:S(2)}) async-start(), calls=%async_computation.11 | async-start | bytes 7864320 | tf_op jit(solution)/shard_map/all_gather | solution.py:1747
  60.8 288.4 %all-gather.5.cloned.1.call-start = ((), (), s32[]{:S(2)}) async-start(), calls=%async_computation.10 | async-start | bytes 7864320 | tf_op jit(solution)/shard_map/all_gather | solution.py:1747
  61.3 366.6 %copy-start.21 = (f32[256,128]{1,0:T(8,128)}, f32[256,128]{1,0:T(8,128)S(1)}, u32[]{:S(2)}) copy-start(f32[256,128]{1,0:T(8,128)S(1)} %copy.52.cos_ref.refs_2_) | copy-start | bytes 393220
  62.9 365.0 %copy-start.22 = (f32[256,128]{1,0:T(8,128)}, f32[256,128]{1,0:T(8,128)S(1)}, u32[]{:S(2)}) copy-start(f32[256,128]{1,0:T(8,128)S(1)} %copy.53.sin_ref.refs_3_) | copy-start | bytes 393220
  63.0 58.2 %copy-start.5 = (bf16[2,256,2048]{2,1,0:T(8,128)(2,1)S(1)}, bf16[2,256,2048]{2,1,0:T(8,128)(2,1)}, u32[]{:S(2)}) copy-start(bf16[2,256,2048]{2,1,0:T(8,128)(2,1)} %param.12) | copy-start | bytes 6291460
  121.2 98.4 %copy-start.26 = (bf16[4,4,128,1536]{3,2,1,0:T(8,128)(2,1)}, bf16[4,4,128,1536]{3,2,1,0:T(8,128)(2,1)S(1)}, u32[]{:S(2)}) copy-start(bf16[4,4,128,1536]{3,2,1,0:T(8,128)(2,1)S(1)} %get-tuple-element.68) | copy-start | bytes 18874372
  126.3 93.3 %copy-start.33 = (bf16[512,2048]{1,0:T(8,128)(2,1)}, bf16[512,2048]{1,0:T(8,128)(2,1)S(1)}, u32[]{:S(2)}) copy-start(bf16[512,2048]{1,0:T(8,128)(2,1)S(1)} %get-tuple-element.101) | copy-start | bytes 6291460
  126.3 93.3 %copy-start.34 = (bf16[512,1024]{1,0:T(8,128)(2,1)}, bf16[512,1024]{1,0:T(8,128)(2,1)S(1)}, u32[]{:S(2)}) copy-start(bf16[512,1024]{1,0:T(8,128)(2,1)S(1)} %get-tuple-element.70.q_ref) | copy-start | bytes 3145732
  226.2 333.3 %reduce-scatter.5.cloned.1.call-start = ((), (), s32[]{:S(2)}) async-start(), calls=%async_computation.6 | async-start | bytes 5242880 | tf_op jit(solution)/shard_map/reduce_scatter | solution.py:1800
  229.3 17.4 %copy-start.28 = (bf16[4,4,128,1024]{3,2,1,0:T(8,128)(2,1)S(1)}, bf16[4,4,128,1024]{3,2,1,0:T(8,128)(2,1)}, u32[]{:S(2)}) copy-start(bf16[4,4,128,1024]{3,2,1,0:T(8,128)(2,1)} %copy-done.27) | copy-start | bytes 12582916
  246.7 6.6 copy-start.6
  249.1 4.2 collective-permute-start
  349.1 211.8 %reduce-scatter.7.cloned.1.call-start = ((), (), s32[]{:S(2)}) async-start(), calls=%async_computation.7 | async-start | bytes 2621440 | tf_op jit(solution)/shard_map/reduce_scatter | solution.py:1800
  413.4 279.2 %reduce-scatter.11.cloned.1.call-start = ((), (), s32[]{:S(2)}) async-start(), calls=%async_computation.9 | async-start | bytes 2621440 | tf_op jit(solution)/shard_map/reduce_scatter | solution.py:1800
  415.1 5.8 copy-start.38
  549.8 147.4 %reduce-scatter.9.cloned.1.call-start = ((), (), s32[]{:S(2)}) async-start(), calls=%async_computation.8 | async-start | bytes 5242880 | tf_op jit(solution)/shard_map/reduce_scatter | solution.py:1800
  551.5 8.1 %copy-start.39 = (bf16[512,1536]{1,0:T(8,128)(2,1)}, bf16[512,1536]{1,0:T(8,128)(2,1)S(1)}, u32[]{:S(2)}) copy-start(bf16[512,1536]{1,0:T(8,128)(2,1)S(1)} %constant_dynamic-update-slice_fusion) | copy-start | bytes 4718596
  559.6 15.8 %collective-permute-start.1 = (bf16[512,2048]{1,0:T(8,128)(2,1)}, bf16[512,2048]{1,0:T(8,128)(2,1)}, u32[]{:S(2)}, u32[]{:S(2)}) collective-permute-start(bf16[512,2048]{1,0:T(8,128)(2,1)} %convolution_convert_fusion.4.part_ref), channel_id=1, source_target_pairs={{0,1},{1,0},{2,3},{3,2},{4,5},{5,4},{6,7},{7,6},{8,9},{9,8},{10,11... | collective-permute-start | bytes 6291464 | tf_op jit(solution)/shard_map/ppermute | solution.py:1698
  563.2 24.0 %all-to-all-start = ((bf16[4,384,512]{2,1,0:T(8,128)(2,1)}), bf16[4,384,512]{2,1,0:T(8,128)(2,1)S(1)}, u32[]{:S(2)}, u32[]{:S(2)}) async-start(bf16[4,384,512]{2,1,0:T(8,128)(2,1)} %pad_maximum_fusion), calls=%async_computation.2 | async-start | bytes 3145728 | tf_op jit(solution)/shard_map/all_to_all | solution.py:1816
  567.1 8.3 %copy-start.7 = (bf16[2,256,2048]{2,1,0:T(8,128)(2,1)S(1)}, bf16[2,256,2048]{2,1,0:T(8,128)(2,1)}, u32[]{:S(2)}) copy-start(bf16[2,256,2048]{2,1,0:T(8,128)(2,1)} %param.12) | copy-start | bytes 6291460
  567.1 8.3 %copy-start.9 = (f32[512,2048]{1,0:T(8,128)S(1)}, f32[512,2048]{1,0:T(8,128)}, u32[]{:S(2)}) copy-start(f32[512,2048]{1,0:T(8,128)} %copy-done.8) | copy-start | bytes 12582916
  567.1 8.3 %copy-start.24 = (f32[1,2048]{1,0:T(1,128)S(1)}, f32[1,2048]{1,0:T(1,128)}, u32[]{:S(2)}) copy-start(f32[1,2048]{1,0:T(1,128)} %copy-done.23) | copy-start | bytes 24580
  692.7 5.9 copy-start.41
  699.8 23.1 %all-to-all-start.1 = ((bf16[4,384,512]{2,1,0:T(8,128)(2,1)}), bf16[4,384,512]{2,1,0:T(8,128)(2,1)S(1)}, u32[]{:S(2)}, u32[]{:S(2)}) async-start(bf16[4,384,512]{2,1,0:T(8,128)(2,1)} %pad_maximum_fusion.1), calls=%async_computation.5 | async-start | bytes 3145728 | tf_op jit(solution)/shard_map/all_to_all | solution.py:1816
  (32 other events, 72.8 us)
Sparse Core Ops, SparseCore 0:
  61.0 127.7 all-gather.6
  226.4 112.8 all-gather.4
  349.3 76.4 reduce-scatter.4
  428.0 43.1 reduce-scatter.6
  549.9 42.3 reduce-scatter.10
  594.6 102.6 reduce-scatter.8

commit v8 on v7

--- a/solution.py
+++ b/solution.py
@@ -1877,16 +1877,21 @@
         kv_all,
         ff_sums.reshape(group, half, model_width),
     )
+    query_grad, late_rows, late_hidden = lax.optimization_barrier(
+        (query_grad, ff_grad_all, hidden)
+    )
+    late_down = unit_term(late_rows, late_hidden)
+    late_down_own = own_units(late_down)
+    kv_parts, _ = lax.optimization_barrier((kv_parts, late_down))
     out_term = jnp.einsum("td,tj->dj", attn_grad, attended, preferred_element_type=wide)
-    w_out_grad, kv_grad, late_both, late_down = sum_weights(
+    w_out_grad, kv_grad, late_both = sum_weights(
         fsdp,
         ctx,
         [out_term.astype(low)],
         (kv_parts, cosines, sines),
-        ((normed_all, both_grad), (ff_grad_all, hidden)),
+        ((normed_all, both_grad),),
     )
     late_both_own = own_units(late_both)
-    late_down_own = own_units(late_down)
     (output,) = by_rows(
         partial(output_kernel, back_dims, local_rows),
         128,

time: 739 us -> 736 us (level)
  matrix products: 39.8 us -> 52.1 us
  Pallas kernels: 604 us -> 595 us
    dot_general x1 -> x2, matrix products: 14.4 us -> 25.1 us  [unit_term(): jnp.einsum('td,tf->df', left, right, preferred_element_type=wide)]
    pallas_call x2, Pallas kernels: 180 us -> 172 us  [sum_weights(): pl.pallas_call(partial(sum_kernel, fsdp, ctx, count, bool(chain), len(pro...]
    unnamed x95 -> x99, local copies, waits for them, and re-layouts: 31.3 us -> 30.9 us
  transfers between devices with their start and end apart: 10 -> 10, of which waited for: 4 -> 3; matrix products, arithmetic and copies ran while one was open for 6% -> 8% of each run, Pallas kernels for 76% -> 75%
where the time goes in v8:
time: 736 us; the launch traced here: 731 us
  Pallas kernels  595 us (81%)
  matrix products  52.1 us (7%)
  local copies, waits for them, and re-layouts  37 us (5%)
  waiting for transfers between devices  17.3 us (2%)
  between operations  15.1 us (2%)
  starting transfers between devices  9.45 us (1%)
    pallas_call x2, Pallas kernels, sum_weights(): pl.pallas_call(partial(sum_kernel, fsdp, ctx, count, bool(chain), len(pro...  172 us
    pallas_call x2, Pallas kernels, spread_weights(): pl.pallas_call(partial(spread_kernel, fsdp, ctx, group, count, len(chain)...  150 us
    pallas_call x1, Pallas kernels, swiglu(): pl.pallas_call(partial(swiglu_kernel, fsdp, group), grid=(2 * group,), in...  64.2 us
    pallas_call x7, Pallas kernels, by_rows(): pl.pallas_call(kernel, grid=(total // rows,), in_specs=in_specs, out_spec...  56.4 us
    pallas_call x1, Pallas kernels, start_exchange(): pl.pallas_call(partial(line_kernel, fsdp, ctx, group, len(lines), len(swa...  46 us
    pallas_call x1, Pallas kernels, attend_back(): pl.pallas_call(partial(attend_back_kernel, ctx, fsdp, group), grid=(seqs,...  44.1 us
    pallas_call x1, Pallas kernels, gather_tokens(): pl.pallas_call(partial(tokens_kernel, group, fsdp), out_shape=token_shape...  40.4 us
    unnamed x99, local copies, waits for them, and re-layouts  30.9 us
  transfers between devices with their start and end apart: 10, of which 3 were waited for; matrix products, arithmetic and copies ran while one was open for 8% of the time, Pallas kernels for 75%

profile of v8, /device:TPU:16, one launch (start us, length us, event | category | flops | bytes accessed | tf_op | source)
XLA Modules:
  0.0 730.9 jit_solution(15587879304896564114)
XLA Ops:
  11.4 46.0 %shard_map.203 = (bf16[4,128,1536]{2,1,0:T(8,128)(2,1)S(1)}, f32[4,16,128]{2,1,0:T(8,128)S(1)}, bf16[4,128,1024]{2,1,0:T(8,128)(2,1)S(1)}, bf16[4,128,1536]{2,1,0:T(8,128)(2,1)S(1)}, bf16[4,128,1536]{2,1,0:T(8,128)(2,1)S(1)}) custom-call(bf16[128,1536]{1,0:T(8,128)(2,1)S(1)} %pad_maximum_fusion.2.refs_0_, f32[16,128]{1,0:T(8,128)S(1)} %fusion.3.refs_1_, ...), custom_call_target="tpu_custom_call" | custom-call | tf_op jit(solution)/shard_map/pallas_call | solution.py:644
  64.4 56.7 %shard_map.204 = (bf16[4,4,128,1536]{3,2,1,0:T(8,128)(2,1)S(1)}, f32[4,4,16,128]{3,2,1,0:T(8,128)S(1)}) custom-call(bf16[4,128,1536]{2,1,0:T(8,128)(2,1)S(1)} %copy-done.16, f32[4,16,128]{2,1,0:T(8,128)S(1)} %get-tuple-element.70.refs_1_), custom_call_target="tpu_custom_call" | custom-call | tf_op jit(solution)/shard_map/pallas_call | solution.py:1229
  121.2 5.1 shard_map.205
  126.3 93.2 %shard_map.207 = (bf16[4,4,128,1024]{3,2,1,0:T(8,128)(2,1)S(1)}, bf16[4,512,512]{2,1,0:T(8,128)(2,1)S(1)}, bf16[4,2,256,2048]{3,2,1,0:T(8,128)(2,1)S(1)}) custom-call(bf16[4,128,1024]{2,1,0:T(8,128)(2,1)S(1)} %get-tuple-element.75.refs_0_, bf16[512,512]{1,0:T(8,128)(2,1)S(1)} %get-tuple-element.76.refs_1_, bf16[512,2048]{1,0:T(8,128)(2,1)S(1)} %shard_map.206.refs_2_), custom_call_target="tpu_custom_call" | custom-call | tf_op jit(solution)/shard_map/pallas_call | solution.py:1229
  229.6 17.4 %shard_map.208 = (bf16[512,1024]{1,0:T(8,128)(2,1)S(1)}, f32[512,256]{1,0:T(8,128)S(1)}) custom-call(s32[2]{0:T(128)S(1)} %copy-done.24, bf16[512,1024]{1,0:T(8,128)(2,1)S(1)} %copy-done.36, bf16[4,512,512]{2,1,0:T(8,128)(2,1)S(1)} %copy-done.31, bf16[4,512,512]{2,1,0:T(8,128)(2,1)S(1)} %copy-done.31, bf16[4,512,512]{2,1,0:T(8,128)(2,1)S(1)} %copy-done.31, ...), custom_call_target="tpu_custom_call" | custom-call | flops 8589934592 | bytes 6291456 | tf_op jit(solution)/shard_map/pallas_call | solution.py:424
  249.4 4.1 collective-permute-done.other_ref
  257.6 40.4 %shard_map.210 = bf16[4,2,256,2048]{3,2,1,0:T(8,128)(2,1)S(1)} custom-call(bf16[512,2048]{1,0:T(8,128)(2,1)S(1)} %get-tuple-element.82.v_ref), custom_call_target="tpu_custom_call" | custom-call | tf_op jit(solution)/shard_map/pallas_call | solution.py:788
  298.0 3.3 copy-done
  301.4 33.7 %shard_map.211 = (bf16[2048,512]{1,0:T(8,128)(2,1)}, bf16[2048,1024]{1,0:T(8,128)(2,1)}, bf16[2048,2048]{1,0:T(8,128)(2,1)}, bf16[2048,2048]{1,0:T(8,128)(2,1)}) custom-call(bf16[2048,2048]{1,0:T(8,128)(2,1)} %bitcast.71, bf16[2048,2048]{1,0:T(8,128)(2,1)} %bitcast.87, bf16[2048,1536]{1,0:T(8,128)(2,1)} %bitcast.115), custom_call_target="tpu_custom_call" | custom-call | flops 25769803776 | bytes 46137344 | tf_op jit(solution)/shard_map/pallas_call | solution.py:399
  335.0 14.1 %convolution_convert_fusion.2 = bf16[2048,1024]{1,0:T(8,128)(2,1)} fusion(bf16[2048,2048]{1,0:T(8,128)(2,1)} %bitcast.72, bf16[2048,1024]{1,0:T(8,128)(2,1)} %get-tuple-element.88), kind=kOutput, calls=%fused_computation.2 | convolution fusion | flops 8592031744 | bytes 16777216 | tf_op jit(solution)/shard_map/td,tf->df/dot_general | solution.py:1796
  349.3 64.2 %shard_map.212 = (bf16[2048,512]{1,0:T(8,128)(2,1)}, bf16[2048,1024]{1,0:T(8,128)(2,1)}, bf16[1024,2048]{1,0:T(8,128)(2,1)}, bf16[2,256,2048]{2,1,0:T(8,128)(2,1)}, bf16[2048,512]{1,0:T(8,128)(2,1)}) custom-call(bf16[2048,2048]{1,0:T(8,128)(2,1)} %bitcast.73, bf16[2048,2048]{1,0:T(8,128)(2,1)} %bitcast.88, bf16[2048,1536]{1,0:T(8,128)(2,1)} %bitcast.116, ...), custom_call_target="tpu_custom_call" | custom-call | flops 25769803776 | bytes 52428800 | tf_op jit(solution)/shard_map/pallas_call | solution.py:1014
  415.2 5.8 shard_map.213
  425.1 44.1 %shard_map.214 = (bf16[512,1024]{1,0:T(8,128)(2,1)S(1)}, bf16[4,2,512,256]{3,2,1,0:T(8,128)(2,1)S(1)}, bf16[2,256,2048]{2,1,0:T(8,128)(2,1)S(1)}) custom-call(s32[2]{0:T(128)S(1)} %copy-done.24, bf16[512,1024]{1,0:T(8,128)(2,1)S(1)} %copy-done.37, bf16[512,1024]{1,0:T(8,128)(2,1)S(1)} %convolution_convert_fusion.6.do_ref, ...), custom_call_target="tpu_custom_call" | custom-call | flops 21474836480 | bytes 10485760 | tf_op jit(solution)/shard_map/pallas_call | solution.py:455
  469.3 10.9 %convolution_convert_fusion.5 = bf16[2048,512]{1,0:T(8,128)(2,1)} fusion(bf16[2048,2048]{1,0:T(8,128)(2,1)} %bitcast.90, bf16[2048,512]{1,0:T(8,128)(2,1)S(1)} %copy-done.47), kind=kOutput, calls=%fused_computation.5 | convolution fusion | flops 4296015872 | bytes 12582912 | tf_op jit(solution)/shard_map/td,tf->df/dot_general | solution.py:1796
  481.4 5.9 convolution_convert_fusion.1
  487.3 97.0 %shard_map.216 = (f32[128,1024]{1,0:T(8,128)}, bf16[512,512]{1,0:T(8,128)(2,1)}, bf16[2048,1024]{1,0:T(8,128)(2,1)}) custom-call(bf16[4,4,128,1024]{3,2,1,0:T(8,128)(2,1)} %bitcast.98, bf16[4,2,512,256]{3,2,1,0:T(8,128)(2,1)} %copy-done.9, f32[256,128]{1,0:T(8,128)} %copy-done.20, f32[256,128]{1,0:T(8,128)} %copy-done.21, bf16[2048,2048]{1,0:T(8,128)(2,1)} %bitcast.74, ...), custom_call_target="tpu_custom_call" | custom-call | tf_op jit(solution)/shard_map/pallas_call | solution.py:1574
  585.5 8.1 %convolution_convert_fusion.4.part_ref = bf16[512,2048]{1,0:T(8,128)(2,1)} fusion(bf16[512,1536]{1,0:T(8,128)(2,1)S(1)} %constant_dynamic-update-slice_fusion, bf16[2048,1536]{1,0:T(8,128)(2,1)} %bitcast.92), kind=kOutput, calls=%fused_computation.4 | convolution fusion | flops 3222274048 | bytes 9961472 | tf_op jit(solution)/shard_map/tj,dj->td/dot_general | solution.py:1903
  597.3 4.0 all-to-all-start
  601.3 8.3 %convolution_convert_fusion = bf16[2048,1536]{1,0:T(8,128)(2,1)} fusion(bf16[512,2048]{1,0:T(8,128)(2,1)} %copy-done.34, bf16[512,1536]{1,0:T(8,128)(2,1)} %copy-done.40), kind=kOutput, calls=%fused_computation | convolution fusion | flops 3224371200 | bytes 9961472 | tf_op jit(solution)/shard_map/td,tj->dj/dot_general | solution.py:1902
  609.6 6.0 shard_map.217
  616.3 5.7 all-to-all-done
  622.0 74.5 %shard_map.218 = (f32[128,1536]{1,0:T(8,128)}, f32[16,128]{1,0:T(8,128)}) custom-call(bf16[4,4,128,1536]{3,2,1,0:T(8,128)(2,1)} %bitcast.95, f32[4,4,16,128]{3,2,1,0:T(8,128)} %bitcast.108), custom_call_target="tpu_custom_call" | custom-call | tf_op jit(solution)/shard_map/pallas_call | solution.py:1574
  699.2 4.2 all-to-all-start.1
  713.6 7.3 %all-to-all-done.1 = bf16[4,384,512]{2,1,0:T(8,128)(2,1)S(1)} async-done(((bf16[4,384,512]{2,1,0:T(8,128)(2,1)}), bf16[4,384,512]{2,1,0:T(8,128)(2,1)S(1)}, u32[]{:S(2)}, u32[]{:S(2)}) %all-to-all-start.1) | async-done | bytes 1572896 | tf_op jit(solution)/shard_map/all_to_all | solution.py:1816
  (148 shorter events, 55.7 us)
Async XLA Ops:
  7.2 294.1 %all-gather.7.cloned.1.call-start = ((), (), s32[]{:S(2)}) async-start(), calls=%async_computation.11 | async-start | bytes 7864320 | tf_op jit(solution)/shard_map/all_gather | solution.py:1747
  60.8 288.4 %all-gather.5.cloned.1.call-start = ((), (), s32[]{:S(2)}) async-start(), calls=%async_computation.10 | async-start | bytes 7864320 | tf_op jit(solution)/shard_map/all_gather | solution.py:1747
  61.3 362.9 %copy-start.20 = (f32[256,128]{1,0:T(8,128)}, f32[256,128]{1,0:T(8,128)S(1)}, u32[]{:S(2)}) copy-start(f32[256,128]{1,0:T(8,128)S(1)} %copy.52.cos_ref.refs_2_) | copy-start | bytes 393220
  62.9 361.2 %copy-start.21 = (f32[256,128]{1,0:T(8,128)}, f32[256,128]{1,0:T(8,128)S(1)}, u32[]{:S(2)}) copy-start(f32[256,128]{1,0:T(8,128)S(1)} %copy.53.sin_ref.refs_3_) | copy-start | bytes 393220
  63.0 58.2 %copy-start.4 = (bf16[2,256,2048]{2,1,0:T(8,128)(2,1)S(1)}, bf16[2,256,2048]{2,1,0:T(8,128)(2,1)}, u32[]{:S(2)}) copy-start(bf16[2,256,2048]{2,1,0:T(8,128)(2,1)} %param.12) | copy-start | bytes 6291460
  126.3 93.3 %copy-start.34 = (bf16[512,2048]{1,0:T(8,128)(2,1)}, bf16[512,2048]{1,0:T(8,128)(2,1)S(1)}, u32[]{:S(2)}) copy-start(bf16[512,2048]{1,0:T(8,128)(2,1)S(1)} %get-tuple-element.108) | copy-start | bytes 6291460
  126.3 93.3 %copy-start.35 = (bf16[512,1024]{1,0:T(8,128)(2,1)}, bf16[512,1024]{1,0:T(8,128)(2,1)S(1)}, u32[]{:S(2)}) copy-start(bf16[512,1024]{1,0:T(8,128)(2,1)S(1)} %get-tuple-element.73.q_ref) | copy-start | bytes 3145732
  226.2 367.4 %reduce-scatter.5.cloned.1.call-start = ((), (), s32[]{:S(2)}) async-start(), calls=%async_computation.6 | async-start | bytes 5242880 | tf_op jit(solution)/shard_map/reduce_scatter | solution.py:1800
  229.6 17.4 %copy-start.28 = (bf16[4,4,128,1024]{3,2,1,0:T(8,128)(2,1)S(1)}, bf16[4,4,128,1024]{3,2,1,0:T(8,128)(2,1)}, u32[]{:S(2)}) copy-start(bf16[4,4,128,1024]{3,2,1,0:T(8,128)(2,1)} %copy-done.27) | copy-start | bytes 12582916
  247.0 6.6 copy-start.5
  249.4 4.2 collective-permute-start
  349.2 245.8 %reduce-scatter.7.cloned.1.call-start = ((), (), s32[]{:S(2)}) async-start(), calls=%async_computation.7 | async-start | bytes 2621440 | tf_op jit(solution)/shard_map/reduce_scatter | solution.py:1800
  413.5 283.0 %reduce-scatter.11.cloned.1.call-start = ((), (), s32[]{:S(2)}) async-start(), calls=%async_computation.9 | async-start | bytes 2621440 | tf_op jit(solution)/shard_map/reduce_scatter | solution.py:1800
  425.1 44.1 %copy-start.47 = (bf16[2048,512]{1,0:T(8,128)(2,1)S(1)}, bf16[2048,512]{1,0:T(8,128)(2,1)}, u32[]{:S(2)}) copy-start(bf16[2048,512]{1,0:T(8,128)(2,1)} %get-tuple-element.102) | copy-start | bytes 6291460
  469.2 11.0 %copy-start.9 = (bf16[4,2,512,256]{3,2,1,0:T(8,128)(2,1)}, bf16[4,2,512,256]{3,2,1,0:T(8,128)(2,1)S(1)}, u32[]{:S(2)}) copy-start(bf16[4,2,512,256]{3,2,1,0:T(8,128)(2,1)S(1)} %get-tuple-element.103.refs_1_) | copy-start | bytes 6291460
  469.2 10.9 %copy-start.11 = (bf16[2,256,2048]{2,1,0:T(8,128)(2,1)}, bf16[2,256,2048]{2,1,0:T(8,128)(2,1)S(1)}, u32[]{:S(2)}) copy-start(bf16[2,256,2048]{2,1,0:T(8,128)(2,1)S(1)} %get-tuple-element.96) | copy-start | bytes 6291460
  480.2 216.3 %reduce-scatter.9.cloned.1.call-start = ((), (), s32[]{:S(2)}) async-start(), calls=%async_computation.8 | async-start | bytes 5242880 | tf_op jit(solution)/shard_map/reduce_scatter | solution.py:1800
  585.5 8.1 %copy-start.40 = (bf16[512,1536]{1,0:T(8,128)(2,1)}, bf16[512,1536]{1,0:T(8,128)(2,1)S(1)}, u32[]{:S(2)}) copy-start(bf16[512,1536]{1,0:T(8,128)(2,1)S(1)} %constant_dynamic-update-slice_fusion) | copy-start | bytes 4718596
  593.6 16.0 %collective-permute-start.1 = (bf16[512,2048]{1,0:T(8,128)(2,1)}, bf16[512,2048]{1,0:T(8,128)(2,1)}, u32[]{:S(2)}, u32[]{:S(2)}) collective-permute-start(bf16[512,2048]{1,0:T(8,128)(2,1)} %convolution_convert_fusion.4.part_ref), channel_id=1, source_target_pairs={{0,1},{1,0},{2,3},{3,2},{4,5},{5,4},{6,7},{7,6},{8,9},{9,8},{10,11... | collective-permute-start | bytes 6291464 | tf_op jit(solution)/shard_map/ppermute | solution.py:1698
  597.3 24.7 %all-to-all-start = ((bf16[4,384,512]{2,1,0:T(8,128)(2,1)}), bf16[4,384,512]{2,1,0:T(8,128)(2,1)S(1)}, u32[]{:S(2)}, u32[]{:S(2)}) async-start(bf16[4,384,512]{2,1,0:T(8,128)(2,1)} %pad_maximum_fusion), calls=%async_computation.2 | async-start | bytes 3145728 | tf_op jit(solution)/shard_map/all_to_all | solution.py:1816
  601.3 8.3 %copy-start.6 = (bf16[2,256,2048]{2,1,0:T(8,128)(2,1)S(1)}, bf16[2,256,2048]{2,1,0:T(8,128)(2,1)}, u32[]{:S(2)}) copy-start(bf16[2,256,2048]{2,1,0:T(8,128)(2,1)} %param.12) | copy-start | bytes 6291460
  601.3 8.3 %copy-start.8 = (f32[512,2048]{1,0:T(8,128)S(1)}, f32[512,2048]{1,0:T(8,128)}, u32[]{:S(2)}) copy-start(f32[512,2048]{1,0:T(8,128)} %copy-done.7) | copy-start | bytes 12582916
  601.3 8.3 %copy-start.23 = (f32[1,2048]{1,0:T(1,128)S(1)}, f32[1,2048]{1,0:T(1,128)}, u32[]{:S(2)}) copy-start(f32[1,2048]{1,0:T(1,128)} %copy-done.22) | copy-start | bytes 24580
  699.2 21.7 %all-to-all-start.1 = ((bf16[4,384,512]{2,1,0:T(8,128)(2,1)}), bf16[4,384,512]{2,1,0:T(8,128)(2,1)S(1)}, u32[]{:S(2)}, u32[]{:S(2)}) async-start(bf16[4,384,512]{2,1,0:T(8,128)(2,1)} %pad_maximum_fusion.1), calls=%async_computation.5 | async-start | bytes 3145728 | tf_op jit(solution)/shard_map/all_to_all | solution.py:1816
  (34 other events, 82.7 us)
Sparse Core Ops, SparseCore 0:
  61.0 127.7 all-gather.6
  226.3 112.8 all-gather.4
  349.3 76.4 reduce-scatter.4
  428.0 43.1 reduce-scatter.6
  480.3 71.8 reduce-scatter.10
  584.5 86.1 reduce-scatter.8

commit v9 on v8

--- a/solution.py
+++ b/solution.py
@@ -299,7 +299,7 @@
         dq = jnp.where(lane < HD, dqs[0], dqs[1]) * score_scale
         dq = dq * cos_ref[...] + turn(dq * sin_ref[...], -1.0)
         dq_ref[:, j * 128 : (j + 1) * 128] = dq.astype(jnp.bfloat16)
-        if j == 1:
+        if j == 0:
 
             @pl.when(step == 1)
             def _():

time: 736 us -> 736 us (level)
  no operation moved by 1% of the time
where the time goes in v9:
time: 736 us; the launch traced here: 731 us
  Pallas kernels  595 us (81%)
  matrix products  52.1 us (7%)
  local copies, waits for them, and re-layouts  37 us (5%)
  waiting for transfers between devices  17.4 us (2%)
  between operations  15.1 us (2%)
  starting transfers between devices  9.47 us (1%)
    pallas_call x2, Pallas kernels, sum_weights(): pl.pallas_call(partial(sum_kernel, fsdp, ctx, count, bool(chain), len(pro...  172 us
    pallas_call x2, Pallas kernels, spread_weights(): pl.pallas_call(partial(spread_kernel, fsdp, ctx, group, count, len(chain)...  150 us
    pallas_call x1, Pallas kernels, swiglu(): pl.pallas_call(partial(swiglu_kernel, fsdp, group), grid=(2 * group,), in...  64.2 us
    pallas_call x7, Pallas kernels, by_rows(): pl.pallas_call(kernel, grid=(total // rows,), in_specs=in_specs, out_spec...  56.4 us
    pallas_call x1, Pallas kernels, start_exchange(): pl.pallas_call(partial(line_kernel, fsdp, ctx, group, len(lines), len(swa...  46 us
    pallas_call x1, Pallas kernels, attend_back(): pl.pallas_call(partial(attend_back_kernel, ctx, fsdp, group), grid=(seqs,...  44.1 us
    pallas_call x1, Pallas kernels, gather_tokens(): pl.pallas_call(partial(tokens_kernel, group, fsdp), out_shape=token_shape...  40.4 us
    unnamed x99, local copies, waits for them, and re-layouts  30.9 us
  transfers between devices with their start and end apart: 10, of which 3 were waited for; matrix products, arithmetic and copies ran while one was open for 8% of the time, Pallas kernels for 75%

profile of v9, /device:TPU:16, one launch (start us, length us, event | category | flops | bytes accessed | tf_op | source)
XLA Modules:
  0.0 730.9 jit_solution(299745635546838159)
XLA Ops:
  11.4 46.0 %shard_map.203 = (bf16[4,128,1536]{2,1,0:T(8,128)(2,1)S(1)}, f32[4,16,128]{2,1,0:T(8,128)S(1)}, bf16[4,128,1024]{2,1,0:T(8,128)(2,1)S(1)}, bf16[4,128,1536]{2,1,0:T(8,128)(2,1)S(1)}, bf16[4,128,1536]{2,1,0:T(8,128)(2,1)S(1)}) custom-call(bf16[128,1536]{1,0:T(8,128)(2,1)S(1)} %pad_maximum_fusion.2.refs_0_, f32[16,128]{1,0:T(8,128)S(1)} %fusion.3.refs_1_, ...), custom_call_target="tpu_custom_call" | custom-call | tf_op jit(solution)/shard_map/pallas_call | solution.py:644
  64.4 56.7 %shard_map.204 = (bf16[4,4,128,1536]{3,2,1,0:T(8,128)(2,1)S(1)}, f32[4,4,16,128]{3,2,1,0:T(8,128)S(1)}) custom-call(bf16[4,128,1536]{2,1,0:T(8,128)(2,1)S(1)} %copy-done.16, f32[4,16,128]{2,1,0:T(8,128)S(1)} %get-tuple-element.70.refs_1_), custom_call_target="tpu_custom_call" | custom-call | tf_op jit(solution)/shard_map/pallas_call | solution.py:1229
  121.2 5.1 shard_map.205
  126.3 93.2 %shard_map.207 = (bf16[4,4,128,1024]{3,2,1,0:T(8,128)(2,1)S(1)}, bf16[4,512,512]{2,1,0:T(8,128)(2,1)S(1)}, bf16[4,2,256,2048]{3,2,1,0:T(8,128)(2,1)S(1)}) custom-call(bf16[4,128,1024]{2,1,0:T(8,128)(2,1)S(1)} %get-tuple-element.75.refs_0_, bf16[512,512]{1,0:T(8,128)(2,1)S(1)} %get-tuple-element.76.refs_1_, bf16[512,2048]{1,0:T(8,128)(2,1)S(1)} %shard_map.206.refs_2_), custom_call_target="tpu_custom_call" | custom-call | tf_op jit(solution)/shard_map/pallas_call | solution.py:1229
  229.6 17.4 %shard_map.208 = (bf16[512,1024]{1,0:T(8,128)(2,1)S(1)}, f32[512,256]{1,0:T(8,128)S(1)}) custom-call(s32[2]{0:T(128)S(1)} %copy-done.24, bf16[512,1024]{1,0:T(8,128)(2,1)S(1)} %copy-done.36, bf16[4,512,512]{2,1,0:T(8,128)(2,1)S(1)} %copy-done.31, bf16[4,512,512]{2,1,0:T(8,128)(2,1)S(1)} %copy-done.31, bf16[4,512,512]{2,1,0:T(8,128)(2,1)S(1)} %copy-done.31, ...), custom_call_target="tpu_custom_call" | custom-call | flops 8589934592 | bytes 6291456 | tf_op jit(solution)/shard_map/pallas_call | solution.py:424
  249.4 4.1 collective-permute-done.other_ref
  257.6 40.4 %shard_map.210 = bf16[4,2,256,2048]{3,2,1,0:T(8,128)(2,1)S(1)} custom-call(bf16[512,2048]{1,0:T(8,128)(2,1)S(1)} %get-tuple-element.82.v_ref), custom_call_target="tpu_custom_call" | custom-call | tf_op jit(solution)/shard_map/pallas_call | solution.py:788
  298.0 3.3 copy-done
  301.4 33.7 %shard_map.211 = (bf16[2048,512]{1,0:T(8,128)(2,1)}, bf16[2048,1024]{1,0:T(8,128)(2,1)}, bf16[2048,2048]{1,0:T(8,128)(2,1)}, bf16[2048,2048]{1,0:T(8,128)(2,1)}) custom-call(bf16[2048,2048]{1,0:T(8,128)(2,1)} %bitcast.71, bf16[2048,2048]{1,0:T(8,128)(2,1)} %bitcast.87, bf16[2048,1536]{1,0:T(8,128)(2,1)} %bitcast.115), custom_call_target="tpu_custom_call" | custom-call | flops 25769803776 | bytes 46137344 | tf_op jit(solution)/shard_map/pallas_call | solution.py:399
  335.0 14.1 %convolution_convert_fusion.2 = bf16[2048,1024]{1,0:T(8,128)(2,1)} fusion(bf16[2048,2048]{1,0:T(8,128)(2,1)} %bitcast.72, bf16[2048,1024]{1,0:T(8,128)(2,1)} %get-tuple-element.88), kind=kOutput, calls=%fused_computation.2 | convolution fusion | flops 8592031744 | bytes 16777216 | tf_op jit(solution)/shard_map/td,tf->df/dot_general | solution.py:1796
  349.3 64.2 %shard_map.212 = (bf16[2048,512]{1,0:T(8,128)(2,1)}, bf16[2048,1024]{1,0:T(8,128)(2,1)}, bf16[1024,2048]{1,0:T(8,128)(2,1)}, bf16[2,256,2048]{2,1,0:T(8,128)(2,1)}, bf16[2048,512]{1,0:T(8,128)(2,1)}) custom-call(bf16[2048,2048]{1,0:T(8,128)(2,1)} %bitcast.73, bf16[2048,2048]{1,0:T(8,128)(2,1)} %bitcast.88, bf16[2048,1536]{1,0:T(8,128)(2,1)} %bitcast.116, ...), custom_call_target="tpu_custom_call" | custom-call | flops 25769803776 | bytes 52428800 | tf_op jit(solution)/shard_map/pallas_call | solution.py:1014
  415.2 5.8 shard_map.213
  425.1 44.1 %shard_map.214 = (bf16[512,1024]{1,0:T(8,128)(2,1)S(1)}, bf16[4,2,512,256]{3,2,1,0:T(8,128)(2,1)S(1)}, bf16[2,256,2048]{2,1,0:T(8,128)(2,1)S(1)}) custom-call(s32[2]{0:T(128)S(1)} %copy-done.24, bf16[512,1024]{1,0:T(8,128)(2,1)S(1)} %copy-done.37, bf16[512,1024]{1,0:T(8,128)(2,1)S(1)} %convolution_convert_fusion.6.do_ref, ...), custom_call_target="tpu_custom_call" | custom-call | flops 21474836480 | bytes 10485760 | tf_op jit(solution)/shard_map/pallas_call | solution.py:455
  469.3 10.9 %convolution_convert_fusion.5 = bf16[2048,512]{1,0:T(8,128)(2,1)} fusion(bf16[2048,2048]{1,0:T(8,128)(2,1)} %bitcast.90, bf16[2048,512]{1,0:T(8,128)(2,1)S(1)} %copy-done.47), kind=kOutput, calls=%fused_computation.5 | convolution fusion | flops 4296015872 | bytes 12582912 | tf_op jit(solution)/shard_map/td,tf->df/dot_general | solution.py:1796
  481.4 5.9 convolution_convert_fusion.1
  487.3 97.0 %shard_map.216 = (f32[128,1024]{1,0:T(8,128)}, bf16[512,512]{1,0:T(8,128)(2,1)}, bf16[2048,1024]{1,0:T(8,128)(2,1)}) custom-call(bf16[4,4,128,1024]{3,2,1,0:T(8,128)(2,1)} %bitcast.98, bf16[4,2,512,256]{3,2,1,0:T(8,128)(2,1)} %copy-done.9, f32[256,128]{1,0:T(8,128)} %copy-done.20, f32[256,128]{1,0:T(8,128)} %copy-done.21, bf16[2048,2048]{1,0:T(8,128)(2,1)} %bitcast.74, ...), custom_call_target="tpu_custom_call" | custom-call | tf_op jit(solution)/shard_map/pallas_call | solution.py:1574
  585.5 8.1 %convolution_convert_fusion.4.part_ref = bf16[512,2048]{1,0:T(8,128)(2,1)} fusion(bf16[512,1536]{1,0:T(8,128)(2,1)S(1)} %constant_dynamic-update-slice_fusion, bf16[2048,1536]{1,0:T(8,128)(2,1)} %bitcast.92), kind=kOutput, calls=%fused_computation.4 | convolution fusion | flops 3222274048 | bytes 9961472 | tf_op jit(solution)/shard_map/tj,dj->td/dot_general | solution.py:1903
  597.3 4.0 all-to-all-start
  601.3 8.3 %convolution_convert_fusion = bf16[2048,1536]{1,0:T(8,128)(2,1)} fusion(bf16[512,2048]{1,0:T(8,128)(2,1)} %copy-done.34, bf16[512,1536]{1,0:T(8,128)(2,1)} %copy-done.40), kind=kOutput, calls=%fused_computation | convolution fusion | flops 3224371200 | bytes 9961472 | tf_op jit(solution)/shard_map/td,tj->dj/dot_general | solution.py:1902
  609.7 6.0 shard_map.217
  616.3 5.7 all-to-all-done
  622.0 74.5 %shard_map.218 = (f32[128,1536]{1,0:T(8,128)}, f32[16,128]{1,0:T(8,128)}) custom-call(bf16[4,4,128,1536]{3,2,1,0:T(8,128)(2,1)} %bitcast.95, f32[4,4,16,128]{3,2,1,0:T(8,128)} %bitcast.108), custom_call_target="tpu_custom_call" | custom-call | tf_op jit(solution)/shard_map/pallas_call | solution.py:1574
  699.2 4.2 all-to-all-start.1
  713.6 7.3 %all-to-all-done.1 = bf16[4,384,512]{2,1,0:T(8,128)(2,1)S(1)} async-done(((bf16[4,384,512]{2,1,0:T(8,128)(2,1)}), bf16[4,384,512]{2,1,0:T(8,128)(2,1)S(1)}, u32[]{:S(2)}, u32[]{:S(2)}) %all-to-all-start.1) | async-done | bytes 1572896 | tf_op jit(solution)/shard_map/all_to_all | solution.py:1816
  (148 shorter events, 55.7 us)
Async XLA Ops:
  7.2 294.1 %all-gather.7.cloned.1.call-start = ((), (), s32[]{:S(2)}) async-start(), calls=%async_computation.11 | async-start | bytes 7864320 | tf_op jit(solution)/shard_map/all_gather | solution.py:1747
  60.8 288.4 %all-gather.5.cloned.1.call-start = ((), (), s32[]{:S(2)}) async-start(), calls=%async_computation.10 | async-start | bytes 7864320 | tf_op jit(solution)/shard_map/all_gather | solution.py:1747
  61.3 362.9 %copy-start.20 = (f32[256,128]{1,0:T(8,128)}, f32[256,128]{1,0:T(8,128)S(1)}, u32[]{:S(2)}) copy-start(f32[256,128]{1,0:T(8,128)S(1)} %copy.52.cos_ref.refs_2_) | copy-start | bytes 393220
  62.9 361.2 %copy-start.21 = (f32[256,128]{1,0:T(8,128)}, f32[256,128]{1,0:T(8,128)S(1)}, u32[]{:S(2)}) copy-start(f32[256,128]{1,0:T(8,128)S(1)} %copy.53.sin_ref.refs_3_) | copy-start | bytes 393220
  63.0 58.2 %copy-start.4 = (bf16[2,256,2048]{2,1,0:T(8,128)(2,1)S(1)}, bf16[2,256,2048]{2,1,0:T(8,128)(2,1)}, u32[]{:S(2)}) copy-start(bf16[2,256,2048]{2,1,0:T(8,128)(2,1)} %param.12) | copy-start | bytes 6291460
  126.3 93.3 %copy-start.34 = (bf16[512,2048]{1,0:T(8,128)(2,1)}, bf16[512,2048]{1,0:T(8,128)(2,1)S(1)}, u32[]{:S(2)}) copy-start(bf16[512,2048]{1,0:T(8,128)(2,1)S(1)} %get-tuple-element.108) | copy-start | bytes 6291460
  126.3 93.3 %copy-start.35 = (bf16[512,1024]{1,0:T(8,128)(2,1)}, bf16[512,1024]{1,0:T(8,128)(2,1)S(1)}, u32[]{:S(2)}) copy-start(bf16[512,1024]{1,0:T(8,128)(2,1)S(1)} %get-tuple-element.73.q_ref) | copy-start | bytes 3145732
  226.2 367.4 %reduce-scatter.5.cloned.1.call-start = ((), (), s32[]{:S(2)}) async-start(), calls=%async_computation.6 | async-start | bytes 5242880 | tf_op jit(solution)/shard_map/reduce_scatter | solution.py:1800
  229.6 17.4 %copy-start.28 = (bf16[4,4,128,1024]{3,2,1,0:T(8,128)(2,1)S(1)}, bf16[4,4,128,1024]{3,2,1,0:T(8,128)(2,1)}, u32[]{:S(2)}) copy-start(bf16[4,4,128,1024]{3,2,1,0:T(8,128)(2,1)} %copy-done.27) | copy-start | bytes 12582916
  247.0 6.6 copy-start.5
  249.4 4.2 collective-permute-start
  349.2 245.8 %reduce-scatter.7.cloned.1.call-start = ((), (), s32[]{:S(2)}) async-start(), calls=%async_computation.7 | async-start | bytes 2621440 | tf_op jit(solution)/shard_map/reduce_scatter | solution.py:1800
  413.5 283.0 %reduce-scatter.11.cloned.1.call-start = ((), (), s32[]{:S(2)}) async-start(), calls=%async_computation.9 | async-start | bytes 2621440 | tf_op jit(solution)/shard_map/reduce_scatter | solution.py:1800
  425.1 44.1 %copy-start.47 = (bf16[2048,512]{1,0:T(8,128)(2,1)S(1)}, bf16[2048,512]{1,0:T(8,128)(2,1)}, u32[]{:S(2)}) copy-start(bf16[2048,512]{1,0:T(8,128)(2,1)} %get-tuple-element.102) | copy-start | bytes 6291460
  469.2 11.0 %copy-start.9 = (bf16[4,2,512,256]{3,2,1,0:T(8,128)(2,1)}, bf16[4,2,512,256]{3,2,1,0:T(8,128)(2,1)S(1)}, u32[]{:S(2)}) copy-start(bf16[4,2,512,256]{3,2,1,0:T(8,128)(2,1)S(1)} %get-tuple-element.103.refs_1_) | copy-start | bytes 6291460
  469.2 10.9 %copy-start.11 = (bf16[2,256,2048]{2,1,0:T(8,128)(2,1)}, bf16[2,256,2048]{2,1,0:T(8,128)(2,1)S(1)}, u32[]{:S(2)}) copy-start(bf16[2,256,2048]{2,1,0:T(8,128)(2,1)S(1)} %get-tuple-element.96) | copy-start | bytes 6291460
  480.2 216.3 %reduce-scatter.9.cloned.1.call-start = ((), (), s32[]{:S(2)}) async-start(), calls=%async_computation.8 | async-start | bytes 5242880 | tf_op jit(solution)/shard_map/reduce_scatter | solution.py:1800
  585.5 8.1 %copy-start.40 = (bf16[512,1536]{1,0:T(8,128)(2,1)}, bf16[512,1536]{1,0:T(8,128)(2,1)S(1)}, u32[]{:S(2)}) copy-start(bf16[512,1536]{1,0:T(8,128)(2,1)S(1)} %constant_dynamic-update-slice_fusion) | copy-start | bytes 4718596
  593.6 16.0 %collective-permute-start.1 = (bf16[512,2048]{1,0:T(8,128)(2,1)}, bf16[512,2048]{1,0:T(8,128)(2,1)}, u32[]{:S(2)}, u32[]{:S(2)}) collective-permute-start(bf16[512,2048]{1,0:T(8,128)(2,1)} %convolution_convert_fusion.4.part_ref), channel_id=1, source_target_pairs={{0,1},{1,0},{2,3},{3,2},{4,5},{5,4},{6,7},{7,6},{8,9},{9,8},{10,11... | collective-permute-start | bytes 6291464 | tf_op jit(solution)/shard_map/ppermute | solution.py:1698
  597.3 24.7 %all-to-all-start = ((bf16[4,384,512]{2,1,0:T(8,128)(2,1)}), bf16[4,384,512]{2,1,0:T(8,128)(2,1)S(1)}, u32[]{:S(2)}, u32[]{:S(2)}) async-start(bf16[4,384,512]{2,1,0:T(8,128)(2,1)} %pad_maximum_fusion), calls=%async_computation.2 | async-start | bytes 3145728 | tf_op jit(solution)/shard_map/all_to_all | solution.py:1816
  601.3 8.3 %copy-start.6 = (bf16[2,256,2048]{2,1,0:T(8,128)(2,1)S(1)}, bf16[2,256,2048]{2,1,0:T(8,128)(2,1)}, u32[]{:S(2)}) copy-start(bf16[2,256,2048]{2,1,0:T(8,128)(2,1)} %param.12) | copy-start | bytes 6291460
  601.3 8.3 %copy-start.8 = (f32[512,2048]{1,0:T(8,128)S(1)}, f32[512,2048]{1,0:T(8,128)}, u32[]{:S(2)}) copy-start(f32[512,2048]{1,0:T(8,128)} %copy-done.7) | copy-start | bytes 12582916
  601.3 8.3 %copy-start.23 = (f32[1,2048]{1,0:T(1,128)S(1)}, f32[1,2048]{1,0:T(1,128)}, u32[]{:S(2)}) copy-start(f32[1,2048]{1,0:T(1,128)} %copy-done.22) | copy-start | bytes 24580
  699.2 21.8 %all-to-all-start.1 = ((bf16[4,384,512]{2,1,0:T(8,128)(2,1)}), bf16[4,384,512]{2,1,0:T(8,128)(2,1)S(1)}, u32[]{:S(2)}, u32[]{:S(2)}) async-start(bf16[4,384,512]{2,1,0:T(8,128)(2,1)} %pad_maximum_fusion.1), calls=%async_computation.5 | async-start | bytes 3145728 | tf_op jit(solution)/shard_map/all_to_all | solution.py:1816
  (34 other events, 82.7 us)
Sparse Core Ops, SparseCore 0:
  61.0 127.7 all-gather.6
  226.3 112.8 all-gather.4
  349.3 76.4 reduce-scatter.4
  428.0 43.1 reduce-scatter.6
  480.3 71.8 reduce-scatter.10
  584.5 86.1 reduce-scatter.8
